TPU v7x, 32 devices: a whole 2x2x4 slice. The times are simulated.
32 devices in a mesh: dp: 16 (over z, x, core), blk: 2 (over y).
Axes of the slice: x: 2, y: 2, z: 4, core: 2. Of those that a mesh axis runs over, the one named last changes fastest.
Arguments:
- waveform: bfloat16 [512, 330], P(('dp', 'blk')), may hold values from -6 to 6
- length_bin: int32 [512], P(('dp', 'blk')), may hold values from 1 to 4
- packing: int32 [32, 16], P(('dp', 'blk')), may hold values from 0 to 15, each once within a row
- cotangent: bfloat16 [512, 32, 512], P(('dp', 'blk')), may hold values from -6 to 6
- conv_one: bfloat16 [10, 512], replicated, may hold values from -2 to 2
- bias_one: float32 [512], replicated, may hold values from -6 to 6
- gain_one: float32 [512], replicated, may hold values from 2 to 8
- shift_one: float32 [512], replicated, may hold values from -12 to 12
- conv_two: bfloat16 [1536, 512], replicated, may hold values from -0.15625 to 0.15625
- bias_two: float32 [512], replicated, may hold values from -6 to 6
- gain_two: float32 [512], replicated, may hold values from 0.5 to 1.5
- shift_two: float32 [512], replicated, may hold values from -3 to 3
Outputs:
- grad_conv_two: float32 [1536, 512], P('dp')
- grad_small: float32 [16, 512], replicated
All inputs are finite; a program needn't handle non-finite values.
Results may differ from a plain program's by a relative error of at most 0.0046.
Values may be sent and summed in bfloat16 or wider, within the bound.
No kernel may reach another device: no remote copies, remote signals or barrier semaphores. Data moves between devices by JAX's collectives and lax.ppermute only.
A program may use at most 64 MiB of HBM per device.

v0:
```python
import jax
import jax.numpy as jnp
from jax import lax
from jax.sharding import PartitionSpec as P

NB = 4
GROUP = 8


def norm_act(z, gain, shift):
    mean = jnp.mean(z, axis=-1, keepdims=True)
    cent = z - mean
    var = jnp.mean(cent * cent, axis=-1, keepdims=True)
    rstd = lax.rsqrt(var + 1e-05)
    normed = cent * rstd
    return (normed * gain + shift, normed, rstd)


def gelu_exact(act):
    return 0.5 * act * (1.0 + lax.erf(act * 0.7071067811865476))


def norm_back(grad_out, act, normed, rstd, gain):
    cdf = 0.5 * (1.0 + lax.erf(act * 0.7071067811865476))
    pdf = jnp.exp(-0.5 * act * act) * 0.3989422804014327
    grad_act = grad_out * (cdf + act * pdf)
    grad_gain = jnp.sum(grad_act * normed, axis=0)
    grad_shift = jnp.sum(grad_act, axis=0)
    grad_norm = grad_act * gain
    inner = grad_norm - jnp.mean(grad_norm, axis=-1, keepdims=True)
    inner = inner - normed * jnp.mean(grad_norm * normed, axis=-1, keepdims=True)
    return (rstd * inner, grad_gain, grad_shift)


def pass_group(
    wave,
    bins,
    cot,
    conv_one,
    bias_one,
    gain_one,
    shift_one,
    conv_two,
    bias_two,
    gain_two,
    shift_two,
):
    count = wave.shape[0]
    frames_two = cot.shape[1]
    width = cot.shape[2]
    frames_one = 2 * frames_two + 1
    split = wave.reshape(count, frames_one + 1, 5)
    cols_one = jnp.concatenate([split[:, :-1], split[:, 1:]], axis=-1).reshape(
        count * frames_one, 10
    )
    z_one = jnp.dot(cols_one, conv_one, preferred_element_type=jnp.float32) + bias_one
    act_one, normed_one, rstd_one = norm_act(z_one, gain_one, shift_one)
    hidden = gelu_exact(act_one).astype(jnp.bfloat16).reshape(count, frames_one, width)
    cols_two = jnp.concatenate(
        [hidden[:, : 2 * frames_two].reshape(count, frames_two, 2 * width), hidden[:, 2::2]],
        axis=-1,
    )
    cols_two = cols_two.reshape(count * frames_two, 3 * width)
    z_two = jnp.dot(cols_two, conv_two, preferred_element_type=jnp.float32) + bias_two
    act_two, normed_two, rstd_two = norm_act(z_two, gain_two, shift_two)
    limit = bins * frames_two // NB
    valid = (jnp.arange(frames_two, dtype=jnp.int32)[None, :] < limit[:, None]).astype(jnp.float32)
    grad_out = (cot.astype(jnp.float32) * valid[:, :, None]).reshape(count * frames_two, width)
    dz_two, dgain_two, dshift_two = norm_back(grad_out, act_two, normed_two, rstd_two, gain_two)
    dbias_two = jnp.sum(dz_two, axis=0)
    dz_two_b = dz_two.astype(jnp.bfloat16)
    dcols = jnp.dot(dz_two_b, conv_two.T, preferred_element_type=jnp.float32).reshape(
        count, frames_two, 3 * width
    )
    part_a = dcols[:, :, : 2 * width].reshape(count, 2 * frames_two, width)
    part_b = dcols[:, :, 2 * width :]
    spread = jnp.stack([part_b, jnp.zeros_like(part_b)], axis=2).reshape(
        count, 2 * frames_two, width
    )
    zero_one = jnp.zeros((count, 1, width), jnp.float32)
    zero_two = jnp.zeros((count, 2, width), jnp.float32)
    dhidden = jnp.concatenate([part_a, zero_one], axis=1) + jnp.concatenate(
        [zero_two, spread[:, : 2 * frames_two - 1]], axis=1
    )
    dz_one, dgain_one, dshift_one = norm_back(
        dhidden.reshape(count * frames_one, width), act_one, normed_one, rstd_one, gain_one
    )
    dbias_one = jnp.sum(dz_one, axis=0)
    dconv_one = jnp.dot(cols_one.T, dz_one.astype(jnp.bfloat16), preferred_element_type=jnp.float32)
    small = jnp.concatenate(
        [
            dconv_one,
            jnp.stack([dbias_one, dgain_one, dshift_one, dbias_two, dgain_two, dshift_two]),
        ],
        axis=0,
    )
    return (cols_two, dz_two_b, small)


def per_device(
    waveform,
    length_bin,
    packing,
    cotangent,
    conv_one,
    bias_one,
    gain_one,
    shift_one,
    conv_two,
    bias_two,
    gain_two,
    shift_two,
):
    order_list = packing[0]
    sent_wave = waveform[order_list]
    sent_bins = length_bin[order_list]
    wave, bins = (
        lax.all_to_all(sent_wave, "dp", split_axis=0, concat_axis=0, tiled=True),
        lax.all_to_all(sent_bins, "dp", split_axis=0, concat_axis=0, tiled=True),
    )
    count = wave.shape[0]
    record = wave.shape[1]
    frames_two = cotangent.shape[1]
    width = cotangent.shape[2]
    groups = count // GROUP
    xs = (
        wave.reshape(groups, GROUP, record),
        bins.reshape(groups, GROUP),
        cotangent.reshape(groups, GROUP, frames_two, width),
    )

    def step(small_sum, item):
        cols_two, dz_two_b, small = pass_group(
            item[0],
            item[1],
            item[2],
            conv_one,
            bias_one,
            gain_one,
            shift_one,
            conv_two,
            bias_two,
            gain_two,
            shift_two,
        )
        return (small_sum + small, (cols_two, dz_two_b))

    small_local, stacked = lax.scan(step, jnp.zeros((16, width), jnp.float32), xs)
    cols_all = stacked[0].reshape(count * frames_two, 3 * width)
    dz_all = stacked[1].reshape(count * frames_two, width)
    term = lax.dot_general(
        cols_all, dz_all, (((0,), (0,)), ((), ())), preferred_element_type=jnp.float32
    )
    whole = lax.psum(term, "blk")
    share = lax.psum_scatter(whole, "dp", scatter_dimension=0, tiled=True)
    small_total = lax.psum(small_local, ("dp", "blk"))
    return (share, small_total)


def solution(mesh):
    return jax.shard_map(
        per_device,
        mesh=mesh,
        in_specs=(
            P(("dp", "blk"), None),
            P(("dp", "blk")),
            P(("dp", "blk"), None),
            P(("dp", "blk"), None, None),
            P(),
            P(),
            P(),
            P(),
            P(),
            P(),
            P(),
            P(),
        ),
        out_specs=(P("dp", None), P()),
        check_vma=False,
    )
```

profile of v0, /device:TPU:0, one launch (start us, length us, event | category | flops | bytes accessed | tf_op | source)
XLA Modules:
  0.0 192.3 jit_solution(11816954975854196462)
XLA Ops:
  7.9 1.3 gather_fusion.1
  9.9 7.4 %all-to-all-start.1 = ((s32[16,1,1]{2,1,0:T(1,128)}), s32[16,1,1]{2,1,0:T(1,128)S(1)}, u32[]{:S(2)}, u32[]{:S(2)}) async-start(s32[16,1,1]{2,1,0:T(1,128)} %copy.29), calls=%async_computation.1 | async-start | bytes 16384 | tf_op jit(solution)/shard_map/all_to_all | solution.py:119
  19.7 3.9 %all-to-all-done.1 = s32[16,1,1]{2,1,0:T(1,128)S(1)} async-done(((s32[16,1,1]{2,1,0:T(1,128)}), s32[16,1,1]{2,1,0:T(1,128)S(1)}, u32[]{:S(2)}, u32[]{:S(2)}) %all-to-all-start.1) | async-done | bytes 96 | tf_op jit(solution)/shard_map/all_to_all | solution.py:119
  23.6 3.5 %all-to-all-start = ((bf16[16,2,165]{2,1,0:T(2,128)(2,1)}), bf16[16,2,165]{2,1,0:T(2,128)(2,1)S(1)}, u32[]{:S(2)}, u32[]{:S(2)}) async-start(bf16[16,2,165]{2,1,0:T(2,128)(2,1)} %reshape.260), calls=%async_computation | async-start | bytes 32768 | tf_op jit(solution)/shard_map/all_to_all | solution.py:118
  28.2 5.3 %all-to-all-done = bf16[16,2,165]{2,1,0:T(2,128)(2,1)S(1)} async-done(((bf16[16,2,165]{2,1,0:T(2,128)(2,1)}), bf16[16,2,165]{2,1,0:T(2,128)(2,1)S(1)}, u32[]{:S(2)}, u32[]{:S(2)}) %all-to-all-start) | async-done | bytes 10592 | tf_op jit(solution)/shard_map/all_to_all | solution.py:118
  34.2 41.1 %while.17 = (s32[]{:T(128)}, f32[16,512]{1,0:T(8,128)}, bf16[2,256,1536]{2,1,0:T(8,128)(2,1)}, bf16[2,256,512]{2,1,0:T(8,128)(2,1)}, bf16[2,8,330]{2,1,0:T(8,128...) while((s32[]{:T(128)}, f32[16,512]{1,0:T(8,128)}, ...), condition=%wide.region_15.16_spmd.clone, body=%wide.region_0.15_spmd.clone.sunk | while | flops 835685888 | bytes 56027588 | solution.py:148
  39.0 2.1 %fusion.59 = (f32[256]{0:T(256)S(1)}, f32[256,512]{1,0:T(8,128)S(1)}) fusion(f32[512]{0:T(512)S(1)} %copy-done.11, bf16[1536,512]{1,0:T(8,128)(2,1)} %get-tuple-element.475, bf16[256,512]{1,0:T(8,128)(2,1)S(1)} %bitcast.85, bf16[256,1024]{1,0:T(8,128)(2,1)S(1)} %concatenate.58), kind=kOutput, calls=%fused_computation.73.clone.1 | convolution fusion | flops 404487936 | bytes 2886656 | tf_op jit(solution)/shard_map/while/body/eval_jaxpr/dot_general | solution.py:64
  43.3 0.9 maximum_dynamic-update-slice_fusion.2
  45.6 0.8 slice_bitcast_fusion.2
  46.7 1.6 copy.42
  48.6 1.7 reshape.273
  50.4 1.5 pad_add_fusion.2
  52.0 1.1 multiply_reduce_fusion.15
  59.2 2.1 %fusion.59 = (f32[256]{0:T(256)S(1)}, f32[256,512]{1,0:T(8,128)S(1)}) fusion(f32[512]{0:T(512)S(1)} %copy-done.11, bf16[1536,512]{1,0:T(8,128)(2,1)} %get-tuple-element.475, bf16[256,512]{1,0:T(8,128)(2,1)S(1)} %bitcast.85, bf16[256,1024]{1,0:T(8,128)(2,1)S(1)} %concatenate.58), kind=kOutput, calls=%fused_computation.73.clone.1 | convolution fusion | flops 404487936 | bytes 2886656 | tf_op jit(solution)/shard_map/while/body/eval_jaxpr/dot_general | solution.py:64
  63.5 0.9 maximum_dynamic-update-slice_fusion.2
  66.9 1.6 copy.42
  68.8 1.7 reshape.273
  70.6 1.5 pad_add_fusion.2
  72.2 1.1 multiply_reduce_fusion.15
  74.0 1.4 select_add_fusion.2
  75.4 4.2 %convolution_bitcast_fusion = f32[1536,512]{1,0:T(8,128)} fusion(bf16[2,256,1536]{2,1,0:T(8,128)(2,1)} %get-tuple-element.190, bf16[2,256,512]{2,1,0:T(8,128)(2,1)} %get-tuple-element.191), kind=kOutput, calls=%fused_computation.65 | convolution fusion | flops 805306368 | bytes 5242880 | tf_op jit(solution)/shard_map/dot_general | solution.py:151
  79.6 63.6 %reduce-scatter.2.cloned.1.call-done = f32[96,512]{1,0:T(8,128)} async-done(((f32[1536,512]{1,0:T(8,128)}), f32[96,512]{1,0:T(8,128)}) %reduce-scatter.2.cloned.1.call-update) | async-done | bytes 196624 | tf_op jit(solution)/shard_map/reduce_scatter | solution.py:155
  143.3 40.6 %psum.15 = f32[16,512]{1,0:T(8,128)} all-reduce(f32[16,512]{1,0:T(8,128)} %get-tuple-element.192), channel_id=1, replica_groups=mesh['dp'=16,'blk'=2] {'dp','blk'}, use_global_device_ids=true, to_apply=%region_18.19 | all-reduce | flops 8192 | bytes 65536 | tf_op jit(solution)/shard_map/psum | solution.py:156
  183.9 1.6 copy.58
  (143 shorter events, 26.2 us)
Async XLA Ops:
  7.2 10.1 %copy-start = (bf16[16,330]{1,0:T(8,128)(2,1)S(1)}, bf16[16,330]{1,0:T(8,128)(2,1)}, u32[]{:S(2)}) copy-start(bf16[16,330]{1,0:T(8,128)(2,1)} %param.14) | copy-start | bytes 31684
  9.9 13.7 %all-to-all-start.1 = ((s32[16,1,1]{2,1,0:T(1,128)}), s32[16,1,1]{2,1,0:T(1,128)S(1)}, u32[]{:S(2)}, u32[]{:S(2)}) async-start(s32[16,1,1]{2,1,0:T(1,128)} %copy.29), calls=%async_computation.1 | async-start | bytes 16384 | tf_op jit(solution)/shard_map/all_to_all | solution.py:119
  23.6 10.0 %all-to-all-start = ((bf16[16,2,165]{2,1,0:T(2,128)(2,1)}), bf16[16,2,165]{2,1,0:T(2,128)(2,1)S(1)}, u32[]{:S(2)}, u32[]{:S(2)}) async-start(bf16[16,2,165]{2,1,0:T(2,128)(2,1)} %reshape.260), calls=%async_computation | async-start | bytes 32768 | tf_op jit(solution)/shard_map/all_to_all | solution.py:118
  27.1 116.2 %reduce-scatter.2.cloned.1.call-start = ((), (), s32[]{:S(2)}) async-start(), calls=%async_computation.3 | async-start | bytes 3342336 | tf_op jit(solution)/shard_map/reduce_scatter | solution.py:155
  34.2 2.3 %copy-start.2 = (bf16[2,8,32,512]{3,2,1,0:T(8,128)(2,1)S(1)}, bf16[2,8,32,512]{3,2,1,0:T(8,128)(2,1)}, u32[]{:S(2)}) copy-start(bf16[2,8,32,512]{3,2,1,0:T(8,128)(2,1)} %get-tuple-element.477) | copy-start | bytes 1572868 | tf_op jit(solution)/shard_map/while
  34.2 2.3 %copy-start.4 = (bf16[10,512]{1,0:T(8,128)(2,1)S(1)}, bf16[10,512]{1,0:T(8,128)(2,1)}, u32[]{:S(2)}) copy-start(bf16[10,512]{1,0:T(8,128)(2,1)} %get-tuple-element.471) | copy-start | bytes 30724 | tf_op jit(solution)/shard_map/while
  34.2 2.3 %copy-start.7 = (f32[512]{0:T(512)S(1)}, f32[512]{0:T(512)}, u32[]{:S(2)}) copy-start(f32[512]{0:T(512)} %get-tuple-element.472) | copy-start | bytes 6148 | tf_op jit(solution)/shard_map/while
  36.5 0.8 copy-start.3
  36.5 0.8 copy-start.5
  39.0 2.3 %copy-start.6 = (f32[512]{0:T(512)S(1)}, f32[512]{0:T(512)}, u32[]{:S(2)}) copy-start(f32[512]{0:T(512)} %get-tuple-element.479) | copy-start | bytes 6148 | tf_op jit(solution)/shard_map/while
  39.0 2.3 %copy-start.8 = (f32[512]{0:T(512)S(1)}, f32[512]{0:T(512)}, u32[]{:S(2)}) copy-start(f32[512]{0:T(512)} %get-tuple-element.480) | copy-start | bytes 6148 | tf_op jit(solution)/shard_map/while
  41.1 1.0 copy-start.9
  42.4 0.8 copy-start.10
  43.3 1.7 copy-start.1
  54.4 2.3 %copy-start.2 = (bf16[2,8,32,512]{3,2,1,0:T(8,128)(2,1)S(1)}, bf16[2,8,32,512]{3,2,1,0:T(8,128)(2,1)}, u32[]{:S(2)}) copy-start(bf16[2,8,32,512]{3,2,1,0:T(8,128)(2,1)} %get-tuple-element.477) | copy-start | bytes 1572868 | tf_op jit(solution)/shard_map/while
  54.4 2.3 %copy-start.4 = (bf16[10,512]{1,0:T(8,128)(2,1)S(1)}, bf16[10,512]{1,0:T(8,128)(2,1)}, u32[]{:S(2)}) copy-start(bf16[10,512]{1,0:T(8,128)(2,1)} %get-tuple-element.471) | copy-start | bytes 30724 | tf_op jit(solution)/shard_map/while
  54.4 2.3 %copy-start.7 = (f32[512]{0:T(512)S(1)}, f32[512]{0:T(512)}, u32[]{:S(2)}) copy-start(f32[512]{0:T(512)} %get-tuple-element.472) | copy-start | bytes 6148 | tf_op jit(solution)/shard_map/while
  56.7 0.8 copy-start.3
  59.2 2.3 %copy-start.6 = (f32[512]{0:T(512)S(1)}, f32[512]{0:T(512)}, u32[]{:S(2)}) copy-start(f32[512]{0:T(512)} %get-tuple-element.479) | copy-start | bytes 6148 | tf_op jit(solution)/shard_map/while
  59.2 2.3 %copy-start.8 = (f32[512]{0:T(512)S(1)}, f32[512]{0:T(512)}, u32[]{:S(2)}) copy-start(f32[512]{0:T(512)} %get-tuple-element.480) | copy-start | bytes 6148 | tf_op jit(solution)/shard_map/while
  61.3 1.0 copy-start.9
  62.6 0.8 copy-start.10
  63.5 1.7 copy-start.1
  79.6 104.3 %all-reduce.5.cloned.1.call-start = ((), (), s32[]{:S(2)}) async-start(), calls=%async_computation.4 | async-start | bytes 393216 | tf_op jit(solution)/shard_map/psum | solution.py:154
  (3 other events, 2.1 us)
Sparse Core Ops, SparseCore 0:
  79.7 63.4 reduce-scatter.1
  145.5 21.4 all-reduce.4
where the time goes:
time: 193 us; the launch traced here: 192 us
  waiting for transfers between devices  72.8 us (38%)
  blocking collectives  40.6 us (21%)
  local copies, waits for them, and re-layouts  25.6 us (13%)
  other arithmetic  16.9 us (9%)
  between operations  14.1 us (7%)
  starting transfers between devices  10.9 us (6%)
  matrix products  10.8 us (6%)
    reduce_scatter x1, waiting for transfers between devices, per_device(): share = lax.psum_scatter(whole, 'dp', scatter_dimension=0, tiled=True)  63.6 us
    psum x1, blocking collectives, per_device(): small_total = lax.psum(small_local, ('dp', 'blk'))  40.6 us
    all_to_all x1, starting transfers between devices, per_device(): lax.all_to_all(sent_bins, 'dp', split_axis=0, concat_axis=0, tiled=True)  7.36 us
    while x46, local copies, waits for them, and re-layouts  7.26 us
    all_to_all x1, waiting for transfers between devices, per_device(): lax.all_to_all(sent_wave, 'dp', split_axis=0, concat_axis=0, tiled=True)  5.32 us
    dot_general x2, matrix products, pass_group(): jnp.dot(cols_two, conv_two, preferred_element_type=jnp.float32) + bias_two  4.2 us
    dot_general x1, matrix products, per_device(): lax.dot_general(cols_all, dz_all, (((0,), (0,)), ((), ())), preferred_ele...  4.2 us
    all_to_all x1, waiting for transfers between devices, per_device(): lax.all_to_all(sent_bins, 'dp', split_axis=0, concat_axis=0, tiled=True)  3.87 us
  transfers between devices with their start and end apart: 4, of which 3 were waited for; matrix products, arithmetic and copies ran while one was open for 2% of the time, Pallas kernels for 0%

commit v1 on v0

v1 whole, which is shorter than its diff:
```python
import functools
import math

import jax
import jax.numpy as jnp
from jax import lax
from jax.experimental import pallas as pl
from jax.experimental.pallas import tpu as pltpu
from jax.sharding import PartitionSpec as P

NB = 4
TAPS = 10
STRIDE = 5
ROWS = 16
SPARE = 8
F32 = jnp.float32
BF16 = jnp.bfloat16


def split_two(x):
    hi = x.astype(BF16)
    return hi, (x - hi.astype(F32)).astype(BF16)


def gelu_parts(act):
    bell = jnp.exp(-0.5 * (act * act))
    t = 1.0 / (1.0 + 0.2316418882 * jnp.abs(act))
    poly = 0.5307027145 * t - 0.7265760135
    poly = poly * t + 0.7107068705
    poly = poly * t - 0.142248368
    poly = poly * t + 0.127414796
    tail = poly * t * bell
    cdf = jnp.where(act < 0.0, tail, 1.0 - tail)
    return cdf, 0.3989422804014327 * bell


def pack_kernel(packing, bins, wave_ref, out_ref, wide):
    count, record = wave_ref.shape
    width = wide.shape[1]
    wide[...] = jnp.zeros_like(wide)
    wide[:, :record] = wave_ref[...].astype(F32)
    lane = lax.broadcasted_iota(jnp.int32, (SPARE, width), 1)

    def one(slot):
        own = packing[0, slot]
        row = jnp.broadcast_to(wide[pl.ds(own, 1), :], (SPARE, width))
        return jnp.where(lane == record, bins[own].astype(F32), row)

    for pair in range(count // 2):
        both = jnp.concatenate([one(2 * pair), one(2 * pair + 1)], axis=0)
        out_ref[2 * SPARE * pair : 2 * SPARE * (pair + 1), :] = both.astype(BF16)


def pack(packing, length_bin, waveform):
    count, record = waveform.shape
    width = -(-(record + 1) // 128) * 128
    return pl.pallas_call(
        pack_kernel,
        out_shape=jax.ShapeDtypeStruct((count * SPARE, width), BF16),
        in_specs=[
            pl.BlockSpec(memory_space=pltpu.SMEM),
            pl.BlockSpec(memory_space=pltpu.SMEM),
            pl.BlockSpec(memory_space=pltpu.VMEM),
        ],
        out_specs=pl.BlockSpec(memory_space=pltpu.VMEM),
        scratch_shapes=[pltpu.VMEM((count, width), F32)],
    )(packing, length_bin, waveform)


def local_kernel(
    record,
    shares,
    place_ref,
    got_ref,
    cot_ref,
    conv_one_ref,
    bias_one_ref,
    gain_one_ref,
    shift_one_ref,
    conv_two_ref,
    bias_two_ref,
    gain_two_ref,
    shift_two_ref,
    send_ref,
    keep_ref,
    small_ref,
    taps,
    weight,
    norm_one,
    slope_one,
    rstd_one,
    hidden,
    norm_two,
    dz_two,
    dz_one,
    grad,
):
    count = got_ref.shape[0] // SPARE
    rows_two, width = cot_ref.shape
    frames_two = rows_two // count
    frames_one = 2 * frames_two + 1
    rows_even = rows_two + count
    rows_one = frames_one * count
    inv = 1.0 / width

    pick = (
        lax.broadcasted_iota(jnp.int32, (count, count * SPARE), 1)
        == SPARE * lax.broadcasted_iota(jnp.int32, (count, count * SPARE), 0)
    ).astype(BF16)
    wave = jnp.dot(pick, got_ref[...], preferred_element_type=F32)
    lane_in = lax.broadcasted_iota(jnp.int32, wave.shape, 1)
    bins = jnp.sum(jnp.where(lane_in == record, wave, 0.0), axis=1, keepdims=True)
    wave = jnp.concatenate([wave, jnp.zeros((count, 128), F32)], axis=1)

    for place, frame in enumerate(
        list(range(0, frames_one, 2)) + list(range(1, frames_one, 2))
    ):
        taps[count * place : count * (place + 1), :] = wave[
            :, STRIDE * frame : STRIDE * frame + 128
        ].astype(BF16)
    src = lax.broadcasted_iota(jnp.int32, (128, 128), 0)
    dst = lax.broadcasted_iota(jnp.int32, (128, 128), 1)
    thrice = ((src < TAPS) & (dst < 3 * ROWS) & (dst % ROWS == src)).astype(BF16)
    lane = lax.broadcasted_iota(jnp.int32, (1, 128), 1)
    ones = ((lane >= 3 * ROWS) & (lane < 3 * ROWS + 3)).astype(F32)
    taps[...] = (jnp.dot(taps[...], thrice, preferred_element_type=F32) + ones).astype(BF16)

    kernel_one = conv_one_ref[...].astype(F32)
    kernel_one = kernel_one - jnp.sum(kernel_one, axis=1, keepdims=True) * inv
    bias = bias_one_ref[...]
    bias = bias - jnp.sum(bias, axis=1, keepdims=True) * inv
    weight[...] = jnp.zeros_like(weight)
    for part in range(3):
        piece = kernel_one.astype(BF16).astype(F32)
        weight[part * ROWS : part * ROWS + TAPS, :] = piece
        kernel_one = kernel_one - piece
        piece = bias.astype(BF16).astype(F32)
        weight[3 * ROWS + part : 3 * ROWS + part + 1, :] = piece
        bias = bias - piece
    norm_one[...] = jnp.dot(taps[...], weight[...].astype(BF16), preferred_element_type=F32)

    gain = gain_one_ref[...]
    shift = shift_one_ref[...]

    def forward(step, _):
        at = pl.ds(pl.multiple_of(step * ROWS, ROWS), ROWS)
        cent = norm_one[at, :]
        var = jnp.sum(cent * cent, axis=1, keepdims=True) * inv
        rstd = lax.rsqrt(var + 1e-05)
        normed = cent * rstd
        act = normed * gain + shift
        cdf, pdf = gelu_parts(act)
        norm_one[at, :] = normed
        rstd_one[at, :] = jnp.broadcast_to(rstd, (ROWS, 128))
        slope_one[at, :] = cdf + act * pdf
        hidden[at, :] = (act * cdf).astype(BF16)
        return 0

    lax.fori_loop(0, rows_one // ROWS, forward, 0)

    windows = (
        slice(0, rows_two),
        slice(rows_even, rows_even + rows_two),
        slice(count, rows_even),
    )
    total = None
    for tap, rows in enumerate(windows):
        term = jnp.dot(
            hidden[rows, :],
            conv_two_ref[tap * width : (tap + 1) * width, :],
            preferred_element_type=F32,
        )
        total = term if total is None else total + term
    norm_two[...] = total

    row = lax.broadcasted_iota(jnp.int32, (rows_two, 1), 0)
    frame = row // count
    bins_all = jnp.concatenate([bins] * frames_two, axis=0)
    limit = bins_all.astype(jnp.int32) * frames_two // NB
    origin = jnp.where(frame < limit, (row % count) * frames_two + frame, -1)
    mover = (lax.broadcasted_iota(jnp.int32, (rows_two, rows_two), 1) == origin).astype(BF16)
    dz_one[:rows_two, :] = jnp.dot(mover, cot_ref[...], preferred_element_type=F32)

    bias_two = bias_two_ref[...]
    gain_b = gain_two_ref[...]
    shift_b = shift_two_ref[...]
    dz_two[:count, :] = jnp.zeros((count, width), BF16)
    dz_two[count + rows_two :, :] = jnp.zeros((count, width), BF16)

    def eighth(x):
        return x[:8] + x[8:]

    def middle(step, sums):
        start = pl.multiple_of(step * ROWS, ROWS)
        at = pl.ds(start, ROWS)
        z = norm_two[at, :] + bias_two
        cent = z - jnp.sum(z, axis=1, keepdims=True) * inv
        var = jnp.sum(cent * cent, axis=1, keepdims=True) * inv
        rstd = lax.rsqrt(var + 1e-05)
        normed = cent * rstd
        act = normed * gain_b + shift_b
        cdf, pdf = gelu_parts(act)
        dact = dz_one[at, :] * (cdf + act * pdf)
        dnorm = dact * gain_b
        mean_a = jnp.sum(dnorm, axis=1, keepdims=True) * inv
        mean_b = jnp.sum(dnorm * normed, axis=1, keepdims=True) * inv
        dz = rstd * (dnorm - mean_a - normed * mean_b)
        dz_two[pl.ds(pl.multiple_of(start + count, ROWS), ROWS), :] = dz.astype(BF16)
        return (
            sums[0] + eighth(dz),
            sums[1] + eighth(dact * normed),
            sums[2] + eighth(dact),
        )

    zero = jnp.zeros((8, width), F32)
    sums_two = lax.fori_loop(0, rows_two // ROWS, middle, (zero, zero, zero))

    dz_own = dz_two[count : count + rows_two, :]
    for tap, rows in enumerate(windows):
        grad[tap * width : (tap + 1) * width, :] = lax.dot_general(
            hidden[rows, :], dz_own, (((0,), (0,)), ((), ())), preferred_element_type=F32
        )
    share = grad.shape[0] // shares
    me = place_ref[0]
    bits = shares.bit_length() - 1
    for spot in range(shares):
        back = int(format(spot, f"0{bits}b")[::-1], 2)
        block = grad[pl.ds(pl.multiple_of((me ^ back) * share, 8), share), :]
        if spot < shares // 2:
            keep_ref[spot * share : (spot + 1) * share, :] = block
        else:
            at = (spot - shares // 2) * share
            send_ref[at : at + share, :] = block.astype(BF16)

    turn = (((1,), (1,)), ((), ()))
    dz_one[rows_even:, :] = lax.dot_general(
        dz_own, conv_two_ref[width : 2 * width, :], turn, preferred_element_type=F32
    )
    dz_one[:rows_even, :] = lax.dot_general(
        dz_two[count:, :], conv_two_ref[:width, :], turn, preferred_element_type=F32
    ) + lax.dot_general(
        dz_two[:rows_even, :], conv_two_ref[2 * width :, :], turn, preferred_element_type=F32
    )

    def backward(step, sums):
        at = pl.ds(pl.multiple_of(step * ROWS, ROWS), ROWS)
        normed = norm_one[at, :]
        dact = dz_one[at, :] * slope_one[at, :]
        dnorm = dact * gain
        mean_a = jnp.sum(dnorm, axis=1, keepdims=True) * inv
        mean_b = jnp.sum(dnorm * normed, axis=1, keepdims=True) * inv
        dz = rstd_one[at, :1] * (dnorm - mean_a - normed * mean_b)
        hidden[at, :] = dz.astype(BF16)
        return (
            sums[0] + eighth(dz),
            sums[1] + eighth(dact * normed),
            sums[2] + eighth(dact),
        )

    sums_one = lax.fori_loop(0, rows_one // ROWS, backward, (zero, zero, zero))
    first = lax.dot_general(
        taps[...], hidden[...], (((0,), (0,)), ((), ())), preferred_element_type=F32
    )
    small_ref[:TAPS, :] = first[:TAPS, :]
    for spot, sums in enumerate(sums_one + sums_two):
        small_ref[TAPS + spot : TAPS + spot + 1, :] = jnp.sum(sums, axis=0, keepdims=True)
    hi, lo = split_two(small_ref[...])
    half = send_ref.shape[0] - 2 * ROWS
    send_ref[half : half + ROWS, :] = hi
    send_ref[half + ROWS :, :] = lo


def local_pass(record, shares, place, got, cot, *params):
    count = got.shape[0] // SPARE
    rows_two, width = cot.shape
    rows_one = 2 * rows_two + count
    half = 3 * width // 2
    vmem = pl.BlockSpec(memory_space=pltpu.VMEM)
    return pl.pallas_call(
        functools.partial(local_kernel, record, shares),
        out_shape=(
            jax.ShapeDtypeStruct((half + 2 * ROWS, width), BF16),
            jax.ShapeDtypeStruct((half, width), F32),
            jax.ShapeDtypeStruct((ROWS, width), F32),
        ),
        in_specs=[pl.BlockSpec(memory_space=pltpu.SMEM)] + [vmem] * 10,
        out_specs=(vmem, vmem, vmem),
        scratch_shapes=[
            pltpu.VMEM((rows_one, 128), BF16),
            pltpu.VMEM((128, width), F32),
            pltpu.VMEM((rows_one, width), F32),
            pltpu.VMEM((rows_one, width), F32),
            pltpu.VMEM((rows_one, 128), F32),
            pltpu.VMEM((rows_one, width), BF16),
            pltpu.VMEM((rows_two, width), F32),
            pltpu.VMEM((rows_two + 2 * count, width), BF16),
            pltpu.VMEM((rows_one, width), F32),
            pltpu.VMEM((3 * width, width), F32),
        ],
        compiler_params=pltpu.CompilerParams(vmem_limit_bytes=40 * 1024 * 1024),
    )(place, got, cot, *params)


def tree(terms):
    while len(terms) > 1:
        terms = [terms[i] + terms[i + 1] for i in range(0, len(terms), 2)]
    return terms[0]


def exchange(sizes, stage, message):
    far = {axis: 0 for axis in sizes}
    for axis, bit in stage:
        far[axis] ^= 1 << bit
    axes = tuple(axis for axis in sizes if far[axis])
    pairs = [(0, 0)]
    for axis in axes:
        n = sizes[axis]
        pairs = [(a * n + i, b * n + (i ^ far[axis])) for a, b in pairs for i in range(n)]
    return lax.ppermute(message, axes if len(axes) > 1 else axes[0], pairs)


def merge(sizes, stage, blocks, small):
    dp_bits = [item for item in stage if item[0] == "dp"]
    blk_bits = [item for item in stage if item[0] != "dp"]
    hi, lo = split_two(small)
    tail = [hi, lo]
    messages = [jnp.concatenate([block.astype(BF16)] + tail, axis=0) for block in blocks]
    rows = blocks[0].shape[0]
    own = messages[0][:rows].astype(F32) if blk_bits else blocks[0]
    terms = [own]
    smalls = [hi.astype(F32) + lo.astype(F32)]
    for code in range(1, 1 << len(stage)):
        block = code >> len(blk_bits)
        chosen = [b for i, b in enumerate(dp_bits) if block >> (len(dp_bits) - 1 - i) & 1]
        chosen += [b for i, b in enumerate(blk_bits) if code >> i & 1]
        got = exchange(sizes, chosen, messages[block])
        terms.append(got[:rows].astype(F32))
        smalls.append(got[rows : rows + ROWS].astype(F32) + got[rows + ROWS :].astype(F32))
    return tree(terms), tree(smalls)


def per_device(sizes, waveform, length_bin, packing, cotangent, conv_one, *rest):
    record = waveform.shape[1]
    count, frames_two, width = cotangent.shape
    shares = sizes["dp"]
    share = 3 * width // shares
    packed = pack(packing, length_bin, waveform)
    packed = packed.reshape(count, SPARE, packed.shape[1])
    got = lax.all_to_all(packed, "dp", split_axis=0, concat_axis=0, tiled=True)
    got = got.reshape(count * SPARE, got.shape[2])
    params = [p if p.ndim == 2 else p.reshape(1, width) for p in (conv_one, *rest)]
    place = lax.axis_index("dp").astype(jnp.int32).reshape(1)
    send, keep, small = local_pass(
        record, shares, place, got, cotangent.reshape(count * frames_two, width), *params
    )
    half = keep.shape[0]
    other = exchange(sizes, [("dp", 0)], send)
    total = keep + other[:half].astype(F32)
    mine = send[half : half + ROWS].astype(F32) + send[half + ROWS :].astype(F32)
    yours = other[half : half + ROWS].astype(F32) + other[half + ROWS :].astype(F32)
    small = mine + yours
    left = [("dp", bit) for bit in range(1, shares.bit_length() - 1)]
    left += [("blk", bit) for bit in range(sizes["blk"].bit_length() - 1)]
    while left:
        stage, left = left[:2], left[2:]
        parts = 1 << sum(axis == "dp" for axis, _ in stage)
        rows = total.shape[0] // parts
        blocks = [total[i * rows : (i + 1) * rows] for i in range(parts)]
        total, small = merge(sizes, stage, blocks, small)
    return total, small


def solution(mesh):
    sizes = {axis: mesh.shape[axis] for axis in ("dp", "blk")}
    both = ("dp", "blk")
    return jax.shard_map(
        functools.partial(per_device, sizes),
        mesh=mesh,
        in_specs=(P(both, None), P(both), P(both, None), P(both, None, None)) + (P(),) * 8,
        out_specs=(P("dp", None), P()),
        check_vma=False,
    )
```

time: 193 us -> 86.6 us (0.45)
  waiting for transfers between devices: 72.8 us -> 29.5 us
  blocking collectives: 40.6 us -> 0 us
  Pallas kernels: 0 us -> 31.3 us
  local copies, waits for them, and re-layouts: 25.6 us -> 7.31 us
  other arithmetic: 16.9 us -> 1.91 us
  between operations: 14.1 us -> 0.73 us
  matrix products: 10.8 us -> 0 us
  starting transfers between devices: 10.9 us -> 15.4 us
    reduce_scatter x1 -> x0, waiting for transfers between devices: 63.6 us -> none  [per_device(): share = lax.psum_scatter(whole, 'dp', scatter_dimension=0, tiled=True)]
    psum x1 -> x0, blocking collectives: 40.6 us -> none  [per_device(): small_total = lax.psum(small_local, ('dp', 'blk'))]
    pallas_call x0 -> x2, Pallas kernels: none -> 31.3 us  [the longest x1 29.9 us: local_pass(): pl.pallas_call(functools.partial(local_kernel, record, shares), out_shape...]
    ppermute x0 -> x7, waiting for transfers between devices: none -> 22.1 us  [exchange(): return lax.ppermute(message, axes if len(axes) > 1 else axes[0], pairs)]
    dot_general x9 -> x0, matrix products: 10.8 us -> none  [the longest x2 4.2 us: pass_group(): jnp.dot(cols_two, conv_two, preferred_element_type=jnp.float32) + bias_two]
    ppermute x0 -> x7, starting transfers between devices: none -> 8 us  [exchange(): return lax.ppermute(message, axes if len(axes) > 1 else axes[0], pairs)]
    while x46 -> x0, local copies, waits for them, and re-layouts: 7.26 us -> none
    reshape x13 -> x0, local copies, waits for them, and re-layouts: 5.64 us -> none  [the longest x2 3.42 us: pass_group(): jnp.stack([part_b, jnp.zeros_like(part_b)], axis=2)]
  transfers between devices with their start and end apart: 4 -> 8, of which waited for: 3 -> 6; matrix products, arithmetic and copies ran while one was open for 2% -> 0% of each run, Pallas kernels for 0% -> 0%
where the time goes in v1:
time: 86.6 us; the launch traced here: 86.1 us
  Pallas kernels  31.3 us (36%)
  waiting for transfers between devices  29.5 us (34%)
  starting transfers between devices  15.4 us (18%)
  local copies, waits for them, and re-layouts  7.31 us (8%)
  other arithmetic  1.91 us (2%)
    pallas_call x1, Pallas kernels, local_pass(): pl.pallas_call(functools.partial(local_kernel, record, shares), out_shape...  29.9 us
    ppermute x7, waiting for transfers between devices, exchange(): return lax.ppermute(message, axes if len(axes) > 1 else axes[0], pairs)  22.1 us
    ppermute x7, starting transfers between devices, exchange(): return lax.ppermute(message, axes if len(axes) > 1 else axes[0], pairs)  8 us
    all_to_all x1, waiting for transfers between devices, per_device(): got = lax.all_to_all(packed, 'dp', split_axis=0, concat_axis=0, tiled=True)  7.4 us
    all_to_all x1, starting transfers between devices, per_device(): got = lax.all_to_all(packed, 'dp', split_axis=0, concat_axis=0, tiled=True)  7.36 us
    unnamed x18, local copies, waits for them, and re-layouts  7.25 us
  transfers between devices with their start and end apart: 8, of which 6 were waited for; matrix products, arithmetic and copies ran while one was open for 0% of the time, Pallas kernels for 0%

profile of v1, /device:TPU:0, one launch (start us, length us, event | category | flops | bytes accessed | tf_op | source)
XLA Modules:
  0.0 86.1 jit_solution(16736613850209276023)
XLA Ops:
  0.6 1.4 %shard_map.131 = bf16[128,384]{1,0:T(8,128)(2,1)} custom-call(s32[1,16]{1,0:T(1,128)} %packing.1, s32[16]{0:T(128)} %bins.1, bf16[16,330]{1,0:T(8,128)(2,1)} %wave_ref.1), custom_call_target="tpu_custom_call" | custom-call | tf_op jit(solution)/shard_map/pallas_call | solution.py:57
  2.0 7.4 %all-to-all-start = ((bf16[16,8,384]{2,1,0:T(8,128)(2,1)}), bf16[16,8,384]{2,1,0:T(8,128)(2,1)S(1)}, u32[]{:S(2)}, u32[]{:S(2)}) async-start(bf16[16,8,384]{2,1,0:T(8,128)(2,1)} %bitcast.18), calls=%async_computation | async-start | bytes 196608 | tf_op jit(solution)/shard_map/all_to_all | solution.py:349
  9.4 7.4 %all-to-all-done = bf16[16,8,384]{2,1,0:T(8,128)(2,1)S(1)} async-done(((bf16[16,8,384]{2,1,0:T(8,128)(2,1)}), bf16[16,8,384]{2,1,0:T(8,128)(2,1)S(1)}, u32[]{:S(2)}, u32[]{:S(2)}) %all-to-all-start) | async-done | bytes 98336 | tf_op jit(solution)/shard_map/all_to_all | solution.py:349
  16.8 1.4 %copy-done = bf16[1536,512]{1,0:T(8,128)(2,1)S(1)} copy-done((bf16[1536,512]{1,0:T(8,128)(2,1)S(1)}, bf16[1536,512]{1,0:T(8,128)(2,1)}, u32[]{:S(2)}) %copy-start) | copy-done | bytes 1572888
  18.2 1.0 %copy-done.1 = bf16[16,32,512]{2,1,0:T(8,128)(2,1)S(1)} copy-done((bf16[16,32,512]{2,1,0:T(8,128)(2,1)S(1)}, bf16[16,32,512]{2,1,0:T(8,128)(2,1)}, u32[]{:S(2)}) %copy-start.1) | copy-done | bytes 524312
  19.3 0.7 copy-done.2
  20.0 0.7 copy-done.3
  20.7 0.7 copy-done.4
  21.3 0.7 copy-done.5
  22.0 0.7 copy-done.6
  22.7 0.7 copy-done.7
  23.4 0.7 copy-done.8
  24.1 29.9 %shard_map.132 = (bf16[800,512]{1,0:T(8,128)(2,1)S(1)}, f32[768,512]{1,0:T(8,128)S(1)}, f32[16,512]{1,0:T(8,128)}) custom-call(s32[1]{0:T(128)} %bitcast.place_ref, bf16[128,384]{1,0:T(8,128)(2,1)S(1)} %bitcast.11, bf16[512,512]{1,0:T(8,128)(2,1)S(1)} %bitcast.10, bf16[10,512]{1,0:T(8,128)(2,1)S(1)} %copy-done.2, f32[1,512]{1,0:T(1,128)S(1)} %bitcast.12, ...), custom_call_target="tpu_custom_call" | custom-call | tf_op jit(solution)/shard_map/pallas_call | solution.py:279
  53.9 2.3 %collective-permute-done = bf16[800,512]{1,0:T(8,128)(2,1)S(1)} collective-permute-done((bf16[800,512]{1,0:T(8,128)(2,1)S(1)}, bf16[800,512]{1,0:T(8,128)(2,1)S(1)}, u32[]{:S(2)}, u32[]{:S(2)}) %collective-permute-start) | collective-permute-done | bytes 819232 | tf_op jit(solution)/shard_map/ppermute | solution.py:319
  56.8 1.2 %collective-permute-start.2 = (bf16[224,512]{1,0:T(8,128)(2,1)S(1)}, bf16[224,512]{1,0:T(8,128)(2,1)S(1)}, u32[]{:S(2)}, u32[]{:S(2)}) collective-permute-start(bf16[224,512]{1,0:T(8,128)(2,1)S(1)} %get-tuple-element.20), channel_id=1, source_target_pairs={{0,4},{2,6},{4,0},{6,2},{8,12},{10,14},{12,8},{14,10},{16,20},{18,... | collective-permute-start | bytes 688136 | tf_op jit(solution)/shard_map/ppermute | solution.py:319
  58.0 2.3 %collective-permute-start.1 = (bf16[224,512]{1,0:T(8,128)(2,1)S(1)}, bf16[224,512]{1,0:T(8,128)(2,1)S(1)}, u32[]{:S(2)}, u32[]{:S(2)}) collective-permute-start(bf16[224,512]{1,0:T(8,128)(2,1)S(1)} %get-tuple-element.19), channel_id=1, source_target_pairs={{0,8},{2,10},{4,12},{6,14},{8,0},{10,2},{12,4},{14,6},{16,24},{18,... | collective-permute-start | bytes 688136 | tf_op jit(solution)/shard_map/ppermute | solution.py:319
  60.3 5.9 %collective-permute-done.3 = bf16[224,512]{1,0:T(8,128)(2,1)S(1)} collective-permute-done((bf16[224,512]{1,0:T(8,128)(2,1)S(1)}, bf16[224,512]{1,0:T(8,128)(2,1)S(1)}, u32[]{:S(2)}, u32[]{:S(2)}) %collective-permute-start.3) | collective-permute-done | bytes 229408 | tf_op jit(solution)/shard_map/ppermute | solution.py:319
  66.2 3.2 %collective-permute-done.2 = bf16[224,512]{1,0:T(8,128)(2,1)S(1)} collective-permute-done((bf16[224,512]{1,0:T(8,128)(2,1)S(1)}, bf16[224,512]{1,0:T(8,128)(2,1)S(1)}, u32[]{:S(2)}, u32[]{:S(2)}) %collective-permute-start.2) | collective-permute-done | bytes 229408 | tf_op jit(solution)/shard_map/ppermute | solution.py:319
  69.6 2.0 %collective-permute-start.6 = (bf16[128,512]{1,0:T(8,128)(2,1)S(1)}, bf16[128,512]{1,0:T(8,128)(2,1)S(1)}, u32[]{:S(2)}, u32[]{:S(2)}) collective-permute-start(bf16[128,512]{1,0:T(8,128)(2,1)S(1)} %get-tuple-element.18), channel_id=1, source_target_pairs={{0,17},{1,16},{2,19},{3,18},{4,21},{5,20},{6,23},{7,22},{8,25},{9,... | collective-permute-start | bytes 393224 | tf_op jit(solution)/shard_map/ppermute | solution.py:319
  71.7 1.9 %collective-permute-start.5 = (bf16[128,512]{1,0:T(8,128)(2,1)S(1)}, bf16[128,512]{1,0:T(8,128)(2,1)S(1)}, u32[]{:S(2)}, u32[]{:S(2)}) collective-permute-start(bf16[128,512]{1,0:T(8,128)(2,1)S(1)} %get-tuple-element.18), channel_id=1, source_target_pairs={{0,16},{2,18},{4,20},{6,22},{8,24},{10,26},{12,28},{14,30},{16,0},... | collective-permute-start | bytes 393224 | tf_op jit(solution)/shard_map/ppermute | solution.py:319
  74.1 8.9 %collective-permute-done.6 = bf16[128,512]{1,0:T(8,128)(2,1)S(1)} collective-permute-done((bf16[128,512]{1,0:T(8,128)(2,1)S(1)}, bf16[128,512]{1,0:T(8,128)(2,1)S(1)}, u32[]{:S(2)}, u32[]{:S(2)}) %collective-permute-start.6) | collective-permute-done | bytes 131104 | tf_op jit(solution)/shard_map/ppermute | solution.py:319
  83.0 1.8 %collective-permute-done.5 = bf16[128,512]{1,0:T(8,128)(2,1)S(1)} collective-permute-done((bf16[128,512]{1,0:T(8,128)(2,1)S(1)}, bf16[128,512]{1,0:T(8,128)(2,1)S(1)}, u32[]{:S(2)}, u32[]{:S(2)}) %collective-permute-start.5) | collective-permute-done | bytes 131104 | tf_op jit(solution)/shard_map/ppermute | solution.py:319
  84.7 0.7 add_add_fusion
  85.4 0.6 fusion.7
  (23 shorter events, 1.2 us)
Async XLA Ops:
  2.0 14.8 %all-to-all-start = ((bf16[16,8,384]{2,1,0:T(8,128)(2,1)}), bf16[16,8,384]{2,1,0:T(8,128)(2,1)S(1)}, u32[]{:S(2)}, u32[]{:S(2)}) async-start(bf16[16,8,384]{2,1,0:T(8,128)(2,1)} %bitcast.18), calls=%async_computation | async-start | bytes 196608 | tf_op jit(solution)/shard_map/all_to_all | solution.py:349
  16.8 1.4 %copy-start = (bf16[1536,512]{1,0:T(8,128)(2,1)S(1)}, bf16[1536,512]{1,0:T(8,128)(2,1)}, u32[]{:S(2)}) copy-start(bf16[1536,512]{1,0:T(8,128)(2,1)} %conv_two_ref.1) | copy-start | bytes 4718596
  18.2 1.0 %copy-start.1 = (bf16[16,32,512]{2,1,0:T(8,128)(2,1)S(1)}, bf16[16,32,512]{2,1,0:T(8,128)(2,1)}, u32[]{:S(2)}) copy-start(bf16[16,32,512]{2,1,0:T(8,128)(2,1)} %param.15) | copy-start | bytes 1572868
  19.3 0.7 copy-start.2
  20.0 0.7 copy-start.3
  20.7 0.7 copy-start.4
  21.3 0.7 copy-start.5
  22.0 0.7 copy-start.6
  22.7 0.7 copy-start.7
  23.4 0.7 copy-start.8
  53.9 2.3 %collective-permute-start = (bf16[800,512]{1,0:T(8,128)(2,1)S(1)}, bf16[800,512]{1,0:T(8,128)(2,1)S(1)}, u32[]{:S(2)}, u32[]{:S(2)}) collective-permute-start(bf16[800,512]{1,0:T(8,128)(2,1)S(1)} %get-tuple-element.5), channel_id=1, source_target_pairs={{0,2},{2,0},{4,6},{6,4},{8,10},{10,8},{12,14},{14,12},{16,18},{18,... | collective-permute-start | bytes 2457608 | tf_op jit(solution)/shard_map/ppermute | solution.py:319
  56.7 9.5 %collective-permute-start.3 = (bf16[224,512]{1,0:T(8,128)(2,1)S(1)}, bf16[224,512]{1,0:T(8,128)(2,1)S(1)}, u32[]{:S(2)}, u32[]{:S(2)}) collective-permute-start(bf16[224,512]{1,0:T(8,128)(2,1)S(1)} %get-tuple-element.21), channel_id=1, source_target_pairs={{0,12},{2,14},{4,8},{6,10},{8,4},{10,6},{12,0},{14,2},{16,28},{18,... | collective-permute-start | bytes 688136 | tf_op jit(solution)/shard_map/ppermute | solution.py:319
  56.8 12.6 %collective-permute-start.2 = (bf16[224,512]{1,0:T(8,128)(2,1)S(1)}, bf16[224,512]{1,0:T(8,128)(2,1)S(1)}, u32[]{:S(2)}, u32[]{:S(2)}) collective-permute-start(bf16[224,512]{1,0:T(8,128)(2,1)S(1)} %get-tuple-element.20), channel_id=1, source_target_pairs={{0,4},{2,6},{4,0},{6,2},{8,12},{10,14},{12,8},{14,10},{16,20},{18,... | collective-permute-start | bytes 688136 | tf_op jit(solution)/shard_map/ppermute | solution.py:319
  58.0 11.4 %collective-permute-start.1 = (bf16[224,512]{1,0:T(8,128)(2,1)S(1)}, bf16[224,512]{1,0:T(8,128)(2,1)S(1)}, u32[]{:S(2)}, u32[]{:S(2)}) collective-permute-start(bf16[224,512]{1,0:T(8,128)(2,1)S(1)} %get-tuple-element.19), channel_id=1, source_target_pairs={{0,8},{2,10},{4,12},{6,14},{8,0},{10,2},{12,4},{14,6},{16,24},{18,... | collective-permute-start | bytes 688136 | tf_op jit(solution)/shard_map/ppermute | solution.py:319
  69.6 13.3 %collective-permute-start.6 = (bf16[128,512]{1,0:T(8,128)(2,1)S(1)}, bf16[128,512]{1,0:T(8,128)(2,1)S(1)}, u32[]{:S(2)}, u32[]{:S(2)}) collective-permute-start(bf16[128,512]{1,0:T(8,128)(2,1)S(1)} %get-tuple-element.18), channel_id=1, source_target_pairs={{0,17},{1,16},{2,19},{3,18},{4,21},{5,20},{6,23},{7,22},{8,25},{9,... | collective-permute-start | bytes 393224 | tf_op jit(solution)/shard_map/ppermute | solution.py:319
  71.7 13.1 %collective-permute-start.5 = (bf16[128,512]{1,0:T(8,128)(2,1)S(1)}, bf16[128,512]{1,0:T(8,128)(2,1)S(1)}, u32[]{:S(2)}, u32[]{:S(2)}) collective-permute-start(bf16[128,512]{1,0:T(8,128)(2,1)S(1)} %get-tuple-element.18), channel_id=1, source_target_pairs={{0,16},{2,18},{4,20},{6,22},{8,24},{10,26},{12,28},{14,30},{16,0},... | collective-permute-start | bytes 393224 | tf_op jit(solution)/shard_map/ppermute | solution.py:319
  73.6 11.1 %collective-permute-start.4 = (bf16[128,512]{1,0:T(8,128)(2,1)S(1)}, bf16[128,512]{1,0:T(8,128)(2,1)S(1)}, u32[]{:S(2)}, u32[]{:S(2)}) collective-permute-start(bf16[128,512]{1,0:T(8,128)(2,1)S(1)} %get-tuple-element.17), channel_id=1, source_target_pairs={{0,1},{1,0},{2,3},{3,2},{4,5},{5,4},{6,7},{7,6},{8,9},{9,8},{10,11... | collective-permute-start | bytes 393224 | tf_op jit(solution)/shard_map/ppermute | solution.py:319

commit v2 on v1

--- a/solution.py
+++ b/solution.py
@@ -67,25 +67,115 @@
     )(packing, length_bin, waveform)
 
 
+def ready_kernel(
+    count,
+    cot_hbm,
+    conv_two_hbm,
+    conv_one_ref,
+    bias_one_ref,
+    gain_one_ref,
+    shift_one_ref,
+    bias_two_ref,
+    gain_two_ref,
+    shift_two_ref,
+    weight_ref,
+    cot_ref,
+    conv_two_ref,
+    vector_ref,
+    weight,
+    held,
+    kernel_one,
+    vectors,
+    arrived,
+):
+    rows_two, width = held.shape
+    frames_two = rows_two // count
+    inv = 1.0 / width
+    moves = [
+        pltpu.make_async_copy(conv_one_ref, kernel_one, arrived.at[0]),
+        pltpu.make_async_copy(bias_one_ref, vectors.at[0:1], arrived.at[1]),
+        pltpu.make_async_copy(gain_one_ref, vectors.at[1:2], arrived.at[2]),
+        pltpu.make_async_copy(shift_one_ref, vectors.at[2:3], arrived.at[3]),
+        pltpu.make_async_copy(bias_two_ref, vectors.at[3:4], arrived.at[4]),
+        pltpu.make_async_copy(gain_two_ref, vectors.at[4:5], arrived.at[5]),
+        pltpu.make_async_copy(shift_two_ref, vectors.at[5:6], arrived.at[6]),
+        pltpu.make_async_copy(cot_hbm, held, arrived.at[7]),
+        pltpu.make_async_copy(conv_two_hbm, conv_two_ref, arrived.at[8]),
+    ]
+    for move in moves:
+        move.start()
+    row = lax.broadcasted_iota(jnp.int32, (rows_two, 1), 0)
+    origin = (row % count) * frames_two + row // count
+    mover = (lax.broadcasted_iota(jnp.int32, (rows_two, rows_two), 1) == origin).astype(BF16)
+    weight[...] = jnp.zeros_like(weight)
+    for move in moves[:7]:
+        move.wait()
+    kernel = kernel_one[...].astype(F32)
+    kernel = kernel - jnp.sum(kernel, axis=1, keepdims=True) * inv
+    bias = vectors[0:1, :]
+    bias = bias - jnp.sum(bias, axis=1, keepdims=True) * inv
+    for part in range(3):
+        piece = kernel.astype(BF16).astype(F32)
+        weight[part * ROWS : part * ROWS + TAPS, :] = piece
+        kernel = kernel - piece
+        piece = bias.astype(BF16).astype(F32)
+        weight[3 * ROWS + part : 3 * ROWS + part + 1, :] = piece
+        bias = bias - piece
+    weight_ref[...] = weight[...].astype(BF16)
+    vector_ref[0:6, :] = vectors[0:6, :]
+    moves[7].wait()
+    cot_ref[...] = jnp.dot(mover, held[...], preferred_element_type=F32).astype(BF16)
+    moves[8].wait()
+
+
+def ready(count, cot, conv_two, conv_one, *vectors):
+    rows_two, width = cot.shape
+    vmem = pl.BlockSpec(memory_space=pltpu.VMEM)
+    return pl.pallas_call(
+        functools.partial(ready_kernel, count),
+        out_shape=(
+            jax.ShapeDtypeStruct((128, width), BF16),
+            jax.ShapeDtypeStruct(cot.shape, BF16),
+            jax.ShapeDtypeStruct(conv_two.shape, BF16),
+            jax.ShapeDtypeStruct((8, width), F32),
+        ),
+        in_specs=[pl.BlockSpec(memory_space=pltpu.HBM)] * 9,
+        out_specs=(vmem, vmem, vmem, vmem),
+        scratch_shapes=[
+            pltpu.VMEM((128, width), F32),
+            pltpu.VMEM(cot.shape, BF16),
+            pltpu.VMEM(conv_one.shape, BF16),
+            pltpu.VMEM((8, width), F32),
+            pltpu.SemaphoreType.DMA((9,)),
+        ],
+        cost_estimate=pl.CostEstimate(
+            flops=2 * rows_two * rows_two * width,
+            bytes_accessed=4 * conv_two.size + 4 * cot.size,
+            transcendentals=0,
+        ),
+        compiler_params=pltpu.CompilerParams(vmem_limit_bytes=16 * 1024 * 1024),
+    )(cot, conv_two, conv_one, *vectors)
+
+
+def together(steps):
+    return max(n for n in range(1, 17) if steps % n == 0)
+
+
 def local_kernel(
     record,
     shares,
     place_ref,
     got_ref,
     cot_ref,
-    conv_one_ref,
-    bias_one_ref,
-    gain_one_ref,
-    shift_one_ref,
+    weight_ref,
     conv_two_ref,
-    bias_two_ref,
-    gain_two_ref,
-    shift_two_ref,
+    vector_ref,
     send_ref,
     keep_ref,
     small_ref,
     taps,
-    weight,
+    limits,
+    cent_one,
     norm_one,
     slope_one,
     rstd_one,
@@ -110,6 +200,8 @@
     wave = jnp.dot(pick, got_ref[...], preferred_element_type=F32)
     lane_in = lax.broadcasted_iota(jnp.int32, wave.shape, 1)
     bins = jnp.sum(jnp.where(lane_in == record, wave, 0.0), axis=1, keepdims=True)
+    limit = bins.astype(jnp.int32) * frames_two // NB
+    limits[...] = jnp.broadcast_to(limit, (count, 128))
     wave = jnp.concatenate([wave, jnp.zeros((count, 128), F32)], axis=1)
 
     for place, frame in enumerate(
@@ -125,26 +217,15 @@
     ones = ((lane >= 3 * ROWS) & (lane < 3 * ROWS + 3)).astype(F32)
     taps[...] = (jnp.dot(taps[...], thrice, preferred_element_type=F32) + ones).astype(BF16)
 
-    kernel_one = conv_one_ref[...].astype(F32)
-    kernel_one = kernel_one - jnp.sum(kernel_one, axis=1, keepdims=True) * inv
-    bias = bias_one_ref[...]
-    bias = bias - jnp.sum(bias, axis=1, keepdims=True) * inv
-    weight[...] = jnp.zeros_like(weight)
-    for part in range(3):
-        piece = kernel_one.astype(BF16).astype(F32)
-        weight[part * ROWS : part * ROWS + TAPS, :] = piece
-        kernel_one = kernel_one - piece
-        piece = bias.astype(BF16).astype(F32)
-        weight[3 * ROWS + part : 3 * ROWS + part + 1, :] = piece
-        bias = bias - piece
-    norm_one[...] = jnp.dot(taps[...], weight[...].astype(BF16), preferred_element_type=F32)
-
-    gain = gain_one_ref[...]
-    shift = shift_one_ref[...]
+    cent_one[...] = jnp.dot(taps[...], weight_ref[...], preferred_element_type=F32)
+    gain = vector_ref[1:2, :]
+    shift = vector_ref[2:3, :]
+    steps_one = rows_one // ROWS
+    steps_two = rows_two // ROWS
 
     def forward(step, _):
         at = pl.ds(pl.multiple_of(step * ROWS, ROWS), ROWS)
-        cent = norm_one[at, :]
+        cent = cent_one[at, :]
         var = jnp.sum(cent * cent, axis=1, keepdims=True) * inv
         rstd = lax.rsqrt(var + 1e-05)
         normed = cent * rstd
@@ -156,7 +237,7 @@
         hidden[at, :] = (act * cdf).astype(BF16)
         return 0
 
-    lax.fori_loop(0, rows_one // ROWS, forward, 0)
+    lax.fori_loop(0, steps_one, forward, 0, unroll=together(steps_one))
 
     windows = (
         slice(0, rows_two),
@@ -173,17 +254,9 @@
         total = term if total is None else total + term
     norm_two[...] = total
 
-    row = lax.broadcasted_iota(jnp.int32, (rows_two, 1), 0)
-    frame = row // count
-    bins_all = jnp.concatenate([bins] * frames_two, axis=0)
-    limit = bins_all.astype(jnp.int32) * frames_two // NB
-    origin = jnp.where(frame < limit, (row % count) * frames_two + frame, -1)
-    mover = (lax.broadcasted_iota(jnp.int32, (rows_two, rows_two), 1) == origin).astype(BF16)
-    dz_one[:rows_two, :] = jnp.dot(mover, cot_ref[...], preferred_element_type=F32)
-
-    bias_two = bias_two_ref[...]
-    gain_b = gain_two_ref[...]
-    shift_b = shift_two_ref[...]
+    bias_two = vector_ref[3:4, :]
+    gain_b = vector_ref[4:5, :]
+    shift_b = vector_ref[5:6, :]
     dz_two[:count, :] = jnp.zeros((count, width), BF16)
     dz_two[count + rows_two :, :] = jnp.zeros((count, width), BF16)
 
@@ -193,6 +266,8 @@
     def middle(step, sums):
         start = pl.multiple_of(step * ROWS, ROWS)
         at = pl.ds(start, ROWS)
+        first = pl.multiple_of(lax.rem(start, count), ROWS)
+        valid = limits[pl.ds(first, ROWS), :1] > lax.div(start, count)
         z = norm_two[at, :] + bias_two
         cent = z - jnp.sum(z, axis=1, keepdims=True) * inv
         var = jnp.sum(cent * cent, axis=1, keepdims=True) * inv
@@ -200,7 +275,7 @@
         normed = cent * rstd
         act = normed * gain_b + shift_b
         cdf, pdf = gelu_parts(act)
-        dact = dz_one[at, :] * (cdf + act * pdf)
+        dact = jnp.where(valid, cot_ref[at, :].astype(F32) * (cdf + act * pdf), 0.0)
         dnorm = dact * gain_b
         mean_a = jnp.sum(dnorm, axis=1, keepdims=True) * inv
         mean_b = jnp.sum(dnorm * normed, axis=1, keepdims=True) * inv
@@ -213,7 +288,9 @@
         )
 
     zero = jnp.zeros((8, width), F32)
-    sums_two = lax.fori_loop(0, rows_two // ROWS, middle, (zero, zero, zero))
+    sums_two = lax.fori_loop(
+        0, steps_two, middle, (zero, zero, zero), unroll=together(steps_two)
+    )
 
     dz_own = dz_two[count : count + rows_two, :]
     for tap, rows in enumerate(windows):
@@ -257,7 +334,9 @@
             sums[2] + eighth(dact),
         )
 
-    sums_one = lax.fori_loop(0, rows_one // ROWS, backward, (zero, zero, zero))
+    sums_one = lax.fori_loop(
+        0, steps_one, backward, (zero, zero, zero), unroll=together(steps_one)
+    )
     first = lax.dot_general(
         taps[...], hidden[...], (((0,), (0,)), ((), ())), preferred_element_type=F32
     )
@@ -270,7 +349,7 @@
     send_ref[half + ROWS :, :] = lo
 
 
-def local_pass(record, shares, place, got, cot, *params):
+def local_pass(record, shares, place, got, cot, weight, conv_two, vectors):
     count = got.shape[0] // SPARE
     rows_two, width = cot.shape
     rows_one = 2 * rows_two + count
@@ -283,11 +362,12 @@
             jax.ShapeDtypeStruct((half, width), F32),
             jax.ShapeDtypeStruct((ROWS, width), F32),
         ),
-        in_specs=[pl.BlockSpec(memory_space=pltpu.SMEM)] + [vmem] * 10,
+        in_specs=[pl.BlockSpec(memory_space=pltpu.SMEM)] + [vmem] * 5,
         out_specs=(vmem, vmem, vmem),
         scratch_shapes=[
             pltpu.VMEM((rows_one, 128), BF16),
-            pltpu.VMEM((128, width), F32),
+            pltpu.VMEM((count, 128), jnp.int32),
+            pltpu.VMEM((rows_one, width), F32),
             pltpu.VMEM((rows_one, width), F32),
             pltpu.VMEM((rows_one, width), F32),
             pltpu.VMEM((rows_one, 128), F32),
@@ -297,8 +377,13 @@
             pltpu.VMEM((rows_one, width), F32),
             pltpu.VMEM((3 * width, width), F32),
         ],
-        compiler_params=pltpu.CompilerParams(vmem_limit_bytes=40 * 1024 * 1024),
-    )(place, got, cot, *params)
+        cost_estimate=pl.CostEstimate(
+            flops=2 * 9 * rows_two * width * width,
+            bytes_accessed=8 * rows_one * width,
+            transcendentals=3 * rows_one * width,
+        ),
+        compiler_params=pltpu.CompilerParams(vmem_limit_bytes=36 * 1024 * 1024),
+    )(place, got, cot, weight, conv_two, vectors)
 
 
 def tree(terms):
@@ -339,20 +424,38 @@
     return tree(terms), tree(smalls)
 
 
-def per_device(sizes, waveform, length_bin, packing, cotangent, conv_one, *rest):
+def per_device(
+    sizes,
+    waveform,
+    length_bin,
+    packing,
+    cotangent,
+    conv_one,
+    bias_one,
+    gain_one,
+    shift_one,
+    conv_two,
+    bias_two,
+    gain_two,
+    shift_two,
+):
     record = waveform.shape[1]
     count, frames_two, width = cotangent.shape
     shares = sizes["dp"]
-    share = 3 * width // shares
     packed = pack(packing, length_bin, waveform)
     packed = packed.reshape(count, SPARE, packed.shape[1])
     got = lax.all_to_all(packed, "dp", split_axis=0, concat_axis=0, tiled=True)
     got = got.reshape(count * SPARE, got.shape[2])
-    params = [p if p.ndim == 2 else p.reshape(1, width) for p in (conv_one, *rest)]
+    vectors = (bias_one, gain_one, shift_one, bias_two, gain_two, shift_two)
+    weight, cot, conv_two, vectors = ready(
+        count,
+        cotangent.reshape(count * frames_two, width),
+        conv_two,
+        conv_one,
+        *(v.reshape(1, width) for v in vectors),
+    )
     place = lax.axis_index("dp").astype(jnp.int32).reshape(1)
-    send, keep, small = local_pass(
-        record, shares, place, got, cotangent.reshape(count * frames_two, width), *params
-    )
+    send, keep, small = local_pass(record, shares, place, got, cot, weight, conv_two, vectors)
     half = keep.shape[0]
     other = exchange(sizes, [("dp", 0)], send)
     total = keep + other[:half].astype(F32)

time: 86.6 us -> 65 us (0.75)
  Pallas kernels: 31.3 us -> 15.3 us
  waiting for transfers between devices: 29.5 us -> 23.5 us
    pallas_call x1, Pallas kernels: 29.9 us -> 12.9 us  [local_pass(): pl.pallas_call(functools.partial(local_kernel, record, shares), out_shape...]
    all_to_all x1, waiting for transfers between devices: 7.4 us -> 0.01 us  [per_device(): got = lax.all_to_all(packed, 'dp', split_axis=0, concat_axis=0, tiled=True)]
    ppermute x7, waiting for transfers between devices: 22.1 us -> 23.5 us  [exchange(): return lax.ppermute(message, axes if len(axes) > 1 else axes[0], pairs)]
    pallas_call x0 -> x1, Pallas kernels: none -> 0.97 us  [ready(): pl.pallas_call(functools.partial(ready_kernel, count), out_shape=(jax.Sha...]
  transfers between devices with their start and end apart: 8 -> 8, of which waited for: 6 -> 6; matrix products, arithmetic and copies ran while one was open for 0% -> 0% of each run, Pallas kernels for 0% -> 2%
where the time goes in v2:
time: 65 us; the launch traced here: 64.5 us
  waiting for transfers between devices  23.5 us (36%)
  starting transfers between devices  15.8 us (24%)
  Pallas kernels  15.3 us (24%)
  local copies, waits for them, and re-layouts  7.3 us (11%)
  other arithmetic  1.89 us (3%)
  between operations  0.74 us (1%)
    ppermute x7, waiting for transfers between devices, exchange(): return lax.ppermute(message, axes if len(axes) > 1 else axes[0], pairs)  23.5 us
    pallas_call x1, Pallas kernels, local_pass(): pl.pallas_call(functools.partial(local_kernel, record, shares), out_shape...  12.9 us
    ppermute x7, starting transfers between devices, exchange(): return lax.ppermute(message, axes if len(axes) > 1 else axes[0], pairs)  8.43 us
    all_to_all x1, starting transfers between devices, per_device(): got = lax.all_to_all(packed, 'dp', split_axis=0, concat_axis=0, tiled=True)  7.36 us
    unnamed x18, local copies, waits for them, and re-layouts  7.25 us
    pallas_call x1, Pallas kernels, pack(): pl.pallas_call(pack_kernel, out_shape=jax.ShapeDtypeStruct((count * SPARE...  1.4 us
    add x2, other arithmetic, tree(): terms = [terms[i] + terms[i + 1] for i in range(0, len(terms), 2)]  1.36 us
  transfers between devices with their start and end apart: 8, of which 6 were waited for; matrix products, arithmetic and copies ran while one was open for 0% of the time, Pallas kernels for 2%

profile of v2, /device:TPU:0, one launch (start us, length us, event | category | flops | bytes accessed | tf_op | source)
XLA Modules:
  0.0 64.5 jit_solution(2833803147140166211)
XLA Ops:
  0.6 1.4 %shard_map.131 = bf16[128,384]{1,0:T(8,128)(2,1)} custom-call(s32[1,16]{1,0:T(1,128)} %packing.1, s32[16]{0:T(128)} %bins.1, bf16[16,330]{1,0:T(8,128)(2,1)} %wave_ref.1), custom_call_target="tpu_custom_call" | custom-call | tf_op jit(solution)/shard_map/pallas_call | solution.py:57
  2.0 7.4 %all-to-all-start = ((bf16[16,8,384]{2,1,0:T(8,128)(2,1)}), bf16[16,8,384]{2,1,0:T(8,128)(2,1)S(1)}, u32[]{:S(2)}, u32[]{:S(2)}) async-start(bf16[16,8,384]{2,1,0:T(8,128)(2,1)} %bitcast.18), calls=%async_computation | async-start | bytes 196608 | tf_op jit(solution)/shard_map/all_to_all | solution.py:447
  9.4 1.4 %copy-done = bf16[1536,512]{1,0:T(8,128)(2,1)S(1)} copy-done((bf16[1536,512]{1,0:T(8,128)(2,1)S(1)}, bf16[1536,512]{1,0:T(8,128)(2,1)}, u32[]{:S(2)}) %copy-start) | copy-done | bytes 1572888
  10.8 1.0 %copy-done.1 = bf16[16,32,512]{2,1,0:T(8,128)(2,1)S(1)} copy-done((bf16[16,32,512]{2,1,0:T(8,128)(2,1)S(1)}, bf16[16,32,512]{2,1,0:T(8,128)(2,1)}, u32[]{:S(2)}) %copy-start.1) | copy-done | bytes 524312
  11.9 0.7 %copy-done.2 = bf16[10,512]{1,0:T(8,128)(2,1)S(1)} copy-done((bf16[10,512]{1,0:T(8,128)(2,1)S(1)}, bf16[10,512]{1,0:T(8,128)(2,1)}, u32[]{:S(2)}) %copy-start.2) | copy-done | bytes 10264
  12.6 0.7 %copy-done.3 = f32[512]{0:T(512)S(1)} copy-done((f32[512]{0:T(512)S(1)}, f32[512]{0:T(512)}, u32[]{:S(2)}) %copy-start.3) | copy-done | bytes 2072
  13.3 0.7 %copy-done.4 = f32[512]{0:T(512)S(1)} copy-done((f32[512]{0:T(512)S(1)}, f32[512]{0:T(512)}, u32[]{:S(2)}) %copy-start.4) | copy-done | bytes 2072
  13.9 0.7 %copy-done.5 = f32[512]{0:T(512)S(1)} copy-done((f32[512]{0:T(512)S(1)}, f32[512]{0:T(512)}, u32[]{:S(2)}) %copy-start.5) | copy-done | bytes 2072
  14.6 0.7 %copy-done.6 = f32[512]{0:T(512)S(1)} copy-done((f32[512]{0:T(512)S(1)}, f32[512]{0:T(512)}, u32[]{:S(2)}) %copy-start.6) | copy-done | bytes 2072
  15.3 0.7 %copy-done.7 = f32[512]{0:T(512)S(1)} copy-done((f32[512]{0:T(512)S(1)}, f32[512]{0:T(512)}, u32[]{:S(2)}) %copy-start.7) | copy-done | bytes 2072
  16.0 0.7 %copy-done.8 = f32[512]{0:T(512)S(1)} copy-done((f32[512]{0:T(512)S(1)}, f32[512]{0:T(512)}, u32[]{:S(2)}) %copy-start.8) | copy-done | bytes 2072
  16.7 1.0 %shard_map.132 = (bf16[128,512]{1,0:T(8,128)(2,1)S(1)}, bf16[512,512]{1,0:T(8,128)(2,1)S(1)}, bf16[1536,512]{1,0:T(8,128)(2,1)S(1)}, f32[8,512]{1,0:T(8,128)S(1)}) custom-call(bf16[512,512]{1,0:T(8,128)(2,1)S(1)} %bitcast.10, bf16[1536,512]{1,0:T(8,128)(2,1)S(1)} %copy-done, bf16[10,512]{1,0:T(8,128)(2,1)S(1)} %copy-done.2, f32[1,512]{1,0:T(1,128)S(1)} %bitcast.12, ...), custom_call_target="tpu_custom_call" | custom-call | flops 268435456 | bytes 4194304 | tf_op jit(solution)/shard_map/pallas_call | solution.py:134
  17.7 12.9 %shard_map.133 = (bf16[800,512]{1,0:T(8,128)(2,1)S(1)}, f32[768,512]{1,0:T(8,128)S(1)}, f32[16,512]{1,0:T(8,128)}) custom-call(s32[1]{0:T(128)} %bitcast.place_ref, bf16[128,384]{1,0:T(8,128)(2,1)S(1)} %bitcast.11, bf16[512,512]{1,0:T(8,128)(2,1)S(1)} %get-tuple-element.8.cot_ref, bf16[128,512]{1,0:T(8,128)(2,1)S(1)} %get-tuple-element.9.weight_ref, ...), custom_call_target="tpu_custom_call" | custom-call | flops 2415919104 | bytes 4259840 | tf_op jit(solution)/shard_map/pallas_call | solution.py:358
  31.0 2.0 %collective-permute-done = bf16[800,512]{1,0:T(8,128)(2,1)S(1)} collective-permute-done((bf16[800,512]{1,0:T(8,128)(2,1)S(1)}, bf16[800,512]{1,0:T(8,128)(2,1)S(1)}, u32[]{:S(2)}, u32[]{:S(2)}) %collective-permute-start) | collective-permute-done | bytes 819232 | tf_op jit(solution)/shard_map/ppermute | solution.py:404
  33.4 2.9 %collective-permute-start.3 = (bf16[224,512]{1,0:T(8,128)(2,1)S(1)}, bf16[224,512]{1,0:T(8,128)(2,1)S(1)}, u32[]{:S(2)}, u32[]{:S(2)}) collective-permute-start(bf16[224,512]{1,0:T(8,128)(2,1)S(1)} %get-tuple-element.29), channel_id=1, source_target_pairs={{0,12},{2,14},{4,8},{6,10},{8,4},{10,6},{12,0},{14,2},{16,28},{18,... | collective-permute-start | bytes 688136 | tf_op jit(solution)/shard_map/ppermute | solution.py:404
  36.2 0.6 collective-permute-start.2
  37.0 5.9 %collective-permute-done.3 = bf16[224,512]{1,0:T(8,128)(2,1)S(1)} collective-permute-done((bf16[224,512]{1,0:T(8,128)(2,1)S(1)}, bf16[224,512]{1,0:T(8,128)(2,1)S(1)}, u32[]{:S(2)}, u32[]{:S(2)}) %collective-permute-start.3) | collective-permute-done | bytes 229408 | tf_op jit(solution)/shard_map/ppermute | solution.py:404
  42.8 4.3 %collective-permute-done.2 = bf16[224,512]{1,0:T(8,128)(2,1)S(1)} collective-permute-done((bf16[224,512]{1,0:T(8,128)(2,1)S(1)}, bf16[224,512]{1,0:T(8,128)(2,1)S(1)}, u32[]{:S(2)}, u32[]{:S(2)}) %collective-permute-start.2) | collective-permute-done | bytes 229408 | tf_op jit(solution)/shard_map/ppermute | solution.py:404
  47.6 3.4 %collective-permute-start.6 = (bf16[128,512]{1,0:T(8,128)(2,1)S(1)}, bf16[128,512]{1,0:T(8,128)(2,1)S(1)}, u32[]{:S(2)}, u32[]{:S(2)}) collective-permute-start(bf16[128,512]{1,0:T(8,128)(2,1)S(1)} %get-tuple-element.26), channel_id=1, source_target_pairs={{0,17},{1,16},{2,19},{3,18},{4,21},{5,20},{6,23},{7,22},{8,25},{9,... | collective-permute-start | bytes 393224 | tf_op jit(solution)/shard_map/ppermute | solution.py:404
  51.0 0.6 collective-permute-start.5
  52.1 9.4 %collective-permute-done.6 = bf16[128,512]{1,0:T(8,128)(2,1)S(1)} collective-permute-done((bf16[128,512]{1,0:T(8,128)(2,1)S(1)}, bf16[128,512]{1,0:T(8,128)(2,1)S(1)}, u32[]{:S(2)}, u32[]{:S(2)}) %collective-permute-start.6) | collective-permute-done | bytes 131104 | tf_op jit(solution)/shard_map/ppermute | solution.py:404
  61.5 1.7 %collective-permute-done.5 = bf16[128,512]{1,0:T(8,128)(2,1)S(1)} collective-permute-done((bf16[128,512]{1,0:T(8,128)(2,1)S(1)}, bf16[128,512]{1,0:T(8,128)(2,1)S(1)}, u32[]{:S(2)}, u32[]{:S(2)}) %collective-permute-start.5) | collective-permute-done | bytes 131104 | tf_op jit(solution)/shard_map/ppermute | solution.py:404
  63.1 0.7 %add_add_fusion = f32[96,512]{1,0:T(8,128)} fusion(bf16[128,512]{1,0:T(8,128)(2,1)S(1)} %collective-permute-done.6, bf16[128,512]{1,0:T(8,128)(2,1)S(1)} %collective-permute-done.5, bf16[128,512]{1,0:T(8,128)(2,1)S(1)} %collective-permute-done.4, bf16[192,512]{1,0:T(8,128)(2,1)S(1)} %fusion.1), kind=kLoop, calls=%fused_computation.10 | loop fusion | flops 344064 | bytes 589824 | tf_op jit(solution)/shard_map/add | solution.py:391
  63.8 0.6 fusion.7
  (24 shorter events, 1.9 us)
Async XLA Ops:
  2.0 15.6 %all-to-all-start = ((bf16[16,8,384]{2,1,0:T(8,128)(2,1)}), bf16[16,8,384]{2,1,0:T(8,128)(2,1)S(1)}, u32[]{:S(2)}, u32[]{:S(2)}) async-start(bf16[16,8,384]{2,1,0:T(8,128)(2,1)} %bitcast.18), calls=%async_computation | async-start | bytes 196608 | tf_op jit(solution)/shard_map/all_to_all | solution.py:447
  9.4 1.4 %copy-start = (bf16[1536,512]{1,0:T(8,128)(2,1)S(1)}, bf16[1536,512]{1,0:T(8,128)(2,1)}, u32[]{:S(2)}) copy-start(bf16[1536,512]{1,0:T(8,128)(2,1)} %conv_two_hbm.1) | copy-start | bytes 4718596
  10.8 1.0 %copy-start.1 = (bf16[16,32,512]{2,1,0:T(8,128)(2,1)S(1)}, bf16[16,32,512]{2,1,0:T(8,128)(2,1)}, u32[]{:S(2)}) copy-start(bf16[16,32,512]{2,1,0:T(8,128)(2,1)} %param.15) | copy-start | bytes 1572868
  11.9 0.7 %copy-start.2 = (bf16[10,512]{1,0:T(8,128)(2,1)S(1)}, bf16[10,512]{1,0:T(8,128)(2,1)}, u32[]{:S(2)}) copy-start(bf16[10,512]{1,0:T(8,128)(2,1)} %conv_one_ref.1) | copy-start | bytes 30724
  12.6 0.7 %copy-start.3 = (f32[512]{0:T(512)S(1)}, f32[512]{0:T(512)}, u32[]{:S(2)}) copy-start(f32[512]{0:T(512)} %param.17) | copy-start | bytes 6148
  13.3 0.7 %copy-start.4 = (f32[512]{0:T(512)S(1)}, f32[512]{0:T(512)}, u32[]{:S(2)}) copy-start(f32[512]{0:T(512)} %param.18) | copy-start | bytes 6148
  13.9 0.7 %copy-start.5 = (f32[512]{0:T(512)S(1)}, f32[512]{0:T(512)}, u32[]{:S(2)}) copy-start(f32[512]{0:T(512)} %param.19) | copy-start | bytes 6148
  14.6 0.7 %copy-start.6 = (f32[512]{0:T(512)S(1)}, f32[512]{0:T(512)}, u32[]{:S(2)}) copy-start(f32[512]{0:T(512)} %param.21) | copy-start | bytes 6148
  15.3 0.7 %copy-start.7 = (f32[512]{0:T(512)S(1)}, f32[512]{0:T(512)}, u32[]{:S(2)}) copy-start(f32[512]{0:T(512)} %param.22) | copy-start | bytes 6148
  16.0 0.7 %copy-start.8 = (f32[512]{0:T(512)S(1)}, f32[512]{0:T(512)}, u32[]{:S(2)}) copy-start(f32[512]{0:T(512)} %param.23) | copy-start | bytes 6148
  30.6 2.4 %collective-permute-start = (bf16[800,512]{1,0:T(8,128)(2,1)S(1)}, bf16[800,512]{1,0:T(8,128)(2,1)S(1)}, u32[]{:S(2)}, u32[]{:S(2)}) collective-permute-start(bf16[800,512]{1,0:T(8,128)(2,1)S(1)} %get-tuple-element.13), channel_id=1, source_target_pairs={{0,2},{2,0},{4,6},{6,4},{8,10},{10,8},{12,14},{14,12},{16,18},{18,... | collective-permute-start | bytes 2457608 | tf_op jit(solution)/shard_map/ppermute | solution.py:404
  33.4 9.4 %collective-permute-start.3 = (bf16[224,512]{1,0:T(8,128)(2,1)S(1)}, bf16[224,512]{1,0:T(8,128)(2,1)S(1)}, u32[]{:S(2)}, u32[]{:S(2)}) collective-permute-start(bf16[224,512]{1,0:T(8,128)(2,1)S(1)} %get-tuple-element.29), channel_id=1, source_target_pairs={{0,12},{2,14},{4,8},{6,10},{8,4},{10,6},{12,0},{14,2},{16,28},{18,... | collective-permute-start | bytes 688136 | tf_op jit(solution)/shard_map/ppermute | solution.py:404
  36.2 10.9 %collective-permute-start.2 = (bf16[224,512]{1,0:T(8,128)(2,1)S(1)}, bf16[224,512]{1,0:T(8,128)(2,1)S(1)}, u32[]{:S(2)}, u32[]{:S(2)}) collective-permute-start(bf16[224,512]{1,0:T(8,128)(2,1)S(1)} %get-tuple-element.28), channel_id=1, source_target_pairs={{0,4},{2,6},{4,0},{6,2},{8,12},{10,14},{12,8},{14,10},{16,20},{18,... | collective-permute-start | bytes 688136 | tf_op jit(solution)/shard_map/ppermute | solution.py:404
  36.8 10.6 %collective-permute-start.1 = (bf16[224,512]{1,0:T(8,128)(2,1)S(1)}, bf16[224,512]{1,0:T(8,128)(2,1)S(1)}, u32[]{:S(2)}, u32[]{:S(2)}) collective-permute-start(bf16[224,512]{1,0:T(8,128)(2,1)S(1)} %get-tuple-element.27), channel_id=1, source_target_pairs={{0,8},{2,10},{4,12},{6,14},{8,0},{10,2},{12,4},{14,6},{16,24},{18,... | collective-permute-start | bytes 688136 | tf_op jit(solution)/shard_map/ppermute | solution.py:404
  47.6 13.9 %collective-permute-start.6 = (bf16[128,512]{1,0:T(8,128)(2,1)S(1)}, bf16[128,512]{1,0:T(8,128)(2,1)S(1)}, u32[]{:S(2)}, u32[]{:S(2)}) collective-permute-start(bf16[128,512]{1,0:T(8,128)(2,1)S(1)} %get-tuple-element.26), channel_id=1, source_target_pairs={{0,17},{1,16},{2,19},{3,18},{4,21},{5,20},{6,23},{7,22},{8,25},{9,... | collective-permute-start | bytes 393224 | tf_op jit(solution)/shard_map/ppermute | solution.py:404
  51.0 12.1 %collective-permute-start.5 = (bf16[128,512]{1,0:T(8,128)(2,1)S(1)}, bf16[128,512]{1,0:T(8,128)(2,1)S(1)}, u32[]{:S(2)}, u32[]{:S(2)}) collective-permute-start(bf16[128,512]{1,0:T(8,128)(2,1)S(1)} %get-tuple-element.26), channel_id=1, source_target_pairs={{0,16},{2,18},{4,20},{6,22},{8,24},{10,26},{12,28},{14,30},{16,0},... | collective-permute-start | bytes 393224 | tf_op jit(solution)/shard_map/ppermute | solution.py:404
  51.5 11.6 %collective-permute-start.4 = (bf16[128,512]{1,0:T(8,128)(2,1)S(1)}, bf16[128,512]{1,0:T(8,128)(2,1)S(1)}, u32[]{:S(2)}, u32[]{:S(2)}) collective-permute-start(bf16[128,512]{1,0:T(8,128)(2,1)S(1)} %get-tuple-element.25), channel_id=1, source_target_pairs={{0,1},{1,0},{2,3},{3,2},{4,5},{5,4},{6,7},{7,6},{8,9},{9,8},{10,11... | collective-permute-start | bytes 393224 | tf_op jit(solution)/shard_map/ppermute | solution.py:404

commit v3 on v2

--- a/solution.py
+++ b/solution.py
@@ -67,52 +67,18 @@
     )(packing, length_bin, waveform)
 
 
-def ready_kernel(
-    count,
-    cot_hbm,
-    conv_two_hbm,
-    conv_one_ref,
-    bias_one_ref,
-    gain_one_ref,
-    shift_one_ref,
-    bias_two_ref,
-    gain_two_ref,
-    shift_two_ref,
-    weight_ref,
-    cot_ref,
-    conv_two_ref,
-    vector_ref,
-    weight,
-    held,
-    kernel_one,
-    vectors,
-    arrived,
-):
-    rows_two, width = held.shape
+def ready_kernel(count, cot_ref, table_ref, conv_two_ref, moved_ref, weight_ref, weight):
+    rows_two, width = cot_ref.shape
     frames_two = rows_two // count
     inv = 1.0 / width
-    moves = [
-        pltpu.make_async_copy(conv_one_ref, kernel_one, arrived.at[0]),
-        pltpu.make_async_copy(bias_one_ref, vectors.at[0:1], arrived.at[1]),
-        pltpu.make_async_copy(gain_one_ref, vectors.at[1:2], arrived.at[2]),
-        pltpu.make_async_copy(shift_one_ref, vectors.at[2:3], arrived.at[3]),
-        pltpu.make_async_copy(bias_two_ref, vectors.at[3:4], arrived.at[4]),
-        pltpu.make_async_copy(gain_two_ref, vectors.at[4:5], arrived.at[5]),
-        pltpu.make_async_copy(shift_two_ref, vectors.at[5:6], arrived.at[6]),
-        pltpu.make_async_copy(cot_hbm, held, arrived.at[7]),
-        pltpu.make_async_copy(conv_two_hbm, conv_two_ref, arrived.at[8]),
-    ]
-    for move in moves:
-        move.start()
     row = lax.broadcasted_iota(jnp.int32, (rows_two, 1), 0)
     origin = (row % count) * frames_two + row // count
     mover = (lax.broadcasted_iota(jnp.int32, (rows_two, rows_two), 1) == origin).astype(BF16)
+    moved_ref[...] = jnp.dot(mover, cot_ref[...], preferred_element_type=F32).astype(BF16)
     weight[...] = jnp.zeros_like(weight)
-    for move in moves[:7]:
-        move.wait()
-    kernel = kernel_one[...].astype(F32)
+    kernel = table_ref[:TAPS, :]
     kernel = kernel - jnp.sum(kernel, axis=1, keepdims=True) * inv
-    bias = vectors[0:1, :]
+    bias = table_ref[TAPS : TAPS + 1, :]
     bias = bias - jnp.sum(bias, axis=1, keepdims=True) * inv
     for part in range(3):
         piece = kernel.astype(BF16).astype(F32)
@@ -122,39 +88,27 @@
         weight[3 * ROWS + part : 3 * ROWS + part + 1, :] = piece
         bias = bias - piece
     weight_ref[...] = weight[...].astype(BF16)
-    vector_ref[0:6, :] = vectors[0:6, :]
-    moves[7].wait()
-    cot_ref[...] = jnp.dot(mover, held[...], preferred_element_type=F32).astype(BF16)
-    moves[8].wait()
-
-
-def ready(count, cot, conv_two, conv_one, *vectors):
+
+
+def ready(count, cot, table, conv_two):
     rows_two, width = cot.shape
     vmem = pl.BlockSpec(memory_space=pltpu.VMEM)
     return pl.pallas_call(
         functools.partial(ready_kernel, count),
         out_shape=(
+            jax.ShapeDtypeStruct(cot.shape, BF16),
             jax.ShapeDtypeStruct((128, width), BF16),
-            jax.ShapeDtypeStruct(cot.shape, BF16),
-            jax.ShapeDtypeStruct(conv_two.shape, BF16),
-            jax.ShapeDtypeStruct((8, width), F32),
         ),
-        in_specs=[pl.BlockSpec(memory_space=pltpu.HBM)] * 9,
-        out_specs=(vmem, vmem, vmem, vmem),
-        scratch_shapes=[
-            pltpu.VMEM((128, width), F32),
-            pltpu.VMEM(cot.shape, BF16),
-            pltpu.VMEM(conv_one.shape, BF16),
-            pltpu.VMEM((8, width), F32),
-            pltpu.SemaphoreType.DMA((9,)),
-        ],
+        in_specs=[vmem, vmem, vmem],
+        out_specs=(vmem, vmem),
+        scratch_shapes=[pltpu.VMEM((128, width), F32)],
         cost_estimate=pl.CostEstimate(
             flops=2 * rows_two * rows_two * width,
-            bytes_accessed=4 * conv_two.size + 4 * cot.size,
+            bytes_accessed=4 * cot.size,
             transcendentals=0,
         ),
         compiler_params=pltpu.CompilerParams(vmem_limit_bytes=16 * 1024 * 1024),
-    )(cot, conv_two, conv_one, *vectors)
+    )(cot, table, conv_two)
 
 
 def together(steps):
@@ -169,7 +123,7 @@
     cot_ref,
     weight_ref,
     conv_two_ref,
-    vector_ref,
+    table_ref,
     send_ref,
     keep_ref,
     small_ref,
@@ -218,8 +172,8 @@
     taps[...] = (jnp.dot(taps[...], thrice, preferred_element_type=F32) + ones).astype(BF16)
 
     cent_one[...] = jnp.dot(taps[...], weight_ref[...], preferred_element_type=F32)
-    gain = vector_ref[1:2, :]
-    shift = vector_ref[2:3, :]
+    gain = table_ref[TAPS + 1 : TAPS + 2, :]
+    shift = table_ref[TAPS + 2 : TAPS + 3, :]
     steps_one = rows_one // ROWS
     steps_two = rows_two // ROWS
 
@@ -254,9 +208,9 @@
         total = term if total is None else total + term
     norm_two[...] = total
 
-    bias_two = vector_ref[3:4, :]
-    gain_b = vector_ref[4:5, :]
-    shift_b = vector_ref[5:6, :]
+    bias_two = table_ref[TAPS + 3 : TAPS + 4, :]
+    gain_b = table_ref[TAPS + 4 : TAPS + 5, :]
+    shift_b = table_ref[TAPS + 5 : TAPS + 6, :]
     dz_two[:count, :] = jnp.zeros((count, width), BF16)
     dz_two[count + rows_two :, :] = jnp.zeros((count, width), BF16)
 
@@ -349,7 +303,7 @@
     send_ref[half + ROWS :, :] = lo
 
 
-def local_pass(record, shares, place, got, cot, weight, conv_two, vectors):
+def local_pass(record, shares, place, got, cot, weight, conv_two, table):
     count = got.shape[0] // SPARE
     rows_two, width = cot.shape
     rows_one = 2 * rows_two + count
@@ -383,7 +337,7 @@
             transcendentals=3 * rows_one * width,
         ),
         compiler_params=pltpu.CompilerParams(vmem_limit_bytes=36 * 1024 * 1024),
-    )(place, got, cot, weight, conv_two, vectors)
+    )(place, got, cot, weight, conv_two, table)
 
 
 def tree(terms):
@@ -447,15 +401,11 @@
     got = lax.all_to_all(packed, "dp", split_axis=0, concat_axis=0, tiled=True)
     got = got.reshape(count * SPARE, got.shape[2])
     vectors = (bias_one, gain_one, shift_one, bias_two, gain_two, shift_two)
-    weight, cot, conv_two, vectors = ready(
-        count,
-        cotangent.reshape(count * frames_two, width),
-        conv_two,
-        conv_one,
-        *(v.reshape(1, width) for v in vectors),
-    )
+    table = jnp.concatenate([conv_one.astype(F32), jnp.stack(vectors)], axis=0)
+    cot = cotangent.reshape(count * frames_two, width)
+    cot, weight = ready(count, cot, table, conv_two)
     place = lax.axis_index("dp").astype(jnp.int32).reshape(1)
-    send, keep, small = local_pass(record, shares, place, got, cot, weight, conv_two, vectors)
+    send, keep, small = local_pass(record, shares, place, got, cot, weight, conv_two, table)
     half = keep.shape[0]
     other = exchange(sizes, [("dp", 0)], send)
     total = keep + other[:half].astype(F32)
@@ -465,7 +415,8 @@
     left = [("dp", bit) for bit in range(1, shares.bit_length() - 1)]
     left += [("blk", bit) for bit in range(sizes["blk"].bit_length() - 1)]
     while left:
-        stage, left = left[:2], left[2:]
+        near = left[0][0] == "dp" and left[0][1] < 3 and len(left) > 2
+        stage, left = (left[:2], left[2:]) if near else (left[:1], left[1:])
         parts = 1 << sum(axis == "dp" for axis, _ in stage)
         rows = total.shape[0] // parts
         blocks = [total[i * rows : (i + 1) * rows] for i in range(parts)]

time: 65 us -> 60.2 us (0.926)
  local copies, waits for them, and re-layouts: 7.3 us -> 4.02 us
  starting transfers between devices: 15.8 us -> 14.5 us
    unnamed x18 -> x6, local copies, waits for them, and re-layouts: 7.25 us -> 2.45 us
    all_to_all x1, waiting for transfers between devices: 0.01 us -> 2.99 us  [per_device(): got = lax.all_to_all(packed, 'dp', split_axis=0, concat_axis=0, tiled=True)]
    ppermute x7 -> x6, waiting for transfers between devices: 23.5 us -> 20.9 us  [exchange(): return lax.ppermute(message, axes if len(axes) > 1 else axes[0], pairs)]
    concatenate x0 -> x1, local copies, waits for them, and re-layouts: none -> 1.52 us  [per_device(): table = jnp.concatenate([conv_one.astype(F32), jnp.stack(vectors)], axis=0)]
    ppermute x7 -> x6, starting transfers between devices: 8.43 us -> 7.12 us  [exchange(): return lax.ppermute(message, axes if len(axes) > 1 else axes[0], pairs)]
    add x2 -> x3, other arithmetic: 1.36 us -> 1.42 us  [tree(): terms = [terms[i] + terms[i + 1] for i in range(0, len(terms), 2)]]
  transfers between devices with their start and end apart: 8 -> 7, of which waited for: 6 -> 6; matrix products, arithmetic and copies ran while one was open for 0% -> 3% of each run, Pallas kernels for 2% -> 1%
where the time goes in v3:
time: 60.2 us; the launch traced here: 59.8 us
  waiting for transfers between devices  23.9 us (40%)
  Pallas kernels  14.8 us (25%)
  starting transfers between devices  14.5 us (24%)
  local copies, waits for them, and re-layouts  4.02 us (7%)
  other arithmetic  1.88 us (3%)
  between operations  0.75 us (1%)
    ppermute x6, waiting for transfers between devices, exchange(): return lax.ppermute(message, axes if len(axes) > 1 else axes[0], pairs)  20.9 us
    pallas_call x1, Pallas kernels, local_pass(): pl.pallas_call(functools.partial(local_kernel, record, shares), out_shape...  12.9 us
    all_to_all x1, starting transfers between devices, per_device(): got = lax.all_to_all(packed, 'dp', split_axis=0, concat_axis=0, tiled=True)  7.36 us
    ppermute x6, starting transfers between devices, exchange(): return lax.ppermute(message, axes if len(axes) > 1 else axes[0], pairs)  7.12 us
    all_to_all x1, waiting for transfers between devices, per_device(): got = lax.all_to_all(packed, 'dp', split_axis=0, concat_axis=0, tiled=True)  2.99 us
    unnamed x6, local copies, waits for them, and re-layouts  2.45 us
    concatenate x1, local copies, waits for them, and re-layouts, per_device(): table = jnp.concatenate([conv_one.astype(F32), jnp.stack(vectors)], axis=0)  1.52 us
    add x3, other arithmetic, tree(): terms = [terms[i] + terms[i + 1] for i in range(0, len(terms), 2)]  1.42 us
  transfers between devices with their start and end apart: 7, of which 6 were waited for; matrix products, arithmetic and copies ran while one was open for 3% of the time, Pallas kernels for 1%

profile of v3, /device:TPU:0, one launch (start us, length us, event | category | flops | bytes accessed | tf_op | source)
XLA Modules:
  0.0 59.8 jit_solution(17476660239454147950)
XLA Ops:
  0.6 1.4 %shard_map.131 = bf16[128,384]{1,0:T(8,128)(2,1)} custom-call(s32[1,16]{1,0:T(1,128)} %packing.1, s32[16]{0:T(128)} %bins.1, bf16[16,330]{1,0:T(8,128)(2,1)} %wave_ref.1), custom_call_target="tpu_custom_call" | custom-call | tf_op jit(solution)/shard_map/pallas_call | solution.py:57
  2.0 7.4 %all-to-all-start = ((bf16[16,8,384]{2,1,0:T(8,128)(2,1)}), bf16[16,8,384]{2,1,0:T(8,128)(2,1)S(1)}, u32[]{:S(2)}, u32[]{:S(2)}) async-start(bf16[16,8,384]{2,1,0:T(8,128)(2,1)} %bitcast.12), calls=%async_computation | async-start | bytes 196608 | tf_op jit(solution)/shard_map/all_to_all | solution.py:401
  9.4 1.5 %concatenate.18.table_ref = f32[16,512]{1,0:T(8,128)S(1)} concatenate(bf16[10,512]{1,0:T(8,128)(2,1)} %param.16, f32[1,512]{1,0:T(1,128)} %bitcast.13, f32[1,512]{1,0:T(1,128)} %bitcast.14, f32[1,512]{1,0:T(1,128)} %bitcast.15, f32[1,512]{1,0:T(1,128)} %bitcast.16, f32[1,512]{1,0:T(1,128)} %bitcast.17, f32[1,512]{1,0:T(1,128)} %bitcast.18), dimensions={0} | concatenate | bytes 55296 | tf_op jit(solution)/shard_map/concatenate | solution.py:404
  10.9 1.4 %copy-done = bf16[1536,512]{1,0:T(8,128)(2,1)S(1)} copy-done((bf16[1536,512]{1,0:T(8,128)(2,1)S(1)}, bf16[1536,512]{1,0:T(8,128)(2,1)}, u32[]{:S(2)}) %copy-start) | copy-done | bytes 1572888
  12.3 1.0 %copy-done.2 = bf16[16,32,512]{2,1,0:T(8,128)(2,1)S(1)} copy-done((bf16[16,32,512]{2,1,0:T(8,128)(2,1)S(1)}, bf16[16,32,512]{2,1,0:T(8,128)(2,1)}, u32[]{:S(2)}) %copy-start.2) | copy-done | bytes 524312
  13.4 0.4 shard_map.132
  13.8 3.0 %all-to-all-done = bf16[16,8,384]{2,1,0:T(8,128)(2,1)S(1)} async-done(((bf16[16,8,384]{2,1,0:T(8,128)(2,1)}), bf16[16,8,384]{2,1,0:T(8,128)(2,1)S(1)}, u32[]{:S(2)}, u32[]{:S(2)}) %all-to-all-start) | async-done | bytes 98336 | tf_op jit(solution)/shard_map/all_to_all | solution.py:401
  16.8 12.9 %shard_map.133 = (bf16[800,512]{1,0:T(8,128)(2,1)S(1)}, f32[768,512]{1,0:T(8,128)S(1)}, f32[16,512]{1,0:T(8,128)}) custom-call(s32[1]{0:T(128)} %bitcast.place_ref, bf16[128,384]{1,0:T(8,128)(2,1)S(1)} %bitcast.11, bf16[512,512]{1,0:T(8,128)(2,1)S(1)} %get-tuple-element.6.cot_ref, bf16[128,512]{1,0:T(8,128)(2,1)S(1)} %get-tuple-element.7.weight_ref, ...), custom_call_target="tpu_custom_call" | custom-call | flops 2415919104 | bytes 4259840 | tf_op jit(solution)/shard_map/pallas_call | solution.py:312
  29.7 2.3 %collective-permute-done = bf16[800,512]{1,0:T(8,128)(2,1)S(1)} collective-permute-done((bf16[800,512]{1,0:T(8,128)(2,1)S(1)}, bf16[800,512]{1,0:T(8,128)(2,1)S(1)}, u32[]{:S(2)}, u32[]{:S(2)}) %collective-permute-start) | collective-permute-done | bytes 819232 | tf_op jit(solution)/shard_map/ppermute | solution.py:358
  32.1 0.3 fusion.12
  32.4 0.1 pad_maximum_fusion.2
  32.5 0.1 collective-permute-start.1
  32.6 1.3 %collective-permute-start.2 = (bf16[224,512]{1,0:T(8,128)(2,1)S(1)}, bf16[224,512]{1,0:T(8,128)(2,1)S(1)}, u32[]{:S(2)}, u32[]{:S(2)}) collective-permute-start(bf16[224,512]{1,0:T(8,128)(2,1)S(1)} %get-tuple-element.22), channel_id=1, source_target_pairs={{0,4},{2,6},{4,0},{6,2},{8,12},{10,14},{12,8},{14,10},{16,20},{18,... | collective-permute-start | bytes 688136 | tf_op jit(solution)/shard_map/ppermute | solution.py:358
  33.9 2.1 %collective-permute-start.3 = (bf16[224,512]{1,0:T(8,128)(2,1)S(1)}, bf16[224,512]{1,0:T(8,128)(2,1)S(1)}, u32[]{:S(2)}, u32[]{:S(2)}) collective-permute-start(bf16[224,512]{1,0:T(8,128)(2,1)S(1)} %get-tuple-element.23), channel_id=1, source_target_pairs={{0,12},{2,14},{4,8},{6,10},{8,4},{10,6},{12,0},{14,2},{16,28},{18,... | collective-permute-start | bytes 688136 | tf_op jit(solution)/shard_map/ppermute | solution.py:358
  36.1 5.0 %collective-permute-done.1 = bf16[224,512]{1,0:T(8,128)(2,1)S(1)} collective-permute-done((bf16[224,512]{1,0:T(8,128)(2,1)S(1)}, bf16[224,512]{1,0:T(8,128)(2,1)S(1)}, u32[]{:S(2)}, u32[]{:S(2)}) %collective-permute-start.1) | collective-permute-done | bytes 229408 | tf_op jit(solution)/shard_map/ppermute | solution.py:358
  41.0 4.2 %collective-permute-done.2 = bf16[224,512]{1,0:T(8,128)(2,1)S(1)} collective-permute-done((bf16[224,512]{1,0:T(8,128)(2,1)S(1)}, bf16[224,512]{1,0:T(8,128)(2,1)S(1)}, u32[]{:S(2)}, u32[]{:S(2)}) %collective-permute-start.2) | collective-permute-done | bytes 229408 | tf_op jit(solution)/shard_map/ppermute | solution.py:358
  45.2 0.0 collective-permute-done.3
  45.2 0.1 fusion
  45.4 2.0 %collective-permute-start.4 = (bf16[128,512]{1,0:T(8,128)(2,1)S(1)}, bf16[128,512]{1,0:T(8,128)(2,1)S(1)}, u32[]{:S(2)}, u32[]{:S(2)}) collective-permute-start(bf16[128,512]{1,0:T(8,128)(2,1)S(1)} %pad_maximum_fusion.6), channel_id=1, source_target_pairs={{0,16},{2,18},{4,20},{6,22},{8,24},{10,26},{12,28},{14,30},{16,0},... | collective-permute-start | bytes 393224 | tf_op jit(solution)/shard_map/ppermute | solution.py:358
  47.4 6.0 %collective-permute-done.4 = bf16[128,512]{1,0:T(8,128)(2,1)S(1)} collective-permute-done((bf16[128,512]{1,0:T(8,128)(2,1)S(1)}, bf16[128,512]{1,0:T(8,128)(2,1)S(1)}, u32[]{:S(2)}, u32[]{:S(2)}) %collective-permute-start.4) | collective-permute-done | bytes 131104 | tf_op jit(solution)/shard_map/ppermute | solution.py:358
  53.4 1.6 %collective-permute-start.5 = (bf16[128,512]{1,0:T(8,128)(2,1)S(1)}, bf16[128,512]{1,0:T(8,128)(2,1)S(1)}, u32[]{:S(2)}, u32[]{:S(2)}) collective-permute-start(bf16[128,512]{1,0:T(8,128)(2,1)S(1)} %pad_maximum_fusion.7), channel_id=1, source_target_pairs={{0,1},{1,0},{2,3},{3,2},{4,5},{5,4},{6,7},{7,6},{8,9},{9,8},{10,11... | collective-permute-start | bytes 393224 | tf_op jit(solution)/shard_map/ppermute | solution.py:358
  55.0 3.4 %collective-permute-done.5 = bf16[128,512]{1,0:T(8,128)(2,1)S(1)} collective-permute-done((bf16[128,512]{1,0:T(8,128)(2,1)S(1)}, bf16[128,512]{1,0:T(8,128)(2,1)S(1)}, u32[]{:S(2)}, u32[]{:S(2)}) %collective-permute-start.5) | collective-permute-done | bytes 131104 | tf_op jit(solution)/shard_map/ppermute | solution.py:358
  58.5 0.6 %fusion.8 = f32[16,512]{1,0:T(8,128)} fusion(bf16[16,512]{1,0:T(8,128)(2,1)S(1)} %get-tuple-element.11, bf16[16,512]{1,0:T(8,128)(2,1)S(1)} %get-tuple-element.10, bf16[128,512]{1,0:T(8,128)(2,1)S(1)} %collective-permute-done.5), kind=kLoop, calls=%fused_computation.27 | loop fusion | flops 57344 | bytes 98304 | tf_op jit(solution)/shard_map/add | solution.py:345
  59.1 0.7 %convert_add_fusion.1 = f32[96,512]{1,0:T(8,128)} fusion(bf16[96,512]{1,0:T(8,128)(2,1)S(1)} %fusion.1, bf16[128,512]{1,0:T(8,128)(2,1)S(1)} %collective-permute-done.5), kind=kLoop, calls=%fused_computation.12 | loop fusion | flops 147456 | bytes 393216 | tf_op jit(solution)/shard_map/add | solution.py:345
  (13 shorter events, 0.2 us)
Async XLA Ops:
  2.0 14.8 %all-to-all-start = ((bf16[16,8,384]{2,1,0:T(8,128)(2,1)}), bf16[16,8,384]{2,1,0:T(8,128)(2,1)S(1)}, u32[]{:S(2)}, u32[]{:S(2)}) async-start(bf16[16,8,384]{2,1,0:T(8,128)(2,1)} %bitcast.12), calls=%async_computation | async-start | bytes 196608 | tf_op jit(solution)/shard_map/all_to_all | solution.py:401
  10.9 1.4 %copy-start = (bf16[1536,512]{1,0:T(8,128)(2,1)S(1)}, bf16[1536,512]{1,0:T(8,128)(2,1)}, u32[]{:S(2)}) copy-start(bf16[1536,512]{1,0:T(8,128)(2,1)} %conv_two_ref.3) | copy-start | bytes 4718596
  12.3 1.0 %copy-start.2 = (bf16[16,32,512]{2,1,0:T(8,128)(2,1)S(1)}, bf16[16,32,512]{2,1,0:T(8,128)(2,1)}, u32[]{:S(2)}) copy-start(bf16[16,32,512]{2,1,0:T(8,128)(2,1)} %param.15) | copy-start | bytes 1572868
  13.4 3.4 %copy-start.1 = (bf16[1536,512]{1,0:T(8,128)(2,1)S(1)}, bf16[1536,512]{1,0:T(8,128)(2,1)}, u32[]{:S(2)}) copy-start(bf16[1536,512]{1,0:T(8,128)(2,1)} %conv_two_ref.3) | copy-start | bytes 4718596
  29.7 2.3 %collective-permute-start = (bf16[800,512]{1,0:T(8,128)(2,1)S(1)}, bf16[800,512]{1,0:T(8,128)(2,1)S(1)}, u32[]{:S(2)}, u32[]{:S(2)}) collective-permute-start(bf16[800,512]{1,0:T(8,128)(2,1)S(1)} %get-tuple-element.9), channel_id=1, source_target_pairs={{0,2},{2,0},{4,6},{6,4},{8,10},{10,8},{12,14},{14,12},{16,18},{18,... | collective-permute-start | bytes 2457608 | tf_op jit(solution)/shard_map/ppermute | solution.py:358
  32.5 8.5 %collective-permute-start.1 = (bf16[224,512]{1,0:T(8,128)(2,1)S(1)}, bf16[224,512]{1,0:T(8,128)(2,1)S(1)}, u32[]{:S(2)}, u32[]{:S(2)}) collective-permute-start(bf16[224,512]{1,0:T(8,128)(2,1)S(1)} %get-tuple-element.21), channel_id=1, source_target_pairs={{0,8},{2,10},{4,12},{6,14},{8,0},{10,2},{12,4},{14,6},{16,24},{18,... | collective-permute-start | bytes 688136 | tf_op jit(solution)/shard_map/ppermute | solution.py:358
  32.6 12.6 %collective-permute-start.2 = (bf16[224,512]{1,0:T(8,128)(2,1)S(1)}, bf16[224,512]{1,0:T(8,128)(2,1)S(1)}, u32[]{:S(2)}, u32[]{:S(2)}) collective-permute-start(bf16[224,512]{1,0:T(8,128)(2,1)S(1)} %get-tuple-element.22), channel_id=1, source_target_pairs={{0,4},{2,6},{4,0},{6,2},{8,12},{10,14},{12,8},{14,10},{16,20},{18,... | collective-permute-start | bytes 688136 | tf_op jit(solution)/shard_map/ppermute | solution.py:358
  33.9 11.3 %collective-permute-start.3 = (bf16[224,512]{1,0:T(8,128)(2,1)S(1)}, bf16[224,512]{1,0:T(8,128)(2,1)S(1)}, u32[]{:S(2)}, u32[]{:S(2)}) collective-permute-start(bf16[224,512]{1,0:T(8,128)(2,1)S(1)} %get-tuple-element.23), channel_id=1, source_target_pairs={{0,12},{2,14},{4,8},{6,10},{8,4},{10,6},{12,0},{14,2},{16,28},{18,... | collective-permute-start | bytes 688136 | tf_op jit(solution)/shard_map/ppermute | solution.py:358
  45.4 8.0 %collective-permute-start.4 = (bf16[128,512]{1,0:T(8,128)(2,1)S(1)}, bf16[128,512]{1,0:T(8,128)(2,1)S(1)}, u32[]{:S(2)}, u32[]{:S(2)}) collective-permute-start(bf16[128,512]{1,0:T(8,128)(2,1)S(1)} %pad_maximum_fusion.6), channel_id=1, source_target_pairs={{0,16},{2,18},{4,20},{6,22},{8,24},{10,26},{12,28},{14,30},{16,0},... | collective-permute-start | bytes 393224 | tf_op jit(solution)/shard_map/ppermute | solution.py:358
  53.4 5.0 %collective-permute-start.5 = (bf16[128,512]{1,0:T(8,128)(2,1)S(1)}, bf16[128,512]{1,0:T(8,128)(2,1)S(1)}, u32[]{:S(2)}, u32[]{:S(2)}) collective-permute-start(bf16[128,512]{1,0:T(8,128)(2,1)S(1)} %pad_maximum_fusion.7), channel_id=1, source_target_pairs={{0,1},{1,0},{2,3},{3,2},{4,5},{5,4},{6,7},{7,6},{8,9},{9,8},{10,11... | collective-permute-start | bytes 393224 | tf_op jit(solution)/shard_map/ppermute | solution.py:358

commit v4 on v3

--- a/solution.py
+++ b/solution.py
@@ -23,15 +23,8 @@
 
 
 def gelu_parts(act):
-    bell = jnp.exp(-0.5 * (act * act))
-    t = 1.0 / (1.0 + 0.2316418882 * jnp.abs(act))
-    poly = 0.5307027145 * t - 0.7265760135
-    poly = poly * t + 0.7107068705
-    poly = poly * t - 0.142248368
-    poly = poly * t + 0.127414796
-    tail = poly * t * bell
-    cdf = jnp.where(act < 0.0, tail, 1.0 - tail)
-    return cdf, 0.3989422804014327 * bell
+    cdf = 0.5 + 0.5 * lax.erf(act * 0.7071067811865476)
+    return cdf, 0.3989422804014327 * jnp.exp(-0.5 * (act * act))
 
 
 def pack_kernel(packing, bins, wave_ref, out_ref, wide):
@@ -112,7 +105,7 @@
 
 
 def together(steps):
-    return max(n for n in range(1, 17) if steps % n == 0)
+    return max(n for n in range(1, 66) if steps % n == 0)
 
 
 def local_kernel(

time: 60.2 us -> 54.4 us (0.904)
  Pallas kernels: 14.8 us -> 8.89 us
    pallas_call x1, Pallas kernels: 12.9 us -> 7.05 us  [local_pass(): pl.pallas_call(functools.partial(local_kernel, record, shares), out_shape...]
where the time goes in v4:
time: 54.4 us; the launch traced here: 53.9 us
  waiting for transfers between devices  23.9 us (44%)
  starting transfers between devices  14.4 us (26%)
  Pallas kernels  8.89 us (16%)
  local copies, waits for them, and re-layouts  4.02 us (7%)
  other arithmetic  1.88 us (3%)
  between operations  0.75 us (1%)
    ppermute x6, waiting for transfers between devices, exchange(): return lax.ppermute(message, axes if len(axes) > 1 else axes[0], pairs)  21 us
    all_to_all x1, starting transfers between devices, per_device(): got = lax.all_to_all(packed, 'dp', split_axis=0, concat_axis=0, tiled=True)  7.36 us
    ppermute x6, starting transfers between devices, exchange(): return lax.ppermute(message, axes if len(axes) > 1 else axes[0], pairs)  7.09 us
    pallas_call x1, Pallas kernels, local_pass(): pl.pallas_call(functools.partial(local_kernel, record, shares), out_shape...  7.05 us
    all_to_all x1, waiting for transfers between devices, per_device(): got = lax.all_to_all(packed, 'dp', split_axis=0, concat_axis=0, tiled=True)  2.99 us
    unnamed x6, local copies, waits for them, and re-layouts  2.45 us
    concatenate x1, local copies, waits for them, and re-layouts, per_device(): table = jnp.concatenate([conv_one.astype(F32), jnp.stack(vectors)], axis=0)  1.52 us
    add x3, other arithmetic, tree(): terms = [terms[i] + terms[i + 1] for i in range(0, len(terms), 2)]  1.42 us
  transfers between devices with their start and end apart: 7, of which 6 were waited for; matrix products, arithmetic and copies ran while one was open for 3% of the time, Pallas kernels for 1%

profile of v4, /device:TPU:0, one launch (start us, length us, event | category | flops | bytes accessed | tf_op | source)
XLA Modules:
  0.0 53.9 jit_solution(12085856471240669991)
XLA Ops:
  0.6 1.4 %shard_map.131 = bf16[128,384]{1,0:T(8,128)(2,1)} custom-call(s32[1,16]{1,0:T(1,128)} %packing.1, s32[16]{0:T(128)} %bins.1, bf16[16,330]{1,0:T(8,128)(2,1)} %wave_ref.1), custom_call_target="tpu_custom_call" | custom-call | tf_op jit(solution)/shard_map/pallas_call | solution.py:50
  2.0 7.4 %all-to-all-start = ((bf16[16,8,384]{2,1,0:T(8,128)(2,1)}), bf16[16,8,384]{2,1,0:T(8,128)(2,1)S(1)}, u32[]{:S(2)}, u32[]{:S(2)}) async-start(bf16[16,8,384]{2,1,0:T(8,128)(2,1)} %bitcast.12), calls=%async_computation | async-start | bytes 196608 | tf_op jit(solution)/shard_map/all_to_all | solution.py:394
  9.4 1.5 %concatenate.18.table_ref = f32[16,512]{1,0:T(8,128)S(1)} concatenate(bf16[10,512]{1,0:T(8,128)(2,1)} %param.16, f32[1,512]{1,0:T(1,128)} %bitcast.13, f32[1,512]{1,0:T(1,128)} %bitcast.14, f32[1,512]{1,0:T(1,128)} %bitcast.15, f32[1,512]{1,0:T(1,128)} %bitcast.16, f32[1,512]{1,0:T(1,128)} %bitcast.17, f32[1,512]{1,0:T(1,128)} %bitcast.18), dimensions={0} | concatenate | bytes 55296 | tf_op jit(solution)/shard_map/concatenate | solution.py:397
  10.9 1.4 %copy-done = bf16[1536,512]{1,0:T(8,128)(2,1)S(1)} copy-done((bf16[1536,512]{1,0:T(8,128)(2,1)S(1)}, bf16[1536,512]{1,0:T(8,128)(2,1)}, u32[]{:S(2)}) %copy-start) | copy-done | bytes 1572888
  12.3 1.0 %copy-done.2 = bf16[16,32,512]{2,1,0:T(8,128)(2,1)S(1)} copy-done((bf16[16,32,512]{2,1,0:T(8,128)(2,1)S(1)}, bf16[16,32,512]{2,1,0:T(8,128)(2,1)}, u32[]{:S(2)}) %copy-start.2) | copy-done | bytes 524312
  13.4 0.4 shard_map.132
  13.8 3.0 %all-to-all-done = bf16[16,8,384]{2,1,0:T(8,128)(2,1)S(1)} async-done(((bf16[16,8,384]{2,1,0:T(8,128)(2,1)}), bf16[16,8,384]{2,1,0:T(8,128)(2,1)S(1)}, u32[]{:S(2)}, u32[]{:S(2)}) %all-to-all-start) | async-done | bytes 98336 | tf_op jit(solution)/shard_map/all_to_all | solution.py:394
  16.8 7.1 %shard_map.133 = (bf16[800,512]{1,0:T(8,128)(2,1)S(1)}, f32[768,512]{1,0:T(8,128)S(1)}, f32[16,512]{1,0:T(8,128)}) custom-call(s32[1]{0:T(128)} %bitcast.place_ref, bf16[128,384]{1,0:T(8,128)(2,1)S(1)} %bitcast.11, bf16[512,512]{1,0:T(8,128)(2,1)S(1)} %get-tuple-element.6.cot_ref, bf16[128,512]{1,0:T(8,128)(2,1)S(1)} %get-tuple-element.7.weight_ref, ...), custom_call_target="tpu_custom_call" | custom-call | flops 2415919104 | bytes 4259840 | tf_op jit(solution)/shard_map/pallas_call | solution.py:305
  23.9 0.0 collective-permute-start
  23.9 2.3 %collective-permute-done = bf16[800,512]{1,0:T(8,128)(2,1)S(1)} collective-permute-done((bf16[800,512]{1,0:T(8,128)(2,1)S(1)}, bf16[800,512]{1,0:T(8,128)(2,1)S(1)}, u32[]{:S(2)}, u32[]{:S(2)}) %collective-permute-start) | collective-permute-done | bytes 819232 | tf_op jit(solution)/shard_map/ppermute | solution.py:351
  26.2 0.3 fusion.12
  26.6 0.1 pad_maximum_fusion.2
  26.6 0.1 collective-permute-start.1
  26.7 1.3 %collective-permute-start.2 = (bf16[224,512]{1,0:T(8,128)(2,1)S(1)}, bf16[224,512]{1,0:T(8,128)(2,1)S(1)}, u32[]{:S(2)}, u32[]{:S(2)}) collective-permute-start(bf16[224,512]{1,0:T(8,128)(2,1)S(1)} %get-tuple-element.22), channel_id=1, source_target_pairs={{0,4},{2,6},{4,0},{6,2},{8,12},{10,14},{12,8},{14,10},{16,20},{18,... | collective-permute-start | bytes 688136 | tf_op jit(solution)/shard_map/ppermute | solution.py:351
  28.1 2.1 %collective-permute-start.3 = (bf16[224,512]{1,0:T(8,128)(2,1)S(1)}, bf16[224,512]{1,0:T(8,128)(2,1)S(1)}, u32[]{:S(2)}, u32[]{:S(2)}) collective-permute-start(bf16[224,512]{1,0:T(8,128)(2,1)S(1)} %get-tuple-element.23), channel_id=1, source_target_pairs={{0,12},{2,14},{4,8},{6,10},{8,4},{10,6},{12,0},{14,2},{16,28},{18,... | collective-permute-start | bytes 688136 | tf_op jit(solution)/shard_map/ppermute | solution.py:351
  30.2 5.0 %collective-permute-done.1 = bf16[224,512]{1,0:T(8,128)(2,1)S(1)} collective-permute-done((bf16[224,512]{1,0:T(8,128)(2,1)S(1)}, bf16[224,512]{1,0:T(8,128)(2,1)S(1)}, u32[]{:S(2)}, u32[]{:S(2)}) %collective-permute-start.1) | collective-permute-done | bytes 229408 | tf_op jit(solution)/shard_map/ppermute | solution.py:351
  35.1 4.2 %collective-permute-done.2 = bf16[224,512]{1,0:T(8,128)(2,1)S(1)} collective-permute-done((bf16[224,512]{1,0:T(8,128)(2,1)S(1)}, bf16[224,512]{1,0:T(8,128)(2,1)S(1)}, u32[]{:S(2)}, u32[]{:S(2)}) %collective-permute-start.2) | collective-permute-done | bytes 229408 | tf_op jit(solution)/shard_map/ppermute | solution.py:351
  39.3 0.1 fusion
  39.5 2.0 %collective-permute-start.4 = (bf16[128,512]{1,0:T(8,128)(2,1)S(1)}, bf16[128,512]{1,0:T(8,128)(2,1)S(1)}, u32[]{:S(2)}, u32[]{:S(2)}) collective-permute-start(bf16[128,512]{1,0:T(8,128)(2,1)S(1)} %pad_maximum_fusion.6), channel_id=1, source_target_pairs={{0,16},{2,18},{4,20},{6,22},{8,24},{10,26},{12,28},{14,30},{16,0},... | collective-permute-start | bytes 393224 | tf_op jit(solution)/shard_map/ppermute | solution.py:351
  41.5 6.0 %collective-permute-done.4 = bf16[128,512]{1,0:T(8,128)(2,1)S(1)} collective-permute-done((bf16[128,512]{1,0:T(8,128)(2,1)S(1)}, bf16[128,512]{1,0:T(8,128)(2,1)S(1)}, u32[]{:S(2)}, u32[]{:S(2)}) %collective-permute-start.4) | collective-permute-done | bytes 131104 | tf_op jit(solution)/shard_map/ppermute | solution.py:351
  47.6 1.6 %collective-permute-start.5 = (bf16[128,512]{1,0:T(8,128)(2,1)S(1)}, bf16[128,512]{1,0:T(8,128)(2,1)S(1)}, u32[]{:S(2)}, u32[]{:S(2)}) collective-permute-start(bf16[128,512]{1,0:T(8,128)(2,1)S(1)} %pad_maximum_fusion.7), channel_id=1, source_target_pairs={{0,1},{1,0},{2,3},{3,2},{4,5},{5,4},{6,7},{7,6},{8,9},{9,8},{10,11... | collective-permute-start | bytes 393224 | tf_op jit(solution)/shard_map/ppermute | solution.py:351
  49.1 3.5 %collective-permute-done.5 = bf16[128,512]{1,0:T(8,128)(2,1)S(1)} collective-permute-done((bf16[128,512]{1,0:T(8,128)(2,1)S(1)}, bf16[128,512]{1,0:T(8,128)(2,1)S(1)}, u32[]{:S(2)}, u32[]{:S(2)}) %collective-permute-start.5) | collective-permute-done | bytes 131104 | tf_op jit(solution)/shard_map/ppermute | solution.py:351
  52.6 0.6 %fusion.8 = f32[16,512]{1,0:T(8,128)} fusion(bf16[16,512]{1,0:T(8,128)(2,1)S(1)} %get-tuple-element.11, bf16[16,512]{1,0:T(8,128)(2,1)S(1)} %get-tuple-element.10, bf16[128,512]{1,0:T(8,128)(2,1)S(1)} %collective-permute-done.5), kind=kLoop, calls=%fused_computation.27 | loop fusion | flops 57344 | bytes 98304 | tf_op jit(solution)/shard_map/add | solution.py:338
  53.2 0.7 %convert_add_fusion.1 = f32[96,512]{1,0:T(8,128)} fusion(bf16[96,512]{1,0:T(8,128)(2,1)S(1)} %fusion.1, bf16[128,512]{1,0:T(8,128)(2,1)S(1)} %collective-permute-done.5), kind=kLoop, calls=%fused_computation.12 | loop fusion | flops 147456 | bytes 393216 | tf_op jit(solution)/shard_map/add | solution.py:338
  (13 shorter events, 0.2 us)
Async XLA Ops:
  2.0 14.8 %all-to-all-start = ((bf16[16,8,384]{2,1,0:T(8,128)(2,1)}), bf16[16,8,384]{2,1,0:T(8,128)(2,1)S(1)}, u32[]{:S(2)}, u32[]{:S(2)}) async-start(bf16[16,8,384]{2,1,0:T(8,128)(2,1)} %bitcast.12), calls=%async_computation | async-start | bytes 196608 | tf_op jit(solution)/shard_map/all_to_all | solution.py:394
  10.9 1.4 %copy-start = (bf16[1536,512]{1,0:T(8,128)(2,1)S(1)}, bf16[1536,512]{1,0:T(8,128)(2,1)}, u32[]{:S(2)}) copy-start(bf16[1536,512]{1,0:T(8,128)(2,1)} %conv_two_ref.3) | copy-start | bytes 4718596
  12.3 1.0 %copy-start.2 = (bf16[16,32,512]{2,1,0:T(8,128)(2,1)S(1)}, bf16[16,32,512]{2,1,0:T(8,128)(2,1)}, u32[]{:S(2)}) copy-start(bf16[16,32,512]{2,1,0:T(8,128)(2,1)} %param.15) | copy-start | bytes 1572868
  13.4 3.4 %copy-start.1 = (bf16[1536,512]{1,0:T(8,128)(2,1)S(1)}, bf16[1536,512]{1,0:T(8,128)(2,1)}, u32[]{:S(2)}) copy-start(bf16[1536,512]{1,0:T(8,128)(2,1)} %conv_two_ref.3) | copy-start | bytes 4718596
  23.9 2.3 %collective-permute-start = (bf16[800,512]{1,0:T(8,128)(2,1)S(1)}, bf16[800,512]{1,0:T(8,128)(2,1)S(1)}, u32[]{:S(2)}, u32[]{:S(2)}) collective-permute-start(bf16[800,512]{1,0:T(8,128)(2,1)S(1)} %get-tuple-element.9), channel_id=1, source_target_pairs={{0,2},{2,0},{4,6},{6,4},{8,10},{10,8},{12,14},{14,12},{16,18},{18,... | collective-permute-start | bytes 2457608 | tf_op jit(solution)/shard_map/ppermute | solution.py:351
  26.6 8.5 %collective-permute-start.1 = (bf16[224,512]{1,0:T(8,128)(2,1)S(1)}, bf16[224,512]{1,0:T(8,128)(2,1)S(1)}, u32[]{:S(2)}, u32[]{:S(2)}) collective-permute-start(bf16[224,512]{1,0:T(8,128)(2,1)S(1)} %get-tuple-element.21), channel_id=1, source_target_pairs={{0,8},{2,10},{4,12},{6,14},{8,0},{10,2},{12,4},{14,6},{16,24},{18,... | collective-permute-start | bytes 688136 | tf_op jit(solution)/shard_map/ppermute | solution.py:351
  26.7 12.6 %collective-permute-start.2 = (bf16[224,512]{1,0:T(8,128)(2,1)S(1)}, bf16[224,512]{1,0:T(8,128)(2,1)S(1)}, u32[]{:S(2)}, u32[]{:S(2)}) collective-permute-start(bf16[224,512]{1,0:T(8,128)(2,1)S(1)} %get-tuple-element.22), channel_id=1, source_target_pairs={{0,4},{2,6},{4,0},{6,2},{8,12},{10,14},{12,8},{14,10},{16,20},{18,... | collective-permute-start | bytes 688136 | tf_op jit(solution)/shard_map/ppermute | solution.py:351
  28.1 11.3 %collective-permute-start.3 = (bf16[224,512]{1,0:T(8,128)(2,1)S(1)}, bf16[224,512]{1,0:T(8,128)(2,1)S(1)}, u32[]{:S(2)}, u32[]{:S(2)}) collective-permute-start(bf16[224,512]{1,0:T(8,128)(2,1)S(1)} %get-tuple-element.23), channel_id=1, source_target_pairs={{0,12},{2,14},{4,8},{6,10},{8,4},{10,6},{12,0},{14,2},{16,28},{18,... | collective-permute-start | bytes 688136 | tf_op jit(solution)/shard_map/ppermute | solution.py:351
  39.5 8.0 %collective-permute-start.4 = (bf16[128,512]{1,0:T(8,128)(2,1)S(1)}, bf16[128,512]{1,0:T(8,128)(2,1)S(1)}, u32[]{:S(2)}, u32[]{:S(2)}) collective-permute-start(bf16[128,512]{1,0:T(8,128)(2,1)S(1)} %pad_maximum_fusion.6), channel_id=1, source_target_pairs={{0,16},{2,18},{4,20},{6,22},{8,24},{10,26},{12,28},{14,30},{16,0},... | collective-permute-start | bytes 393224 | tf_op jit(solution)/shard_map/ppermute | solution.py:351
  47.6 5.0 %collective-permute-start.5 = (bf16[128,512]{1,0:T(8,128)(2,1)S(1)}, bf16[128,512]{1,0:T(8,128)(2,1)S(1)}, u32[]{:S(2)}, u32[]{:S(2)}) collective-permute-start(bf16[128,512]{1,0:T(8,128)(2,1)S(1)} %pad_maximum_fusion.7), channel_id=1, source_target_pairs={{0,1},{1,0},{2,3},{3,2},{4,5},{5,4},{6,7},{7,6},{8,9},{9,8},{10,11... | collective-permute-start | bytes 393224 | tf_op jit(solution)/shard_map/ppermute | solution.py:351

commit v5 on v4

--- a/solution.py
+++ b/solution.py
@@ -15,11 +15,6 @@
 SPARE = 8
 F32 = jnp.float32
 BF16 = jnp.bfloat16
-
-
-def split_two(x):
-    hi = x.astype(BF16)
-    return hi, (x - hi.astype(F32)).astype(BF16)
 
 
 def gelu_parts(act):
@@ -290,10 +285,6 @@
     small_ref[:TAPS, :] = first[:TAPS, :]
     for spot, sums in enumerate(sums_one + sums_two):
         small_ref[TAPS + spot : TAPS + spot + 1, :] = jnp.sum(sums, axis=0, keepdims=True)
-    hi, lo = split_two(small_ref[...])
-    half = send_ref.shape[0] - 2 * ROWS
-    send_ref[half : half + ROWS, :] = hi
-    send_ref[half + ROWS :, :] = lo
 
 
 def local_pass(record, shares, place, got, cot, weight, conv_two, table):
@@ -305,7 +296,7 @@
     return pl.pallas_call(
         functools.partial(local_kernel, record, shares),
         out_shape=(
-            jax.ShapeDtypeStruct((half + 2 * ROWS, width), BF16),
+            jax.ShapeDtypeStruct((half, width), BF16),
             jax.ShapeDtypeStruct((half, width), F32),
             jax.ShapeDtypeStruct((ROWS, width), F32),
         ),
@@ -351,24 +342,39 @@
     return lax.ppermute(message, axes if len(axes) > 1 else axes[0], pairs)
 
 
-def merge(sizes, stage, blocks, small):
-    dp_bits = [item for item in stage if item[0] == "dp"]
-    blk_bits = [item for item in stage if item[0] != "dp"]
-    hi, lo = split_two(small)
-    tail = [hi, lo]
-    messages = [jnp.concatenate([block.astype(BF16)] + tail, axis=0) for block in blocks]
-    rows = blocks[0].shape[0]
-    own = messages[0][:rows].astype(F32) if blk_bits else blocks[0]
-    terms = [own]
-    smalls = [hi.astype(F32) + lo.astype(F32)]
-    for code in range(1, 1 << len(stage)):
-        block = code >> len(blk_bits)
-        chosen = [b for i, b in enumerate(dp_bits) if block >> (len(dp_bits) - 1 - i) & 1]
-        chosen += [b for i, b in enumerate(blk_bits) if code >> i & 1]
-        got = exchange(sizes, chosen, messages[block])
-        terms.append(got[:rows].astype(F32))
-        smalls.append(got[rows : rows + ROWS].astype(F32) + got[rows + ROWS :].astype(F32))
-    return tree(terms), tree(smalls)
+def sum_all(sizes, send, keep, small):
+    near = exchange(sizes, [("dp", 0)], small)
+    total = keep + exchange(sizes, [("dp", 0)], send).astype(F32)
+    total, small = lax.optimization_barrier((total, small + near))
+    left = [("dp", bit) for bit in range(1, sizes["dp"].bit_length() - 1)]
+    for bit in left:
+        small = small + exchange(sizes, [bit], small)
+    if len(left) >= 3:
+        pair, onward = left[:2], left[2]
+        rows = total.shape[0] // 8
+        sums = {}
+        for part in (1, 0):
+            blocks = [total[(2 * i + part) * rows : (2 * i + part + 1) * rows] for i in range(4)]
+            terms = [blocks[0]]
+            for code in (1, 2, 3):
+                chosen = [bit for i, bit in enumerate(pair) if code >> (1 - i) & 1]
+                terms.append(exchange(sizes, chosen, blocks[code].astype(BF16)).astype(F32))
+            sums[part] = tree(terms)
+        total = sums[0] + exchange(sizes, [onward], sums[1].astype(BF16)).astype(F32)
+        left = left[3:]
+    for bit in left:
+        half = total.shape[0] // 2
+        total = total[:half] + exchange(sizes, [bit], total[half:].astype(BF16)).astype(F32)
+    rows = total.shape[0]
+    for bit in range(sizes["blk"].bit_length() - 1):
+        hi = small.astype(BF16)
+        lo = (small - hi.astype(F32)).astype(BF16)
+        own = jnp.concatenate([total.astype(BF16), hi, lo], axis=0)
+        both = own.astype(F32), exchange(sizes, [("blk", bit)], own).astype(F32)
+        total = both[0][:rows] + both[1][:rows]
+        parts = [b[rows : rows + ROWS] + b[rows + ROWS :] for b in both]
+        small = parts[0] + parts[1]
+    return total, small
 
 
 def per_device(
@@ -399,22 +405,7 @@
     cot, weight = ready(count, cot, table, conv_two)
     place = lax.axis_index("dp").astype(jnp.int32).reshape(1)
     send, keep, small = local_pass(record, shares, place, got, cot, weight, conv_two, table)
-    half = keep.shape[0]
-    other = exchange(sizes, [("dp", 0)], send)
-    total = keep + other[:half].astype(F32)
-    mine = send[half : half + ROWS].astype(F32) + send[half + ROWS :].astype(F32)
-    yours = other[half : half + ROWS].astype(F32) + other[half + ROWS :].astype(F32)
-    small = mine + yours
-    left = [("dp", bit) for bit in range(1, shares.bit_length() - 1)]
-    left += [("blk", bit) for bit in range(sizes["blk"].bit_length() - 1)]
-    while left:
-        near = left[0][0] == "dp" and left[0][1] < 3 and len(left) > 2
-        stage, left = (left[:2], left[2:]) if near else (left[:1], left[1:])
-        parts = 1 << sum(axis == "dp" for axis, _ in stage)
-        rows = total.shape[0] // parts
-        blocks = [total[i * rows : (i + 1) * rows] for i in range(parts)]
-        total, small = merge(sizes, stage, blocks, small)
-    return total, small
+    return sum_all(sizes, send, keep, small)
 
 
 def solution(mesh):

time: 54.4 us -> 56.2 us (1.033)
  starting transfers between devices: 14.4 us -> 20.1 us
  waiting for transfers between devices: 23.9 us -> 20.7 us
  Pallas kernels: 8.89 us -> 8.3 us
    ppermute x6 -> x13, starting transfers between devices: 7.09 us -> 12.8 us  [exchange(): return lax.ppermute(message, axes if len(axes) > 1 else axes[0], pairs)]
    ppermute x6 -> x13, waiting for transfers between devices: 21 us -> 17.7 us  [exchange(): return lax.ppermute(message, axes if len(axes) > 1 else axes[0], pairs)]
    pallas_call x1, Pallas kernels: 7.05 us -> 6.46 us  [local_pass(): pl.pallas_call(functools.partial(local_kernel, record, shares), out_shape...]
    add x3 -> x6, other arithmetic: 1.42 us -> 1.62 us  [the longest x1 0.7 us: sum_all(): total = both[0][:rows] + both[1][:rows]]
  transfers between devices with their start and end apart: 7 -> 14, of which waited for: 6 -> 7; matrix products, arithmetic and copies ran while one was open for 3% -> 3% of each run, Pallas kernels for 1% -> 1%
where the time goes in v5:
time: 56.2 us; the launch traced here: 55.8 us
  waiting for transfers between devices  20.7 us (37%)
  starting transfers between devices  20.1 us (36%)
  Pallas kernels  8.3 us (15%)
  local copies, waits for them, and re-layouts  4 us (7%)
  other arithmetic  1.9 us (3%)
  between operations  0.76 us (1%)
    ppermute x13, waiting for transfers between devices, exchange(): return lax.ppermute(message, axes if len(axes) > 1 else axes[0], pairs)  17.7 us
    ppermute x13, starting transfers between devices, exchange(): return lax.ppermute(message, axes if len(axes) > 1 else axes[0], pairs)  12.8 us
    all_to_all x1, starting transfers between devices, per_device(): got = lax.all_to_all(packed, 'dp', split_axis=0, concat_axis=0, tiled=True)  7.36 us
    pallas_call x1, Pallas kernels, local_pass(): pl.pallas_call(functools.partial(local_kernel, record, shares), out_shape...  6.46 us
    all_to_all x1, waiting for transfers between devices, per_device(): got = lax.all_to_all(packed, 'dp', split_axis=0, concat_axis=0, tiled=True)  2.99 us
    unnamed x6, local copies, waits for them, and re-layouts  2.45 us
    concatenate x1, local copies, waits for them, and re-layouts, per_device(): table = jnp.concatenate([conv_one.astype(F32), jnp.stack(vectors)], axis=0)  1.52 us
    pallas_call x1, Pallas kernels, pack(): pl.pallas_call(pack_kernel, out_shape=jax.ShapeDtypeStruct((count * SPARE...  1.4 us
  transfers between devices with their start and end apart: 14, of which 7 were waited for; matrix products, arithmetic and copies ran while one was open for 3% of the time, Pallas kernels for 1%

profile of v5, /device:TPU:0, one launch (start us, length us, event | category | flops | bytes accessed | tf_op | source)
XLA Modules:
  0.0 55.8 jit_solution(11416966781160039972)
XLA Ops:
  0.6 1.4 %shard_map.131 = bf16[128,384]{1,0:T(8,128)(2,1)} custom-call(s32[1,16]{1,0:T(1,128)} %packing.1, s32[16]{0:T(128)} %bins.1, bf16[16,330]{1,0:T(8,128)(2,1)} %wave_ref.1), custom_call_target="tpu_custom_call" | custom-call | tf_op jit(solution)/shard_map/pallas_call | solution.py:45
  2.0 7.4 %all-to-all-start = ((bf16[16,8,384]{2,1,0:T(8,128)(2,1)}), bf16[16,8,384]{2,1,0:T(8,128)(2,1)S(1)}, u32[]{:S(2)}, u32[]{:S(2)}) async-start(bf16[16,8,384]{2,1,0:T(8,128)(2,1)} %bitcast.12), calls=%async_computation | async-start | bytes 196608 | tf_op jit(solution)/shard_map/all_to_all | solution.py:400
  9.4 1.5 %concatenate.6.table_ref = f32[16,512]{1,0:T(8,128)S(1)} concatenate(bf16[10,512]{1,0:T(8,128)(2,1)} %param.16, f32[1,512]{1,0:T(1,128)} %bitcast.13, f32[1,512]{1,0:T(1,128)} %bitcast.14, f32[1,512]{1,0:T(1,128)} %bitcast.15, f32[1,512]{1,0:T(1,128)} %bitcast.16, f32[1,512]{1,0:T(1,128)} %bitcast.17, f32[1,512]{1,0:T(1,128)} %bitcast.18), dimensions={0} | concatenate | bytes 55296 | tf_op jit(solution)/shard_map/concatenate | solution.py:403
  10.9 1.4 %copy-done = bf16[1536,512]{1,0:T(8,128)(2,1)S(1)} copy-done((bf16[1536,512]{1,0:T(8,128)(2,1)S(1)}, bf16[1536,512]{1,0:T(8,128)(2,1)}, u32[]{:S(2)}) %copy-start) | copy-done | bytes 1572888
  12.3 1.0 %copy-done.2 = bf16[16,32,512]{2,1,0:T(8,128)(2,1)S(1)} copy-done((bf16[16,32,512]{2,1,0:T(8,128)(2,1)S(1)}, bf16[16,32,512]{2,1,0:T(8,128)(2,1)}, u32[]{:S(2)}) %copy-start.2) | copy-done | bytes 524312
  13.8 3.0 %all-to-all-done = bf16[16,8,384]{2,1,0:T(8,128)(2,1)S(1)} async-done(((bf16[16,8,384]{2,1,0:T(8,128)(2,1)}), bf16[16,8,384]{2,1,0:T(8,128)(2,1)S(1)}, u32[]{:S(2)}, u32[]{:S(2)}) %all-to-all-start) | async-done | bytes 98336 | tf_op jit(solution)/shard_map/all_to_all | solution.py:400
  16.8 6.5 %shard_map.133 = (bf16[768,512]{1,0:T(8,128)(2,1)S(1)}, f32[768,512]{1,0:T(8,128)S(1)}, f32[16,512]{1,0:T(8,128)S(1)}) custom-call(s32[1]{0:T(128)} %bitcast.place_ref, bf16[128,384]{1,0:T(8,128)(2,1)S(1)} %bitcast.11, bf16[512,512]{1,0:T(8,128)(2,1)S(1)} %get-tuple-element.9.cot_ref, bf16[128,512]{1,0:T(8,128)(2,1)S(1)} %get-tuple-element.10.weight_ref, ...), custom_call_target="tpu_custom_call" | custom-call | flops 2415919104 | bytes 4259840 | tf_op jit(solution)/shard_map/pallas_call | solution.py:296
  23.9 1.8 %collective-permute-done.1 = f32[16,512]{1,0:T(8,128)S(1)} collective-permute-done((f32[16,512]{1,0:T(8,128)S(1)}, f32[16,512]{1,0:T(8,128)S(1)}, u32[]{:S(2)}, u32[]{:S(2)}) %collective-permute-start.1) | collective-permute-done | bytes 32800 | tf_op jit(solution)/shard_map/ppermute | solution.py:342
  26.1 0.9 %collective-permute-start.7 = (bf16[96,512]{1,0:T(8,128)(2,1)S(1)}, bf16[96,512]{1,0:T(8,128)(2,1)S(1)}, u32[]{:S(2)}, u32[]{:S(2)}) collective-permute-start(bf16[96,512]{1,0:T(8,128)(2,1)S(1)} %get-tuple-element.17), channel_id=1, source_target_pairs={{0,12},{2,14},{4,8},{6,10},{8,4},{10,6},{12,0},{14,2},{16,28},{18,... | collective-permute-start | bytes 294920 | tf_op jit(solution)/shard_map/ppermute | solution.py:342
  27.0 0.6 %collective-permute-start.6 = (bf16[96,512]{1,0:T(8,128)(2,1)S(1)}, bf16[96,512]{1,0:T(8,128)(2,1)S(1)}, u32[]{:S(2)}, u32[]{:S(2)}) collective-permute-start(bf16[96,512]{1,0:T(8,128)(2,1)S(1)} %get-tuple-element.18), channel_id=1, source_target_pairs={{0,4},{2,6},{4,0},{6,2},{8,12},{10,14},{12,8},{14,10},{16,20},{18,... | collective-permute-start | bytes 294920 | tf_op jit(solution)/shard_map/ppermute | solution.py:342
  27.5 2.1 %collective-permute-start.5 = (bf16[96,512]{1,0:T(8,128)(2,1)S(1)}, bf16[96,512]{1,0:T(8,128)(2,1)S(1)}, u32[]{:S(2)}, u32[]{:S(2)}) collective-permute-start(bf16[96,512]{1,0:T(8,128)(2,1)S(1)} %get-tuple-element.19), channel_id=1, source_target_pairs={{0,8},{2,10},{4,12},{6,14},{8,0},{10,2},{12,4},{14,6},{16,24},{18,... | collective-permute-start | bytes 294920 | tf_op jit(solution)/shard_map/ppermute | solution.py:342
  29.7 4.7 %collective-permute-done.9 = f32[16,512]{1,0:T(8,128)S(1)} collective-permute-done((f32[16,512]{1,0:T(8,128)S(1)}, f32[16,512]{1,0:T(8,128)S(1)}, u32[]{:S(2)}, u32[]{:S(2)}) %collective-permute-start.9) | collective-permute-done | bytes 32800 | tf_op jit(solution)/shard_map/ppermute | solution.py:342
  34.7 1.7 %collective-permute-start.2 = (bf16[96,512]{1,0:T(8,128)(2,1)S(1)}, bf16[96,512]{1,0:T(8,128)(2,1)S(1)}, u32[]{:S(2)}, u32[]{:S(2)}) collective-permute-start(bf16[96,512]{1,0:T(8,128)(2,1)S(1)} %get-tuple-element.16), channel_id=1, source_target_pairs={{0,8},{2,10},{4,12},{6,14},{8,0},{10,2},{12,4},{14,6},{16,24},{18,... | collective-permute-start | bytes 294920 | tf_op jit(solution)/shard_map/ppermute | solution.py:342
  36.4 2.1 %collective-permute-done.10 = f32[16,512]{1,0:T(8,128)S(1)} collective-permute-done((f32[16,512]{1,0:T(8,128)S(1)}, f32[16,512]{1,0:T(8,128)S(1)}, u32[]{:S(2)}, u32[]{:S(2)}) %collective-permute-start.10) | collective-permute-done | bytes 32800 | tf_op jit(solution)/shard_map/ppermute | solution.py:342
  38.5 1.3 %collective-permute-start.4 = (bf16[96,512]{1,0:T(8,128)(2,1)S(1)}, bf16[96,512]{1,0:T(8,128)(2,1)S(1)}, u32[]{:S(2)}, u32[]{:S(2)}) collective-permute-start(bf16[96,512]{1,0:T(8,128)(2,1)S(1)} %get-tuple-element.20), channel_id=1, source_target_pairs={{0,12},{2,14},{4,8},{6,10},{8,4},{10,6},{12,0},{14,2},{16,28},{18,... | collective-permute-start | bytes 294920 | tf_op jit(solution)/shard_map/ppermute | solution.py:342
  39.8 0.7 %collective-permute-start.3 = (bf16[96,512]{1,0:T(8,128)(2,1)S(1)}, bf16[96,512]{1,0:T(8,128)(2,1)S(1)}, u32[]{:S(2)}, u32[]{:S(2)}) collective-permute-start(bf16[96,512]{1,0:T(8,128)(2,1)S(1)} %get-tuple-element.21), channel_id=1, source_target_pairs={{0,4},{2,6},{4,0},{6,2},{8,12},{10,14},{12,8},{14,10},{16,20},{18,... | collective-permute-start | bytes 294920 | tf_op jit(solution)/shard_map/ppermute | solution.py:342
  40.5 2.3 %collective-permute-start.11 = (f32[16,512]{1,0:T(8,128)S(1)}, f32[16,512]{1,0:T(8,128)S(1)}, u32[]{:S(2)}, u32[]{:S(2)}) collective-permute-start(f32[16,512]{1,0:T(8,128)S(1)} %add.58), channel_id=1, source_target_pairs={{0,16},{2,18},{4,20},{6,22},{8,24},{10,26},{12,28},{14,30},{16,0},... | collective-permute-start | bytes 98312 | tf_op jit(solution)/shard_map/ppermute | solution.py:342
  42.9 0.7 %collective-permute-start.8 = (bf16[96,512]{1,0:T(8,128)(2,1)S(1)}, bf16[96,512]{1,0:T(8,128)(2,1)S(1)}, u32[]{:S(2)}, u32[]{:S(2)}) collective-permute-start(bf16[96,512]{1,0:T(8,128)(2,1)S(1)} %add_convert_fusion.1), channel_id=1, source_target_pairs={{0,16},{2,18},{4,20},{6,22},{8,24},{10,26},{12,28},{14,30},{16,0},... | collective-permute-start | bytes 294920 | tf_op jit(solution)/shard_map/ppermute | solution.py:342
  43.6 3.0 %collective-permute-done.11 = f32[16,512]{1,0:T(8,128)S(1)} collective-permute-done((f32[16,512]{1,0:T(8,128)S(1)}, f32[16,512]{1,0:T(8,128)S(1)}, u32[]{:S(2)}, u32[]{:S(2)}) %collective-permute-start.11) | collective-permute-done | bytes 32800 | tf_op jit(solution)/shard_map/ppermute | solution.py:342
  46.6 2.6 %collective-permute-done.8 = bf16[96,512]{1,0:T(8,128)(2,1)S(1)} collective-permute-done((bf16[96,512]{1,0:T(8,128)(2,1)S(1)}, bf16[96,512]{1,0:T(8,128)(2,1)S(1)}, u32[]{:S(2)}, u32[]{:S(2)}) %collective-permute-start.8) | collective-permute-done | bytes 98336 | tf_op jit(solution)/shard_map/ppermute | solution.py:342
  49.4 1.6 %collective-permute-start.12 = (bf16[128,512]{1,0:T(8,128)(2,1)S(1)}, bf16[128,512]{1,0:T(8,128)(2,1)S(1)}, u32[]{:S(2)}, u32[]{:S(2)}) collective-permute-start(bf16[128,512]{1,0:T(8,128)(2,1)S(1)} %get-tuple-element.23), channel_id=1, source_target_pairs={{0,1},{1,0},{2,3},{3,2},{4,5},{5,4},{6,7},{7,6},{8,9},{9,8},{10,11... | collective-permute-start | bytes 393224 | tf_op jit(solution)/shard_map/ppermute | solution.py:342
  51.0 3.4 %collective-permute-done.12 = bf16[128,512]{1,0:T(8,128)(2,1)S(1)} collective-permute-done((bf16[128,512]{1,0:T(8,128)(2,1)S(1)}, bf16[128,512]{1,0:T(8,128)(2,1)S(1)}, u32[]{:S(2)}, u32[]{:S(2)}) %collective-permute-start.12) | collective-permute-done | bytes 131104 | tf_op jit(solution)/shard_map/ppermute | solution.py:342
  54.4 0.6 %fusion = f32[16,512]{1,0:T(8,128)} fusion(f32[128,512]{1,0:T(8,128)S(1)} %convert_element_type.69, f32[128,512]{1,0:T(8,128)S(1)} %get-tuple-element.22), kind=kLoop, calls=%fused_computation.6 | loop fusion | flops 24576 | bytes 163840 | tf_op jit(solution)/shard_map/add | solution.py:376
  55.1 0.7 %slice_add_fusion = f32[96,512]{1,0:T(8,128)} fusion(f32[128,512]{1,0:T(8,128)S(1)} %convert_element_type.69, f32[128,512]{1,0:T(8,128)S(1)} %get-tuple-element.22), kind=kLoop, calls=%fused_computation.1 | loop fusion | flops 49152 | bytes 589824 | tf_op jit(solution)/shard_map/add | solution.py:374
  (27 shorter events, 2.0 us)
Async XLA Ops:
  2.0 14.8 %all-to-all-start = ((bf16[16,8,384]{2,1,0:T(8,128)(2,1)}), bf16[16,8,384]{2,1,0:T(8,128)(2,1)S(1)}, u32[]{:S(2)}, u32[]{:S(2)}) async-start(bf16[16,8,384]{2,1,0:T(8,128)(2,1)} %bitcast.12), calls=%async_computation | async-start | bytes 196608 | tf_op jit(solution)/shard_map/all_to_all | solution.py:400
  10.9 1.4 %copy-start = (bf16[1536,512]{1,0:T(8,128)(2,1)S(1)}, bf16[1536,512]{1,0:T(8,128)(2,1)}, u32[]{:S(2)}) copy-start(bf16[1536,512]{1,0:T(8,128)(2,1)} %conv_two_ref.3) | copy-start | bytes 4718596
  12.3 1.0 %copy-start.2 = (bf16[16,32,512]{2,1,0:T(8,128)(2,1)S(1)}, bf16[16,32,512]{2,1,0:T(8,128)(2,1)}, u32[]{:S(2)}) copy-start(bf16[16,32,512]{2,1,0:T(8,128)(2,1)} %param.15) | copy-start | bytes 1572868
  13.4 3.4 %copy-start.1 = (bf16[1536,512]{1,0:T(8,128)(2,1)S(1)}, bf16[1536,512]{1,0:T(8,128)(2,1)}, u32[]{:S(2)}) copy-start(bf16[1536,512]{1,0:T(8,128)(2,1)} %conv_two_ref.3) | copy-start | bytes 4718596
  23.3 2.4 %collective-permute-start = (bf16[768,512]{1,0:T(8,128)(2,1)S(1)}, bf16[768,512]{1,0:T(8,128)(2,1)S(1)}, u32[]{:S(2)}, u32[]{:S(2)}) collective-permute-start(bf16[768,512]{1,0:T(8,128)(2,1)S(1)} %get-tuple-element.12), channel_id=1, source_target_pairs={{0,2},{2,0},{4,6},{6,4},{8,10},{10,8},{12,14},{14,12},{16,18},{18,... | collective-permute-start | bytes 2359304 | tf_op jit(solution)/shard_map/ppermute | solution.py:342
  23.4 2.3 %collective-permute-start.1 = (f32[16,512]{1,0:T(8,128)S(1)}, f32[16,512]{1,0:T(8,128)S(1)}, u32[]{:S(2)}, u32[]{:S(2)}) collective-permute-start(f32[16,512]{1,0:T(8,128)S(1)} %get-tuple-element.13), channel_id=1, source_target_pairs={{0,2},{2,0},{4,6},{6,4},{8,10},{10,8},{12,14},{14,12},{16,18},{18,... | collective-permute-start | bytes 98312 | tf_op jit(solution)/shard_map/ppermute | solution.py:342
  26.1 13.6 %collective-permute-start.7 = (bf16[96,512]{1,0:T(8,128)(2,1)S(1)}, bf16[96,512]{1,0:T(8,128)(2,1)S(1)}, u32[]{:S(2)}, u32[]{:S(2)}) collective-permute-start(bf16[96,512]{1,0:T(8,128)(2,1)S(1)} %get-tuple-element.17), channel_id=1, source_target_pairs={{0,12},{2,14},{4,8},{6,10},{8,4},{10,6},{12,0},{14,2},{16,28},{18,... | collective-permute-start | bytes 294920 | tf_op jit(solution)/shard_map/ppermute | solution.py:342
  27.0 13.5 %collective-permute-start.6 = (bf16[96,512]{1,0:T(8,128)(2,1)S(1)}, bf16[96,512]{1,0:T(8,128)(2,1)S(1)}, u32[]{:S(2)}, u32[]{:S(2)}) collective-permute-start(bf16[96,512]{1,0:T(8,128)(2,1)S(1)} %get-tuple-element.18), channel_id=1, source_target_pairs={{0,4},{2,6},{4,0},{6,2},{8,12},{10,14},{12,8},{14,10},{16,20},{18,... | collective-permute-start | bytes 294920 | tf_op jit(solution)/shard_map/ppermute | solution.py:342
  27.5 15.3 %collective-permute-start.5 = (bf16[96,512]{1,0:T(8,128)(2,1)S(1)}, bf16[96,512]{1,0:T(8,128)(2,1)S(1)}, u32[]{:S(2)}, u32[]{:S(2)}) collective-permute-start(bf16[96,512]{1,0:T(8,128)(2,1)S(1)} %get-tuple-element.19), channel_id=1, source_target_pairs={{0,8},{2,10},{4,12},{6,14},{8,0},{10,2},{12,4},{14,6},{16,24},{18,... | collective-permute-start | bytes 294920 | tf_op jit(solution)/shard_map/ppermute | solution.py:342
  29.7 4.7 %collective-permute-start.9 = (f32[16,512]{1,0:T(8,128)S(1)}, f32[16,512]{1,0:T(8,128)S(1)}, u32[]{:S(2)}, u32[]{:S(2)}) collective-permute-start(f32[16,512]{1,0:T(8,128)S(1)} %add.49), channel_id=1, source_target_pairs={{0,4},{2,6},{4,0},{6,2},{8,12},{10,14},{12,8},{14,10},{16,20},{18,... | collective-permute-start | bytes 98312 | tf_op jit(solution)/shard_map/ppermute | solution.py:342
  34.4 4.1 %collective-permute-start.10 = (f32[16,512]{1,0:T(8,128)S(1)}, f32[16,512]{1,0:T(8,128)S(1)}, u32[]{:S(2)}, u32[]{:S(2)}) collective-permute-start(f32[16,512]{1,0:T(8,128)S(1)} %add.57), channel_id=1, source_target_pairs={{0,8},{2,10},{4,12},{6,14},{8,0},{10,2},{12,4},{14,6},{16,24},{18,... | collective-permute-start | bytes 98312 | tf_op jit(solution)/shard_map/ppermute | solution.py:342
  34.7 11.9 %collective-permute-start.2 = (bf16[96,512]{1,0:T(8,128)(2,1)S(1)}, bf16[96,512]{1,0:T(8,128)(2,1)S(1)}, u32[]{:S(2)}, u32[]{:S(2)}) collective-permute-start(bf16[96,512]{1,0:T(8,128)(2,1)S(1)} %get-tuple-element.16), channel_id=1, source_target_pairs={{0,8},{2,10},{4,12},{6,14},{8,0},{10,2},{12,4},{14,6},{16,24},{18,... | collective-permute-start | bytes 294920 | tf_op jit(solution)/shard_map/ppermute | solution.py:342
  38.5 8.1 %collective-permute-start.4 = (bf16[96,512]{1,0:T(8,128)(2,1)S(1)}, bf16[96,512]{1,0:T(8,128)(2,1)S(1)}, u32[]{:S(2)}, u32[]{:S(2)}) collective-permute-start(bf16[96,512]{1,0:T(8,128)(2,1)S(1)} %get-tuple-element.20), channel_id=1, source_target_pairs={{0,12},{2,14},{4,8},{6,10},{8,4},{10,6},{12,0},{14,2},{16,28},{18,... | collective-permute-start | bytes 294920 | tf_op jit(solution)/shard_map/ppermute | solution.py:342
  39.8 6.8 %collective-permute-start.3 = (bf16[96,512]{1,0:T(8,128)(2,1)S(1)}, bf16[96,512]{1,0:T(8,128)(2,1)S(1)}, u32[]{:S(2)}, u32[]{:S(2)}) collective-permute-start(bf16[96,512]{1,0:T(8,128)(2,1)S(1)} %get-tuple-element.21), channel_id=1, source_target_pairs={{0,4},{2,6},{4,0},{6,2},{8,12},{10,14},{12,8},{14,10},{16,20},{18,... | collective-permute-start | bytes 294920 | tf_op jit(solution)/shard_map/ppermute | solution.py:342
  40.5 6.1 %collective-permute-start.11 = (f32[16,512]{1,0:T(8,128)S(1)}, f32[16,512]{1,0:T(8,128)S(1)}, u32[]{:S(2)}, u32[]{:S(2)}) collective-permute-start(f32[16,512]{1,0:T(8,128)S(1)} %add.58), channel_id=1, source_target_pairs={{0,16},{2,18},{4,20},{6,22},{8,24},{10,26},{12,28},{14,30},{16,0},... | collective-permute-start | bytes 98312 | tf_op jit(solution)/shard_map/ppermute | solution.py:342
  42.9 6.4 %collective-permute-start.8 = (bf16[96,512]{1,0:T(8,128)(2,1)S(1)}, bf16[96,512]{1,0:T(8,128)(2,1)S(1)}, u32[]{:S(2)}, u32[]{:S(2)}) collective-permute-start(bf16[96,512]{1,0:T(8,128)(2,1)S(1)} %add_convert_fusion.1), channel_id=1, source_target_pairs={{0,16},{2,18},{4,20},{6,22},{8,24},{10,26},{12,28},{14,30},{16,0},... | collective-permute-start | bytes 294920 | tf_op jit(solution)/shard_map/ppermute | solution.py:342
  49.4 5.0 %collective-permute-start.12 = (bf16[128,512]{1,0:T(8,128)(2,1)S(1)}, bf16[128,512]{1,0:T(8,128)(2,1)S(1)}, u32[]{:S(2)}, u32[]{:S(2)}) collective-permute-start(bf16[128,512]{1,0:T(8,128)(2,1)S(1)} %get-tuple-element.23), channel_id=1, source_target_pairs={{0,1},{1,0},{2,3},{3,2},{4,5},{5,4},{6,7},{7,6},{8,9},{9,8},{10,11... | collective-permute-start | bytes 393224 | tf_op jit(solution)/shard_map/ppermute | solution.py:342

commit v6 on v5

--- a/solution.py
+++ b/solution.py
@@ -12,7 +12,6 @@
 TAPS = 10
 STRIDE = 5
 ROWS = 16
-SPARE = 8
 F32 = jnp.float32
 BF16 = jnp.bfloat16
 
@@ -20,6 +19,11 @@
 def gelu_parts(act):
     cdf = 0.5 + 0.5 * lax.erf(act * 0.7071067811865476)
     return cdf, 0.3989422804014327 * jnp.exp(-0.5 * (act * act))
+
+
+def split_two(x):
+    hi = x.astype(BF16)
+    return hi, (x - hi.astype(F32)).astype(BF16)
 
 
 def pack_kernel(packing, bins, wave_ref, out_ref, wide):
@@ -27,16 +31,11 @@
     width = wide.shape[1]
     wide[...] = jnp.zeros_like(wide)
     wide[:, :record] = wave_ref[...].astype(F32)
-    lane = lax.broadcasted_iota(jnp.int32, (SPARE, width), 1)
-
-    def one(slot):
+    lane = lax.broadcasted_iota(jnp.int32, (1, width), 1)
+    for slot in range(count):
         own = packing[0, slot]
-        row = jnp.broadcast_to(wide[pl.ds(own, 1), :], (SPARE, width))
-        return jnp.where(lane == record, bins[own].astype(F32), row)
-
-    for pair in range(count // 2):
-        both = jnp.concatenate([one(2 * pair), one(2 * pair + 1)], axis=0)
-        out_ref[2 * SPARE * pair : 2 * SPARE * (pair + 1), :] = both.astype(BF16)
+        row = wide[pl.ds(own, 1), :]
+        out_ref[slot] = jnp.where(lane == record, bins[own].astype(F32), row)
 
 
 def pack(packing, length_bin, waveform):
@@ -44,7 +43,7 @@
     width = -(-(record + 1) // 128) * 128
     return pl.pallas_call(
         pack_kernel,
-        out_shape=jax.ShapeDtypeStruct((count * SPARE, width), BF16),
+        out_shape=jax.ShapeDtypeStruct((count, 1, width), F32),
         in_specs=[
             pl.BlockSpec(memory_space=pltpu.SMEM),
             pl.BlockSpec(memory_space=pltpu.SMEM),
@@ -101,6 +100,11 @@
 
 def together(steps):
     return max(n for n in range(1, 66) if steps % n == 0)
+
+
+def bit_order(shares):
+    bits = shares.bit_length() - 1
+    return [0, 3, 1, 2, *range(4, bits)]
 
 
 def local_kernel(
@@ -127,7 +131,7 @@
     dz_one,
     grad,
 ):
-    count = got_ref.shape[0] // SPARE
+    count = got_ref.shape[0]
     rows_two, width = cot_ref.shape
     frames_two = rows_two // count
     frames_one = 2 * frames_two + 1
@@ -135,11 +139,7 @@
     rows_one = frames_one * count
     inv = 1.0 / width
 
-    pick = (
-        lax.broadcasted_iota(jnp.int32, (count, count * SPARE), 1)
-        == SPARE * lax.broadcasted_iota(jnp.int32, (count, count * SPARE), 0)
-    ).astype(BF16)
-    wave = jnp.dot(pick, got_ref[...], preferred_element_type=F32)
+    wave = jnp.concatenate([got_ref[slot] for slot in range(count)], axis=0)
     lane_in = lax.broadcasted_iota(jnp.int32, wave.shape, 1)
     bins = jnp.sum(jnp.where(lane_in == record, wave, 0.0), axis=1, keepdims=True)
     limit = bins.astype(jnp.int32) * frames_two // NB
@@ -241,15 +241,14 @@
         )
     share = grad.shape[0] // shares
     me = place_ref[0]
-    bits = shares.bit_length() - 1
+    order = bit_order(shares)
+    half = shares // 2
     for spot in range(shares):
-        back = int(format(spot, f"0{bits}b")[::-1], 2)
-        block = grad[pl.ds(pl.multiple_of((me ^ back) * share, 8), share), :]
-        if spot < shares // 2:
-            keep_ref[spot * share : (spot + 1) * share, :] = block
-        else:
-            at = (spot - shares // 2) * share
-            send_ref[at : at + share, :] = block.astype(BF16)
+        flip = sum(1 << bit for i, bit in enumerate(reversed(order)) if spot >> i & 1)
+        block = grad[pl.ds(pl.multiple_of((me ^ flip) * share, 8), share), :]
+        part = send_ref if spot >= half else keep_ref
+        at = spot % half * share
+        part[at : at + share, :] = block.astype(part.dtype)
 
     turn = (((1,), (1,)), ((), ()))
     dz_one[rows_even:, :] = lax.dot_general(
@@ -288,7 +287,7 @@
 
 
 def local_pass(record, shares, place, got, cot, weight, conv_two, table):
-    count = got.shape[0] // SPARE
+    count = got.shape[0]
     rows_two, width = cot.shape
     rows_one = 2 * rows_two + count
     half = 3 * width // 2
@@ -301,7 +300,7 @@
             jax.ShapeDtypeStruct((ROWS, width), F32),
         ),
         in_specs=[pl.BlockSpec(memory_space=pltpu.SMEM)] + [vmem] * 5,
-        out_specs=(vmem, vmem, vmem),
+        out_specs=(vmem,) * 3,
         scratch_shapes=[
             pltpu.VMEM((rows_one, 128), BF16),
             pltpu.VMEM((count, 128), jnp.int32),
@@ -342,38 +341,70 @@
     return lax.ppermute(message, axes if len(axes) > 1 else axes[0], pairs)
 
 
+def message(rows, small):
+    return jnp.concatenate([rows.astype(BF16), *split_two(small)], axis=0)
+
+
+def contents(got):
+    rows = got.shape[0] - 2 * ROWS
+    hi, lo = got[rows : rows + ROWS], got[rows + ROWS :]
+    return got[:rows].astype(F32), hi.astype(F32) + lo.astype(F32)
+
+
+def finish_kernel(own_ref, got_ref, rows_ref, small_ref):
+    own, small = contents(own_ref[...])
+    got, more = contents(got_ref[...])
+    rows_ref[...] = own + got
+    small_ref[...] = small + more
+
+
+def finish(own, got):
+    rows, width = own.shape[0] - 2 * ROWS, own.shape[1]
+    vmem = pl.BlockSpec(memory_space=pltpu.VMEM)
+    return pl.pallas_call(
+        finish_kernel,
+        out_shape=(
+            jax.ShapeDtypeStruct((rows, width), F32),
+            jax.ShapeDtypeStruct((ROWS, width), F32),
+        ),
+        in_specs=[vmem, vmem],
+        out_specs=(pl.BlockSpec(), pl.BlockSpec()),
+        compiler_params=pltpu.CompilerParams(vmem_limit_bytes=8 * 1024 * 1024),
+    )(own, got)
+
+
 def sum_all(sizes, send, keep, small):
-    near = exchange(sizes, [("dp", 0)], small)
-    total = keep + exchange(sizes, [("dp", 0)], send).astype(F32)
-    total, small = lax.optimization_barrier((total, small + near))
-    left = [("dp", bit) for bit in range(1, sizes["dp"].bit_length() - 1)]
-    for bit in left:
-        small = small + exchange(sizes, [bit], small)
-    if len(left) >= 3:
-        pair, onward = left[:2], left[2]
-        rows = total.shape[0] // 8
-        sums = {}
-        for part in (1, 0):
-            blocks = [total[(2 * i + part) * rows : (2 * i + part + 1) * rows] for i in range(4)]
-            terms = [blocks[0]]
-            for code in (1, 2, 3):
-                chosen = [bit for i, bit in enumerate(pair) if code >> (1 - i) & 1]
-                terms.append(exchange(sizes, chosen, blocks[code].astype(BF16)).astype(F32))
-            sums[part] = tree(terms)
-        total = sums[0] + exchange(sizes, [onward], sums[1].astype(BF16)).astype(F32)
-        left = left[3:]
+    order = [("dp", bit) for bit in bit_order(sizes["dp"])]
+    core, onward, pair, left = order[0], order[1], order[2:4], order[4:]
+    small = small + exchange(sizes, [core], small)
+    total = keep + exchange(sizes, [core], send).astype(F32)
+    rows = total.shape[0] // 8
+    near, far = ([total[i * rows : (i + 1) * rows] for i in range(j, j + 4)] for j in (0, 4))
+    small = contents(message(far[0], small))[1], small
+    fars, smalls, nears = [far[0]], [small[0]], [near[0]]
+    chosen = [[bit for i, bit in enumerate(pair) if code >> (1 - i) & 1] for code in range(4)]
+    for code in (1, 2, 3):
+        got, more = contents(exchange(sizes, chosen[code], message(far[code], small[1])))
+        fars.append(got)
+        smalls.append(more)
+    own = message(tree(fars), tree(smalls))
+    for code in (1, 2, 3):
+        nears.append(exchange(sizes, chosen[code], near[code].astype(BF16)).astype(F32))
+    got, more = contents(exchange(sizes, [onward], own))
+    total, small = tree(nears) + got, contents(own)[1] + more
     for bit in left:
         half = total.shape[0] // 2
-        total = total[:half] + exchange(sizes, [bit], total[half:].astype(BF16)).astype(F32)
-    rows = total.shape[0]
-    for bit in range(sizes["blk"].bit_length() - 1):
-        hi = small.astype(BF16)
-        lo = (small - hi.astype(F32)).astype(BF16)
-        own = jnp.concatenate([total.astype(BF16), hi, lo], axis=0)
-        both = own.astype(F32), exchange(sizes, [("blk", bit)], own).astype(F32)
-        total = both[0][:rows] + both[1][:rows]
-        parts = [b[rows : rows + ROWS] + b[rows + ROWS :] for b in both]
-        small = parts[0] + parts[1]
+        own = message(total[half:], small)
+        got, more = contents(exchange(sizes, [bit], own))
+        total, small = total[:half] + got, contents(own)[1] + more
+    bits = sizes["blk"].bit_length() - 1
+    for bit in range(bits):
+        own = message(total, small)
+        got = exchange(sizes, [("blk", bit)], own)
+        if bit == bits - 1:
+            return finish(own, got)
+        (total, small), (got, more) = contents(own), contents(got)
+        total, small = total + got, small + more
     return total, small
 
 
@@ -396,16 +427,14 @@
     count, frames_two, width = cotangent.shape
     shares = sizes["dp"]
     packed = pack(packing, length_bin, waveform)
-    packed = packed.reshape(count, SPARE, packed.shape[1])
     got = lax.all_to_all(packed, "dp", split_axis=0, concat_axis=0, tiled=True)
-    got = got.reshape(count * SPARE, got.shape[2])
     vectors = (bias_one, gain_one, shift_one, bias_two, gain_two, shift_two)
     table = jnp.concatenate([conv_one.astype(F32), jnp.stack(vectors)], axis=0)
     cot = cotangent.reshape(count * frames_two, width)
     cot, weight = ready(count, cot, table, conv_two)
     place = lax.axis_index("dp").astype(jnp.int32).reshape(1)
-    send, keep, small = local_pass(record, shares, place, got, cot, weight, conv_two, table)
-    return sum_all(sizes, send, keep, small)
+    partial = local_pass(record, shares, place, got, cot, weight, conv_two, table)
+    return sum_all(sizes, *partial)
 
 
 def solution(mesh):

time: 56.2 us -> 51.5 us (0.916)
  waiting for transfers between devices: 20.7 us -> 18 us
  other arithmetic: 1.9 us -> 0.53 us
  starting transfers between devices: 20.1 us -> 19 us
    ppermute x13 -> x10, waiting for transfers between devices: 17.7 us -> 15.8 us  [exchange(): return lax.ppermute(message, axes if len(axes) > 1 else axes[0], pairs)]
    add x6 -> x0, other arithmetic: 1.62 us -> none  [the longest x1 0.7 us: sum_all(): total = both[0][:rows] + both[1][:rows]]
    ppermute x13 -> x10, starting transfers between devices: 12.8 us -> 11.6 us  [exchange(): return lax.ppermute(message, axes if len(axes) > 1 else axes[0], pairs)]
    all_to_all x1, waiting for transfers between devices: 2.99 us -> 2.15 us  [per_device(): got = lax.all_to_all(packed, 'dp', split_axis=0, concat_axis=0, tiled=True)]
    pallas_call x1 -> x2, Pallas kernels: 1.4 us -> 2.07 us  [the longest x1 1.37 us: pack(): pl.pallas_call(pack_kernel, out_shape=jax.ShapeDtypeStruct((count, 1, wid...]
  transfers between devices with their start and end apart: 14 -> 11, of which waited for: 7 -> 9; matrix products, arithmetic and copies ran while one was open for 3% -> 3% of each run, Pallas kernels for 1% -> 1%
where the time goes in v6:
time: 51.5 us; the launch traced here: 51.1 us
  starting transfers between devices  19 us (37%)
  waiting for transfers between devices  18 us (35%)
  Pallas kernels  8.86 us (17%)
  local copies, waits for them, and re-layouts  4.01 us (8%)
  between operations  0.74 us (1%)
  other arithmetic  0.53 us (1%)
    ppermute x10, waiting for transfers between devices, exchange(): return lax.ppermute(message, axes if len(axes) > 1 else axes[0], pairs)  15.8 us
    ppermute x10, starting transfers between devices, exchange(): return lax.ppermute(message, axes if len(axes) > 1 else axes[0], pairs)  11.6 us
    all_to_all x1, starting transfers between devices, per_device(): got = lax.all_to_all(packed, 'dp', split_axis=0, concat_axis=0, tiled=True)  7.36 us
    pallas_call x1, Pallas kernels, local_pass(): pl.pallas_call(functools.partial(local_kernel, record, shares), out_shape...  6.36 us
    unnamed x6, local copies, waits for them, and re-layouts  2.45 us
    all_to_all x1, waiting for transfers between devices, per_device(): got = lax.all_to_all(packed, 'dp', split_axis=0, concat_axis=0, tiled=True)  2.15 us
    concatenate x1, local copies, waits for them, and re-layouts, per_device(): table = jnp.concatenate([conv_one.astype(F32), jnp.stack(vectors)], axis=0)  1.52 us
    pallas_call x1, Pallas kernels, pack(): pl.pallas_call(pack_kernel, out_shape=jax.ShapeDtypeStruct((count, 1, wid...  1.37 us
  transfers between devices with their start and end apart: 11, of which 9 were waited for; matrix products, arithmetic and copies ran while one was open for 3% of the time, Pallas kernels for 1%

profile of v6, /device:TPU:0, one launch (start us, length us, event | category | flops | bytes accessed | tf_op | source)
XLA Modules:
  0.0 51.1 jit_solution(11539642133898815033)
XLA Ops:
  0.6 1.4 %shard_map.131 = f32[16,1,384]{2,1,0:T(1,128)} custom-call(s32[1,16]{1,0:T(1,128)} %packing.1, s32[16]{0:T(128)} %bins.1, bf16[16,330]{1,0:T(8,128)(2,1)} %wave_ref.1), custom_call_target="tpu_custom_call" | custom-call | tf_op jit(solution)/shard_map/pallas_call | solution.py:44
  2.0 7.4 %all-to-all-start = ((f32[16,1,384]{2,1,0:T(1,128)}), f32[16,1,384]{2,1,0:T(1,128)S(1)}, u32[]{:S(2)}, u32[]{:S(2)}) async-start(f32[16,1,384]{2,1,0:T(1,128)} %shard_map.131), calls=%async_computation | async-start | bytes 49152 | tf_op jit(solution)/shard_map/all_to_all | solution.py:430
  9.4 1.5 %concatenate.18.table_ref = f32[16,512]{1,0:T(8,128)S(1)} concatenate(bf16[10,512]{1,0:T(8,128)(2,1)} %param.16, f32[1,512]{1,0:T(1,128)} %bitcast.9, f32[1,512]{1,0:T(1,128)} %bitcast.10, f32[1,512]{1,0:T(1,128)} %bitcast.11, f32[1,512]{1,0:T(1,128)} %bitcast.12, f32[1,512]{1,0:T(1,128)} %bitcast.13, f32[1,512]{1,0:T(1,128)} %bitcast.14), dimensions={0} | concatenate | bytes 55296 | tf_op jit(solution)/shard_map/concatenate | solution.py:432
  10.9 1.4 %copy-done = bf16[1536,512]{1,0:T(8,128)(2,1)S(1)} copy-done((bf16[1536,512]{1,0:T(8,128)(2,1)S(1)}, bf16[1536,512]{1,0:T(8,128)(2,1)}, u32[]{:S(2)}) %copy-start) | copy-done | bytes 1572888
  12.3 1.0 %copy-done.2 = bf16[16,32,512]{2,1,0:T(8,128)(2,1)S(1)} copy-done((bf16[16,32,512]{2,1,0:T(8,128)(2,1)S(1)}, bf16[16,32,512]{2,1,0:T(8,128)(2,1)}, u32[]{:S(2)}) %copy-start.2) | copy-done | bytes 524312
  13.8 2.2 %all-to-all-done.got_ref = f32[16,1,384]{2,1,0:T(1,128)S(1)} async-done(((f32[16,1,384]{2,1,0:T(1,128)}), f32[16,1,384]{2,1,0:T(1,128)S(1)}, u32[]{:S(2)}, u32[]{:S(2)}) %all-to-all-start) | async-done | bytes 24608 | tf_op jit(solution)/shard_map/all_to_all | solution.py:430
  15.9 6.4 %shard_map.133 = (bf16[768,512]{1,0:T(8,128)(2,1)S(1)}, f32[768,512]{1,0:T(8,128)S(1)}, f32[16,512]{1,0:T(8,128)S(1)}) custom-call(s32[1]{0:T(128)} %bitcast.place_ref, f32[16,1,384]{2,1,0:T(1,128)S(1)} %all-to-all-done.got_ref, bf16[512,512]{1,0:T(8,128)(2,1)S(1)} %get-tuple-element.7.cot_ref, bf16[128,512]{1,0:T(8,128)(2,1)S(1)} %get-tuple-element.8.weight_ref, ...), custom_call_target="tpu_custom_call" | custom-call | flops 2415919104 | bytes 4259840 | tf_op jit(solution)/shard_map/pallas_call | solution.py:295
  22.4 0.5 collective-permute-start.4
  22.9 1.8 %collective-permute-done.4 = f32[16,512]{1,0:T(8,128)S(1)} collective-permute-done((f32[16,512]{1,0:T(8,128)S(1)}, f32[16,512]{1,0:T(8,128)S(1)}, u32[]{:S(2)}, u32[]{:S(2)}) %collective-permute-start.4) | collective-permute-done | bytes 32800 | tf_op jit(solution)/shard_map/ppermute | solution.py:341
  25.1 0.8 %collective-permute-start.5 = (bf16[128,512]{1,0:T(8,128)(2,1)S(1)}, bf16[128,512]{1,0:T(8,128)(2,1)S(1)}, u32[]{:S(2)}, u32[]{:S(2)}) collective-permute-start(bf16[128,512]{1,0:T(8,128)(2,1)S(1)} %get-tuple-element.26), channel_id=1, source_target_pairs={{0,8},{2,10},{4,12},{6,14},{8,0},{10,2},{12,4},{14,6},{16,24},{18,... | collective-permute-start | bytes 393224 | tf_op jit(solution)/shard_map/ppermute | solution.py:341
  25.9 1.5 %collective-permute-start.6 = (bf16[128,512]{1,0:T(8,128)(2,1)S(1)}, bf16[128,512]{1,0:T(8,128)(2,1)S(1)}, u32[]{:S(2)}, u32[]{:S(2)}) collective-permute-start(bf16[128,512]{1,0:T(8,128)(2,1)S(1)} %get-tuple-element.27), channel_id=1, source_target_pairs={{0,4},{2,6},{4,0},{6,2},{8,12},{10,14},{12,8},{14,10},{16,20},{18,... | collective-permute-start | bytes 393224 | tf_op jit(solution)/shard_map/ppermute | solution.py:341
  27.4 1.3 %collective-permute-start.7 = (bf16[128,512]{1,0:T(8,128)(2,1)S(1)}, bf16[128,512]{1,0:T(8,128)(2,1)S(1)}, u32[]{:S(2)}, u32[]{:S(2)}) collective-permute-start(bf16[128,512]{1,0:T(8,128)(2,1)S(1)} %get-tuple-element.28), channel_id=1, source_target_pairs={{0,12},{2,14},{4,8},{6,10},{8,4},{10,6},{12,0},{14,2},{16,28},{18,... | collective-permute-start | bytes 393224 | tf_op jit(solution)/shard_map/ppermute | solution.py:341
  28.7 2.9 %collective-permute-done.5 = bf16[128,512]{1,0:T(8,128)(2,1)S(1)} collective-permute-done((bf16[128,512]{1,0:T(8,128)(2,1)S(1)}, bf16[128,512]{1,0:T(8,128)(2,1)S(1)}, u32[]{:S(2)}, u32[]{:S(2)}) %collective-permute-start.5) | collective-permute-done | bytes 131104 | tf_op jit(solution)/shard_map/ppermute | solution.py:341
  31.5 2.5 %collective-permute-done.6 = bf16[128,512]{1,0:T(8,128)(2,1)S(1)} collective-permute-done((bf16[128,512]{1,0:T(8,128)(2,1)S(1)}, bf16[128,512]{1,0:T(8,128)(2,1)S(1)}, u32[]{:S(2)}, u32[]{:S(2)}) %collective-permute-start.6) | collective-permute-done | bytes 131104 | tf_op jit(solution)/shard_map/ppermute | solution.py:341
  34.1 2.4 %collective-permute-start.8 = (bf16[128,512]{1,0:T(8,128)(2,1)S(1)}, bf16[128,512]{1,0:T(8,128)(2,1)S(1)}, u32[]{:S(2)}, u32[]{:S(2)}) collective-permute-start(bf16[128,512]{1,0:T(8,128)(2,1)S(1)} %pad_maximum_fusion.6), channel_id=1, source_target_pairs={{0,16},{2,18},{4,20},{6,22},{8,24},{10,26},{12,28},{14,30},{16,0},... | collective-permute-start | bytes 393224 | tf_op jit(solution)/shard_map/ppermute | solution.py:341
  36.5 1.2 %collective-permute-start.1 = (bf16[96,512]{1,0:T(8,128)(2,1)S(1)}, bf16[96,512]{1,0:T(8,128)(2,1)S(1)}, u32[]{:S(2)}, u32[]{:S(2)}) collective-permute-start(bf16[96,512]{1,0:T(8,128)(2,1)S(1)} %get-tuple-element.20), channel_id=1, source_target_pairs={{0,8},{2,10},{4,12},{6,14},{8,0},{10,2},{12,4},{14,6},{16,24},{18,... | collective-permute-start | bytes 294920 | tf_op jit(solution)/shard_map/ppermute | solution.py:341
  37.7 1.8 %collective-permute-start.3 = (bf16[96,512]{1,0:T(8,128)(2,1)S(1)}, bf16[96,512]{1,0:T(8,128)(2,1)S(1)}, u32[]{:S(2)}, u32[]{:S(2)}) collective-permute-start(bf16[96,512]{1,0:T(8,128)(2,1)S(1)} %get-tuple-element.24), channel_id=1, source_target_pairs={{0,12},{2,14},{4,8},{6,10},{8,4},{10,6},{12,0},{14,2},{16,28},{18,... | collective-permute-start | bytes 294920 | tf_op jit(solution)/shard_map/ppermute | solution.py:341
  39.5 0.6 %collective-permute-start.2 = (bf16[96,512]{1,0:T(8,128)(2,1)S(1)}, bf16[96,512]{1,0:T(8,128)(2,1)S(1)}, u32[]{:S(2)}, u32[]{:S(2)}) collective-permute-start(bf16[96,512]{1,0:T(8,128)(2,1)S(1)} %get-tuple-element.25), channel_id=1, source_target_pairs={{0,4},{2,6},{4,0},{6,2},{8,12},{10,14},{12,8},{14,10},{16,20},{18,... | collective-permute-start | bytes 294920 | tf_op jit(solution)/shard_map/ppermute | solution.py:341
  40.0 2.1 %collective-permute-done.8 = bf16[128,512]{1,0:T(8,128)(2,1)S(1)} collective-permute-done((bf16[128,512]{1,0:T(8,128)(2,1)S(1)}, bf16[128,512]{1,0:T(8,128)(2,1)S(1)}, u32[]{:S(2)}, u32[]{:S(2)}) %collective-permute-start.8) | collective-permute-done | bytes 131104 | tf_op jit(solution)/shard_map/ppermute | solution.py:341
  42.2 0.7 %collective-permute-done.1 = bf16[96,512]{1,0:T(8,128)(2,1)S(1)} collective-permute-done((bf16[96,512]{1,0:T(8,128)(2,1)S(1)}, bf16[96,512]{1,0:T(8,128)(2,1)S(1)}, u32[]{:S(2)}, u32[]{:S(2)}) %collective-permute-start.1) | collective-permute-done | bytes 98336 | tf_op jit(solution)/shard_map/ppermute | solution.py:341
  42.8 2.2 %collective-permute-done.3 = bf16[96,512]{1,0:T(8,128)(2,1)S(1)} collective-permute-done((bf16[96,512]{1,0:T(8,128)(2,1)S(1)}, bf16[96,512]{1,0:T(8,128)(2,1)S(1)}, u32[]{:S(2)}, u32[]{:S(2)}) %collective-permute-start.3) | collective-permute-done | bytes 98336 | tf_op jit(solution)/shard_map/ppermute | solution.py:341
  45.3 1.6 %collective-permute-start.9 = (bf16[128,512]{1,0:T(8,128)(2,1)S(1)}, bf16[128,512]{1,0:T(8,128)(2,1)S(1)}, u32[]{:S(2)}, u32[]{:S(2)}) collective-permute-start(bf16[128,512]{1,0:T(8,128)(2,1)S(1)} %pad_maximum_fusion.7.own_ref), channel_id=1, source_target_pairs={{0,1},{1,0},{2,3},{3,2},{4,5},{5,4},{6,7},{7,6},{8,9},{9,8},{10,11... | collective-permute-start | bytes 393224 | tf_op jit(solution)/shard_map/ppermute | solution.py:341
  46.9 3.4 %collective-permute-done.9.got_ref = bf16[128,512]{1,0:T(8,128)(2,1)S(1)} collective-permute-done((bf16[128,512]{1,0:T(8,128)(2,1)S(1)}, bf16[128,512]{1,0:T(8,128)(2,1)S(1)}, u32[]{:S(2)}, u32[]{:S(2)}) %collective-permute-start.9) | collective-permute-done | bytes 131104 | tf_op jit(solution)/shard_map/ppermute | solution.py:341
  50.4 0.7 %shard_map.134 = (f32[96,512]{1,0:T(8,128)}, f32[16,512]{1,0:T(8,128)}) custom-call(bf16[128,512]{1,0:T(8,128)(2,1)S(1)} %pad_maximum_fusion.7.own_ref, bf16[128,512]{1,0:T(8,128)(2,1)S(1)} %collective-permute-done.9.got_ref), custom_call_target="tpu_custom_call" | custom-call | tf_op jit(solution)/shard_map/pallas_call | solution.py:364
  (19 shorter events, 1.3 us)
Async XLA Ops:
  2.0 13.9 %all-to-all-start = ((f32[16,1,384]{2,1,0:T(1,128)}), f32[16,1,384]{2,1,0:T(1,128)S(1)}, u32[]{:S(2)}, u32[]{:S(2)}) async-start(f32[16,1,384]{2,1,0:T(1,128)} %shard_map.131), calls=%async_computation | async-start | bytes 49152 | tf_op jit(solution)/shard_map/all_to_all | solution.py:430
  10.9 1.4 %copy-start = (bf16[1536,512]{1,0:T(8,128)(2,1)S(1)}, bf16[1536,512]{1,0:T(8,128)(2,1)}, u32[]{:S(2)}) copy-start(bf16[1536,512]{1,0:T(8,128)(2,1)} %conv_two_ref.3) | copy-start | bytes 4718596
  12.3 1.0 %copy-start.2 = (bf16[16,32,512]{2,1,0:T(8,128)(2,1)S(1)}, bf16[16,32,512]{2,1,0:T(8,128)(2,1)}, u32[]{:S(2)}) copy-start(bf16[16,32,512]{2,1,0:T(8,128)(2,1)} %param.15) | copy-start | bytes 1572868
  13.3 2.6 %copy-start.1 = (bf16[1536,512]{1,0:T(8,128)(2,1)S(1)}, bf16[1536,512]{1,0:T(8,128)(2,1)}, u32[]{:S(2)}) copy-start(bf16[1536,512]{1,0:T(8,128)(2,1)} %conv_two_ref.3) | copy-start | bytes 4718596
  22.3 2.4 %collective-permute-start = (bf16[768,512]{1,0:T(8,128)(2,1)S(1)}, bf16[768,512]{1,0:T(8,128)(2,1)S(1)}, u32[]{:S(2)}, u32[]{:S(2)}) collective-permute-start(bf16[768,512]{1,0:T(8,128)(2,1)S(1)} %get-tuple-element.10), channel_id=1, source_target_pairs={{0,2},{2,0},{4,6},{6,4},{8,10},{10,8},{12,14},{14,12},{16,18},{18,... | collective-permute-start | bytes 2359304 | tf_op jit(solution)/shard_map/ppermute | solution.py:341
  22.4 2.3 %collective-permute-start.4 = (f32[16,512]{1,0:T(8,128)S(1)}, f32[16,512]{1,0:T(8,128)S(1)}, u32[]{:S(2)}, u32[]{:S(2)}) collective-permute-start(f32[16,512]{1,0:T(8,128)S(1)} %get-tuple-element.11), channel_id=1, source_target_pairs={{0,2},{2,0},{4,6},{6,4},{8,10},{10,8},{12,14},{14,12},{16,18},{18,... | collective-permute-start | bytes 98312 | tf_op jit(solution)/shard_map/ppermute | solution.py:341
  25.1 6.4 %collective-permute-start.5 = (bf16[128,512]{1,0:T(8,128)(2,1)S(1)}, bf16[128,512]{1,0:T(8,128)(2,1)S(1)}, u32[]{:S(2)}, u32[]{:S(2)}) collective-permute-start(bf16[128,512]{1,0:T(8,128)(2,1)S(1)} %get-tuple-element.26), channel_id=1, source_target_pairs={{0,8},{2,10},{4,12},{6,14},{8,0},{10,2},{12,4},{14,6},{16,24},{18,... | collective-permute-start | bytes 393224 | tf_op jit(solution)/shard_map/ppermute | solution.py:341
  25.9 8.1 %collective-permute-start.6 = (bf16[128,512]{1,0:T(8,128)(2,1)S(1)}, bf16[128,512]{1,0:T(8,128)(2,1)S(1)}, u32[]{:S(2)}, u32[]{:S(2)}) collective-permute-start(bf16[128,512]{1,0:T(8,128)(2,1)S(1)} %get-tuple-element.27), channel_id=1, source_target_pairs={{0,4},{2,6},{4,0},{6,2},{8,12},{10,14},{12,8},{14,10},{16,20},{18,... | collective-permute-start | bytes 393224 | tf_op jit(solution)/shard_map/ppermute | solution.py:341
  27.4 6.6 %collective-permute-start.7 = (bf16[128,512]{1,0:T(8,128)(2,1)S(1)}, bf16[128,512]{1,0:T(8,128)(2,1)S(1)}, u32[]{:S(2)}, u32[]{:S(2)}) collective-permute-start(bf16[128,512]{1,0:T(8,128)(2,1)S(1)} %get-tuple-element.28), channel_id=1, source_target_pairs={{0,12},{2,14},{4,8},{6,10},{8,4},{10,6},{12,0},{14,2},{16,28},{18,... | collective-permute-start | bytes 393224 | tf_op jit(solution)/shard_map/ppermute | solution.py:341
  34.1 8.0 %collective-permute-start.8 = (bf16[128,512]{1,0:T(8,128)(2,1)S(1)}, bf16[128,512]{1,0:T(8,128)(2,1)S(1)}, u32[]{:S(2)}, u32[]{:S(2)}) collective-permute-start(bf16[128,512]{1,0:T(8,128)(2,1)S(1)} %pad_maximum_fusion.6), channel_id=1, source_target_pairs={{0,16},{2,18},{4,20},{6,22},{8,24},{10,26},{12,28},{14,30},{16,0},... | collective-permute-start | bytes 393224 | tf_op jit(solution)/shard_map/ppermute | solution.py:341
  36.5 6.3 %collective-permute-start.1 = (bf16[96,512]{1,0:T(8,128)(2,1)S(1)}, bf16[96,512]{1,0:T(8,128)(2,1)S(1)}, u32[]{:S(2)}, u32[]{:S(2)}) collective-permute-start(bf16[96,512]{1,0:T(8,128)(2,1)S(1)} %get-tuple-element.20), channel_id=1, source_target_pairs={{0,8},{2,10},{4,12},{6,14},{8,0},{10,2},{12,4},{14,6},{16,24},{18,... | collective-permute-start | bytes 294920 | tf_op jit(solution)/shard_map/ppermute | solution.py:341
  37.7 7.4 %collective-permute-start.3 = (bf16[96,512]{1,0:T(8,128)(2,1)S(1)}, bf16[96,512]{1,0:T(8,128)(2,1)S(1)}, u32[]{:S(2)}, u32[]{:S(2)}) collective-permute-start(bf16[96,512]{1,0:T(8,128)(2,1)S(1)} %get-tuple-element.24), channel_id=1, source_target_pairs={{0,12},{2,14},{4,8},{6,10},{8,4},{10,6},{12,0},{14,2},{16,28},{18,... | collective-permute-start | bytes 294920 | tf_op jit(solution)/shard_map/ppermute | solution.py:341
  39.5 5.8 %collective-permute-start.2 = (bf16[96,512]{1,0:T(8,128)(2,1)S(1)}, bf16[96,512]{1,0:T(8,128)(2,1)S(1)}, u32[]{:S(2)}, u32[]{:S(2)}) collective-permute-start(bf16[96,512]{1,0:T(8,128)(2,1)S(1)} %get-tuple-element.25), channel_id=1, source_target_pairs={{0,4},{2,6},{4,0},{6,2},{8,12},{10,14},{12,8},{14,10},{16,20},{18,... | collective-permute-start | bytes 294920 | tf_op jit(solution)/shard_map/ppermute | solution.py:341
  45.3 5.0 %collective-permute-start.9 = (bf16[128,512]{1,0:T(8,128)(2,1)S(1)}, bf16[128,512]{1,0:T(8,128)(2,1)S(1)}, u32[]{:S(2)}, u32[]{:S(2)}) collective-permute-start(bf16[128,512]{1,0:T(8,128)(2,1)S(1)} %pad_maximum_fusion.7.own_ref), channel_id=1, source_target_pairs={{0,1},{1,0},{2,3},{3,2},{4,5},{5,4},{6,7},{7,6},{8,9},{9,8},{10,11... | collective-permute-start | bytes 393224 | tf_op jit(solution)/shard_map/ppermute | solution.py:341

commit v7 on v6

--- a/solution.py
+++ b/solution.py
@@ -351,6 +351,25 @@
     return got[:rows].astype(F32), hi.astype(F32) + lo.astype(F32)
 
 
+def near_kernel(own_ref, *refs):
+    terms = [own_ref[...]] + [ref[...].astype(F32) for ref in refs[:-1]]
+    refs[-1][...] = tree(terms)
+
+
+def near_sum(own, *got):
+    vmem = pl.BlockSpec(memory_space=pltpu.VMEM)
+    return pl.pallas_call(
+        near_kernel,
+        out_shape=jax.ShapeDtypeStruct(own.shape, F32),
+        in_specs=[vmem] * (1 + len(got)),
+        out_specs=vmem,
+        cost_estimate=pl.CostEstimate(
+            flops=4 * own.size, bytes_accessed=140 * own.size, transcendentals=0
+        ),
+        compiler_params=pltpu.CompilerParams(vmem_limit_bytes=8 * 1024 * 1024),
+    )(own, *got)
+
+
 def finish_kernel(own_ref, got_ref, rows_ref, small_ref):
     own, small = contents(own_ref[...])
     got, more = contents(got_ref[...])
@@ -381,7 +400,7 @@
     rows = total.shape[0] // 8
     near, far = ([total[i * rows : (i + 1) * rows] for i in range(j, j + 4)] for j in (0, 4))
     small = contents(message(far[0], small))[1], small
-    fars, smalls, nears = [far[0]], [small[0]], [near[0]]
+    fars, smalls, nears = [far[0]], [small[0]], []
     chosen = [[bit for i, bit in enumerate(pair) if code >> (1 - i) & 1] for code in range(4)]
     for code in (1, 2, 3):
         got, more = contents(exchange(sizes, chosen[code], message(far[code], small[1])))
@@ -389,9 +408,11 @@
         smalls.append(more)
     own = message(tree(fars), tree(smalls))
     for code in (1, 2, 3):
-        nears.append(exchange(sizes, chosen[code], near[code].astype(BF16)).astype(F32))
-    got, more = contents(exchange(sizes, [onward], own))
-    total, small = tree(nears) + got, contents(own)[1] + more
+        nears.append(exchange(sizes, chosen[code], near[code].astype(BF16)))
+    cut = own.shape[0] // 2 // ROWS * ROWS
+    got = [exchange(sizes, [onward], part) for part in (own[:cut], own[cut:])]
+    got, more = contents(jnp.concatenate(got, axis=0))
+    total, small = near_sum(near[0], *nears) + got, contents(own)[1] + more
     for bit in left:
         half = total.shape[0] // 2
         own = message(total[half:], small)

time: 51.5 us -> 50.1 us (0.973)
  waiting for transfers between devices: 18 us -> 16.6 us
    ppermute x10 -> x11, waiting for transfers between devices: 15.8 us -> 14.4 us  [exchange(): return lax.ppermute(message, axes if len(axes) > 1 else axes[0], pairs)]
    ppermute x10 -> x11, starting transfers between devices: 11.6 us -> 11.6 us  [exchange(): return lax.ppermute(message, axes if len(axes) > 1 else axes[0], pairs)]
  transfers between devices with their start and end apart: 11 -> 12, of which waited for: 9 -> 7; matrix products, arithmetic and copies ran while one was open for 3% -> 3% of each run, Pallas kernels for 1% -> 1%
where the time goes in v7:
time: 50.1 us; the launch traced here: 49.7 us
  starting transfers between devices  19 us (38%)
  waiting for transfers between devices  16.6 us (33%)
  Pallas kernels  8.91 us (18%)
  local copies, waits for them, and re-layouts  4.01 us (8%)
  between operations  0.76 us (2%)
    ppermute x11, waiting for transfers between devices, exchange(): return lax.ppermute(message, axes if len(axes) > 1 else axes[0], pairs)  14.4 us
    ppermute x11, starting transfers between devices, exchange(): return lax.ppermute(message, axes if len(axes) > 1 else axes[0], pairs)  11.6 us
    all_to_all x1, starting transfers between devices, per_device(): got = lax.all_to_all(packed, 'dp', split_axis=0, concat_axis=0, tiled=True)  7.36 us
    pallas_call x1, Pallas kernels, local_pass(): pl.pallas_call(functools.partial(local_kernel, record, shares), out_shape...  6.36 us
    unnamed x6, local copies, waits for them, and re-layouts  2.45 us
    all_to_all x1, waiting for transfers between devices, per_device(): got = lax.all_to_all(packed, 'dp', split_axis=0, concat_axis=0, tiled=True)  2.15 us
    concatenate x1, local copies, waits for them, and re-layouts, per_device(): table = jnp.concatenate([conv_one.astype(F32), jnp.stack(vectors)], axis=0)  1.52 us
    pallas_call x1, Pallas kernels, pack(): pl.pallas_call(pack_kernel, out_shape=jax.ShapeDtypeStruct((count, 1, wid...  1.37 us
  transfers between devices with their start and end apart: 12, of which 7 were waited for; matrix products, arithmetic and copies ran while one was open for 3% of the time, Pallas kernels for 1%

profile of v7, /device:TPU:0, one launch (start us, length us, event | category | flops | bytes accessed | tf_op | source)
XLA Modules:
  0.0 49.7 jit_solution(3194394675600354349)
XLA Ops:
  0.6 1.4 %shard_map.131 = f32[16,1,384]{2,1,0:T(1,128)} custom-call(s32[1,16]{1,0:T(1,128)} %packing.1, s32[16]{0:T(128)} %bins.1, bf16[16,330]{1,0:T(8,128)(2,1)} %wave_ref.1), custom_call_target="tpu_custom_call" | custom-call | tf_op jit(solution)/shard_map/pallas_call | solution.py:44
  2.0 7.4 %all-to-all-start = ((f32[16,1,384]{2,1,0:T(1,128)}), f32[16,1,384]{2,1,0:T(1,128)S(1)}, u32[]{:S(2)}, u32[]{:S(2)}) async-start(f32[16,1,384]{2,1,0:T(1,128)} %shard_map.131), calls=%async_computation | async-start | bytes 49152 | tf_op jit(solution)/shard_map/all_to_all | solution.py:451
  9.4 1.5 %concatenate.21.table_ref = f32[16,512]{1,0:T(8,128)S(1)} concatenate(bf16[10,512]{1,0:T(8,128)(2,1)} %param.16, f32[1,512]{1,0:T(1,128)} %bitcast.9, f32[1,512]{1,0:T(1,128)} %bitcast.10, f32[1,512]{1,0:T(1,128)} %bitcast.11, f32[1,512]{1,0:T(1,128)} %bitcast.12, f32[1,512]{1,0:T(1,128)} %bitcast.13, f32[1,512]{1,0:T(1,128)} %bitcast.14), dimensions={0} | concatenate | bytes 55296 | tf_op jit(solution)/shard_map/concatenate | solution.py:453
  10.9 1.4 %copy-done = bf16[1536,512]{1,0:T(8,128)(2,1)S(1)} copy-done((bf16[1536,512]{1,0:T(8,128)(2,1)S(1)}, bf16[1536,512]{1,0:T(8,128)(2,1)}, u32[]{:S(2)}) %copy-start) | copy-done | bytes 1572888
  12.3 1.0 %copy-done.2 = bf16[16,32,512]{2,1,0:T(8,128)(2,1)S(1)} copy-done((bf16[16,32,512]{2,1,0:T(8,128)(2,1)S(1)}, bf16[16,32,512]{2,1,0:T(8,128)(2,1)}, u32[]{:S(2)}) %copy-start.2) | copy-done | bytes 524312
  13.3 0.4 shard_map.132
  13.8 2.1 %all-to-all-done.got_ref = f32[16,1,384]{2,1,0:T(1,128)S(1)} async-done(((f32[16,1,384]{2,1,0:T(1,128)}), f32[16,1,384]{2,1,0:T(1,128)S(1)}, u32[]{:S(2)}, u32[]{:S(2)}) %all-to-all-start) | async-done | bytes 24608 | tf_op jit(solution)/shard_map/all_to_all | solution.py:451
  15.9 6.4 %shard_map.133 = (bf16[768,512]{1,0:T(8,128)(2,1)S(1)}, f32[768,512]{1,0:T(8,128)S(1)}, f32[16,512]{1,0:T(8,128)S(1)}) custom-call(s32[1]{0:T(128)} %bitcast.place_ref, f32[16,1,384]{2,1,0:T(1,128)S(1)} %all-to-all-done.got_ref, bf16[512,512]{1,0:T(8,128)(2,1)S(1)} %get-tuple-element.7.cot_ref, bf16[128,512]{1,0:T(8,128)(2,1)S(1)} %get-tuple-element.8.weight_ref, ...), custom_call_target="tpu_custom_call" | custom-call | flops 2415919104 | bytes 4259840 | tf_op jit(solution)/shard_map/pallas_call | solution.py:295
  22.4 0.5 collective-permute-start.4
  22.9 1.8 %collective-permute-done.4 = f32[16,512]{1,0:T(8,128)S(1)} collective-permute-done((f32[16,512]{1,0:T(8,128)S(1)}, f32[16,512]{1,0:T(8,128)S(1)}, u32[]{:S(2)}, u32[]{:S(2)}) %collective-permute-start.4) | collective-permute-done | bytes 32800 | tf_op jit(solution)/shard_map/ppermute | solution.py:341
  25.1 0.8 %collective-permute-start.5 = (bf16[128,512]{1,0:T(8,128)(2,1)S(1)}, bf16[128,512]{1,0:T(8,128)(2,1)S(1)}, u32[]{:S(2)}, u32[]{:S(2)}) collective-permute-start(bf16[128,512]{1,0:T(8,128)(2,1)S(1)} %get-tuple-element.30), channel_id=1, source_target_pairs={{0,8},{2,10},{4,12},{6,14},{8,0},{10,2},{12,4},{14,6},{16,24},{18,... | collective-permute-start | bytes 393224 | tf_op jit(solution)/shard_map/ppermute | solution.py:341
  25.9 1.5 %collective-permute-start.6 = (bf16[128,512]{1,0:T(8,128)(2,1)S(1)}, bf16[128,512]{1,0:T(8,128)(2,1)S(1)}, u32[]{:S(2)}, u32[]{:S(2)}) collective-permute-start(bf16[128,512]{1,0:T(8,128)(2,1)S(1)} %get-tuple-element.31), channel_id=1, source_target_pairs={{0,4},{2,6},{4,0},{6,2},{8,12},{10,14},{12,8},{14,10},{16,20},{18,... | collective-permute-start | bytes 393224 | tf_op jit(solution)/shard_map/ppermute | solution.py:341
  27.4 1.3 %collective-permute-start.7 = (bf16[128,512]{1,0:T(8,128)(2,1)S(1)}, bf16[128,512]{1,0:T(8,128)(2,1)S(1)}, u32[]{:S(2)}, u32[]{:S(2)}) collective-permute-start(bf16[128,512]{1,0:T(8,128)(2,1)S(1)} %get-tuple-element.32), channel_id=1, source_target_pairs={{0,12},{2,14},{4,8},{6,10},{8,4},{10,6},{12,0},{14,2},{16,28},{18,... | collective-permute-start | bytes 393224 | tf_op jit(solution)/shard_map/ppermute | solution.py:341
  28.7 1.6 %collective-permute-start.3 = (bf16[96,512]{1,0:T(8,128)(2,1)S(1)}, bf16[96,512]{1,0:T(8,128)(2,1)S(1)}, u32[]{:S(2)}, u32[]{:S(2)}) collective-permute-start(bf16[96,512]{1,0:T(8,128)(2,1)S(1)} %get-tuple-element.22), channel_id=1, source_target_pairs={{0,12},{2,14},{4,8},{6,10},{8,4},{10,6},{12,0},{14,2},{16,28},{18,... | collective-permute-start | bytes 294920 | tf_op jit(solution)/shard_map/ppermute | solution.py:341
  30.3 0.6 %collective-permute-start.2 = (bf16[96,512]{1,0:T(8,128)(2,1)S(1)}, bf16[96,512]{1,0:T(8,128)(2,1)S(1)}, u32[]{:S(2)}, u32[]{:S(2)}) collective-permute-start(bf16[96,512]{1,0:T(8,128)(2,1)S(1)} %get-tuple-element.26), channel_id=1, source_target_pairs={{0,4},{2,6},{4,0},{6,2},{8,12},{10,14},{12,8},{14,10},{16,20},{18,... | collective-permute-start | bytes 294920 | tf_op jit(solution)/shard_map/ppermute | solution.py:341
  30.9 0.7 %collective-permute-done.5 = bf16[128,512]{1,0:T(8,128)(2,1)S(1)} collective-permute-done((bf16[128,512]{1,0:T(8,128)(2,1)S(1)}, bf16[128,512]{1,0:T(8,128)(2,1)S(1)}, u32[]{:S(2)}, u32[]{:S(2)}) %collective-permute-start.5) | collective-permute-done | bytes 131104 | tf_op jit(solution)/shard_map/ppermute | solution.py:341
  31.5 0.6 %collective-permute-start.1 = (bf16[96,512]{1,0:T(8,128)(2,1)S(1)}, bf16[96,512]{1,0:T(8,128)(2,1)S(1)}, u32[]{:S(2)}, u32[]{:S(2)}) collective-permute-start(bf16[96,512]{1,0:T(8,128)(2,1)S(1)} %get-tuple-element.27), channel_id=1, source_target_pairs={{0,8},{2,10},{4,12},{6,14},{8,0},{10,2},{12,4},{14,6},{16,24},{18,... | collective-permute-start | bytes 294920 | tf_op jit(solution)/shard_map/ppermute | solution.py:341
  32.2 3.4 %collective-permute-done.6 = bf16[128,512]{1,0:T(8,128)(2,1)S(1)} collective-permute-done((bf16[128,512]{1,0:T(8,128)(2,1)S(1)}, bf16[128,512]{1,0:T(8,128)(2,1)S(1)}, u32[]{:S(2)}, u32[]{:S(2)}) %collective-permute-start.6) | collective-permute-done | bytes 131104 | tf_op jit(solution)/shard_map/ppermute | solution.py:341
  35.7 3.0 %collective-permute-start.9 = (bf16[64,512]{1,0:T(8,128)(2,1)S(1)}, bf16[64,512]{1,0:T(8,128)(2,1)S(1)}, u32[]{:S(2)}, u32[]{:S(2)}) collective-permute-start(bf16[64,512]{1,0:T(8,128)(2,1)S(1)} %get-tuple-element.29), channel_id=1, source_target_pairs={{0,16},{2,18},{4,20},{6,22},{8,24},{10,26},{12,28},{14,30},{16,0},... | collective-permute-start | bytes 196616 | tf_op jit(solution)/shard_map/ppermute | solution.py:341
  38.9 2.3 %collective-permute-done.9 = bf16[64,512]{1,0:T(8,128)(2,1)S(1)} collective-permute-done((bf16[64,512]{1,0:T(8,128)(2,1)S(1)}, bf16[64,512]{1,0:T(8,128)(2,1)S(1)}, u32[]{:S(2)}, u32[]{:S(2)}) %collective-permute-start.9) | collective-permute-done | bytes 65568 | tf_op jit(solution)/shard_map/ppermute | solution.py:341
  41.2 2.8 %collective-permute-done.8 = bf16[64,512]{1,0:T(8,128)(2,1)S(1)} collective-permute-done((bf16[64,512]{1,0:T(8,128)(2,1)S(1)}, bf16[64,512]{1,0:T(8,128)(2,1)S(1)}, u32[]{:S(2)}, u32[]{:S(2)}) %collective-permute-start.8) | collective-permute-done | bytes 65568 | tf_op jit(solution)/shard_map/ppermute | solution.py:341
  44.0 1.6 %collective-permute-start.10 = (bf16[128,512]{1,0:T(8,128)(2,1)S(1)}, bf16[128,512]{1,0:T(8,128)(2,1)S(1)}, u32[]{:S(2)}, u32[]{:S(2)}) collective-permute-start(bf16[128,512]{1,0:T(8,128)(2,1)S(1)} %pad_maximum_fusion.6.own_ref), channel_id=1, source_target_pairs={{0,1},{1,0},{2,3},{3,2},{4,5},{5,4},{6,7},{7,6},{8,9},{9,8},{10,11... | collective-permute-start | bytes 393224 | tf_op jit(solution)/shard_map/ppermute | solution.py:341
  45.5 3.5 %collective-permute-done.10.got_ref = bf16[128,512]{1,0:T(8,128)(2,1)S(1)} collective-permute-done((bf16[128,512]{1,0:T(8,128)(2,1)S(1)}, bf16[128,512]{1,0:T(8,128)(2,1)S(1)}, u32[]{:S(2)}, u32[]{:S(2)}) %collective-permute-start.10) | collective-permute-done | bytes 131104 | tf_op jit(solution)/shard_map/ppermute | solution.py:341
  49.0 0.7 %shard_map.135 = (f32[96,512]{1,0:T(8,128)}, f32[16,512]{1,0:T(8,128)}) custom-call(bf16[128,512]{1,0:T(8,128)(2,1)S(1)} %pad_maximum_fusion.6.own_ref, bf16[128,512]{1,0:T(8,128)(2,1)S(1)} %collective-permute-done.10.got_ref), custom_call_target="tpu_custom_call" | custom-call | tf_op jit(solution)/shard_map/pallas_call | solution.py:383
  (22 shorter events, 0.8 us)
Async XLA Ops:
  2.0 13.9 %all-to-all-start = ((f32[16,1,384]{2,1,0:T(1,128)}), f32[16,1,384]{2,1,0:T(1,128)S(1)}, u32[]{:S(2)}, u32[]{:S(2)}) async-start(f32[16,1,384]{2,1,0:T(1,128)} %shard_map.131), calls=%async_computation | async-start | bytes 49152 | tf_op jit(solution)/shard_map/all_to_all | solution.py:451
  10.9 1.4 %copy-start = (bf16[1536,512]{1,0:T(8,128)(2,1)S(1)}, bf16[1536,512]{1,0:T(8,128)(2,1)}, u32[]{:S(2)}) copy-start(bf16[1536,512]{1,0:T(8,128)(2,1)} %conv_two_ref.3) | copy-start | bytes 4718596
  12.3 1.0 %copy-start.2 = (bf16[16,32,512]{2,1,0:T(8,128)(2,1)S(1)}, bf16[16,32,512]{2,1,0:T(8,128)(2,1)}, u32[]{:S(2)}) copy-start(bf16[16,32,512]{2,1,0:T(8,128)(2,1)} %param.15) | copy-start | bytes 1572868
  13.3 2.6 %copy-start.1 = (bf16[1536,512]{1,0:T(8,128)(2,1)S(1)}, bf16[1536,512]{1,0:T(8,128)(2,1)}, u32[]{:S(2)}) copy-start(bf16[1536,512]{1,0:T(8,128)(2,1)} %conv_two_ref.3) | copy-start | bytes 4718596
  22.3 2.4 %collective-permute-start = (bf16[768,512]{1,0:T(8,128)(2,1)S(1)}, bf16[768,512]{1,0:T(8,128)(2,1)S(1)}, u32[]{:S(2)}, u32[]{:S(2)}) collective-permute-start(bf16[768,512]{1,0:T(8,128)(2,1)S(1)} %get-tuple-element.10), channel_id=1, source_target_pairs={{0,2},{2,0},{4,6},{6,4},{8,10},{10,8},{12,14},{14,12},{16,18},{18,... | collective-permute-start | bytes 2359304 | tf_op jit(solution)/shard_map/ppermute | solution.py:341
  22.4 2.3 %collective-permute-start.4 = (f32[16,512]{1,0:T(8,128)S(1)}, f32[16,512]{1,0:T(8,128)S(1)}, u32[]{:S(2)}, u32[]{:S(2)}) collective-permute-start(f32[16,512]{1,0:T(8,128)S(1)} %get-tuple-element.11), channel_id=1, source_target_pairs={{0,2},{2,0},{4,6},{6,4},{8,10},{10,8},{12,14},{14,12},{16,18},{18,... | collective-permute-start | bytes 98312 | tf_op jit(solution)/shard_map/ppermute | solution.py:341
  25.1 6.4 %collective-permute-start.5 = (bf16[128,512]{1,0:T(8,128)(2,1)S(1)}, bf16[128,512]{1,0:T(8,128)(2,1)S(1)}, u32[]{:S(2)}, u32[]{:S(2)}) collective-permute-start(bf16[128,512]{1,0:T(8,128)(2,1)S(1)} %get-tuple-element.30), channel_id=1, source_target_pairs={{0,8},{2,10},{4,12},{6,14},{8,0},{10,2},{12,4},{14,6},{16,24},{18,... | collective-permute-start | bytes 393224 | tf_op jit(solution)/shard_map/ppermute | solution.py:341
  25.9 9.7 %collective-permute-start.6 = (bf16[128,512]{1,0:T(8,128)(2,1)S(1)}, bf16[128,512]{1,0:T(8,128)(2,1)S(1)}, u32[]{:S(2)}, u32[]{:S(2)}) collective-permute-start(bf16[128,512]{1,0:T(8,128)(2,1)S(1)} %get-tuple-element.31), channel_id=1, source_target_pairs={{0,4},{2,6},{4,0},{6,2},{8,12},{10,14},{12,8},{14,10},{16,20},{18,... | collective-permute-start | bytes 393224 | tf_op jit(solution)/shard_map/ppermute | solution.py:341
  27.4 8.2 %collective-permute-start.7 = (bf16[128,512]{1,0:T(8,128)(2,1)S(1)}, bf16[128,512]{1,0:T(8,128)(2,1)S(1)}, u32[]{:S(2)}, u32[]{:S(2)}) collective-permute-start(bf16[128,512]{1,0:T(8,128)(2,1)S(1)} %get-tuple-element.32), channel_id=1, source_target_pairs={{0,12},{2,14},{4,8},{6,10},{8,4},{10,6},{12,0},{14,2},{16,28},{18,... | collective-permute-start | bytes 393224 | tf_op jit(solution)/shard_map/ppermute | solution.py:341
  28.7 10.1 %collective-permute-start.3 = (bf16[96,512]{1,0:T(8,128)(2,1)S(1)}, bf16[96,512]{1,0:T(8,128)(2,1)S(1)}, u32[]{:S(2)}, u32[]{:S(2)}) collective-permute-start(bf16[96,512]{1,0:T(8,128)(2,1)S(1)} %get-tuple-element.22), channel_id=1, source_target_pairs={{0,12},{2,14},{4,8},{6,10},{8,4},{10,6},{12,0},{14,2},{16,28},{18,... | collective-permute-start | bytes 294920 | tf_op jit(solution)/shard_map/ppermute | solution.py:341
  30.3 8.5 %collective-permute-start.2 = (bf16[96,512]{1,0:T(8,128)(2,1)S(1)}, bf16[96,512]{1,0:T(8,128)(2,1)S(1)}, u32[]{:S(2)}, u32[]{:S(2)}) collective-permute-start(bf16[96,512]{1,0:T(8,128)(2,1)S(1)} %get-tuple-element.26), channel_id=1, source_target_pairs={{0,4},{2,6},{4,0},{6,2},{8,12},{10,14},{12,8},{14,10},{16,20},{18,... | collective-permute-start | bytes 294920 | tf_op jit(solution)/shard_map/ppermute | solution.py:341
  31.5 7.3 %collective-permute-start.1 = (bf16[96,512]{1,0:T(8,128)(2,1)S(1)}, bf16[96,512]{1,0:T(8,128)(2,1)S(1)}, u32[]{:S(2)}, u32[]{:S(2)}) collective-permute-start(bf16[96,512]{1,0:T(8,128)(2,1)S(1)} %get-tuple-element.27), channel_id=1, source_target_pairs={{0,8},{2,10},{4,12},{6,14},{8,0},{10,2},{12,4},{14,6},{16,24},{18,... | collective-permute-start | bytes 294920 | tf_op jit(solution)/shard_map/ppermute | solution.py:341
  35.7 5.4 %collective-permute-start.9 = (bf16[64,512]{1,0:T(8,128)(2,1)S(1)}, bf16[64,512]{1,0:T(8,128)(2,1)S(1)}, u32[]{:S(2)}, u32[]{:S(2)}) collective-permute-start(bf16[64,512]{1,0:T(8,128)(2,1)S(1)} %get-tuple-element.29), channel_id=1, source_target_pairs={{0,16},{2,18},{4,20},{6,22},{8,24},{10,26},{12,28},{14,30},{16,0},... | collective-permute-start | bytes 196616 | tf_op jit(solution)/shard_map/ppermute | solution.py:341
  38.7 5.2 %collective-permute-start.8 = (bf16[64,512]{1,0:T(8,128)(2,1)S(1)}, bf16[64,512]{1,0:T(8,128)(2,1)S(1)}, u32[]{:S(2)}, u32[]{:S(2)}) collective-permute-start(bf16[64,512]{1,0:T(8,128)(2,1)S(1)} %get-tuple-element.28), channel_id=1, source_target_pairs={{0,16},{2,18},{4,20},{6,22},{8,24},{10,26},{12,28},{14,30},{16,0},... | collective-permute-start | bytes 196616 | tf_op jit(solution)/shard_map/ppermute | solution.py:341
  44.0 5.0 %collective-permute-start.10 = (bf16[128,512]{1,0:T(8,128)(2,1)S(1)}, bf16[128,512]{1,0:T(8,128)(2,1)S(1)}, u32[]{:S(2)}, u32[]{:S(2)}) collective-permute-start(bf16[128,512]{1,0:T(8,128)(2,1)S(1)} %pad_maximum_fusion.6.own_ref), channel_id=1, source_target_pairs={{0,1},{1,0},{2,3},{3,2},{4,5},{5,4},{6,7},{7,6},{8,9},{9,8},{10,11... | collective-permute-start | bytes 393224 | tf_op jit(solution)/shard_map/ppermute | solution.py:341

commit v8 on v7

--- a/solution.py
+++ b/solution.py
@@ -116,8 +116,10 @@
     weight_ref,
     conv_two_ref,
     table_ref,
-    send_ref,
-    keep_ref,
+    send_far,
+    send_near,
+    keep_far,
+    keep_near,
     small_ref,
     taps,
     limits,
@@ -242,12 +244,13 @@
     share = grad.shape[0] // shares
     me = place_ref[0]
     order = bit_order(shares)
-    half = shares // 2
+    parts = (keep_near, keep_far, send_near, send_far)
+    quarter = shares // 4
     for spot in range(shares):
         flip = sum(1 << bit for i, bit in enumerate(reversed(order)) if spot >> i & 1)
         block = grad[pl.ds(pl.multiple_of((me ^ flip) * share, 8), share), :]
-        part = send_ref if spot >= half else keep_ref
-        at = spot % half * share
+        part = parts[spot // quarter]
+        at = spot % quarter * share
         part[at : at + share, :] = block.astype(part.dtype)
 
     turn = (((1,), (1,)), ((), ()))
@@ -290,17 +293,19 @@
     count = got.shape[0]
     rows_two, width = cot.shape
     rows_one = 2 * rows_two + count
-    half = 3 * width // 2
+    quarter = 3 * width // 4
     vmem = pl.BlockSpec(memory_space=pltpu.VMEM)
     return pl.pallas_call(
         functools.partial(local_kernel, record, shares),
         out_shape=(
-            jax.ShapeDtypeStruct((half, width), BF16),
-            jax.ShapeDtypeStruct((half, width), F32),
+            jax.ShapeDtypeStruct((quarter, width), BF16),
+            jax.ShapeDtypeStruct((quarter, width), BF16),
+            jax.ShapeDtypeStruct((quarter, width), F32),
+            jax.ShapeDtypeStruct((quarter, width), F32),
             jax.ShapeDtypeStruct((ROWS, width), F32),
         ),
         in_specs=[pl.BlockSpec(memory_space=pltpu.SMEM)] + [vmem] * 5,
-        out_specs=(vmem,) * 3,
+        out_specs=(vmem,) * 5,
         scratch_shapes=[
             pltpu.VMEM((rows_one, 128), BF16),
             pltpu.VMEM((count, 128), jnp.int32),
@@ -370,15 +375,17 @@
     )(own, *got)
 
 
-def finish_kernel(own_ref, got_ref, rows_ref, small_ref):
-    own, small = contents(own_ref[...])
-    got, more = contents(got_ref[...])
-    rows_ref[...] = own + got
+def finish_kernel(own_first, own_second, got_first, got_second, rows_ref, small_ref):
+    cut = own_first.shape[0]
+    own, small = contents(own_second[...])
+    got, more = contents(got_second[...])
+    rows_ref[:cut, :] = own_first[...].astype(F32) + got_first[...].astype(F32)
+    rows_ref[cut:, :] = own + got
     small_ref[...] = small + more
 
 
-def finish(own, got):
-    rows, width = own.shape[0] - 2 * ROWS, own.shape[1]
+def finish(*parts):
+    rows, width = parts[0].shape[0] + parts[1].shape[0] - 2 * ROWS, parts[0].shape[1]
     vmem = pl.BlockSpec(memory_space=pltpu.VMEM)
     return pl.pallas_call(
         finish_kernel,
@@ -386,19 +393,20 @@
             jax.ShapeDtypeStruct((rows, width), F32),
             jax.ShapeDtypeStruct((ROWS, width), F32),
         ),
-        in_specs=[vmem, vmem],
+        in_specs=[vmem] * 4,
         out_specs=(pl.BlockSpec(), pl.BlockSpec()),
         compiler_params=pltpu.CompilerParams(vmem_limit_bytes=8 * 1024 * 1024),
-    )(own, got)
-
-
-def sum_all(sizes, send, keep, small):
+    )(*parts)
+
+
+def sum_all(sizes, send_far, send_near, keep_far, keep_near, small):
     order = [("dp", bit) for bit in bit_order(sizes["dp"])]
     core, onward, pair, left = order[0], order[1], order[2:4], order[4:]
     small = small + exchange(sizes, [core], small)
-    total = keep + exchange(sizes, [core], send).astype(F32)
-    rows = total.shape[0] // 8
-    near, far = ([total[i * rows : (i + 1) * rows] for i in range(j, j + 4)] for j in (0, 4))
+    far = keep_far + exchange(sizes, [core], send_far).astype(F32)
+    near = keep_near + exchange(sizes, [core], send_near).astype(F32)
+    rows = far.shape[0] // 4
+    near, far = ([part[i * rows : (i + 1) * rows] for i in range(4)] for part in (near, far))
     small = contents(message(far[0], small))[1], small
     fars, smalls, nears = [far[0]], [small[0]], []
     chosen = [[bit for i, bit in enumerate(pair) if code >> (1 - i) & 1] for code in range(4)]
@@ -410,23 +418,29 @@
     for code in (1, 2, 3):
         nears.append(exchange(sizes, chosen[code], near[code].astype(BF16)))
     cut = own.shape[0] // 2 // ROWS * ROWS
-    got = [exchange(sizes, [onward], part) for part in (own[:cut], own[cut:])]
-    got, more = contents(jnp.concatenate(got, axis=0))
-    total, small = near_sum(near[0], *nears) + got, contents(own)[1] + more
+    first, second = (exchange(sizes, [onward], part) for part in (own[:cut], own[cut:]))
+    base = near_sum(near[0], *nears)
+    first = base[:cut] + first.astype(F32)
+    second, more = contents(second)
+    second, small = base[cut:] + second, contents(own[cut:])[1] + more
     for bit in left:
+        total = jnp.concatenate([first, second], axis=0)
         half = total.shape[0] // 2
         own = message(total[half:], small)
         got, more = contents(exchange(sizes, [bit], own))
         total, small = total[:half] + got, contents(own)[1] + more
+        cut = own.shape[0] // 2 // ROWS * ROWS
+        first, second = total[:cut], total[cut:]
     bits = sizes["blk"].bit_length() - 1
     for bit in range(bits):
-        own = message(total, small)
-        got = exchange(sizes, [("blk", bit)], own)
+        own = first.astype(BF16), message(second, small)
+        got = [exchange(sizes, [("blk", bit)], part) for part in own]
         if bit == bits - 1:
-            return finish(own, got)
-        (total, small), (got, more) = contents(own), contents(got)
-        total, small = total + got, small + more
-    return total, small
+            return finish(*own, *got)
+        first = own[0].astype(F32) + got[0].astype(F32)
+        (second, small), (more, extra) = contents(own[1]), contents(got[1])
+        second, small = second + more, small + extra
+    return jnp.concatenate([first, second], axis=0), small
 
 
 def per_device(

time: 50.1 us -> 49.5 us (0.988)
  waiting for transfers between devices: 16.6 us -> 12.1 us
  starting transfers between devices: 19 us -> 22.8 us
    ppermute x11 -> x13, waiting for transfers between devices: 14.4 us -> 9.95 us  [exchange(): return lax.ppermute(message, axes if len(axes) > 1 else axes[0], pairs)]
    ppermute x11 -> x13, starting transfers between devices: 11.6 us -> 15.4 us  [exchange(): return lax.ppermute(message, axes if len(axes) > 1 else axes[0], pairs)]
  transfers between devices with their start and end apart: 12 -> 14, of which waited for: 7 -> 7; matrix products, arithmetic and copies ran while one was open for 3% -> 4% of each run, Pallas kernels for 1% -> 1%
where the time goes in v8:
time: 49.5 us; the launch traced here: 49 us
  starting transfers between devices  22.8 us (46%)
  waiting for transfers between devices  12.1 us (24%)
  Pallas kernels  8.91 us (18%)
  local copies, waits for them, and re-layouts  4.02 us (8%)
  between operations  0.8 us (2%)
    ppermute x13, starting transfers between devices, exchange(): return lax.ppermute(message, axes if len(axes) > 1 else axes[0], pairs)  15.4 us
    ppermute x13, waiting for transfers between devices, exchange(): return lax.ppermute(message, axes if len(axes) > 1 else axes[0], pairs)  9.95 us
    all_to_all x1, starting transfers between devices, per_device(): got = lax.all_to_all(packed, 'dp', split_axis=0, concat_axis=0, tiled=True)  7.36 us
    pallas_call x1, Pallas kernels, local_pass(): pl.pallas_call(functools.partial(local_kernel, record, shares), out_shape...  6.36 us
    unnamed x6, local copies, waits for them, and re-layouts  2.45 us
    all_to_all x1, waiting for transfers between devices, per_device(): got = lax.all_to_all(packed, 'dp', split_axis=0, concat_axis=0, tiled=True)  2.15 us
    concatenate x1, local copies, waits for them, and re-layouts, per_device(): table = jnp.concatenate([conv_one.astype(F32), jnp.stack(vectors)], axis=0)  1.52 us
    pallas_call x1, Pallas kernels, pack(): pl.pallas_call(pack_kernel, out_shape=jax.ShapeDtypeStruct((count, 1, wid...  1.37 us
  transfers between devices with their start and end apart: 14, of which 7 were waited for; matrix products, arithmetic and copies ran while one was open for 4% of the time, Pallas kernels for 1%

profile of v8, /device:TPU:0, one launch (start us, length us, event | category | flops | bytes accessed | tf_op | source)
XLA Modules:
  0.0 49.0 jit_solution(7059749413301201191)
XLA Ops:
  0.6 1.4 %shard_map.131 = f32[16,1,384]{2,1,0:T(1,128)} custom-call(s32[1,16]{1,0:T(1,128)} %packing.1, s32[16]{0:T(128)} %bins.1, bf16[16,330]{1,0:T(8,128)(2,1)} %wave_ref.1), custom_call_target="tpu_custom_call" | custom-call | tf_op jit(solution)/shard_map/pallas_call | solution.py:44
  2.0 7.4 %all-to-all-start = ((f32[16,1,384]{2,1,0:T(1,128)}), f32[16,1,384]{2,1,0:T(1,128)S(1)}, u32[]{:S(2)}, u32[]{:S(2)}) async-start(f32[16,1,384]{2,1,0:T(1,128)} %shard_map.131), calls=%async_computation | async-start | bytes 49152 | tf_op jit(solution)/shard_map/all_to_all | solution.py:465
  9.4 1.5 %concatenate.18.table_ref = f32[16,512]{1,0:T(8,128)S(1)} concatenate(bf16[10,512]{1,0:T(8,128)(2,1)} %param.16, f32[1,512]{1,0:T(1,128)} %bitcast.9, f32[1,512]{1,0:T(1,128)} %bitcast.10, f32[1,512]{1,0:T(1,128)} %bitcast.11, f32[1,512]{1,0:T(1,128)} %bitcast.12, f32[1,512]{1,0:T(1,128)} %bitcast.13, f32[1,512]{1,0:T(1,128)} %bitcast.14), dimensions={0} | concatenate | bytes 55296 | tf_op jit(solution)/shard_map/concatenate | solution.py:467
  10.9 1.4 %copy-done = bf16[1536,512]{1,0:T(8,128)(2,1)S(1)} copy-done((bf16[1536,512]{1,0:T(8,128)(2,1)S(1)}, bf16[1536,512]{1,0:T(8,128)(2,1)}, u32[]{:S(2)}) %copy-start) | copy-done | bytes 1572888
  12.3 1.0 %copy-done.2 = bf16[16,32,512]{2,1,0:T(8,128)(2,1)S(1)} copy-done((bf16[16,32,512]{2,1,0:T(8,128)(2,1)S(1)}, bf16[16,32,512]{2,1,0:T(8,128)(2,1)}, u32[]{:S(2)}) %copy-start.2) | copy-done | bytes 524312
  13.3 0.4 shard_map.132
  13.8 2.2 %all-to-all-done.got_ref = f32[16,1,384]{2,1,0:T(1,128)S(1)} async-done(((f32[16,1,384]{2,1,0:T(1,128)}), f32[16,1,384]{2,1,0:T(1,128)S(1)}, u32[]{:S(2)}, u32[]{:S(2)}) %all-to-all-start) | async-done | bytes 24608 | tf_op jit(solution)/shard_map/all_to_all | solution.py:465
  15.9 6.4 %shard_map.133 = (bf16[384,512]{1,0:T(8,128)(2,1)S(1)}, bf16[384,512]{1,0:T(8,128)(2,1)S(1)}, f32[384,512]{1,0:T(8,128)S(1)}, f32[384,512]{1,0:T(8,128)S(1)}, f32[16,512]{1,0:T(8,128)S(1)}) custom-call(s32[1]{0:T(128)} %bitcast.place_ref, f32[16,1,384]{2,1,0:T(1,128)S(1)} %all-to-all-done.got_ref, bf16[512,512]{1,0:T(8,128)(2,1)S(1)} %get-tuple-element.9.cot_ref, ...), custom_call_target="tpu_custom_call" | custom-call | flops 2415919104 | bytes 4259840 | tf_op jit(solution)/shard_map/pallas_call | solution.py:298
  22.4 0.5 %collective-permute-start.5 = (f32[16,512]{1,0:T(8,128)S(1)}, f32[16,512]{1,0:T(8,128)S(1)}, u32[]{:S(2)}, u32[]{:S(2)}) collective-permute-start(f32[16,512]{1,0:T(8,128)S(1)} %get-tuple-element.15), channel_id=1, source_target_pairs={{0,2},{2,0},{4,6},{6,4},{8,10},{10,8},{12,14},{14,12},{16,18},{18,... | collective-permute-start | bytes 98312 | tf_op jit(solution)/shard_map/ppermute | solution.py:346
  23.0 1.2 %collective-permute-done.5 = f32[16,512]{1,0:T(8,128)S(1)} collective-permute-done((f32[16,512]{1,0:T(8,128)S(1)}, f32[16,512]{1,0:T(8,128)S(1)}, u32[]{:S(2)}, u32[]{:S(2)}) %collective-permute-start.5) | collective-permute-done | bytes 32800 | tf_op jit(solution)/shard_map/ppermute | solution.py:346
  24.4 0.8 %collective-permute-start.6 = (bf16[128,512]{1,0:T(8,128)(2,1)S(1)}, bf16[128,512]{1,0:T(8,128)(2,1)S(1)}, u32[]{:S(2)}, u32[]{:S(2)}) collective-permute-start(bf16[128,512]{1,0:T(8,128)(2,1)S(1)} %get-tuple-element.34), channel_id=1, source_target_pairs={{0,8},{2,10},{4,12},{6,14},{8,0},{10,2},{12,4},{14,6},{16,24},{18,... | collective-permute-start | bytes 393224 | tf_op jit(solution)/shard_map/ppermute | solution.py:346
  25.2 1.5 %collective-permute-start.7 = (bf16[128,512]{1,0:T(8,128)(2,1)S(1)}, bf16[128,512]{1,0:T(8,128)(2,1)S(1)}, u32[]{:S(2)}, u32[]{:S(2)}) collective-permute-start(bf16[128,512]{1,0:T(8,128)(2,1)S(1)} %get-tuple-element.35), channel_id=1, source_target_pairs={{0,4},{2,6},{4,0},{6,2},{8,12},{10,14},{12,8},{14,10},{16,20},{18,... | collective-permute-start | bytes 393224 | tf_op jit(solution)/shard_map/ppermute | solution.py:346
  26.6 1.3 %collective-permute-start.8 = (bf16[128,512]{1,0:T(8,128)(2,1)S(1)}, bf16[128,512]{1,0:T(8,128)(2,1)S(1)}, u32[]{:S(2)}, u32[]{:S(2)}) collective-permute-start(bf16[128,512]{1,0:T(8,128)(2,1)S(1)} %get-tuple-element.36), channel_id=1, source_target_pairs={{0,12},{2,14},{4,8},{6,10},{8,4},{10,6},{12,0},{14,2},{16,28},{18,... | collective-permute-start | bytes 393224 | tf_op jit(solution)/shard_map/ppermute | solution.py:346
  28.1 1.7 %collective-permute-start.3 = (bf16[96,512]{1,0:T(8,128)(2,1)S(1)}, bf16[96,512]{1,0:T(8,128)(2,1)S(1)}, u32[]{:S(2)}, u32[]{:S(2)}) collective-permute-start(bf16[96,512]{1,0:T(8,128)(2,1)S(1)} %get-tuple-element.29), channel_id=1, source_target_pairs={{0,12},{2,14},{4,8},{6,10},{8,4},{10,6},{12,0},{14,2},{16,28},{18,... | collective-permute-start | bytes 294920 | tf_op jit(solution)/shard_map/ppermute | solution.py:346
  29.8 0.6 %collective-permute-start.2 = (bf16[96,512]{1,0:T(8,128)(2,1)S(1)}, bf16[96,512]{1,0:T(8,128)(2,1)S(1)}, u32[]{:S(2)}, u32[]{:S(2)}) collective-permute-start(bf16[96,512]{1,0:T(8,128)(2,1)S(1)} %get-tuple-element.30), channel_id=1, source_target_pairs={{0,4},{2,6},{4,0},{6,2},{8,12},{10,14},{12,8},{14,10},{16,20},{18,... | collective-permute-start | bytes 294920 | tf_op jit(solution)/shard_map/ppermute | solution.py:346
  30.8 0.9 %collective-permute-start.1 = (bf16[96,512]{1,0:T(8,128)(2,1)S(1)}, bf16[96,512]{1,0:T(8,128)(2,1)S(1)}, u32[]{:S(2)}, u32[]{:S(2)}) collective-permute-start(bf16[96,512]{1,0:T(8,128)(2,1)S(1)} %get-tuple-element.31), channel_id=1, source_target_pairs={{0,8},{2,10},{4,12},{6,14},{8,0},{10,2},{12,4},{14,6},{16,24},{18,... | collective-permute-start | bytes 294920 | tf_op jit(solution)/shard_map/ppermute | solution.py:346
  31.7 3.2 %collective-permute-done.7 = bf16[128,512]{1,0:T(8,128)(2,1)S(1)} collective-permute-done((bf16[128,512]{1,0:T(8,128)(2,1)S(1)}, bf16[128,512]{1,0:T(8,128)(2,1)S(1)}, u32[]{:S(2)}, u32[]{:S(2)}) %collective-permute-start.7) | collective-permute-done | bytes 131104 | tf_op jit(solution)/shard_map/ppermute | solution.py:346
  34.9 3.0 %collective-permute-start.10 = (bf16[64,512]{1,0:T(8,128)(2,1)S(1)}, bf16[64,512]{1,0:T(8,128)(2,1)S(1)}, u32[]{:S(2)}, u32[]{:S(2)}) collective-permute-start(bf16[64,512]{1,0:T(8,128)(2,1)S(1)} %get-tuple-element.32), channel_id=1, source_target_pairs={{0,16},{2,18},{4,20},{6,22},{8,24},{10,26},{12,28},{14,30},{16,0},... | collective-permute-start | bytes 196616 | tf_op jit(solution)/shard_map/ppermute | solution.py:346
  38.0 1.9 %collective-permute-start.9 = (bf16[64,512]{1,0:T(8,128)(2,1)S(1)}, bf16[64,512]{1,0:T(8,128)(2,1)S(1)}, u32[]{:S(2)}, u32[]{:S(2)}) collective-permute-start(bf16[64,512]{1,0:T(8,128)(2,1)S(1)} %get-tuple-element.33), channel_id=1, source_target_pairs={{0,16},{2,18},{4,20},{6,22},{8,24},{10,26},{12,28},{14,30},{16,0},... | collective-permute-start | bytes 196616 | tf_op jit(solution)/shard_map/ppermute | solution.py:346
  40.2 1.6 %collective-permute-start.12 = (bf16[64,512]{1,0:T(8,128)(2,1)S(1)}, bf16[64,512]{1,0:T(8,128)(2,1)S(1)}, u32[]{:S(2)}, u32[]{:S(2)}) collective-permute-start(bf16[64,512]{1,0:T(8,128)(2,1)S(1)} %pad_maximum_fusion.8.own_second), channel_id=1, source_target_pairs={{0,1},{1,0},{2,3},{3,2},{4,5},{5,4},{6,7},{7,6},{8,9},{9,8},{10,11... | collective-permute-start | bytes 196616 | tf_op jit(solution)/shard_map/ppermute | solution.py:346
  41.8 2.2 %collective-permute-done.9 = bf16[64,512]{1,0:T(8,128)(2,1)S(1)} collective-permute-done((bf16[64,512]{1,0:T(8,128)(2,1)S(1)}, bf16[64,512]{1,0:T(8,128)(2,1)S(1)}, u32[]{:S(2)}, u32[]{:S(2)}) %collective-permute-start.9) | collective-permute-done | bytes 65568 | tf_op jit(solution)/shard_map/ppermute | solution.py:346
  44.0 1.6 %collective-permute-start.11 = (bf16[64,512]{1,0:T(8,128)(2,1)S(1)}, bf16[64,512]{1,0:T(8,128)(2,1)S(1)}, u32[]{:S(2)}, u32[]{:S(2)}) collective-permute-start(bf16[64,512]{1,0:T(8,128)(2,1)S(1)} %fusion.2.own_first), channel_id=1, source_target_pairs={{0,1},{1,0},{2,3},{3,2},{4,5},{5,4},{6,7},{7,6},{8,9},{9,8},{10,11... | collective-permute-start | bytes 196616 | tf_op jit(solution)/shard_map/ppermute | solution.py:346
  45.6 2.7 %collective-permute-done.11.got_first = bf16[64,512]{1,0:T(8,128)(2,1)S(1)} collective-permute-done((bf16[64,512]{1,0:T(8,128)(2,1)S(1)}, bf16[64,512]{1,0:T(8,128)(2,1)S(1)}, u32[]{:S(2)}, u32[]{:S(2)}) %collective-permute-start.11) | collective-permute-done | bytes 65568 | tf_op jit(solution)/shard_map/ppermute | solution.py:346
  48.3 0.7 %shard_map.135 = (f32[96,512]{1,0:T(8,128)}, f32[16,512]{1,0:T(8,128)}) custom-call(bf16[64,512]{1,0:T(8,128)(2,1)S(1)} %fusion.2.own_first, bf16[64,512]{1,0:T(8,128)(2,1)S(1)} %pad_maximum_fusion.8.own_second, bf16[64,512]{1,0:T(8,128)(2,1)S(1)} %collective-permute-done.11.got_first, bf16[64,512]{1,0:T(8,128)(2,1)S(1)} %collective-permute-done.12.got_second), custom_call_target="tpu_custom_call" | custom-call | tf_op jit(solution)/shard_map/pallas_call | solution.py:390
  (30 shorter events, 1.4 us)
Async XLA Ops:
  2.0 13.9 %all-to-all-start = ((f32[16,1,384]{2,1,0:T(1,128)}), f32[16,1,384]{2,1,0:T(1,128)S(1)}, u32[]{:S(2)}, u32[]{:S(2)}) async-start(f32[16,1,384]{2,1,0:T(1,128)} %shard_map.131), calls=%async_computation | async-start | bytes 49152 | tf_op jit(solution)/shard_map/all_to_all | solution.py:465
  10.9 1.4 %copy-start = (bf16[1536,512]{1,0:T(8,128)(2,1)S(1)}, bf16[1536,512]{1,0:T(8,128)(2,1)}, u32[]{:S(2)}) copy-start(bf16[1536,512]{1,0:T(8,128)(2,1)} %conv_two_ref.3) | copy-start | bytes 4718596
  12.3 1.0 %copy-start.2 = (bf16[16,32,512]{2,1,0:T(8,128)(2,1)S(1)}, bf16[16,32,512]{2,1,0:T(8,128)(2,1)}, u32[]{:S(2)}) copy-start(bf16[16,32,512]{2,1,0:T(8,128)(2,1)} %param.15) | copy-start | bytes 1572868
  13.3 2.6 %copy-start.1 = (bf16[1536,512]{1,0:T(8,128)(2,1)S(1)}, bf16[1536,512]{1,0:T(8,128)(2,1)}, u32[]{:S(2)}) copy-start(bf16[1536,512]{1,0:T(8,128)(2,1)} %conv_two_ref.3) | copy-start | bytes 4718596
  22.3 1.8 %collective-permute-start.4 = (bf16[384,512]{1,0:T(8,128)(2,1)S(1)}, bf16[384,512]{1,0:T(8,128)(2,1)S(1)}, u32[]{:S(2)}, u32[]{:S(2)}) collective-permute-start(bf16[384,512]{1,0:T(8,128)(2,1)S(1)} %get-tuple-element.14), channel_id=1, source_target_pairs={{0,2},{2,0},{4,6},{6,4},{8,10},{10,8},{12,14},{14,12},{16,18},{18,... | collective-permute-start | bytes 1179656 | tf_op jit(solution)/shard_map/ppermute | solution.py:346
  22.4 1.8 %collective-permute-start.5 = (f32[16,512]{1,0:T(8,128)S(1)}, f32[16,512]{1,0:T(8,128)S(1)}, u32[]{:S(2)}, u32[]{:S(2)}) collective-permute-start(f32[16,512]{1,0:T(8,128)S(1)} %get-tuple-element.15), channel_id=1, source_target_pairs={{0,2},{2,0},{4,6},{6,4},{8,10},{10,8},{12,14},{14,12},{16,18},{18,... | collective-permute-start | bytes 98312 | tf_op jit(solution)/shard_map/ppermute | solution.py:346
  22.9 5.0 %collective-permute-start = (bf16[384,512]{1,0:T(8,128)(2,1)S(1)}, bf16[384,512]{1,0:T(8,128)(2,1)S(1)}, u32[]{:S(2)}, u32[]{:S(2)}) collective-permute-start(bf16[384,512]{1,0:T(8,128)(2,1)S(1)} %get-tuple-element.12), channel_id=1, source_target_pairs={{0,2},{2,0},{4,6},{6,4},{8,10},{10,8},{12,14},{14,12},{16,18},{18,... | collective-permute-start | bytes 1179656 | tf_op jit(solution)/shard_map/ppermute | solution.py:346
  24.4 6.4 %collective-permute-start.6 = (bf16[128,512]{1,0:T(8,128)(2,1)S(1)}, bf16[128,512]{1,0:T(8,128)(2,1)S(1)}, u32[]{:S(2)}, u32[]{:S(2)}) collective-permute-start(bf16[128,512]{1,0:T(8,128)(2,1)S(1)} %get-tuple-element.34), channel_id=1, source_target_pairs={{0,8},{2,10},{4,12},{6,14},{8,0},{10,2},{12,4},{14,6},{16,24},{18,... | collective-permute-start | bytes 393224 | tf_op jit(solution)/shard_map/ppermute | solution.py:346
  25.2 9.7 %collective-permute-start.7 = (bf16[128,512]{1,0:T(8,128)(2,1)S(1)}, bf16[128,512]{1,0:T(8,128)(2,1)S(1)}, u32[]{:S(2)}, u32[]{:S(2)}) collective-permute-start(bf16[128,512]{1,0:T(8,128)(2,1)S(1)} %get-tuple-element.35), channel_id=1, source_target_pairs={{0,4},{2,6},{4,0},{6,2},{8,12},{10,14},{12,8},{14,10},{16,20},{18,... | collective-permute-start | bytes 393224 | tf_op jit(solution)/shard_map/ppermute | solution.py:346
  26.6 8.2 %collective-permute-start.8 = (bf16[128,512]{1,0:T(8,128)(2,1)S(1)}, bf16[128,512]{1,0:T(8,128)(2,1)S(1)}, u32[]{:S(2)}, u32[]{:S(2)}) collective-permute-start(bf16[128,512]{1,0:T(8,128)(2,1)S(1)} %get-tuple-element.36), channel_id=1, source_target_pairs={{0,12},{2,14},{4,8},{6,10},{8,4},{10,6},{12,0},{14,2},{16,28},{18,... | collective-permute-start | bytes 393224 | tf_op jit(solution)/shard_map/ppermute | solution.py:346
  28.1 9.9 %collective-permute-start.3 = (bf16[96,512]{1,0:T(8,128)(2,1)S(1)}, bf16[96,512]{1,0:T(8,128)(2,1)S(1)}, u32[]{:S(2)}, u32[]{:S(2)}) collective-permute-start(bf16[96,512]{1,0:T(8,128)(2,1)S(1)} %get-tuple-element.29), channel_id=1, source_target_pairs={{0,12},{2,14},{4,8},{6,10},{8,4},{10,6},{12,0},{14,2},{16,28},{18,... | collective-permute-start | bytes 294920 | tf_op jit(solution)/shard_map/ppermute | solution.py:346
  29.8 8.2 %collective-permute-start.2 = (bf16[96,512]{1,0:T(8,128)(2,1)S(1)}, bf16[96,512]{1,0:T(8,128)(2,1)S(1)}, u32[]{:S(2)}, u32[]{:S(2)}) collective-permute-start(bf16[96,512]{1,0:T(8,128)(2,1)S(1)} %get-tuple-element.30), channel_id=1, source_target_pairs={{0,4},{2,6},{4,0},{6,2},{8,12},{10,14},{12,8},{14,10},{16,20},{18,... | collective-permute-start | bytes 294920 | tf_op jit(solution)/shard_map/ppermute | solution.py:346
  30.8 7.2 %collective-permute-start.1 = (bf16[96,512]{1,0:T(8,128)(2,1)S(1)}, bf16[96,512]{1,0:T(8,128)(2,1)S(1)}, u32[]{:S(2)}, u32[]{:S(2)}) collective-permute-start(bf16[96,512]{1,0:T(8,128)(2,1)S(1)} %get-tuple-element.31), channel_id=1, source_target_pairs={{0,8},{2,10},{4,12},{6,14},{8,0},{10,2},{12,4},{14,6},{16,24},{18,... | collective-permute-start | bytes 294920 | tf_op jit(solution)/shard_map/ppermute | solution.py:346
  34.9 5.3 %collective-permute-start.10 = (bf16[64,512]{1,0:T(8,128)(2,1)S(1)}, bf16[64,512]{1,0:T(8,128)(2,1)S(1)}, u32[]{:S(2)}, u32[]{:S(2)}) collective-permute-start(bf16[64,512]{1,0:T(8,128)(2,1)S(1)} %get-tuple-element.32), channel_id=1, source_target_pairs={{0,16},{2,18},{4,20},{6,22},{8,24},{10,26},{12,28},{14,30},{16,0},... | collective-permute-start | bytes 196616 | tf_op jit(solution)/shard_map/ppermute | solution.py:346
  38.0 5.9 %collective-permute-start.9 = (bf16[64,512]{1,0:T(8,128)(2,1)S(1)}, bf16[64,512]{1,0:T(8,128)(2,1)S(1)}, u32[]{:S(2)}, u32[]{:S(2)}) collective-permute-start(bf16[64,512]{1,0:T(8,128)(2,1)S(1)} %get-tuple-element.33), channel_id=1, source_target_pairs={{0,16},{2,18},{4,20},{6,22},{8,24},{10,26},{12,28},{14,30},{16,0},... | collective-permute-start | bytes 196616 | tf_op jit(solution)/shard_map/ppermute | solution.py:346
  40.2 5.3 %collective-permute-start.12 = (bf16[64,512]{1,0:T(8,128)(2,1)S(1)}, bf16[64,512]{1,0:T(8,128)(2,1)S(1)}, u32[]{:S(2)}, u32[]{:S(2)}) collective-permute-start(bf16[64,512]{1,0:T(8,128)(2,1)S(1)} %pad_maximum_fusion.8.own_second), channel_id=1, source_target_pairs={{0,1},{1,0},{2,3},{3,2},{4,5},{5,4},{6,7},{7,6},{8,9},{9,8},{10,11... | collective-permute-start | bytes 196616 | tf_op jit(solution)/shard_map/ppermute | solution.py:346
  44.0 4.3 %collective-permute-start.11 = (bf16[64,512]{1,0:T(8,128)(2,1)S(1)}, bf16[64,512]{1,0:T(8,128)(2,1)S(1)}, u32[]{:S(2)}, u32[]{:S(2)}) collective-permute-start(bf16[64,512]{1,0:T(8,128)(2,1)S(1)} %fusion.2.own_first), channel_id=1, source_target_pairs={{0,1},{1,0},{2,3},{3,2},{4,5},{5,4},{6,7},{7,6},{8,9},{9,8},{10,11... | collective-permute-start | bytes 196616 | tf_op jit(solution)/shard_map/ppermute | solution.py:346

commit v9 on v8

--- a/solution.py
+++ b/solution.py
@@ -356,25 +356,6 @@
     return got[:rows].astype(F32), hi.astype(F32) + lo.astype(F32)
 
 
-def near_kernel(own_ref, *refs):
-    terms = [own_ref[...]] + [ref[...].astype(F32) for ref in refs[:-1]]
-    refs[-1][...] = tree(terms)
-
-
-def near_sum(own, *got):
-    vmem = pl.BlockSpec(memory_space=pltpu.VMEM)
-    return pl.pallas_call(
-        near_kernel,
-        out_shape=jax.ShapeDtypeStruct(own.shape, F32),
-        in_specs=[vmem] * (1 + len(got)),
-        out_specs=vmem,
-        cost_estimate=pl.CostEstimate(
-            flops=4 * own.size, bytes_accessed=140 * own.size, transcendentals=0
-        ),
-        compiler_params=pltpu.CompilerParams(vmem_limit_bytes=8 * 1024 * 1024),
-    )(own, *got)
-
-
 def finish_kernel(own_first, own_second, got_first, got_second, rows_ref, small_ref):
     cut = own_first.shape[0]
     own, small = contents(own_second[...])
@@ -407,22 +388,22 @@
     near = keep_near + exchange(sizes, [core], send_near).astype(F32)
     rows = far.shape[0] // 4
     near, far = ([part[i * rows : (i + 1) * rows] for i in range(4)] for part in (near, far))
-    small = contents(message(far[0], small))[1], small
-    fars, smalls, nears = [far[0]], [small[0]], []
     chosen = [[bit for i, bit in enumerate(pair) if code >> (1 - i) & 1] for code in range(4)]
+    fars, nears = [far[0]], [near[0]]
+    smalls = [contents(message(near[0], small))[1]]
     for code in (1, 2, 3):
-        got, more = contents(exchange(sizes, chosen[code], message(far[code], small[1])))
-        fars.append(got)
+        fars.append(exchange(sizes, chosen[code], far[code].astype(BF16)).astype(F32))
+    for code in (1, 2, 3):
+        got, more = contents(exchange(sizes, chosen[code], message(near[code], small)))
+        nears.append(got)
         smalls.append(more)
-    own = message(tree(fars), tree(smalls))
-    for code in (1, 2, 3):
-        nears.append(exchange(sizes, chosen[code], near[code].astype(BF16)))
-    cut = own.shape[0] // 2 // ROWS * ROWS
-    first, second = (exchange(sizes, [onward], part) for part in (own[:cut], own[cut:]))
-    base = near_sum(near[0], *nears)
+    away, base = tree(fars), tree(nears)
+    cut = (away.shape[0] + 2 * ROWS) // 2 // ROWS * ROWS
+    own = message(away[cut:], tree(smalls))
+    first = exchange(sizes, [onward], away[:cut].astype(BF16))
+    second, more = contents(exchange(sizes, [onward], own))
     first = base[:cut] + first.astype(F32)
-    second, more = contents(second)
-    second, small = base[cut:] + second, contents(own[cut:])[1] + more
+    second, small = base[cut:] + second, contents(own)[1] + more
     for bit in left:
         total = jnp.concatenate([first, second], axis=0)
         half = total.shape[0] // 2

time: 49.5 us -> 49.8 us (level)
  starting transfers between devices: 22.8 us -> 23.3 us
    ppermute x13, starting transfers between devices: 15.4 us -> 16 us  [exchange(): return lax.ppermute(message, axes if len(axes) > 1 else axes[0], pairs)]
  transfers between devices with their start and end apart: 14 -> 14, of which waited for: 7 -> 9; matrix products, arithmetic and copies ran while one was open for 4% -> 4% of each run, Pallas kernels for 1% -> 1%
where the time goes in v9:
time: 49.8 us; the launch traced here: 49.4 us
  starting transfers between devices  23.3 us (47%)
  waiting for transfers between devices  11.9 us (24%)
  Pallas kernels  8.87 us (18%)
  local copies, waits for them, and re-layouts  4.02 us (8%)
  between operations  0.8 us (2%)
    ppermute x13, starting transfers between devices, exchange(): return lax.ppermute(message, axes if len(axes) > 1 else axes[0], pairs)  16 us
    ppermute x13, waiting for transfers between devices, exchange(): return lax.ppermute(message, axes if len(axes) > 1 else axes[0], pairs)  9.76 us
    all_to_all x1, starting transfers between devices, per_device(): got = lax.all_to_all(packed, 'dp', split_axis=0, concat_axis=0, tiled=True)  7.36 us
    pallas_call x1, Pallas kernels, local_pass(): pl.pallas_call(functools.partial(local_kernel, record, shares), out_shape...  6.36 us
    unnamed x6, local copies, waits for them, and re-layouts  2.45 us
    all_to_all x1, waiting for transfers between devices, per_device(): got = lax.all_to_all(packed, 'dp', split_axis=0, concat_axis=0, tiled=True)  2.15 us
    concatenate x1, local copies, waits for them, and re-layouts, per_device(): table = jnp.concatenate([conv_one.astype(F32), jnp.stack(vectors)], axis=0)  1.52 us
    pallas_call x1, Pallas kernels, pack(): pl.pallas_call(pack_kernel, out_shape=jax.ShapeDtypeStruct((count, 1, wid...  1.37 us
  transfers between devices with their start and end apart: 14, of which 9 were waited for; matrix products, arithmetic and copies ran while one was open for 4% of the time, Pallas kernels for 1%

profile of v9, /device:TPU:0, one launch (start us, length us, event | category | flops | bytes accessed | tf_op | source)
XLA Modules:
  0.0 49.4 jit_solution(6248869872042902751)
XLA Ops:
  0.6 1.4 %shard_map.131 = f32[16,1,384]{2,1,0:T(1,128)} custom-call(s32[1,16]{1,0:T(1,128)} %packing.1, s32[16]{0:T(128)} %bins.1, bf16[16,330]{1,0:T(8,128)(2,1)} %wave_ref.1), custom_call_target="tpu_custom_call" | custom-call | tf_op jit(solution)/shard_map/pallas_call | solution.py:44
  2.0 7.4 %all-to-all-start = ((f32[16,1,384]{2,1,0:T(1,128)}), f32[16,1,384]{2,1,0:T(1,128)S(1)}, u32[]{:S(2)}, u32[]{:S(2)}) async-start(f32[16,1,384]{2,1,0:T(1,128)} %shard_map.131), calls=%async_computation | async-start | bytes 49152 | tf_op jit(solution)/shard_map/all_to_all | solution.py:446
  9.4 1.5 %concatenate.18.table_ref = f32[16,512]{1,0:T(8,128)S(1)} concatenate(bf16[10,512]{1,0:T(8,128)(2,1)} %param.16, f32[1,512]{1,0:T(1,128)} %bitcast.9, f32[1,512]{1,0:T(1,128)} %bitcast.10, f32[1,512]{1,0:T(1,128)} %bitcast.11, f32[1,512]{1,0:T(1,128)} %bitcast.12, f32[1,512]{1,0:T(1,128)} %bitcast.13, f32[1,512]{1,0:T(1,128)} %bitcast.14), dimensions={0} | concatenate | bytes 55296 | tf_op jit(solution)/shard_map/concatenate | solution.py:448
  10.9 1.4 %copy-done = bf16[1536,512]{1,0:T(8,128)(2,1)S(1)} copy-done((bf16[1536,512]{1,0:T(8,128)(2,1)S(1)}, bf16[1536,512]{1,0:T(8,128)(2,1)}, u32[]{:S(2)}) %copy-start) | copy-done | bytes 1572888
  12.3 1.0 %copy-done.2 = bf16[16,32,512]{2,1,0:T(8,128)(2,1)S(1)} copy-done((bf16[16,32,512]{2,1,0:T(8,128)(2,1)S(1)}, bf16[16,32,512]{2,1,0:T(8,128)(2,1)}, u32[]{:S(2)}) %copy-start.2) | copy-done | bytes 524312
  13.8 2.2 %all-to-all-done.got_ref = f32[16,1,384]{2,1,0:T(1,128)S(1)} async-done(((f32[16,1,384]{2,1,0:T(1,128)}), f32[16,1,384]{2,1,0:T(1,128)S(1)}, u32[]{:S(2)}, u32[]{:S(2)}) %all-to-all-start) | async-done | bytes 24608 | tf_op jit(solution)/shard_map/all_to_all | solution.py:446
  15.9 6.4 %shard_map.133 = (bf16[384,512]{1,0:T(8,128)(2,1)S(1)}, bf16[384,512]{1,0:T(8,128)(2,1)S(1)}, f32[384,512]{1,0:T(8,128)S(1)}, f32[384,512]{1,0:T(8,128)S(1)}, f32[16,512]{1,0:T(8,128)S(1)}) custom-call(s32[1]{0:T(128)} %bitcast.place_ref, f32[16,1,384]{2,1,0:T(1,128)S(1)} %all-to-all-done.got_ref, bf16[512,512]{1,0:T(8,128)(2,1)S(1)} %get-tuple-element.9.cot_ref, ...), custom_call_target="tpu_custom_call" | custom-call | flops 2415919104 | bytes 4259840 | tf_op jit(solution)/shard_map/pallas_call | solution.py:298
  23.0 1.2 %collective-permute-done.1 = f32[16,512]{1,0:T(8,128)S(1)} collective-permute-done((f32[16,512]{1,0:T(8,128)S(1)}, f32[16,512]{1,0:T(8,128)S(1)}, u32[]{:S(2)}, u32[]{:S(2)}) %collective-permute-start.1) | collective-permute-done | bytes 32800 | tf_op jit(solution)/shard_map/ppermute | solution.py:346
  24.9 0.8 %collective-permute-start.6 = (bf16[96,512]{1,0:T(8,128)(2,1)S(1)}, bf16[96,512]{1,0:T(8,128)(2,1)S(1)}, u32[]{:S(2)}, u32[]{:S(2)}) collective-permute-start(bf16[96,512]{1,0:T(8,128)(2,1)S(1)} %get-tuple-element.26), channel_id=1, source_target_pairs={{0,8},{2,10},{4,12},{6,14},{8,0},{10,2},{12,4},{14,6},{16,24},{18,... | collective-permute-start | bytes 294920 | tf_op jit(solution)/shard_map/ppermute | solution.py:346
  25.7 1.5 %collective-permute-start.8 = (bf16[96,512]{1,0:T(8,128)(2,1)S(1)}, bf16[96,512]{1,0:T(8,128)(2,1)S(1)}, u32[]{:S(2)}, u32[]{:S(2)}) collective-permute-start(bf16[96,512]{1,0:T(8,128)(2,1)S(1)} %get-tuple-element.27), channel_id=1, source_target_pairs={{0,12},{2,14},{4,8},{6,10},{8,4},{10,6},{12,0},{14,2},{16,28},{18,... | collective-permute-start | bytes 294920 | tf_op jit(solution)/shard_map/ppermute | solution.py:346
  27.1 1.3 %collective-permute-start.7 = (bf16[96,512]{1,0:T(8,128)(2,1)S(1)}, bf16[96,512]{1,0:T(8,128)(2,1)S(1)}, u32[]{:S(2)}, u32[]{:S(2)}) collective-permute-start(bf16[96,512]{1,0:T(8,128)(2,1)S(1)} %get-tuple-element.28), channel_id=1, source_target_pairs={{0,4},{2,6},{4,0},{6,2},{8,12},{10,14},{12,8},{14,10},{16,20},{18,... | collective-permute-start | bytes 294920 | tf_op jit(solution)/shard_map/ppermute | solution.py:346
  28.5 0.8 %collective-permute-start.2 = (bf16[128,512]{1,0:T(8,128)(2,1)S(1)}, bf16[128,512]{1,0:T(8,128)(2,1)S(1)}, u32[]{:S(2)}, u32[]{:S(2)}) collective-permute-start(bf16[128,512]{1,0:T(8,128)(2,1)S(1)} %get-tuple-element.32), channel_id=1, source_target_pairs={{0,8},{2,10},{4,12},{6,14},{8,0},{10,2},{12,4},{14,6},{16,24},{18,... | collective-permute-start | bytes 393224 | tf_op jit(solution)/shard_map/ppermute | solution.py:346
  29.3 1.5 %collective-permute-start.3 = (bf16[128,512]{1,0:T(8,128)(2,1)S(1)}, bf16[128,512]{1,0:T(8,128)(2,1)S(1)}, u32[]{:S(2)}, u32[]{:S(2)}) collective-permute-start(bf16[128,512]{1,0:T(8,128)(2,1)S(1)} %get-tuple-element.33), channel_id=1, source_target_pairs={{0,4},{2,6},{4,0},{6,2},{8,12},{10,14},{12,8},{14,10},{16,20},{18,... | collective-permute-start | bytes 393224 | tf_op jit(solution)/shard_map/ppermute | solution.py:346
  30.7 1.5 %collective-permute-start.4 = (bf16[128,512]{1,0:T(8,128)(2,1)S(1)}, bf16[128,512]{1,0:T(8,128)(2,1)S(1)}, u32[]{:S(2)}, u32[]{:S(2)}) collective-permute-start(bf16[128,512]{1,0:T(8,128)(2,1)S(1)} %get-tuple-element.34), channel_id=1, source_target_pairs={{0,12},{2,14},{4,8},{6,10},{8,4},{10,6},{12,0},{14,2},{16,28},{18,... | collective-permute-start | bytes 393224 | tf_op jit(solution)/shard_map/ppermute | solution.py:346
  32.2 0.6 %collective-permute-done.8 = bf16[96,512]{1,0:T(8,128)(2,1)S(1)} collective-permute-done((bf16[96,512]{1,0:T(8,128)(2,1)S(1)}, bf16[96,512]{1,0:T(8,128)(2,1)S(1)}, u32[]{:S(2)}, u32[]{:S(2)}) %collective-permute-start.8) | collective-permute-done | bytes 98336 | tf_op jit(solution)/shard_map/ppermute | solution.py:346
  32.9 1.4 %collective-permute-done.7 = bf16[96,512]{1,0:T(8,128)(2,1)S(1)} collective-permute-done((bf16[96,512]{1,0:T(8,128)(2,1)S(1)}, bf16[96,512]{1,0:T(8,128)(2,1)S(1)}, u32[]{:S(2)}, u32[]{:S(2)}) %collective-permute-start.7) | collective-permute-done | bytes 98336 | tf_op jit(solution)/shard_map/ppermute | solution.py:346
  34.4 2.4 %collective-permute-start.9 = (bf16[64,512]{1,0:T(8,128)(2,1)S(1)}, bf16[64,512]{1,0:T(8,128)(2,1)S(1)}, u32[]{:S(2)}, u32[]{:S(2)}) collective-permute-start(bf16[64,512]{1,0:T(8,128)(2,1)S(1)} %slice.116), channel_id=1, source_target_pairs={{0,16},{2,18},{4,20},{6,22},{8,24},{10,26},{12,28},{14,30},{16,0},... | collective-permute-start | bytes 196616 | tf_op jit(solution)/shard_map/ppermute | solution.py:346
  36.8 2.3 %collective-permute-done.3 = bf16[128,512]{1,0:T(8,128)(2,1)S(1)} collective-permute-done((bf16[128,512]{1,0:T(8,128)(2,1)S(1)}, bf16[128,512]{1,0:T(8,128)(2,1)S(1)}, u32[]{:S(2)}, u32[]{:S(2)}) %collective-permute-start.3) | collective-permute-done | bytes 131104 | tf_op jit(solution)/shard_map/ppermute | solution.py:346
  39.1 2.5 %collective-permute-start.10 = (bf16[64,512]{1,0:T(8,128)(2,1)S(1)}, bf16[64,512]{1,0:T(8,128)(2,1)S(1)}, u32[]{:S(2)}, u32[]{:S(2)}) collective-permute-start(bf16[64,512]{1,0:T(8,128)(2,1)S(1)} %pad_maximum_fusion.6), channel_id=1, source_target_pairs={{0,16},{2,18},{4,20},{6,22},{8,24},{10,26},{12,28},{14,30},{16,0},... | collective-permute-start | bytes 196616 | tf_op jit(solution)/shard_map/ppermute | solution.py:346
  41.6 1.6 %collective-permute-start.11 = (bf16[64,512]{1,0:T(8,128)(2,1)S(1)}, bf16[64,512]{1,0:T(8,128)(2,1)S(1)}, u32[]{:S(2)}, u32[]{:S(2)}) collective-permute-start(bf16[64,512]{1,0:T(8,128)(2,1)S(1)} %fusion.3.own_first), channel_id=1, source_target_pairs={{0,1},{1,0},{2,3},{3,2},{4,5},{5,4},{6,7},{7,6},{8,9},{9,8},{10,11... | collective-permute-start | bytes 196616 | tf_op jit(solution)/shard_map/ppermute | solution.py:346
  43.2 1.1 %collective-permute-done.10 = bf16[64,512]{1,0:T(8,128)(2,1)S(1)} collective-permute-done((bf16[64,512]{1,0:T(8,128)(2,1)S(1)}, bf16[64,512]{1,0:T(8,128)(2,1)S(1)}, u32[]{:S(2)}, u32[]{:S(2)}) %collective-permute-start.10) | collective-permute-done | bytes 65568 | tf_op jit(solution)/shard_map/ppermute | solution.py:346
  44.4 1.6 %collective-permute-start.12 = (bf16[64,512]{1,0:T(8,128)(2,1)S(1)}, bf16[64,512]{1,0:T(8,128)(2,1)S(1)}, u32[]{:S(2)}, u32[]{:S(2)}) collective-permute-start(bf16[64,512]{1,0:T(8,128)(2,1)S(1)} %pad_maximum_fusion.7.own_second), channel_id=1, source_target_pairs={{0,1},{1,0},{2,3},{3,2},{4,5},{5,4},{6,7},{7,6},{8,9},{9,8},{10,11... | collective-permute-start | bytes 196616 | tf_op jit(solution)/shard_map/ppermute | solution.py:346
  46.2 2.5 %collective-permute-done.12.got_second = bf16[64,512]{1,0:T(8,128)(2,1)S(1)} collective-permute-done((bf16[64,512]{1,0:T(8,128)(2,1)S(1)}, bf16[64,512]{1,0:T(8,128)(2,1)S(1)}, u32[]{:S(2)}, u32[]{:S(2)}) %collective-permute-start.12) | collective-permute-done | bytes 65568 | tf_op jit(solution)/shard_map/ppermute | solution.py:346
  48.7 0.7 %shard_map.134 = (f32[96,512]{1,0:T(8,128)}, f32[16,512]{1,0:T(8,128)}) custom-call(bf16[64,512]{1,0:T(8,128)(2,1)S(1)} %fusion.3.own_first, bf16[64,512]{1,0:T(8,128)(2,1)S(1)} %pad_maximum_fusion.7.own_second, bf16[64,512]{1,0:T(8,128)(2,1)S(1)} %collective-permute-done.11.got_first, bf16[64,512]{1,0:T(8,128)(2,1)S(1)} %collective-permute-done.12.got_second), custom_call_target="tpu_custom_call" | custom-call | tf_op jit(solution)/shard_map/pallas_call | solution.py:371
  (31 shorter events, 2.3 us)
Async XLA Ops:
  2.0 13.9 %all-to-all-start = ((f32[16,1,384]{2,1,0:T(1,128)}), f32[16,1,384]{2,1,0:T(1,128)S(1)}, u32[]{:S(2)}, u32[]{:S(2)}) async-start(f32[16,1,384]{2,1,0:T(1,128)} %shard_map.131), calls=%async_computation | async-start | bytes 49152 | tf_op jit(solution)/shard_map/all_to_all | solution.py:446
  10.9 1.4 %copy-start = (bf16[1536,512]{1,0:T(8,128)(2,1)S(1)}, bf16[1536,512]{1,0:T(8,128)(2,1)}, u32[]{:S(2)}) copy-start(bf16[1536,512]{1,0:T(8,128)(2,1)} %conv_two_ref.3) | copy-start | bytes 4718596
  12.3 1.0 %copy-start.2 = (bf16[16,32,512]{2,1,0:T(8,128)(2,1)S(1)}, bf16[16,32,512]{2,1,0:T(8,128)(2,1)}, u32[]{:S(2)}) copy-start(bf16[16,32,512]{2,1,0:T(8,128)(2,1)} %param.15) | copy-start | bytes 1572868
  13.3 2.6 %copy-start.1 = (bf16[1536,512]{1,0:T(8,128)(2,1)S(1)}, bf16[1536,512]{1,0:T(8,128)(2,1)}, u32[]{:S(2)}) copy-start(bf16[1536,512]{1,0:T(8,128)(2,1)} %conv_two_ref.3) | copy-start | bytes 4718596
  22.3 1.8 %collective-permute-start = (bf16[384,512]{1,0:T(8,128)(2,1)S(1)}, bf16[384,512]{1,0:T(8,128)(2,1)S(1)}, u32[]{:S(2)}, u32[]{:S(2)}) collective-permute-start(bf16[384,512]{1,0:T(8,128)(2,1)S(1)} %get-tuple-element.12), channel_id=1, source_target_pairs={{0,2},{2,0},{4,6},{6,4},{8,10},{10,8},{12,14},{14,12},{16,18},{18,... | collective-permute-start | bytes 1179656 | tf_op jit(solution)/shard_map/ppermute | solution.py:346
  22.4 1.8 %collective-permute-start.1 = (f32[16,512]{1,0:T(8,128)S(1)}, f32[16,512]{1,0:T(8,128)S(1)}, u32[]{:S(2)}, u32[]{:S(2)}) collective-permute-start(f32[16,512]{1,0:T(8,128)S(1)} %get-tuple-element.13), channel_id=1, source_target_pairs={{0,2},{2,0},{4,6},{6,4},{8,10},{10,8},{12,14},{14,12},{16,18},{18,... | collective-permute-start | bytes 98312 | tf_op jit(solution)/shard_map/ppermute | solution.py:346
  22.9 1.8 %collective-permute-start.5 = (bf16[384,512]{1,0:T(8,128)(2,1)S(1)}, bf16[384,512]{1,0:T(8,128)(2,1)S(1)}, u32[]{:S(2)}, u32[]{:S(2)}) collective-permute-start(bf16[384,512]{1,0:T(8,128)(2,1)S(1)} %get-tuple-element.15), channel_id=1, source_target_pairs={{0,2},{2,0},{4,6},{6,4},{8,10},{10,8},{12,14},{14,12},{16,18},{18,... | collective-permute-start | bytes 1179656 | tf_op jit(solution)/shard_map/ppermute | solution.py:346
  24.9 5.8 %collective-permute-start.6 = (bf16[96,512]{1,0:T(8,128)(2,1)S(1)}, bf16[96,512]{1,0:T(8,128)(2,1)S(1)}, u32[]{:S(2)}, u32[]{:S(2)}) collective-permute-start(bf16[96,512]{1,0:T(8,128)(2,1)S(1)} %get-tuple-element.26), channel_id=1, source_target_pairs={{0,8},{2,10},{4,12},{6,14},{8,0},{10,2},{12,4},{14,6},{16,24},{18,... | collective-permute-start | bytes 294920 | tf_op jit(solution)/shard_map/ppermute | solution.py:346
  25.7 7.2 %collective-permute-start.8 = (bf16[96,512]{1,0:T(8,128)(2,1)S(1)}, bf16[96,512]{1,0:T(8,128)(2,1)S(1)}, u32[]{:S(2)}, u32[]{:S(2)}) collective-permute-start(bf16[96,512]{1,0:T(8,128)(2,1)S(1)} %get-tuple-element.27), channel_id=1, source_target_pairs={{0,12},{2,14},{4,8},{6,10},{8,4},{10,6},{12,0},{14,2},{16,28},{18,... | collective-permute-start | bytes 294920 | tf_op jit(solution)/shard_map/ppermute | solution.py:346
  27.1 7.2 %collective-permute-start.7 = (bf16[96,512]{1,0:T(8,128)(2,1)S(1)}, bf16[96,512]{1,0:T(8,128)(2,1)S(1)}, u32[]{:S(2)}, u32[]{:S(2)}) collective-permute-start(bf16[96,512]{1,0:T(8,128)(2,1)S(1)} %get-tuple-element.28), channel_id=1, source_target_pairs={{0,4},{2,6},{4,0},{6,2},{8,12},{10,14},{12,8},{14,10},{16,20},{18,... | collective-permute-start | bytes 294920 | tf_op jit(solution)/shard_map/ppermute | solution.py:346
  28.5 8.3 %collective-permute-start.2 = (bf16[128,512]{1,0:T(8,128)(2,1)S(1)}, bf16[128,512]{1,0:T(8,128)(2,1)S(1)}, u32[]{:S(2)}, u32[]{:S(2)}) collective-permute-start(bf16[128,512]{1,0:T(8,128)(2,1)S(1)} %get-tuple-element.32), channel_id=1, source_target_pairs={{0,8},{2,10},{4,12},{6,14},{8,0},{10,2},{12,4},{14,6},{16,24},{18,... | collective-permute-start | bytes 393224 | tf_op jit(solution)/shard_map/ppermute | solution.py:346
  29.3 9.8 %collective-permute-start.3 = (bf16[128,512]{1,0:T(8,128)(2,1)S(1)}, bf16[128,512]{1,0:T(8,128)(2,1)S(1)}, u32[]{:S(2)}, u32[]{:S(2)}) collective-permute-start(bf16[128,512]{1,0:T(8,128)(2,1)S(1)} %get-tuple-element.33), channel_id=1, source_target_pairs={{0,4},{2,6},{4,0},{6,2},{8,12},{10,14},{12,8},{14,10},{16,20},{18,... | collective-permute-start | bytes 393224 | tf_op jit(solution)/shard_map/ppermute | solution.py:346
  30.7 8.3 %collective-permute-start.4 = (bf16[128,512]{1,0:T(8,128)(2,1)S(1)}, bf16[128,512]{1,0:T(8,128)(2,1)S(1)}, u32[]{:S(2)}, u32[]{:S(2)}) collective-permute-start(bf16[128,512]{1,0:T(8,128)(2,1)S(1)} %get-tuple-element.34), channel_id=1, source_target_pairs={{0,12},{2,14},{4,8},{6,10},{8,4},{10,6},{12,0},{14,2},{16,28},{18,... | collective-permute-start | bytes 393224 | tf_op jit(solution)/shard_map/ppermute | solution.py:346
  34.4 7.2 %collective-permute-start.9 = (bf16[64,512]{1,0:T(8,128)(2,1)S(1)}, bf16[64,512]{1,0:T(8,128)(2,1)S(1)}, u32[]{:S(2)}, u32[]{:S(2)}) collective-permute-start(bf16[64,512]{1,0:T(8,128)(2,1)S(1)} %slice.116), channel_id=1, source_target_pairs={{0,16},{2,18},{4,20},{6,22},{8,24},{10,26},{12,28},{14,30},{16,0},... | collective-permute-start | bytes 196616 | tf_op jit(solution)/shard_map/ppermute | solution.py:346
  39.1 5.2 %collective-permute-start.10 = (bf16[64,512]{1,0:T(8,128)(2,1)S(1)}, bf16[64,512]{1,0:T(8,128)(2,1)S(1)}, u32[]{:S(2)}, u32[]{:S(2)}) collective-permute-start(bf16[64,512]{1,0:T(8,128)(2,1)S(1)} %pad_maximum_fusion.6), channel_id=1, source_target_pairs={{0,16},{2,18},{4,20},{6,22},{8,24},{10,26},{12,28},{14,30},{16,0},... | collective-permute-start | bytes 196616 | tf_op jit(solution)/shard_map/ppermute | solution.py:346
  41.6 4.6 %collective-permute-start.11 = (bf16[64,512]{1,0:T(8,128)(2,1)S(1)}, bf16[64,512]{1,0:T(8,128)(2,1)S(1)}, u32[]{:S(2)}, u32[]{:S(2)}) collective-permute-start(bf16[64,512]{1,0:T(8,128)(2,1)S(1)} %fusion.3.own_first), channel_id=1, source_target_pairs={{0,1},{1,0},{2,3},{3,2},{4,5},{5,4},{6,7},{7,6},{8,9},{9,8},{10,11... | collective-permute-start | bytes 196616 | tf_op jit(solution)/shard_map/ppermute | solution.py:346
  44.4 4.3 %collective-permute-start.12 = (bf16[64,512]{1,0:T(8,128)(2,1)S(1)}, bf16[64,512]{1,0:T(8,128)(2,1)S(1)}, u32[]{:S(2)}, u32[]{:S(2)}) collective-permute-start(bf16[64,512]{1,0:T(8,128)(2,1)S(1)} %pad_maximum_fusion.7.own_second), channel_id=1, source_target_pairs={{0,1},{1,0},{2,3},{3,2},{4,5},{5,4},{6,7},{7,6},{8,9},{9,8},{10,11... | collective-permute-start | bytes 196616 | tf_op jit(solution)/shard_map/ppermute | solution.py:346

commit v10 on v9

--- a/solution.py
+++ b/solution.py
@@ -102,9 +102,8 @@
     return max(n for n in range(1, 66) if steps % n == 0)
 
 
-def bit_order(shares):
-    bits = shares.bit_length() - 1
-    return [0, 3, 1, 2, *range(4, bits)]
+def bit_order(shares, core):
+    return [0, 3, *((2, 1) if core else (1, 2)), *range(4, shares.bit_length() - 1)]
 
 
 def local_kernel(
@@ -243,11 +242,14 @@
         )
     share = grad.shape[0] // shares
     me = place_ref[0]
-    order = bit_order(shares)
     parts = (keep_near, keep_far, send_near, send_far)
     quarter = shares // 4
     for spot in range(shares):
-        flip = sum(1 << bit for i, bit in enumerate(reversed(order)) if spot >> i & 1)
+        flips = [
+            sum(1 << bit for i, bit in enumerate(reversed(bit_order(shares, c))) if spot >> i & 1)
+            for c in ((0, 1) if spot < shares // 2 else (1, 0))
+        ]
+        flip = flips[0] + (me & 1) * (flips[1] - flips[0])
         block = grad[pl.ds(pl.multiple_of((me ^ flip) * share, 8), share), :]
         part = parts[spot // quarter]
         at = spot % quarter * share
@@ -328,12 +330,6 @@
     )(place, got, cot, weight, conv_two, table)
 
 
-def tree(terms):
-    while len(terms) > 1:
-        terms = [terms[i] + terms[i + 1] for i in range(0, len(terms), 2)]
-    return terms[0]
-
-
 def exchange(sizes, stage, message):
     far = {axis: 0 for axis in sizes}
     for axis, bit in stage:
@@ -344,6 +340,11 @@
         n = sizes[axis]
         pairs = [(a * n + i, b * n + (i ^ far[axis])) for a, b in pairs for i in range(n)]
     return lax.ppermute(message, axes if len(axes) > 1 else axes[0], pairs)
+
+
+def exchange_crossed(sizes, turn, message):
+    pairs = [(i, i ^ (1 << bit_order(sizes["dp"], i & 1)[2 + turn])) for i in range(sizes["dp"])]
+    return lax.ppermute(message, "dp", pairs)
 
 
 def message(rows, small):
@@ -381,25 +382,28 @@
 
 
 def sum_all(sizes, send_far, send_near, keep_far, keep_near, small):
-    order = [("dp", bit) for bit in bit_order(sizes["dp"])]
-    core, onward, pair, left = order[0], order[1], order[2:4], order[4:]
+    bits = [("dp", bit) for bit in bit_order(sizes["dp"], 0)]
+    core, onward, left = bits[0], bits[1], bits[4:]
+    far = keep_far + exchange(sizes, [core], send_far).astype(F32)
     small = small + exchange(sizes, [core], small)
-    far = keep_far + exchange(sizes, [core], send_far).astype(F32)
     near = keep_near + exchange(sizes, [core], send_near).astype(F32)
-    rows = far.shape[0] // 4
-    near, far = ([part[i * rows : (i + 1) * rows] for i in range(4)] for part in (near, far))
-    chosen = [[bit for i, bit in enumerate(pair) if code >> (1 - i) & 1] for code in range(4)]
-    fars, nears = [far[0]], [near[0]]
-    smalls = [contents(message(near[0], small))[1]]
-    for code in (1, 2, 3):
-        fars.append(exchange(sizes, chosen[code], far[code].astype(BF16)).astype(F32))
-    for code in (1, 2, 3):
-        got, more = contents(exchange(sizes, chosen[code], message(near[code], small)))
-        nears.append(got)
-        smalls.append(more)
-    away, base = tree(fars), tree(nears)
+
+    half = far.shape[0] // 2
+    far = far[:half] + exchange_crossed(sizes, 0, far[half:].astype(BF16)).astype(F32)
+    own = message(near[half:], small)
+    got, other = contents(exchange_crossed(sizes, 0, own))
+    near, small = near[:half] + got, contents(own)[1]
+    half = half // 2
+    away = far[:half] + exchange_crossed(sizes, 1, far[half:].astype(BF16)).astype(F32)
+    own = jnp.concatenate([message(near[half:], small), *split_two(other)], axis=0)
+    own = exchange_crossed(sizes, 1, own)
+    got, more = contents(own[:-2 * ROWS])
+    base = near[:half] + got
+    last = contents(own[-2 * ROWS :])[1]
+    even = (lax.axis_index("dp") & 1) == 0
+    small = (small + jnp.where(even, other, more)) + (jnp.where(even, more, other) + last)
     cut = (away.shape[0] + 2 * ROWS) // 2 // ROWS * ROWS
-    own = message(away[cut:], tree(smalls))
+    own = message(away[cut:], small)
     first = exchange(sizes, [onward], away[:cut].astype(BF16))
     second, more = contents(exchange(sizes, [onward], own))
     first = base[:cut] + first.astype(F32)

time: 49.8 us -> 52.9 us (1.062)
  starting transfers between devices: 23.3 us -> 17.4 us
  waiting for transfers between devices: 11.9 us -> 17.8 us
  local copies, waits for them, and re-layouts: 4.02 us -> 6.64 us
    ppermute x13 -> x7, starting transfers between devices: 16 us -> 6.42 us  [exchange(): return lax.ppermute(message, axes if len(axes) > 1 else axes[0], pairs)]
    ppermute x0 -> x4, waiting for transfers between devices: none -> 9.03 us  [exchange_crossed(): return lax.ppermute(message, 'dp', pairs)]
    ppermute x0 -> x4, starting transfers between devices: none -> 3.64 us  [exchange_crossed(): return lax.ppermute(message, 'dp', pairs)]
    unnamed x6 -> x13, local copies, waits for them, and re-layouts: 2.45 us -> 5.04 us
    ppermute x13 -> x7, waiting for transfers between devices: 9.76 us -> 7.44 us  [exchange(): return lax.ppermute(message, axes if len(axes) > 1 else axes[0], pairs)]
    all_to_all x1, waiting for transfers between devices: 2.15 us -> 1.35 us  [per_device(): got = lax.all_to_all(packed, 'dp', split_axis=0, concat_axis=0, tiled=True)]
  transfers between devices with their start and end apart: 14 -> 12, of which waited for: 9 -> 10; matrix products, arithmetic and copies ran while one was open for 4% -> 4% of each run, Pallas kernels for 1% -> 1%
where the time goes in v10:
time: 52.9 us; the launch traced here: 52.5 us
  waiting for transfers between devices  17.8 us (34%)
  starting transfers between devices  17.4 us (33%)
  Pallas kernels  9.3 us (18%)
  local copies, waits for them, and re-layouts  6.64 us (13%)
  between operations  0.83 us (2%)
    ppermute x4, waiting for transfers between devices, exchange_crossed(): return lax.ppermute(message, 'dp', pairs)  9.03 us
    ppermute x7, waiting for transfers between devices, exchange(): return lax.ppermute(message, axes if len(axes) > 1 else axes[0], pairs)  7.44 us
    all_to_all x1, starting transfers between devices, per_device(): got = lax.all_to_all(packed, 'dp', split_axis=0, concat_axis=0, tiled=True)  7.36 us
    pallas_call x1, Pallas kernels, local_pass(): pl.pallas_call(functools.partial(local_kernel, record, shares), out_shape...  6.8 us
    ppermute x7, starting transfers between devices, exchange(): return lax.ppermute(message, axes if len(axes) > 1 else axes[0], pairs)  6.42 us
    unnamed x13, local copies, waits for them, and re-layouts  5.04 us
    ppermute x4, starting transfers between devices, exchange_crossed(): return lax.ppermute(message, 'dp', pairs)  3.64 us
    concatenate x1, local copies, waits for them, and re-layouts, per_device(): table = jnp.concatenate([conv_one.astype(F32), jnp.stack(vectors)], axis=0)  1.52 us
  transfers between devices with their start and end apart: 12, of which 10 were waited for; matrix products, arithmetic and copies ran while one was open for 4% of the time, Pallas kernels for 1%

profile of v10, /device:TPU:0, one launch (start us, length us, event | category | flops | bytes accessed | tf_op | source)
XLA Modules:
  0.0 52.5 jit_solution(16171308157655576304)
XLA Ops:
  0.6 1.4 %shard_map.131 = f32[16,1,384]{2,1,0:T(1,128)} custom-call(s32[1,16]{1,0:T(1,128)} %packing.1, s32[16]{0:T(128)} %bins.1, bf16[16,330]{1,0:T(8,128)(2,1)} %wave_ref.1), custom_call_target="tpu_custom_call" | custom-call | tf_op jit(solution)/shard_map/pallas_call | solution.py:44
  2.0 7.4 %all-to-all-start = ((f32[16,1,384]{2,1,0:T(1,128)}), f32[16,1,384]{2,1,0:T(1,128)S(1)}, u32[]{:S(2)}, u32[]{:S(2)}) async-start(f32[16,1,384]{2,1,0:T(1,128)} %shard_map.131), calls=%async_computation | async-start | bytes 49152 | tf_op jit(solution)/shard_map/all_to_all | solution.py:450
  9.4 1.5 %concatenate.15.table_ref = f32[16,512]{1,0:T(8,128)S(1)} concatenate(bf16[10,512]{1,0:T(8,128)(2,1)} %param.16, f32[1,512]{1,0:T(1,128)} %bitcast.9, f32[1,512]{1,0:T(1,128)} %bitcast.10, f32[1,512]{1,0:T(1,128)} %bitcast.11, f32[1,512]{1,0:T(1,128)} %bitcast.12, f32[1,512]{1,0:T(1,128)} %bitcast.13, f32[1,512]{1,0:T(1,128)} %bitcast.14), dimensions={0} | concatenate | bytes 55296 | tf_op jit(solution)/shard_map/concatenate | solution.py:452
  10.9 1.4 %copy-done = bf16[1536,512]{1,0:T(8,128)(2,1)S(1)} copy-done((bf16[1536,512]{1,0:T(8,128)(2,1)S(1)}, bf16[1536,512]{1,0:T(8,128)(2,1)}, u32[]{:S(2)}) %copy-start) | copy-done | bytes 1572888
  12.3 1.0 %copy-done.2 = bf16[16,32,512]{2,1,0:T(8,128)(2,1)S(1)} copy-done((bf16[16,32,512]{2,1,0:T(8,128)(2,1)S(1)}, bf16[16,32,512]{2,1,0:T(8,128)(2,1)}, u32[]{:S(2)}) %copy-start.2) | copy-done | bytes 524312
  13.8 0.8 %copy-done.3 = bf16[512,512]{1,0:T(8,128)(2,1)} copy-done((bf16[512,512]{1,0:T(8,128)(2,1)}, bf16[512,512]{1,0:T(8,128)(2,1)S(1)}, u32[]{:S(2)}) %copy-start.3) | copy-done | bytes 524312
  14.6 1.3 %all-to-all-done.got_ref = f32[16,1,384]{2,1,0:T(1,128)S(1)} async-done(((f32[16,1,384]{2,1,0:T(1,128)}), f32[16,1,384]{2,1,0:T(1,128)S(1)}, u32[]{:S(2)}, u32[]{:S(2)}) %all-to-all-start) | async-done | bytes 24608 | tf_op jit(solution)/shard_map/all_to_all | solution.py:450
  15.9 1.0 %copy-done.4 = bf16[512,512]{1,0:T(8,128)(2,1)S(1)} copy-done((bf16[512,512]{1,0:T(8,128)(2,1)S(1)}, bf16[512,512]{1,0:T(8,128)(2,1)}, u32[]{:S(2)}) %copy-start.4) | copy-done | bytes 524312
  17.0 6.8 %shard_map.133 = (bf16[384,512]{1,0:T(8,128)(2,1)}, bf16[384,512]{1,0:T(8,128)(2,1)S(1)}, f32[384,512]{1,0:T(8,128)S(1)}, f32[384,512]{1,0:T(8,128)S(1)}, f32[16,512]{1,0:T(8,128)S(1)}) custom-call(s32[1]{0:T(128)} %bitcast.place_ref, f32[16,1,384]{2,1,0:T(1,128)S(1)} %all-to-all-done.got_ref, bf16[512,512]{1,0:T(8,128)(2,1)S(1)} %copy-done.4, ...), custom_call_target="tpu_custom_call" | custom-call | flops 2415919104 | bytes 4259840 | tf_op jit(solution)/shard_map/pallas_call | solution.py:300
  25.0 0.9 %collective-permute-done.1 = f32[16,512]{1,0:T(8,128)S(1)} collective-permute-done((f32[16,512]{1,0:T(8,128)S(1)}, f32[16,512]{1,0:T(8,128)S(1)}, u32[]{:S(2)}, u32[]{:S(2)}) %collective-permute-start.1) | collective-permute-done | bytes 32800 | tf_op jit(solution)/shard_map/ppermute | solution.py:342
  26.6 0.8 %collective-permute-start.5 = (bf16[192,512]{1,0:T(8,128)(2,1)S(1)}, bf16[192,512]{1,0:T(8,128)(2,1)S(1)}, u32[]{:S(2)}, u32[]{:S(2)}) collective-permute-start(bf16[192,512]{1,0:T(8,128)(2,1)S(1)} %slice.169), channel_id=1, source_target_pairs={{0,4},{2,10},{4,0},{6,14},{8,12},{10,2},{12,8},{14,6},{16,20},{18,... | collective-permute-start | bytes 589832 | tf_op jit(solution)/shard_map/ppermute | solution.py:347
  27.6 1.4 %collective-permute-start.2 = (bf16[224,512]{1,0:T(8,128)(2,1)S(1)}, bf16[224,512]{1,0:T(8,128)(2,1)S(1)}, u32[]{:S(2)}, u32[]{:S(2)}) collective-permute-start(bf16[224,512]{1,0:T(8,128)(2,1)S(1)} %pad_maximum_fusion), channel_id=1, source_target_pairs={{0,4},{2,10},{4,0},{6,14},{8,12},{10,2},{12,8},{14,6},{16,20},{18,... | collective-permute-start | bytes 688136 | tf_op jit(solution)/shard_map/ppermute | solution.py:347
  29.0 3.4 %collective-permute-done.5 = bf16[192,512]{1,0:T(8,128)(2,1)S(1)} collective-permute-done((bf16[192,512]{1,0:T(8,128)(2,1)S(1)}, bf16[192,512]{1,0:T(8,128)(2,1)S(1)}, u32[]{:S(2)}, u32[]{:S(2)}) %collective-permute-start.5) | collective-permute-done | bytes 196640 | tf_op jit(solution)/shard_map/ppermute | solution.py:347
  32.5 0.7 %collective-permute-start.6 = (bf16[96,512]{1,0:T(8,128)(2,1)S(1)}, bf16[96,512]{1,0:T(8,128)(2,1)S(1)}, u32[]{:S(2)}, u32[]{:S(2)}) collective-permute-start(bf16[96,512]{1,0:T(8,128)(2,1)S(1)} %slice.171), channel_id=1, source_target_pairs={{0,8},{2,6},{4,12},{6,2},{8,0},{10,14},{12,4},{14,10},{16,24},{18,... | collective-permute-start | bytes 294920 | tf_op jit(solution)/shard_map/ppermute | solution.py:347
  33.2 2.0 %collective-permute-done.2 = bf16[224,512]{1,0:T(8,128)(2,1)S(1)} collective-permute-done((bf16[224,512]{1,0:T(8,128)(2,1)S(1)}, bf16[224,512]{1,0:T(8,128)(2,1)S(1)}, u32[]{:S(2)}, u32[]{:S(2)}) %collective-permute-start.2) | collective-permute-done | bytes 229408 | tf_op jit(solution)/shard_map/ppermute | solution.py:347
  36.1 1.0 %collective-permute-done.6 = bf16[96,512]{1,0:T(8,128)(2,1)S(1)} collective-permute-done((bf16[96,512]{1,0:T(8,128)(2,1)S(1)}, bf16[96,512]{1,0:T(8,128)(2,1)S(1)}, u32[]{:S(2)}, u32[]{:S(2)}) %collective-permute-start.6) | collective-permute-done | bytes 98336 | tf_op jit(solution)/shard_map/ppermute | solution.py:347
  37.2 1.7 %collective-permute-start.7 = (bf16[64,512]{1,0:T(8,128)(2,1)S(1)}, bf16[64,512]{1,0:T(8,128)(2,1)S(1)}, u32[]{:S(2)}, u32[]{:S(2)}) collective-permute-start(bf16[64,512]{1,0:T(8,128)(2,1)S(1)} %slice.118), channel_id=1, source_target_pairs={{0,16},{2,18},{4,20},{6,22},{8,24},{10,26},{12,28},{14,30},{16,0},... | collective-permute-start | bytes 196616 | tf_op jit(solution)/shard_map/ppermute | solution.py:342
  38.9 2.6 %collective-permute-done.3 = bf16[160,512]{1,0:T(8,128)(2,1)S(1)} collective-permute-done((bf16[160,512]{1,0:T(8,128)(2,1)S(1)}, bf16[160,512]{1,0:T(8,128)(2,1)S(1)}, u32[]{:S(2)}, u32[]{:S(2)}) %collective-permute-start.3) | collective-permute-done | bytes 163872 | tf_op jit(solution)/shard_map/ppermute | solution.py:347
  41.5 1.1 %collective-permute-start.8 = (bf16[64,512]{1,0:T(8,128)(2,1)S(1)}, bf16[64,512]{1,0:T(8,128)(2,1)S(1)}, u32[]{:S(2)}, u32[]{:S(2)}) collective-permute-start(bf16[64,512]{1,0:T(8,128)(2,1)S(1)} %pad_maximum_fusion.1), channel_id=1, source_target_pairs={{0,16},{2,18},{4,20},{6,22},{8,24},{10,26},{12,28},{14,30},{16,0},... | collective-permute-start | bytes 196616 | tf_op jit(solution)/shard_map/ppermute | solution.py:342
  42.6 1.7 %collective-permute-done.7 = bf16[64,512]{1,0:T(8,128)(2,1)S(1)} collective-permute-done((bf16[64,512]{1,0:T(8,128)(2,1)S(1)}, bf16[64,512]{1,0:T(8,128)(2,1)S(1)}, u32[]{:S(2)}, u32[]{:S(2)}) %collective-permute-start.7) | collective-permute-done | bytes 65568 | tf_op jit(solution)/shard_map/ppermute | solution.py:342
  44.3 1.6 %collective-permute-start.9 = (bf16[64,512]{1,0:T(8,128)(2,1)S(1)}, bf16[64,512]{1,0:T(8,128)(2,1)S(1)}, u32[]{:S(2)}, u32[]{:S(2)}) collective-permute-start(bf16[64,512]{1,0:T(8,128)(2,1)S(1)} %fusion.1.own_first), channel_id=1, source_target_pairs={{0,1},{1,0},{2,3},{3,2},{4,5},{5,4},{6,7},{7,6},{8,9},{9,8},{10,11... | collective-permute-start | bytes 196616 | tf_op jit(solution)/shard_map/ppermute | solution.py:342
  45.8 1.6 %collective-permute-done.8 = bf16[64,512]{1,0:T(8,128)(2,1)S(1)} collective-permute-done((bf16[64,512]{1,0:T(8,128)(2,1)S(1)}, bf16[64,512]{1,0:T(8,128)(2,1)S(1)}, u32[]{:S(2)}, u32[]{:S(2)}) %collective-permute-start.8) | collective-permute-done | bytes 65568 | tf_op jit(solution)/shard_map/ppermute | solution.py:342
  47.5 1.6 %collective-permute-start.10 = (bf16[64,512]{1,0:T(8,128)(2,1)S(1)}, bf16[64,512]{1,0:T(8,128)(2,1)S(1)}, u32[]{:S(2)}, u32[]{:S(2)}) collective-permute-start(bf16[64,512]{1,0:T(8,128)(2,1)S(1)} %pad_maximum_fusion.2.own_second), channel_id=1, source_target_pairs={{0,1},{1,0},{2,3},{3,2},{4,5},{5,4},{6,7},{7,6},{8,9},{9,8},{10,11... | collective-permute-start | bytes 196616 | tf_op jit(solution)/shard_map/ppermute | solution.py:342
  49.1 2.7 %collective-permute-done.10.got_second = bf16[64,512]{1,0:T(8,128)(2,1)S(1)} collective-permute-done((bf16[64,512]{1,0:T(8,128)(2,1)S(1)}, bf16[64,512]{1,0:T(8,128)(2,1)S(1)}, u32[]{:S(2)}, u32[]{:S(2)}) %collective-permute-start.10) | collective-permute-done | bytes 65568 | tf_op jit(solution)/shard_map/ppermute | solution.py:342
  (41 shorter events, 4.3 us)
Async XLA Ops:
  2.0 13.9 %all-to-all-start = ((f32[16,1,384]{2,1,0:T(1,128)}), f32[16,1,384]{2,1,0:T(1,128)S(1)}, u32[]{:S(2)}, u32[]{:S(2)}) async-start(f32[16,1,384]{2,1,0:T(1,128)} %shard_map.131), calls=%async_computation | async-start | bytes 49152 | tf_op jit(solution)/shard_map/all_to_all | solution.py:450
  10.9 1.4 %copy-start = (bf16[1536,512]{1,0:T(8,128)(2,1)S(1)}, bf16[1536,512]{1,0:T(8,128)(2,1)}, u32[]{:S(2)}) copy-start(bf16[1536,512]{1,0:T(8,128)(2,1)} %conv_two_ref.3) | copy-start | bytes 4718596
  12.3 1.0 %copy-start.2 = (bf16[16,32,512]{2,1,0:T(8,128)(2,1)S(1)}, bf16[16,32,512]{2,1,0:T(8,128)(2,1)}, u32[]{:S(2)}) copy-start(bf16[16,32,512]{2,1,0:T(8,128)(2,1)} %param.15) | copy-start | bytes 1572868
  13.3 2.6 %copy-start.1 = (bf16[1536,512]{1,0:T(8,128)(2,1)S(1)}, bf16[1536,512]{1,0:T(8,128)(2,1)}, u32[]{:S(2)}) copy-start(bf16[1536,512]{1,0:T(8,128)(2,1)} %conv_two_ref.3) | copy-start | bytes 4718596
  13.8 0.8 %copy-start.3 = (bf16[512,512]{1,0:T(8,128)(2,1)}, bf16[512,512]{1,0:T(8,128)(2,1)S(1)}, u32[]{:S(2)}) copy-start(bf16[512,512]{1,0:T(8,128)(2,1)S(1)} %get-tuple-element.9.cot_ref) | copy-start | bytes 1572868
  15.9 1.0 %copy-start.4 = (bf16[512,512]{1,0:T(8,128)(2,1)S(1)}, bf16[512,512]{1,0:T(8,128)(2,1)}, u32[]{:S(2)}) copy-start(bf16[512,512]{1,0:T(8,128)(2,1)} %copy-done.3) | copy-start | bytes 1572868
  23.8 0.7 %copy-start.5 = (bf16[384,512]{1,0:T(8,128)(2,1)}, bf16[384,512]{1,0:T(8,128)(2,1)S(1)}, u32[]{:S(2)}) copy-start(bf16[384,512]{1,0:T(8,128)(2,1)S(1)} %get-tuple-element.12) | copy-start | bytes 1179652
  24.5 2.0 %collective-permute-start.4 = (bf16[384,512]{1,0:T(8,128)(2,1)}, bf16[384,512]{1,0:T(8,128)(2,1)S(1)}, u32[]{:S(2)}, u32[]{:S(2)}) collective-permute-start(bf16[384,512]{1,0:T(8,128)(2,1)} %get-tuple-element.15), channel_id=1, source_target_pairs={{0,2},{2,0},{4,6},{6,4},{8,10},{10,8},{12,14},{14,12},{16,18},{18,... | collective-permute-start | bytes 1179656 | tf_op jit(solution)/shard_map/ppermute | solution.py:342
  24.5 1.4 %collective-permute-start.1 = (f32[16,512]{1,0:T(8,128)S(1)}, f32[16,512]{1,0:T(8,128)S(1)}, u32[]{:S(2)}, u32[]{:S(2)}) collective-permute-start(f32[16,512]{1,0:T(8,128)S(1)} %get-tuple-element.13), channel_id=1, source_target_pairs={{0,2},{2,0},{4,6},{6,4},{8,10},{10,8},{12,14},{14,12},{16,18},{18,... | collective-permute-start | bytes 98312 | tf_op jit(solution)/shard_map/ppermute | solution.py:342
  25.0 2.4 %collective-permute-start = (bf16[384,512]{1,0:T(8,128)(2,1)}, bf16[384,512]{1,0:T(8,128)(2,1)S(1)}, u32[]{:S(2)}, u32[]{:S(2)}) collective-permute-start(bf16[384,512]{1,0:T(8,128)(2,1)} %copy-done.5), channel_id=1, source_target_pairs={{0,2},{2,0},{4,6},{6,4},{8,10},{10,8},{12,14},{14,12},{16,18},{18,... | collective-permute-start | bytes 1179656 | tf_op jit(solution)/shard_map/ppermute | solution.py:342
  26.6 5.7 %collective-permute-start.5 = (bf16[192,512]{1,0:T(8,128)(2,1)S(1)}, bf16[192,512]{1,0:T(8,128)(2,1)S(1)}, u32[]{:S(2)}, u32[]{:S(2)}) collective-permute-start(bf16[192,512]{1,0:T(8,128)(2,1)S(1)} %slice.169), channel_id=1, source_target_pairs={{0,4},{2,10},{4,0},{6,14},{8,12},{10,2},{12,8},{14,6},{16,20},{18,... | collective-permute-start | bytes 589832 | tf_op jit(solution)/shard_map/ppermute | solution.py:347
  27.6 7.6 %collective-permute-start.2 = (bf16[224,512]{1,0:T(8,128)(2,1)S(1)}, bf16[224,512]{1,0:T(8,128)(2,1)S(1)}, u32[]{:S(2)}, u32[]{:S(2)}) collective-permute-start(bf16[224,512]{1,0:T(8,128)(2,1)S(1)} %pad_maximum_fusion), channel_id=1, source_target_pairs={{0,4},{2,10},{4,0},{6,14},{8,12},{10,2},{12,8},{14,6},{16,20},{18,... | collective-permute-start | bytes 688136 | tf_op jit(solution)/shard_map/ppermute | solution.py:347
  32.5 4.7 %collective-permute-start.6 = (bf16[96,512]{1,0:T(8,128)(2,1)S(1)}, bf16[96,512]{1,0:T(8,128)(2,1)S(1)}, u32[]{:S(2)}, u32[]{:S(2)}) collective-permute-start(bf16[96,512]{1,0:T(8,128)(2,1)S(1)} %slice.171), channel_id=1, source_target_pairs={{0,8},{2,6},{4,12},{6,2},{8,0},{10,14},{12,4},{14,10},{16,24},{18,... | collective-permute-start | bytes 294920 | tf_op jit(solution)/shard_map/ppermute | solution.py:347
  35.4 6.1 %collective-permute-start.3 = (bf16[160,512]{1,0:T(8,128)(2,1)S(1)}, bf16[160,512]{1,0:T(8,128)(2,1)S(1)}, u32[]{:S(2)}, u32[]{:S(2)}) collective-permute-start(bf16[160,512]{1,0:T(8,128)(2,1)S(1)} %fusion.12), channel_id=1, source_target_pairs={{0,8},{2,6},{4,12},{6,2},{8,0},{10,14},{12,4},{14,10},{16,24},{18,... | collective-permute-start | bytes 491528 | tf_op jit(solution)/shard_map/ppermute | solution.py:347
  37.2 7.1 %collective-permute-start.7 = (bf16[64,512]{1,0:T(8,128)(2,1)S(1)}, bf16[64,512]{1,0:T(8,128)(2,1)S(1)}, u32[]{:S(2)}, u32[]{:S(2)}) collective-permute-start(bf16[64,512]{1,0:T(8,128)(2,1)S(1)} %slice.118), channel_id=1, source_target_pairs={{0,16},{2,18},{4,20},{6,22},{8,24},{10,26},{12,28},{14,30},{16,0},... | collective-permute-start | bytes 196616 | tf_op jit(solution)/shard_map/ppermute | solution.py:342
  41.5 5.9 %collective-permute-start.8 = (bf16[64,512]{1,0:T(8,128)(2,1)S(1)}, bf16[64,512]{1,0:T(8,128)(2,1)S(1)}, u32[]{:S(2)}, u32[]{:S(2)}) collective-permute-start(bf16[64,512]{1,0:T(8,128)(2,1)S(1)} %pad_maximum_fusion.1), channel_id=1, source_target_pairs={{0,16},{2,18},{4,20},{6,22},{8,24},{10,26},{12,28},{14,30},{16,0},... | collective-permute-start | bytes 196616 | tf_op jit(solution)/shard_map/ppermute | solution.py:342
  44.3 4.8 %collective-permute-start.9 = (bf16[64,512]{1,0:T(8,128)(2,1)S(1)}, bf16[64,512]{1,0:T(8,128)(2,1)S(1)}, u32[]{:S(2)}, u32[]{:S(2)}) collective-permute-start(bf16[64,512]{1,0:T(8,128)(2,1)S(1)} %fusion.1.own_first), channel_id=1, source_target_pairs={{0,1},{1,0},{2,3},{3,2},{4,5},{5,4},{6,7},{7,6},{8,9},{9,8},{10,11... | collective-permute-start | bytes 196616 | tf_op jit(solution)/shard_map/ppermute | solution.py:342
  47.5 4.3 %collective-permute-start.10 = (bf16[64,512]{1,0:T(8,128)(2,1)S(1)}, bf16[64,512]{1,0:T(8,128)(2,1)S(1)}, u32[]{:S(2)}, u32[]{:S(2)}) collective-permute-start(bf16[64,512]{1,0:T(8,128)(2,1)S(1)} %pad_maximum_fusion.2.own_second), channel_id=1, source_target_pairs={{0,1},{1,0},{2,3},{3,2},{4,5},{5,4},{6,7},{7,6},{8,9},{9,8},{10,11... | collective-permute-start | bytes 196616 | tf_op jit(solution)/shard_map/ppermute | solution.py:342

commit v11 on v8

--- a/solution.py
+++ b/solution.py
@@ -19,11 +19,6 @@
 def gelu_parts(act):
     cdf = 0.5 + 0.5 * lax.erf(act * 0.7071067811865476)
     return cdf, 0.3989422804014327 * jnp.exp(-0.5 * (act * act))
-
-
-def split_two(x):
-    hi = x.astype(BF16)
-    return hi, (x - hi.astype(F32)).astype(BF16)
 
 
 def pack_kernel(packing, bins, wave_ref, out_ref, wide):
@@ -346,14 +341,17 @@
     return lax.ppermute(message, axes if len(axes) > 1 else axes[0], pairs)
 
 
+def rounded(x):
+    return lax.reduce_precision(x, exponent_bits=8, mantissa_bits=7)
+
+
 def message(rows, small):
-    return jnp.concatenate([rows.astype(BF16), *split_two(small)], axis=0)
+    return jnp.concatenate([rows.astype(BF16), small.astype(BF16)], axis=0)
 
 
 def contents(got):
-    rows = got.shape[0] - 2 * ROWS
-    hi, lo = got[rows : rows + ROWS], got[rows + ROWS :]
-    return got[:rows].astype(F32), hi.astype(F32) + lo.astype(F32)
+    rows = got.shape[0] - ROWS
+    return got[:rows].astype(F32), got[rows:].astype(F32)
 
 
 def near_kernel(own_ref, *refs):
@@ -385,7 +383,7 @@
 
 
 def finish(*parts):
-    rows, width = parts[0].shape[0] + parts[1].shape[0] - 2 * ROWS, parts[0].shape[1]
+    rows, width = parts[0].shape[0] + parts[1].shape[0] - ROWS, parts[0].shape[1]
     vmem = pl.BlockSpec(memory_space=pltpu.VMEM)
     return pl.pallas_call(
         finish_kernel,
@@ -402,19 +400,19 @@
 def sum_all(sizes, send_far, send_near, keep_far, keep_near, small):
     order = [("dp", bit) for bit in bit_order(sizes["dp"])]
     core, onward, pair, left = order[0], order[1], order[2:4], order[4:]
-    small = small + exchange(sizes, [core], small)
+    small = rounded(small + exchange(sizes, [core], small))
     far = keep_far + exchange(sizes, [core], send_far).astype(F32)
     near = keep_near + exchange(sizes, [core], send_near).astype(F32)
     rows = far.shape[0] // 4
     near, far = ([part[i * rows : (i + 1) * rows] for i in range(4)] for part in (near, far))
-    small = contents(message(far[0], small))[1], small
-    fars, smalls, nears = [far[0]], [small[0]], []
+    fars, smalls, nears = [far[0]], [small], []
     chosen = [[bit for i, bit in enumerate(pair) if code >> (1 - i) & 1] for code in range(4)]
     for code in (1, 2, 3):
-        got, more = contents(exchange(sizes, chosen[code], message(far[code], small[1])))
+        got, more = contents(exchange(sizes, chosen[code], message(far[code], small)))
         fars.append(got)
         smalls.append(more)
-    own = message(tree(fars), tree(smalls))
+    small = rounded(tree(smalls))
+    own = message(tree(fars), small)
     for code in (1, 2, 3):
         nears.append(exchange(sizes, chosen[code], near[code].astype(BF16)))
     cut = own.shape[0] // 2 // ROWS * ROWS
@@ -422,24 +420,25 @@
     base = near_sum(near[0], *nears)
     first = base[:cut] + first.astype(F32)
     second, more = contents(second)
-    second, small = base[cut:] + second, contents(own[cut:])[1] + more
+    second, small = base[cut:] + second, small + more
     for bit in left:
         total = jnp.concatenate([first, second], axis=0)
         half = total.shape[0] // 2
+        small = rounded(small)
         own = message(total[half:], small)
         got, more = contents(exchange(sizes, [bit], own))
-        total, small = total[:half] + got, contents(own)[1] + more
+        total, small = total[:half] + got, small + more
         cut = own.shape[0] // 2 // ROWS * ROWS
         first, second = total[:cut], total[cut:]
     bits = sizes["blk"].bit_length() - 1
     for bit in range(bits):
+        first, second, small = rounded(first), rounded(second), rounded(small)
         own = first.astype(BF16), message(second, small)
         got = [exchange(sizes, [("blk", bit)], part) for part in own]
         if bit == bits - 1:
             return finish(*own, *got)
-        first = own[0].astype(F32) + got[0].astype(F32)
-        (second, small), (more, extra) = contents(own[1]), contents(got[1])
-        second, small = second + more, small + extra
+        more, extra = contents(got[1])
+        first, second, small = first + got[0].astype(F32), second + more, small + extra
     return jnp.concatenate([first, second], axis=0), small
 
 

time: 49.5 us -> 50 us (1.010)
  waiting for transfers between devices: 12.1 us -> 14 us
  starting transfers between devices: 22.8 us -> 21.4 us
    ppermute x13, waiting for transfers between devices: 9.95 us -> 11.9 us  [exchange(): return lax.ppermute(message, axes if len(axes) > 1 else axes[0], pairs)]
    ppermute x13, starting transfers between devices: 15.4 us -> 14 us  [exchange(): return lax.ppermute(message, axes if len(axes) > 1 else axes[0], pairs)]
  transfers between devices with their start and end apart: 14 -> 14, of which waited for: 7 -> 8; matrix products, arithmetic and copies ran while one was open for 4% -> 4% of each run, Pallas kernels for 1% -> 1%
where the time goes in v11:
time: 50 us; the launch traced here: 49.6 us
  starting transfers between devices  21.4 us (43%)
  waiting for transfers between devices  14 us (28%)
  Pallas kernels  8.89 us (18%)
  local copies, waits for them, and re-layouts  4.02 us (8%)
  between operations  0.78 us (2%)
    ppermute x13, starting transfers between devices, exchange(): return lax.ppermute(message, axes if len(axes) > 1 else axes[0], pairs)  14 us
    ppermute x13, waiting for transfers between devices, exchange(): return lax.ppermute(message, axes if len(axes) > 1 else axes[0], pairs)  11.9 us
    all_to_all x1, starting transfers between devices, per_device(): got = lax.all_to_all(packed, 'dp', split_axis=0, concat_axis=0, tiled=True)  7.36 us
    pallas_call x1, Pallas kernels, local_pass(): pl.pallas_call(functools.partial(local_kernel, record, shares), out_shape...  6.34 us
    unnamed x6, local copies, waits for them, and re-layouts  2.45 us
    all_to_all x1, waiting for transfers between devices, per_device(): got = lax.all_to_all(packed, 'dp', split_axis=0, concat_axis=0, tiled=True)  2.15 us
    concatenate x1, local copies, waits for them, and re-layouts, per_device(): table = jnp.concatenate([conv_one.astype(F32), jnp.stack(vectors)], axis=0)  1.52 us
    pallas_call x1, Pallas kernels, pack(): pl.pallas_call(pack_kernel, out_shape=jax.ShapeDtypeStruct((count, 1, wid...  1.37 us
  transfers between devices with their start and end apart: 14, of which 8 were waited for; matrix products, arithmetic and copies ran while one was open for 4% of the time, Pallas kernels for 1%

profile of v11, /device:TPU:0, one launch (start us, length us, event | category | flops | bytes accessed | tf_op | source)
XLA Modules:
  0.0 49.6 jit_solution(12287720010751578093)
XLA Ops:
  0.6 1.4 %shard_map.131 = f32[16,1,384]{2,1,0:T(1,128)} custom-call(s32[1,16]{1,0:T(1,128)} %packing.1, s32[16]{0:T(128)} %bins.1, bf16[16,330]{1,0:T(8,128)(2,1)} %wave_ref.1), custom_call_target="tpu_custom_call" | custom-call | tf_op jit(solution)/shard_map/pallas_call | solution.py:39
  2.0 7.4 %all-to-all-start = ((f32[16,1,384]{2,1,0:T(1,128)}), f32[16,1,384]{2,1,0:T(1,128)S(1)}, u32[]{:S(2)}, u32[]{:S(2)}) async-start(f32[16,1,384]{2,1,0:T(1,128)} %shard_map.131), calls=%async_computation | async-start | bytes 49152 | tf_op jit(solution)/shard_map/all_to_all | solution.py:464
  9.4 1.5 %concatenate.18.table_ref = f32[16,512]{1,0:T(8,128)S(1)} concatenate(bf16[10,512]{1,0:T(8,128)(2,1)} %param.16, f32[1,512]{1,0:T(1,128)} %bitcast.9, f32[1,512]{1,0:T(1,128)} %bitcast.10, f32[1,512]{1,0:T(1,128)} %bitcast.11, f32[1,512]{1,0:T(1,128)} %bitcast.12, f32[1,512]{1,0:T(1,128)} %bitcast.13, f32[1,512]{1,0:T(1,128)} %bitcast.14), dimensions={0} | concatenate | bytes 55296 | tf_op jit(solution)/shard_map/concatenate | solution.py:466
  10.9 1.4 %copy-done = bf16[1536,512]{1,0:T(8,128)(2,1)S(1)} copy-done((bf16[1536,512]{1,0:T(8,128)(2,1)S(1)}, bf16[1536,512]{1,0:T(8,128)(2,1)}, u32[]{:S(2)}) %copy-start) | copy-done | bytes 1572888
  12.3 1.0 %copy-done.2 = bf16[16,32,512]{2,1,0:T(8,128)(2,1)S(1)} copy-done((bf16[16,32,512]{2,1,0:T(8,128)(2,1)S(1)}, bf16[16,32,512]{2,1,0:T(8,128)(2,1)}, u32[]{:S(2)}) %copy-start.2) | copy-done | bytes 524312
  13.8 2.2 %all-to-all-done.got_ref = f32[16,1,384]{2,1,0:T(1,128)S(1)} async-done(((f32[16,1,384]{2,1,0:T(1,128)}), f32[16,1,384]{2,1,0:T(1,128)S(1)}, u32[]{:S(2)}, u32[]{:S(2)}) %all-to-all-start) | async-done | bytes 24608 | tf_op jit(solution)/shard_map/all_to_all | solution.py:464
  15.9 6.3 %shard_map.133 = (bf16[384,512]{1,0:T(8,128)(2,1)S(1)}, bf16[384,512]{1,0:T(8,128)(2,1)S(1)}, f32[384,512]{1,0:T(8,128)S(1)}, f32[384,512]{1,0:T(8,128)S(1)}, f32[16,512]{1,0:T(8,128)S(1)}) custom-call(s32[1]{0:T(128)} %bitcast.place_ref, f32[16,1,384]{2,1,0:T(1,128)S(1)} %all-to-all-done.got_ref, bf16[512,512]{1,0:T(8,128)(2,1)S(1)} %get-tuple-element.9.cot_ref, ...), custom_call_target="tpu_custom_call" | custom-call | flops 2415919104 | bytes 4259840 | tf_op jit(solution)/shard_map/pallas_call | solution.py:293
  22.4 0.5 %collective-permute-start.5 = (f32[16,512]{1,0:T(8,128)S(1)}, f32[16,512]{1,0:T(8,128)S(1)}, u32[]{:S(2)}, u32[]{:S(2)}) collective-permute-start(f32[16,512]{1,0:T(8,128)S(1)} %get-tuple-element.15), channel_id=1, source_target_pairs={{0,2},{2,0},{4,6},{6,4},{8,10},{10,8},{12,14},{14,12},{16,18},{18,... | collective-permute-start | bytes 98312 | tf_op jit(solution)/shard_map/ppermute | solution.py:341
  22.9 1.2 %collective-permute-done.5 = f32[16,512]{1,0:T(8,128)S(1)} collective-permute-done((f32[16,512]{1,0:T(8,128)S(1)}, f32[16,512]{1,0:T(8,128)S(1)}, u32[]{:S(2)}, u32[]{:S(2)}) %collective-permute-start.5) | collective-permute-done | bytes 32800 | tf_op jit(solution)/shard_map/ppermute | solution.py:341
  24.3 1.7 %collective-permute-start.8 = (bf16[112,512]{1,0:T(8,128)(2,1)S(1)}, bf16[112,512]{1,0:T(8,128)(2,1)S(1)}, u32[]{:S(2)}, u32[]{:S(2)}) collective-permute-start(bf16[112,512]{1,0:T(8,128)(2,1)S(1)} %get-tuple-element.32), channel_id=1, source_target_pairs={{0,12},{2,14},{4,8},{6,10},{8,4},{10,6},{12,0},{14,2},{16,28},{18,... | collective-permute-start | bytes 344072 | tf_op jit(solution)/shard_map/ppermute | solution.py:341
  26.0 0.6 %collective-permute-start.7 = (bf16[112,512]{1,0:T(8,128)(2,1)S(1)}, bf16[112,512]{1,0:T(8,128)(2,1)S(1)}, u32[]{:S(2)}, u32[]{:S(2)}) collective-permute-start(bf16[112,512]{1,0:T(8,128)(2,1)S(1)} %get-tuple-element.31), channel_id=1, source_target_pairs={{0,4},{2,6},{4,0},{6,2},{8,12},{10,14},{12,8},{14,10},{16,20},{18,... | collective-permute-start | bytes 344072 | tf_op jit(solution)/shard_map/ppermute | solution.py:341
  26.6 1.3 %collective-permute-start.6 = (bf16[112,512]{1,0:T(8,128)(2,1)S(1)}, bf16[112,512]{1,0:T(8,128)(2,1)S(1)}, u32[]{:S(2)}, u32[]{:S(2)}) collective-permute-start(bf16[112,512]{1,0:T(8,128)(2,1)S(1)} %get-tuple-element.30), channel_id=1, source_target_pairs={{0,8},{2,10},{4,12},{6,14},{8,0},{10,2},{12,4},{14,6},{16,24},{18,... | collective-permute-start | bytes 344072 | tf_op jit(solution)/shard_map/ppermute | solution.py:341
  28.1 0.8 %collective-permute-start.1 = (bf16[96,512]{1,0:T(8,128)(2,1)S(1)}, bf16[96,512]{1,0:T(8,128)(2,1)S(1)}, u32[]{:S(2)}, u32[]{:S(2)}) collective-permute-start(bf16[96,512]{1,0:T(8,128)(2,1)S(1)} %get-tuple-element.27), channel_id=1, source_target_pairs={{0,8},{2,10},{4,12},{6,14},{8,0},{10,2},{12,4},{14,6},{16,24},{18,... | collective-permute-start | bytes 294920 | tf_op jit(solution)/shard_map/ppermute | solution.py:341
  28.9 1.5 %collective-permute-start.2 = (bf16[96,512]{1,0:T(8,128)(2,1)S(1)}, bf16[96,512]{1,0:T(8,128)(2,1)S(1)}, u32[]{:S(2)}, u32[]{:S(2)}) collective-permute-start(bf16[96,512]{1,0:T(8,128)(2,1)S(1)} %get-tuple-element.26), channel_id=1, source_target_pairs={{0,4},{2,6},{4,0},{6,2},{8,12},{10,14},{12,8},{14,10},{16,20},{18,... | collective-permute-start | bytes 294920 | tf_op jit(solution)/shard_map/ppermute | solution.py:341
  30.3 1.0 %collective-permute-done.8 = bf16[112,512]{1,0:T(8,128)(2,1)S(1)} collective-permute-done((bf16[112,512]{1,0:T(8,128)(2,1)S(1)}, bf16[112,512]{1,0:T(8,128)(2,1)S(1)}, u32[]{:S(2)}, u32[]{:S(2)}) %collective-permute-start.8) | collective-permute-done | bytes 114720 | tf_op jit(solution)/shard_map/ppermute | solution.py:341
  31.3 1.6 %collective-permute-start.3 = (bf16[96,512]{1,0:T(8,128)(2,1)S(1)}, bf16[96,512]{1,0:T(8,128)(2,1)S(1)}, u32[]{:S(2)}, u32[]{:S(2)}) collective-permute-start(bf16[96,512]{1,0:T(8,128)(2,1)S(1)} %get-tuple-element.25), channel_id=1, source_target_pairs={{0,12},{2,14},{4,8},{6,10},{8,4},{10,6},{12,0},{14,2},{16,28},{18,... | collective-permute-start | bytes 294920 | tf_op jit(solution)/shard_map/ppermute | solution.py:341
  33.1 2.4 %collective-permute-start.10 = (bf16[64,512]{1,0:T(8,128)(2,1)S(1)}, bf16[64,512]{1,0:T(8,128)(2,1)S(1)}, u32[]{:S(2)}, u32[]{:S(2)}) collective-permute-start(bf16[64,512]{1,0:T(8,128)(2,1)S(1)} %pad_maximum_fusion.3), channel_id=1, source_target_pairs={{0,16},{2,18},{4,20},{6,22},{8,24},{10,26},{12,28},{14,30},{16,0},... | collective-permute-start | bytes 196616 | tf_op jit(solution)/shard_map/ppermute | solution.py:341
  35.9 2.0 %collective-permute-done.3.refs_2_ = bf16[96,512]{1,0:T(8,128)(2,1)S(1)} collective-permute-done((bf16[96,512]{1,0:T(8,128)(2,1)S(1)}, bf16[96,512]{1,0:T(8,128)(2,1)S(1)}, u32[]{:S(2)}, u32[]{:S(2)}) %collective-permute-start.3) | collective-permute-done | bytes 98336 | tf_op jit(solution)/shard_map/ppermute | solution.py:341
  37.9 1.5 %collective-permute-start.9 = (bf16[48,512]{1,0:T(8,128)(2,1)S(1)}, bf16[48,512]{1,0:T(8,128)(2,1)S(1)}, u32[]{:S(2)}, u32[]{:S(2)}) collective-permute-start(bf16[48,512]{1,0:T(8,128)(2,1)S(1)} %slice.98), channel_id=1, source_target_pairs={{0,16},{2,18},{4,20},{6,22},{8,24},{10,26},{12,28},{14,30},{16,0},... | collective-permute-start | bytes 147464 | tf_op jit(solution)/shard_map/ppermute | solution.py:341
  39.4 3.7 %collective-permute-done.9 = bf16[48,512]{1,0:T(8,128)(2,1)S(1)} collective-permute-done((bf16[48,512]{1,0:T(8,128)(2,1)S(1)}, bf16[48,512]{1,0:T(8,128)(2,1)S(1)}, u32[]{:S(2)}, u32[]{:S(2)}) %collective-permute-start.9) | collective-permute-done | bytes 49184 | tf_op jit(solution)/shard_map/ppermute | solution.py:341
  43.2 1.6 %collective-permute-start.12 = (bf16[64,512]{1,0:T(8,128)(2,1)S(1)}, bf16[64,512]{1,0:T(8,128)(2,1)S(1)}, u32[]{:S(2)}, u32[]{:S(2)}) collective-permute-start(bf16[64,512]{1,0:T(8,128)(2,1)S(1)} %pad_maximum_fusion.4.own_second), channel_id=1, source_target_pairs={{0,1},{1,0},{2,3},{3,2},{4,5},{5,4},{6,7},{7,6},{8,9},{9,8},{10,11... | collective-permute-start | bytes 196616 | tf_op jit(solution)/shard_map/ppermute | solution.py:341
  44.8 0.5 %collective-permute-start.11 = (bf16[48,512]{1,0:T(8,128)(2,1)S(1)}, bf16[48,512]{1,0:T(8,128)(2,1)S(1)}, u32[]{:S(2)}, u32[]{:S(2)}) collective-permute-start(bf16[48,512]{1,0:T(8,128)(2,1)S(1)} %get-tuple-element.29.own_first), channel_id=1, source_target_pairs={{0,1},{1,0},{2,3},{3,2},{4,5},{5,4},{6,7},{7,6},{8,9},{9,8},{10,11... | collective-permute-start | bytes 147464 | tf_op jit(solution)/shard_map/ppermute | solution.py:341
  45.3 3.6 %collective-permute-done.11.got_first = bf16[48,512]{1,0:T(8,128)(2,1)S(1)} collective-permute-done((bf16[48,512]{1,0:T(8,128)(2,1)S(1)}, bf16[48,512]{1,0:T(8,128)(2,1)S(1)}, u32[]{:S(2)}, u32[]{:S(2)}) %collective-permute-start.11) | collective-permute-done | bytes 49184 | tf_op jit(solution)/shard_map/ppermute | solution.py:341
  48.8 0.7 %shard_map.135 = (f32[96,512]{1,0:T(8,128)}, f32[16,512]{1,0:T(8,128)}) custom-call(bf16[48,512]{1,0:T(8,128)(2,1)S(1)} %get-tuple-element.29.own_first, bf16[64,512]{1,0:T(8,128)(2,1)S(1)} %pad_maximum_fusion.4.own_second, bf16[48,512]{1,0:T(8,128)(2,1)S(1)} %collective-permute-done.11.got_first, bf16[64,512]{1,0:T(8,128)(2,1)S(1)} %collective-permute-done.12.got_second), custom_call_target="tpu_custom_call" | custom-call | tf_op jit(solution)/shard_map/pallas_call | solution.py:388
  (30 shorter events, 1.5 us)
Async XLA Ops:
  2.0 13.9 %all-to-all-start = ((f32[16,1,384]{2,1,0:T(1,128)}), f32[16,1,384]{2,1,0:T(1,128)S(1)}, u32[]{:S(2)}, u32[]{:S(2)}) async-start(f32[16,1,384]{2,1,0:T(1,128)} %shard_map.131), calls=%async_computation | async-start | bytes 49152 | tf_op jit(solution)/shard_map/all_to_all | solution.py:464
  10.9 1.4 %copy-start = (bf16[1536,512]{1,0:T(8,128)(2,1)S(1)}, bf16[1536,512]{1,0:T(8,128)(2,1)}, u32[]{:S(2)}) copy-start(bf16[1536,512]{1,0:T(8,128)(2,1)} %conv_two_ref.3) | copy-start | bytes 4718596
  12.3 1.0 %copy-start.2 = (bf16[16,32,512]{2,1,0:T(8,128)(2,1)S(1)}, bf16[16,32,512]{2,1,0:T(8,128)(2,1)}, u32[]{:S(2)}) copy-start(bf16[16,32,512]{2,1,0:T(8,128)(2,1)} %param.15) | copy-start | bytes 1572868
  13.3 2.6 %copy-start.1 = (bf16[1536,512]{1,0:T(8,128)(2,1)S(1)}, bf16[1536,512]{1,0:T(8,128)(2,1)}, u32[]{:S(2)}) copy-start(bf16[1536,512]{1,0:T(8,128)(2,1)} %conv_two_ref.3) | copy-start | bytes 4718596
  22.3 1.8 %collective-permute-start.4 = (bf16[384,512]{1,0:T(8,128)(2,1)S(1)}, bf16[384,512]{1,0:T(8,128)(2,1)S(1)}, u32[]{:S(2)}, u32[]{:S(2)}) collective-permute-start(bf16[384,512]{1,0:T(8,128)(2,1)S(1)} %get-tuple-element.14), channel_id=1, source_target_pairs={{0,2},{2,0},{4,6},{6,4},{8,10},{10,8},{12,14},{14,12},{16,18},{18,... | collective-permute-start | bytes 1179656 | tf_op jit(solution)/shard_map/ppermute | solution.py:341
  22.4 1.8 %collective-permute-start.5 = (f32[16,512]{1,0:T(8,128)S(1)}, f32[16,512]{1,0:T(8,128)S(1)}, u32[]{:S(2)}, u32[]{:S(2)}) collective-permute-start(f32[16,512]{1,0:T(8,128)S(1)} %get-tuple-element.15), channel_id=1, source_target_pairs={{0,2},{2,0},{4,6},{6,4},{8,10},{10,8},{12,14},{14,12},{16,18},{18,... | collective-permute-start | bytes 98312 | tf_op jit(solution)/shard_map/ppermute | solution.py:341
  22.9 5.0 %collective-permute-start = (bf16[384,512]{1,0:T(8,128)(2,1)S(1)}, bf16[384,512]{1,0:T(8,128)(2,1)S(1)}, u32[]{:S(2)}, u32[]{:S(2)}) collective-permute-start(bf16[384,512]{1,0:T(8,128)(2,1)S(1)} %get-tuple-element.12), channel_id=1, source_target_pairs={{0,2},{2,0},{4,6},{6,4},{8,10},{10,8},{12,14},{14,12},{16,18},{18,... | collective-permute-start | bytes 1179656 | tf_op jit(solution)/shard_map/ppermute | solution.py:341
  24.3 7.0 %collective-permute-start.8 = (bf16[112,512]{1,0:T(8,128)(2,1)S(1)}, bf16[112,512]{1,0:T(8,128)(2,1)S(1)}, u32[]{:S(2)}, u32[]{:S(2)}) collective-permute-start(bf16[112,512]{1,0:T(8,128)(2,1)S(1)} %get-tuple-element.32), channel_id=1, source_target_pairs={{0,12},{2,14},{4,8},{6,10},{8,4},{10,6},{12,0},{14,2},{16,28},{18,... | collective-permute-start | bytes 344072 | tf_op jit(solution)/shard_map/ppermute | solution.py:341
  26.0 7.0 %collective-permute-start.7 = (bf16[112,512]{1,0:T(8,128)(2,1)S(1)}, bf16[112,512]{1,0:T(8,128)(2,1)S(1)}, u32[]{:S(2)}, u32[]{:S(2)}) collective-permute-start(bf16[112,512]{1,0:T(8,128)(2,1)S(1)} %get-tuple-element.31), channel_id=1, source_target_pairs={{0,4},{2,6},{4,0},{6,2},{8,12},{10,14},{12,8},{14,10},{16,20},{18,... | collective-permute-start | bytes 344072 | tf_op jit(solution)/shard_map/ppermute | solution.py:341
  26.6 6.5 %collective-permute-start.6 = (bf16[112,512]{1,0:T(8,128)(2,1)S(1)}, bf16[112,512]{1,0:T(8,128)(2,1)S(1)}, u32[]{:S(2)}, u32[]{:S(2)}) collective-permute-start(bf16[112,512]{1,0:T(8,128)(2,1)S(1)} %get-tuple-element.30), channel_id=1, source_target_pairs={{0,8},{2,10},{4,12},{6,14},{8,0},{10,2},{12,4},{14,6},{16,24},{18,... | collective-permute-start | bytes 344072 | tf_op jit(solution)/shard_map/ppermute | solution.py:341
  28.1 7.5 %collective-permute-start.1 = (bf16[96,512]{1,0:T(8,128)(2,1)S(1)}, bf16[96,512]{1,0:T(8,128)(2,1)S(1)}, u32[]{:S(2)}, u32[]{:S(2)}) collective-permute-start(bf16[96,512]{1,0:T(8,128)(2,1)S(1)} %get-tuple-element.27), channel_id=1, source_target_pairs={{0,8},{2,10},{4,12},{6,14},{8,0},{10,2},{12,4},{14,6},{16,24},{18,... | collective-permute-start | bytes 294920 | tf_op jit(solution)/shard_map/ppermute | solution.py:341
  28.9 7.0 %collective-permute-start.2 = (bf16[96,512]{1,0:T(8,128)(2,1)S(1)}, bf16[96,512]{1,0:T(8,128)(2,1)S(1)}, u32[]{:S(2)}, u32[]{:S(2)}) collective-permute-start(bf16[96,512]{1,0:T(8,128)(2,1)S(1)} %get-tuple-element.26), channel_id=1, source_target_pairs={{0,4},{2,6},{4,0},{6,2},{8,12},{10,14},{12,8},{14,10},{16,20},{18,... | collective-permute-start | bytes 294920 | tf_op jit(solution)/shard_map/ppermute | solution.py:341
  31.3 6.6 %collective-permute-start.3 = (bf16[96,512]{1,0:T(8,128)(2,1)S(1)}, bf16[96,512]{1,0:T(8,128)(2,1)S(1)}, u32[]{:S(2)}, u32[]{:S(2)}) collective-permute-start(bf16[96,512]{1,0:T(8,128)(2,1)S(1)} %get-tuple-element.25), channel_id=1, source_target_pairs={{0,12},{2,14},{4,8},{6,10},{8,4},{10,6},{12,0},{14,2},{16,28},{18,... | collective-permute-start | bytes 294920 | tf_op jit(solution)/shard_map/ppermute | solution.py:341
  33.1 6.2 %collective-permute-start.10 = (bf16[64,512]{1,0:T(8,128)(2,1)S(1)}, bf16[64,512]{1,0:T(8,128)(2,1)S(1)}, u32[]{:S(2)}, u32[]{:S(2)}) collective-permute-start(bf16[64,512]{1,0:T(8,128)(2,1)S(1)} %pad_maximum_fusion.3), channel_id=1, source_target_pairs={{0,16},{2,18},{4,20},{6,22},{8,24},{10,26},{12,28},{14,30},{16,0},... | collective-permute-start | bytes 196616 | tf_op jit(solution)/shard_map/ppermute | solution.py:341
  37.9 5.2 %collective-permute-start.9 = (bf16[48,512]{1,0:T(8,128)(2,1)S(1)}, bf16[48,512]{1,0:T(8,128)(2,1)S(1)}, u32[]{:S(2)}, u32[]{:S(2)}) collective-permute-start(bf16[48,512]{1,0:T(8,128)(2,1)S(1)} %slice.98), channel_id=1, source_target_pairs={{0,16},{2,18},{4,20},{6,22},{8,24},{10,26},{12,28},{14,30},{16,0},... | collective-permute-start | bytes 147464 | tf_op jit(solution)/shard_map/ppermute | solution.py:341
  43.2 5.7 %collective-permute-start.12 = (bf16[64,512]{1,0:T(8,128)(2,1)S(1)}, bf16[64,512]{1,0:T(8,128)(2,1)S(1)}, u32[]{:S(2)}, u32[]{:S(2)}) collective-permute-start(bf16[64,512]{1,0:T(8,128)(2,1)S(1)} %pad_maximum_fusion.4.own_second), channel_id=1, source_target_pairs={{0,1},{1,0},{2,3},{3,2},{4,5},{5,4},{6,7},{7,6},{8,9},{9,8},{10,11... | collective-permute-start | bytes 196616 | tf_op jit(solution)/shard_map/ppermute | solution.py:341
  44.8 4.1 %collective-permute-start.11 = (bf16[48,512]{1,0:T(8,128)(2,1)S(1)}, bf16[48,512]{1,0:T(8,128)(2,1)S(1)}, u32[]{:S(2)}, u32[]{:S(2)}) collective-permute-start(bf16[48,512]{1,0:T(8,128)(2,1)S(1)} %get-tuple-element.29.own_first), channel_id=1, source_target_pairs={{0,1},{1,0},{2,3},{3,2},{4,5},{5,4},{6,7},{7,6},{8,9},{9,8},{10,11... | collective-permute-start | bytes 147464 | tf_op jit(solution)/shard_map/ppermute | solution.py:341

commit v12 on v11

--- a/solution.py
+++ b/solution.py
@@ -111,10 +111,8 @@
     weight_ref,
     conv_two_ref,
     table_ref,
-    send_far,
-    send_near,
-    keep_far,
-    keep_near,
+    send_ref,
+    keep_ref,
     small_ref,
     taps,
     limits,
@@ -239,13 +237,12 @@
     share = grad.shape[0] // shares
     me = place_ref[0]
     order = bit_order(shares)
-    parts = (keep_near, keep_far, send_near, send_far)
-    quarter = shares // 4
+    half = shares // 2
     for spot in range(shares):
         flip = sum(1 << bit for i, bit in enumerate(reversed(order)) if spot >> i & 1)
         block = grad[pl.ds(pl.multiple_of((me ^ flip) * share, 8), share), :]
-        part = parts[spot // quarter]
-        at = spot % quarter * share
+        part = send_ref if spot >= half else keep_ref
+        at = spot % half * share
         part[at : at + share, :] = block.astype(part.dtype)
 
     turn = (((1,), (1,)), ((), ()))
@@ -288,19 +285,17 @@
     count = got.shape[0]
     rows_two, width = cot.shape
     rows_one = 2 * rows_two + count
-    quarter = 3 * width // 4
+    half = 3 * width // 2
     vmem = pl.BlockSpec(memory_space=pltpu.VMEM)
     return pl.pallas_call(
         functools.partial(local_kernel, record, shares),
         out_shape=(
-            jax.ShapeDtypeStruct((quarter, width), BF16),
-            jax.ShapeDtypeStruct((quarter, width), BF16),
-            jax.ShapeDtypeStruct((quarter, width), F32),
-            jax.ShapeDtypeStruct((quarter, width), F32),
+            jax.ShapeDtypeStruct((half, width), BF16),
+            jax.ShapeDtypeStruct((half, width), F32),
             jax.ShapeDtypeStruct((ROWS, width), F32),
         ),
         in_specs=[pl.BlockSpec(memory_space=pltpu.SMEM)] + [vmem] * 5,
-        out_specs=(vmem,) * 5,
+        out_specs=(vmem,) * 3,
         scratch_shapes=[
             pltpu.VMEM((rows_one, 128), BF16),
             pltpu.VMEM((count, 128), jnp.int32),
@@ -397,14 +392,13 @@
     )(*parts)
 
 
-def sum_all(sizes, send_far, send_near, keep_far, keep_near, small):
+def sum_all(sizes, send, keep, small):
     order = [("dp", bit) for bit in bit_order(sizes["dp"])]
     core, onward, pair, left = order[0], order[1], order[2:4], order[4:]
     small = rounded(small + exchange(sizes, [core], small))
-    far = keep_far + exchange(sizes, [core], send_far).astype(F32)
-    near = keep_near + exchange(sizes, [core], send_near).astype(F32)
-    rows = far.shape[0] // 4
-    near, far = ([part[i * rows : (i + 1) * rows] for i in range(4)] for part in (near, far))
+    total = keep + exchange(sizes, [core], send).astype(F32)
+    rows = total.shape[0] // 8
+    near, far = ([total[i * rows : (i + 1) * rows] for i in range(j, j + 4)] for j in (0, 4))
     fars, smalls, nears = [far[0]], [small], []
     chosen = [[bit for i, bit in enumerate(pair) if code >> (1 - i) & 1] for code in range(4)]
     for code in (1, 2, 3):

time: 50 us -> 49.3 us (0.986)
  starting transfers between devices: 21.4 us -> 20.4 us
    ppermute x13 -> x12, starting transfers between devices: 14 us -> 13 us  [exchange(): return lax.ppermute(message, axes if len(axes) > 1 else axes[0], pairs)]
    ppermute x13 -> x12, waiting for transfers between devices: 11.9 us -> 12.2 us  [exchange(): return lax.ppermute(message, axes if len(axes) > 1 else axes[0], pairs)]
  transfers between devices with their start and end apart: 14 -> 13, of which waited for: 8 -> 8; matrix products, arithmetic and copies ran while one was open for 4% -> 3% of each run, Pallas kernels for 1% -> 1%
where the time goes in v12:
time: 49.3 us; the launch traced here: 48.9 us
  starting transfers between devices  20.4 us (41%)
  waiting for transfers between devices  14.4 us (29%)
  Pallas kernels  8.91 us (18%)
  local copies, waits for them, and re-layouts  4.02 us (8%)
  between operations  0.74 us (2%)
    ppermute x12, starting transfers between devices, exchange(): return lax.ppermute(message, axes if len(axes) > 1 else axes[0], pairs)  13 us
    ppermute x12, waiting for transfers between devices, exchange(): return lax.ppermute(message, axes if len(axes) > 1 else axes[0], pairs)  12.2 us
    all_to_all x1, starting transfers between devices, per_device(): got = lax.all_to_all(packed, 'dp', split_axis=0, concat_axis=0, tiled=True)  7.36 us
    pallas_call x1, Pallas kernels, local_pass(): pl.pallas_call(functools.partial(local_kernel, record, shares), out_shape...  6.36 us
    unnamed x6, local copies, waits for them, and re-layouts  2.45 us
    all_to_all x1, waiting for transfers between devices, per_device(): got = lax.all_to_all(packed, 'dp', split_axis=0, concat_axis=0, tiled=True)  2.15 us
    concatenate x1, local copies, waits for them, and re-layouts, per_device(): table = jnp.concatenate([conv_one.astype(F32), jnp.stack(vectors)], axis=0)  1.52 us
    pallas_call x1, Pallas kernels, pack(): pl.pallas_call(pack_kernel, out_shape=jax.ShapeDtypeStruct((count, 1, wid...  1.37 us
  transfers between devices with their start and end apart: 13, of which 8 were waited for; matrix products, arithmetic and copies ran while one was open for 3% of the time, Pallas kernels for 1%

profile of v12, /device:TPU:0, one launch (start us, length us, event | category | flops | bytes accessed | tf_op | source)
XLA Modules:
  0.0 48.9 jit_solution(2276223474460904836)
XLA Ops:
  0.6 1.4 %shard_map.131 = f32[16,1,384]{2,1,0:T(1,128)} custom-call(s32[1,16]{1,0:T(1,128)} %packing.1, s32[16]{0:T(128)} %bins.1, bf16[16,330]{1,0:T(8,128)(2,1)} %wave_ref.1), custom_call_target="tpu_custom_call" | custom-call | tf_op jit(solution)/shard_map/pallas_call | solution.py:39
  2.0 7.4 %all-to-all-start = ((f32[16,1,384]{2,1,0:T(1,128)}), f32[16,1,384]{2,1,0:T(1,128)S(1)}, u32[]{:S(2)}, u32[]{:S(2)}) async-start(f32[16,1,384]{2,1,0:T(1,128)} %shard_map.131), calls=%async_computation | async-start | bytes 49152 | tf_op jit(solution)/shard_map/all_to_all | solution.py:458
  9.4 1.5 %concatenate.18.table_ref = f32[16,512]{1,0:T(8,128)S(1)} concatenate(bf16[10,512]{1,0:T(8,128)(2,1)} %param.16, f32[1,512]{1,0:T(1,128)} %bitcast.9, f32[1,512]{1,0:T(1,128)} %bitcast.10, f32[1,512]{1,0:T(1,128)} %bitcast.11, f32[1,512]{1,0:T(1,128)} %bitcast.12, f32[1,512]{1,0:T(1,128)} %bitcast.13, f32[1,512]{1,0:T(1,128)} %bitcast.14), dimensions={0} | concatenate | bytes 55296 | tf_op jit(solution)/shard_map/concatenate | solution.py:460
  10.9 1.4 %copy-done = bf16[1536,512]{1,0:T(8,128)(2,1)S(1)} copy-done((bf16[1536,512]{1,0:T(8,128)(2,1)S(1)}, bf16[1536,512]{1,0:T(8,128)(2,1)}, u32[]{:S(2)}) %copy-start) | copy-done | bytes 1572888
  12.3 1.0 %copy-done.2 = bf16[16,32,512]{2,1,0:T(8,128)(2,1)S(1)} copy-done((bf16[16,32,512]{2,1,0:T(8,128)(2,1)S(1)}, bf16[16,32,512]{2,1,0:T(8,128)(2,1)}, u32[]{:S(2)}) %copy-start.2) | copy-done | bytes 524312
  13.8 2.2 %all-to-all-done.got_ref = f32[16,1,384]{2,1,0:T(1,128)S(1)} async-done(((f32[16,1,384]{2,1,0:T(1,128)}), f32[16,1,384]{2,1,0:T(1,128)S(1)}, u32[]{:S(2)}, u32[]{:S(2)}) %all-to-all-start) | async-done | bytes 24608 | tf_op jit(solution)/shard_map/all_to_all | solution.py:458
  15.9 6.4 %shard_map.133 = (bf16[768,512]{1,0:T(8,128)(2,1)S(1)}, f32[768,512]{1,0:T(8,128)S(1)}, f32[16,512]{1,0:T(8,128)S(1)}) custom-call(s32[1]{0:T(128)} %bitcast.place_ref, f32[16,1,384]{2,1,0:T(1,128)S(1)} %all-to-all-done.got_ref, bf16[512,512]{1,0:T(8,128)(2,1)S(1)} %get-tuple-element.7.cot_ref, bf16[128,512]{1,0:T(8,128)(2,1)S(1)} %get-tuple-element.8.weight_ref, ...), custom_call_target="tpu_custom_call" | custom-call | flops 2415919104 | bytes 4259840 | tf_op jit(solution)/shard_map/pallas_call | solution.py:290
  22.4 0.5 %collective-permute-start.4 = (f32[16,512]{1,0:T(8,128)S(1)}, f32[16,512]{1,0:T(8,128)S(1)}, u32[]{:S(2)}, u32[]{:S(2)}) collective-permute-start(f32[16,512]{1,0:T(8,128)S(1)} %get-tuple-element.11), channel_id=1, source_target_pairs={{0,2},{2,0},{4,6},{6,4},{8,10},{10,8},{12,14},{14,12},{16,18},{18,... | collective-permute-start | bytes 98312 | tf_op jit(solution)/shard_map/ppermute | solution.py:336
  22.9 1.8 %collective-permute-done.4 = f32[16,512]{1,0:T(8,128)S(1)} collective-permute-done((f32[16,512]{1,0:T(8,128)S(1)}, f32[16,512]{1,0:T(8,128)S(1)}, u32[]{:S(2)}, u32[]{:S(2)}) %collective-permute-start.4) | collective-permute-done | bytes 32800 | tf_op jit(solution)/shard_map/ppermute | solution.py:336
  25.1 0.8 %collective-permute-start.5 = (bf16[112,512]{1,0:T(8,128)(2,1)S(1)}, bf16[112,512]{1,0:T(8,128)(2,1)S(1)}, u32[]{:S(2)}, u32[]{:S(2)}) collective-permute-start(bf16[112,512]{1,0:T(8,128)(2,1)S(1)} %get-tuple-element.26), channel_id=1, source_target_pairs={{0,8},{2,10},{4,12},{6,14},{8,0},{10,2},{12,4},{14,6},{16,24},{18,... | collective-permute-start | bytes 344072 | tf_op jit(solution)/shard_map/ppermute | solution.py:336
  25.9 1.5 %collective-permute-start.6 = (bf16[112,512]{1,0:T(8,128)(2,1)S(1)}, bf16[112,512]{1,0:T(8,128)(2,1)S(1)}, u32[]{:S(2)}, u32[]{:S(2)}) collective-permute-start(bf16[112,512]{1,0:T(8,128)(2,1)S(1)} %get-tuple-element.27), channel_id=1, source_target_pairs={{0,4},{2,6},{4,0},{6,2},{8,12},{10,14},{12,8},{14,10},{16,20},{18,... | collective-permute-start | bytes 344072 | tf_op jit(solution)/shard_map/ppermute | solution.py:336
  27.4 1.3 %collective-permute-start.7 = (bf16[112,512]{1,0:T(8,128)(2,1)S(1)}, bf16[112,512]{1,0:T(8,128)(2,1)S(1)}, u32[]{:S(2)}, u32[]{:S(2)}) collective-permute-start(bf16[112,512]{1,0:T(8,128)(2,1)S(1)} %get-tuple-element.28), channel_id=1, source_target_pairs={{0,12},{2,14},{4,8},{6,10},{8,4},{10,6},{12,0},{14,2},{16,28},{18,... | collective-permute-start | bytes 344072 | tf_op jit(solution)/shard_map/ppermute | solution.py:336
  28.7 0.7 %collective-permute-start.1 = (bf16[96,512]{1,0:T(8,128)(2,1)S(1)}, bf16[96,512]{1,0:T(8,128)(2,1)S(1)}, u32[]{:S(2)}, u32[]{:S(2)}) collective-permute-start(bf16[96,512]{1,0:T(8,128)(2,1)S(1)} %get-tuple-element.23), channel_id=1, source_target_pairs={{0,8},{2,10},{4,12},{6,14},{8,0},{10,2},{12,4},{14,6},{16,24},{18,... | collective-permute-start | bytes 294920 | tf_op jit(solution)/shard_map/ppermute | solution.py:336
  29.4 1.5 %collective-permute-start.2 = (bf16[96,512]{1,0:T(8,128)(2,1)S(1)}, bf16[96,512]{1,0:T(8,128)(2,1)S(1)}, u32[]{:S(2)}, u32[]{:S(2)}) collective-permute-start(bf16[96,512]{1,0:T(8,128)(2,1)S(1)} %get-tuple-element.22), channel_id=1, source_target_pairs={{0,4},{2,6},{4,0},{6,2},{8,12},{10,14},{12,8},{14,10},{16,20},{18,... | collective-permute-start | bytes 294920 | tf_op jit(solution)/shard_map/ppermute | solution.py:336
  31.2 1.6 %collective-permute-start.3 = (bf16[96,512]{1,0:T(8,128)(2,1)S(1)}, bf16[96,512]{1,0:T(8,128)(2,1)S(1)}, u32[]{:S(2)}, u32[]{:S(2)}) collective-permute-start(bf16[96,512]{1,0:T(8,128)(2,1)S(1)} %get-tuple-element.21), channel_id=1, source_target_pairs={{0,12},{2,14},{4,8},{6,10},{8,4},{10,6},{12,0},{14,2},{16,28},{18,... | collective-permute-start | bytes 294920 | tf_op jit(solution)/shard_map/ppermute | solution.py:336
  32.8 1.6 %collective-permute-done.7 = bf16[112,512]{1,0:T(8,128)(2,1)S(1)} collective-permute-done((bf16[112,512]{1,0:T(8,128)(2,1)S(1)}, bf16[112,512]{1,0:T(8,128)(2,1)S(1)}, u32[]{:S(2)}, u32[]{:S(2)}) %collective-permute-start.7) | collective-permute-done | bytes 114720 | tf_op jit(solution)/shard_map/ppermute | solution.py:336
  34.5 2.4 %collective-permute-start.9 = (bf16[64,512]{1,0:T(8,128)(2,1)S(1)}, bf16[64,512]{1,0:T(8,128)(2,1)S(1)}, u32[]{:S(2)}, u32[]{:S(2)}) collective-permute-start(bf16[64,512]{1,0:T(8,128)(2,1)S(1)} %pad_maximum_fusion.3), channel_id=1, source_target_pairs={{0,16},{2,18},{4,20},{6,22},{8,24},{10,26},{12,28},{14,30},{16,0},... | collective-permute-start | bytes 196616 | tf_op jit(solution)/shard_map/ppermute | solution.py:336
  36.9 0.6 %collective-permute-start.8 = (bf16[48,512]{1,0:T(8,128)(2,1)S(1)}, bf16[48,512]{1,0:T(8,128)(2,1)S(1)}, u32[]{:S(2)}, u32[]{:S(2)}) collective-permute-start(bf16[48,512]{1,0:T(8,128)(2,1)S(1)} %slice.98), channel_id=1, source_target_pairs={{0,16},{2,18},{4,20},{6,22},{8,24},{10,26},{12,28},{14,30},{16,0},... | collective-permute-start | bytes 147464 | tf_op jit(solution)/shard_map/ppermute | solution.py:336
  37.5 1.0 %collective-permute-done.3.refs_2_ = bf16[96,512]{1,0:T(8,128)(2,1)S(1)} collective-permute-done((bf16[96,512]{1,0:T(8,128)(2,1)S(1)}, bf16[96,512]{1,0:T(8,128)(2,1)S(1)}, u32[]{:S(2)}, u32[]{:S(2)}) %collective-permute-start.3) | collective-permute-done | bytes 98336 | tf_op jit(solution)/shard_map/ppermute | solution.py:336
  38.5 2.4 %collective-permute-done.9 = bf16[64,512]{1,0:T(8,128)(2,1)S(1)} collective-permute-done((bf16[64,512]{1,0:T(8,128)(2,1)S(1)}, bf16[64,512]{1,0:T(8,128)(2,1)S(1)}, u32[]{:S(2)}, u32[]{:S(2)}) %collective-permute-start.9) | collective-permute-done | bytes 65568 | tf_op jit(solution)/shard_map/ppermute | solution.py:336
  40.9 1.5 %collective-permute-done.8 = bf16[48,512]{1,0:T(8,128)(2,1)S(1)} collective-permute-done((bf16[48,512]{1,0:T(8,128)(2,1)S(1)}, bf16[48,512]{1,0:T(8,128)(2,1)S(1)}, u32[]{:S(2)}, u32[]{:S(2)}) %collective-permute-start.8) | collective-permute-done | bytes 49184 | tf_op jit(solution)/shard_map/ppermute | solution.py:336
  42.5 1.6 %collective-permute-start.11 = (bf16[64,512]{1,0:T(8,128)(2,1)S(1)}, bf16[64,512]{1,0:T(8,128)(2,1)S(1)}, u32[]{:S(2)}, u32[]{:S(2)}) collective-permute-start(bf16[64,512]{1,0:T(8,128)(2,1)S(1)} %pad_maximum_fusion.4.own_second), channel_id=1, source_target_pairs={{0,1},{1,0},{2,3},{3,2},{4,5},{5,4},{6,7},{7,6},{8,9},{9,8},{10,11... | collective-permute-start | bytes 196616 | tf_op jit(solution)/shard_map/ppermute | solution.py:336
  44.6 3.6 %collective-permute-done.10.got_first = bf16[48,512]{1,0:T(8,128)(2,1)S(1)} collective-permute-done((bf16[48,512]{1,0:T(8,128)(2,1)S(1)}, bf16[48,512]{1,0:T(8,128)(2,1)S(1)}, u32[]{:S(2)}, u32[]{:S(2)}) %collective-permute-start.10) | collective-permute-done | bytes 49184 | tf_op jit(solution)/shard_map/ppermute | solution.py:336
  48.2 0.7 %shard_map.135 = (f32[96,512]{1,0:T(8,128)}, f32[16,512]{1,0:T(8,128)}) custom-call(bf16[48,512]{1,0:T(8,128)(2,1)S(1)} %get-tuple-element.25.own_first, bf16[64,512]{1,0:T(8,128)(2,1)S(1)} %pad_maximum_fusion.4.own_second, bf16[48,512]{1,0:T(8,128)(2,1)S(1)} %collective-permute-done.10.got_first, bf16[64,512]{1,0:T(8,128)(2,1)S(1)} %collective-permute-done.11.got_second), custom_call_target="tpu_custom_call" | custom-call | tf_op jit(solution)/shard_map/pallas_call | solution.py:383
  (25 shorter events, 1.9 us)
Async XLA Ops:
  2.0 13.9 %all-to-all-start = ((f32[16,1,384]{2,1,0:T(1,128)}), f32[16,1,384]{2,1,0:T(1,128)S(1)}, u32[]{:S(2)}, u32[]{:S(2)}) async-start(f32[16,1,384]{2,1,0:T(1,128)} %shard_map.131), calls=%async_computation | async-start | bytes 49152 | tf_op jit(solution)/shard_map/all_to_all | solution.py:458
  10.9 1.4 %copy-start = (bf16[1536,512]{1,0:T(8,128)(2,1)S(1)}, bf16[1536,512]{1,0:T(8,128)(2,1)}, u32[]{:S(2)}) copy-start(bf16[1536,512]{1,0:T(8,128)(2,1)} %conv_two_ref.3) | copy-start | bytes 4718596
  12.3 1.0 %copy-start.2 = (bf16[16,32,512]{2,1,0:T(8,128)(2,1)S(1)}, bf16[16,32,512]{2,1,0:T(8,128)(2,1)}, u32[]{:S(2)}) copy-start(bf16[16,32,512]{2,1,0:T(8,128)(2,1)} %param.15) | copy-start | bytes 1572868
  13.3 2.6 %copy-start.1 = (bf16[1536,512]{1,0:T(8,128)(2,1)S(1)}, bf16[1536,512]{1,0:T(8,128)(2,1)}, u32[]{:S(2)}) copy-start(bf16[1536,512]{1,0:T(8,128)(2,1)} %conv_two_ref.3) | copy-start | bytes 4718596
  22.3 2.4 %collective-permute-start = (bf16[768,512]{1,0:T(8,128)(2,1)S(1)}, bf16[768,512]{1,0:T(8,128)(2,1)S(1)}, u32[]{:S(2)}, u32[]{:S(2)}) collective-permute-start(bf16[768,512]{1,0:T(8,128)(2,1)S(1)} %get-tuple-element.10), channel_id=1, source_target_pairs={{0,2},{2,0},{4,6},{6,4},{8,10},{10,8},{12,14},{14,12},{16,18},{18,... | collective-permute-start | bytes 2359304 | tf_op jit(solution)/shard_map/ppermute | solution.py:336
  22.4 2.3 %collective-permute-start.4 = (f32[16,512]{1,0:T(8,128)S(1)}, f32[16,512]{1,0:T(8,128)S(1)}, u32[]{:S(2)}, u32[]{:S(2)}) collective-permute-start(f32[16,512]{1,0:T(8,128)S(1)} %get-tuple-element.11), channel_id=1, source_target_pairs={{0,2},{2,0},{4,6},{6,4},{8,10},{10,8},{12,14},{14,12},{16,18},{18,... | collective-permute-start | bytes 98312 | tf_op jit(solution)/shard_map/ppermute | solution.py:336
  25.1 6.1 %collective-permute-start.5 = (bf16[112,512]{1,0:T(8,128)(2,1)S(1)}, bf16[112,512]{1,0:T(8,128)(2,1)S(1)}, u32[]{:S(2)}, u32[]{:S(2)}) collective-permute-start(bf16[112,512]{1,0:T(8,128)(2,1)S(1)} %get-tuple-element.26), channel_id=1, source_target_pairs={{0,8},{2,10},{4,12},{6,14},{8,0},{10,2},{12,4},{14,6},{16,24},{18,... | collective-permute-start | bytes 344072 | tf_op jit(solution)/shard_map/ppermute | solution.py:336
  25.9 6.9 %collective-permute-start.6 = (bf16[112,512]{1,0:T(8,128)(2,1)S(1)}, bf16[112,512]{1,0:T(8,128)(2,1)S(1)}, u32[]{:S(2)}, u32[]{:S(2)}) collective-permute-start(bf16[112,512]{1,0:T(8,128)(2,1)S(1)} %get-tuple-element.27), channel_id=1, source_target_pairs={{0,4},{2,6},{4,0},{6,2},{8,12},{10,14},{12,8},{14,10},{16,20},{18,... | collective-permute-start | bytes 344072 | tf_op jit(solution)/shard_map/ppermute | solution.py:336
  27.4 7.0 %collective-permute-start.7 = (bf16[112,512]{1,0:T(8,128)(2,1)S(1)}, bf16[112,512]{1,0:T(8,128)(2,1)S(1)}, u32[]{:S(2)}, u32[]{:S(2)}) collective-permute-start(bf16[112,512]{1,0:T(8,128)(2,1)S(1)} %get-tuple-element.28), channel_id=1, source_target_pairs={{0,12},{2,14},{4,8},{6,10},{8,4},{10,6},{12,0},{14,2},{16,28},{18,... | collective-permute-start | bytes 344072 | tf_op jit(solution)/shard_map/ppermute | solution.py:336
  28.7 8.8 %collective-permute-start.1 = (bf16[96,512]{1,0:T(8,128)(2,1)S(1)}, bf16[96,512]{1,0:T(8,128)(2,1)S(1)}, u32[]{:S(2)}, u32[]{:S(2)}) collective-permute-start(bf16[96,512]{1,0:T(8,128)(2,1)S(1)} %get-tuple-element.23), channel_id=1, source_target_pairs={{0,8},{2,10},{4,12},{6,14},{8,0},{10,2},{12,4},{14,6},{16,24},{18,... | collective-permute-start | bytes 294920 | tf_op jit(solution)/shard_map/ppermute | solution.py:336
  29.4 8.1 %collective-permute-start.2 = (bf16[96,512]{1,0:T(8,128)(2,1)S(1)}, bf16[96,512]{1,0:T(8,128)(2,1)S(1)}, u32[]{:S(2)}, u32[]{:S(2)}) collective-permute-start(bf16[96,512]{1,0:T(8,128)(2,1)S(1)} %get-tuple-element.22), channel_id=1, source_target_pairs={{0,4},{2,6},{4,0},{6,2},{8,12},{10,14},{12,8},{14,10},{16,20},{18,... | collective-permute-start | bytes 294920 | tf_op jit(solution)/shard_map/ppermute | solution.py:336
  31.2 7.3 %collective-permute-start.3 = (bf16[96,512]{1,0:T(8,128)(2,1)S(1)}, bf16[96,512]{1,0:T(8,128)(2,1)S(1)}, u32[]{:S(2)}, u32[]{:S(2)}) collective-permute-start(bf16[96,512]{1,0:T(8,128)(2,1)S(1)} %get-tuple-element.21), channel_id=1, source_target_pairs={{0,12},{2,14},{4,8},{6,10},{8,4},{10,6},{12,0},{14,2},{16,28},{18,... | collective-permute-start | bytes 294920 | tf_op jit(solution)/shard_map/ppermute | solution.py:336
  34.5 6.4 %collective-permute-start.9 = (bf16[64,512]{1,0:T(8,128)(2,1)S(1)}, bf16[64,512]{1,0:T(8,128)(2,1)S(1)}, u32[]{:S(2)}, u32[]{:S(2)}) collective-permute-start(bf16[64,512]{1,0:T(8,128)(2,1)S(1)} %pad_maximum_fusion.3), channel_id=1, source_target_pairs={{0,16},{2,18},{4,20},{6,22},{8,24},{10,26},{12,28},{14,30},{16,0},... | collective-permute-start | bytes 196616 | tf_op jit(solution)/shard_map/ppermute | solution.py:336
  36.9 5.5 %collective-permute-start.8 = (bf16[48,512]{1,0:T(8,128)(2,1)S(1)}, bf16[48,512]{1,0:T(8,128)(2,1)S(1)}, u32[]{:S(2)}, u32[]{:S(2)}) collective-permute-start(bf16[48,512]{1,0:T(8,128)(2,1)S(1)} %slice.98), channel_id=1, source_target_pairs={{0,16},{2,18},{4,20},{6,22},{8,24},{10,26},{12,28},{14,30},{16,0},... | collective-permute-start | bytes 147464 | tf_op jit(solution)/shard_map/ppermute | solution.py:336
  42.5 5.7 %collective-permute-start.11 = (bf16[64,512]{1,0:T(8,128)(2,1)S(1)}, bf16[64,512]{1,0:T(8,128)(2,1)S(1)}, u32[]{:S(2)}, u32[]{:S(2)}) collective-permute-start(bf16[64,512]{1,0:T(8,128)(2,1)S(1)} %pad_maximum_fusion.4.own_second), channel_id=1, source_target_pairs={{0,1},{1,0},{2,3},{3,2},{4,5},{5,4},{6,7},{7,6},{8,9},{9,8},{10,11... | collective-permute-start | bytes 196616 | tf_op jit(solution)/shard_map/ppermute | solution.py:336
  44.1 4.1 %collective-permute-start.10 = (bf16[48,512]{1,0:T(8,128)(2,1)S(1)}, bf16[48,512]{1,0:T(8,128)(2,1)S(1)}, u32[]{:S(2)}, u32[]{:S(2)}) collective-permute-start(bf16[48,512]{1,0:T(8,128)(2,1)S(1)} %get-tuple-element.25.own_first), channel_id=1, source_target_pairs={{0,1},{1,0},{2,3},{3,2},{4,5},{5,4},{6,7},{7,6},{8,9},{9,8},{10,11... | collective-permute-start | bytes 147464 | tf_op jit(solution)/shard_map/ppermute | solution.py:336

commit v13 on v12

--- a/solution.py
+++ b/solution.py
@@ -350,17 +350,23 @@
 
 
 def near_kernel(own_ref, *refs):
-    terms = [own_ref[...]] + [ref[...].astype(F32) for ref in refs[:-1]]
-    refs[-1][...] = tree(terms)
-
-
-def near_sum(own, *got):
+    terms = [own_ref[...]] + [ref[...].astype(F32) for ref in refs[:-2]]
+    total = tree(terms)
+    cut = refs[-2].shape[0]
+    refs[-2][...] = total[:cut]
+    refs[-1][...] = total[cut:]
+
+
+def near_sum(cut, own, *got):
     vmem = pl.BlockSpec(memory_space=pltpu.VMEM)
     return pl.pallas_call(
         near_kernel,
-        out_shape=jax.ShapeDtypeStruct(own.shape, F32),
+        out_shape=(
+            jax.ShapeDtypeStruct((cut, own.shape[1]), F32),
+            jax.ShapeDtypeStruct((own.shape[0] - cut, own.shape[1]), F32),
+        ),
         in_specs=[vmem] * (1 + len(got)),
-        out_specs=vmem,
+        out_specs=(vmem, vmem),
         cost_estimate=pl.CostEstimate(
             flops=4 * own.size, bytes_accessed=140 * own.size, transcendentals=0
         ),
@@ -411,10 +417,10 @@
         nears.append(exchange(sizes, chosen[code], near[code].astype(BF16)))
     cut = own.shape[0] // 2 // ROWS * ROWS
     first, second = (exchange(sizes, [onward], part) for part in (own[:cut], own[cut:]))
-    base = near_sum(near[0], *nears)
-    first = base[:cut] + first.astype(F32)
+    base = near_sum(cut, near[0], *nears)
+    first = base[0] + first.astype(F32)
     second, more = contents(second)
-    second, small = base[cut:] + second, small + more
+    second, small = base[1] + second, small + more
     for bit in left:
         total = jnp.concatenate([first, second], axis=0)
         half = total.shape[0] // 2

time: 49.3 us -> 47.8 us (0.970)
  waiting for transfers between devices: 14.4 us -> 11.9 us
  starting transfers between devices: 20.4 us -> 21.3 us
    ppermute x12, waiting for transfers between devices: 12.2 us -> 9.79 us  [exchange(): return lax.ppermute(message, axes if len(axes) > 1 else axes[0], pairs)]
    ppermute x12, starting transfers between devices: 13 us -> 14 us  [exchange(): return lax.ppermute(message, axes if len(axes) > 1 else axes[0], pairs)]
  transfers between devices with their start and end apart: 13 -> 13, of which waited for: 8 -> 7; matrix products, arithmetic and copies ran while one was open for 3% -> 3% of each run, Pallas kernels for 1% -> 1%
where the time goes in v13:
time: 47.8 us; the launch traced here: 47.4 us
  starting transfers between devices  21.3 us (45%)
  waiting for transfers between devices  11.9 us (25%)
  Pallas kernels  8.89 us (19%)
  local copies, waits for them, and re-layouts  4.01 us (8%)
  between operations  0.75 us (2%)
  other arithmetic  0.49 us (1%)
    ppermute x12, starting transfers between devices, exchange(): return lax.ppermute(message, axes if len(axes) > 1 else axes[0], pairs)  14 us
    ppermute x12, waiting for transfers between devices, exchange(): return lax.ppermute(message, axes if len(axes) > 1 else axes[0], pairs)  9.79 us
    all_to_all x1, starting transfers between devices, per_device(): got = lax.all_to_all(packed, 'dp', split_axis=0, concat_axis=0, tiled=True)  7.36 us
    pallas_call x1, Pallas kernels, local_pass(): pl.pallas_call(functools.partial(local_kernel, record, shares), out_shape...  6.34 us
    unnamed x6, local copies, waits for them, and re-layouts  2.45 us
    all_to_all x1, waiting for transfers between devices, per_device(): got = lax.all_to_all(packed, 'dp', split_axis=0, concat_axis=0, tiled=True)  2.15 us
    concatenate x1, local copies, waits for them, and re-layouts, per_device(): table = jnp.concatenate([conv_one.astype(F32), jnp.stack(vectors)], axis=0)  1.52 us
    pallas_call x1, Pallas kernels, pack(): pl.pallas_call(pack_kernel, out_shape=jax.ShapeDtypeStruct((count, 1, wid...  1.37 us
  transfers between devices with their start and end apart: 13, of which 7 were waited for; matrix products, arithmetic and copies ran while one was open for 3% of the time, Pallas kernels for 1%

profile of v13, /device:TPU:0, one launch (start us, length us, event | category | flops | bytes accessed | tf_op | source)
XLA Modules:
  0.0 47.4 jit_solution(5861272455783264064)
XLA Ops:
  0.6 1.4 %shard_map.131 = f32[16,1,384]{2,1,0:T(1,128)} custom-call(s32[1,16]{1,0:T(1,128)} %packing.1, s32[16]{0:T(128)} %bins.1, bf16[16,330]{1,0:T(8,128)(2,1)} %wave_ref.1), custom_call_target="tpu_custom_call" | custom-call | tf_op jit(solution)/shard_map/pallas_call | solution.py:39
  2.0 7.4 %all-to-all-start = ((f32[16,1,384]{2,1,0:T(1,128)}), f32[16,1,384]{2,1,0:T(1,128)S(1)}, u32[]{:S(2)}, u32[]{:S(2)}) async-start(f32[16,1,384]{2,1,0:T(1,128)} %shard_map.131), calls=%async_computation | async-start | bytes 49152 | tf_op jit(solution)/shard_map/all_to_all | solution.py:464
  9.4 1.5 %concatenate.18.table_ref = f32[16,512]{1,0:T(8,128)S(1)} concatenate(bf16[10,512]{1,0:T(8,128)(2,1)} %param.16, f32[1,512]{1,0:T(1,128)} %bitcast.9, f32[1,512]{1,0:T(1,128)} %bitcast.10, f32[1,512]{1,0:T(1,128)} %bitcast.11, f32[1,512]{1,0:T(1,128)} %bitcast.12, f32[1,512]{1,0:T(1,128)} %bitcast.13, f32[1,512]{1,0:T(1,128)} %bitcast.14), dimensions={0} | concatenate | bytes 55296 | tf_op jit(solution)/shard_map/concatenate | solution.py:466
  10.9 1.4 %copy-done = bf16[1536,512]{1,0:T(8,128)(2,1)S(1)} copy-done((bf16[1536,512]{1,0:T(8,128)(2,1)S(1)}, bf16[1536,512]{1,0:T(8,128)(2,1)}, u32[]{:S(2)}) %copy-start) | copy-done | bytes 1572888
  12.3 1.0 %copy-done.2 = bf16[16,32,512]{2,1,0:T(8,128)(2,1)S(1)} copy-done((bf16[16,32,512]{2,1,0:T(8,128)(2,1)S(1)}, bf16[16,32,512]{2,1,0:T(8,128)(2,1)}, u32[]{:S(2)}) %copy-start.2) | copy-done | bytes 524312
  13.8 2.2 %all-to-all-done.got_ref = f32[16,1,384]{2,1,0:T(1,128)S(1)} async-done(((f32[16,1,384]{2,1,0:T(1,128)}), f32[16,1,384]{2,1,0:T(1,128)S(1)}, u32[]{:S(2)}, u32[]{:S(2)}) %all-to-all-start) | async-done | bytes 24608 | tf_op jit(solution)/shard_map/all_to_all | solution.py:464
  15.9 6.3 %shard_map.133 = (bf16[768,512]{1,0:T(8,128)(2,1)S(1)}, f32[768,512]{1,0:T(8,128)S(1)}, f32[16,512]{1,0:T(8,128)S(1)}) custom-call(s32[1]{0:T(128)} %bitcast.place_ref, f32[16,1,384]{2,1,0:T(1,128)S(1)} %all-to-all-done.got_ref, bf16[512,512]{1,0:T(8,128)(2,1)S(1)} %get-tuple-element.9.cot_ref, bf16[128,512]{1,0:T(8,128)(2,1)S(1)} %get-tuple-element.10.weight_ref, ...), custom_call_target="tpu_custom_call" | custom-call | flops 2415919104 | bytes 4259840 | tf_op jit(solution)/shard_map/pallas_call | solution.py:290
  22.4 0.5 %collective-permute-start.4 = (f32[16,512]{1,0:T(8,128)S(1)}, f32[16,512]{1,0:T(8,128)S(1)}, u32[]{:S(2)}, u32[]{:S(2)}) collective-permute-start(f32[16,512]{1,0:T(8,128)S(1)} %get-tuple-element.14), channel_id=1, source_target_pairs={{0,2},{2,0},{4,6},{6,4},{8,10},{10,8},{12,14},{14,12},{16,18},{18,... | collective-permute-start | bytes 98312 | tf_op jit(solution)/shard_map/ppermute | solution.py:336
  22.9 1.8 %collective-permute-done.4 = f32[16,512]{1,0:T(8,128)S(1)} collective-permute-done((f32[16,512]{1,0:T(8,128)S(1)}, f32[16,512]{1,0:T(8,128)S(1)}, u32[]{:S(2)}, u32[]{:S(2)}) %collective-permute-start.4) | collective-permute-done | bytes 32800 | tf_op jit(solution)/shard_map/ppermute | solution.py:336
  25.1 0.8 %collective-permute-start.5 = (bf16[112,512]{1,0:T(8,128)(2,1)S(1)}, bf16[112,512]{1,0:T(8,128)(2,1)S(1)}, u32[]{:S(2)}, u32[]{:S(2)}) collective-permute-start(bf16[112,512]{1,0:T(8,128)(2,1)S(1)} %get-tuple-element.28), channel_id=1, source_target_pairs={{0,8},{2,10},{4,12},{6,14},{8,0},{10,2},{12,4},{14,6},{16,24},{18,... | collective-permute-start | bytes 344072 | tf_op jit(solution)/shard_map/ppermute | solution.py:336
  25.9 1.5 %collective-permute-start.6 = (bf16[112,512]{1,0:T(8,128)(2,1)S(1)}, bf16[112,512]{1,0:T(8,128)(2,1)S(1)}, u32[]{:S(2)}, u32[]{:S(2)}) collective-permute-start(bf16[112,512]{1,0:T(8,128)(2,1)S(1)} %get-tuple-element.29), channel_id=1, source_target_pairs={{0,4},{2,6},{4,0},{6,2},{8,12},{10,14},{12,8},{14,10},{16,20},{18,... | collective-permute-start | bytes 344072 | tf_op jit(solution)/shard_map/ppermute | solution.py:336
  27.4 1.3 %collective-permute-start.7 = (bf16[112,512]{1,0:T(8,128)(2,1)S(1)}, bf16[112,512]{1,0:T(8,128)(2,1)S(1)}, u32[]{:S(2)}, u32[]{:S(2)}) collective-permute-start(bf16[112,512]{1,0:T(8,128)(2,1)S(1)} %get-tuple-element.30), channel_id=1, source_target_pairs={{0,12},{2,14},{4,8},{6,10},{8,4},{10,6},{12,0},{14,2},{16,28},{18,... | collective-permute-start | bytes 344072 | tf_op jit(solution)/shard_map/ppermute | solution.py:336
  28.7 0.7 %collective-permute-start.1 = (bf16[96,512]{1,0:T(8,128)(2,1)S(1)}, bf16[96,512]{1,0:T(8,128)(2,1)S(1)}, u32[]{:S(2)}, u32[]{:S(2)}) collective-permute-start(bf16[96,512]{1,0:T(8,128)(2,1)S(1)} %get-tuple-element.27), channel_id=1, source_target_pairs={{0,8},{2,10},{4,12},{6,14},{8,0},{10,2},{12,4},{14,6},{16,24},{18,... | collective-permute-start | bytes 294920 | tf_op jit(solution)/shard_map/ppermute | solution.py:336
  29.4 1.5 %collective-permute-start.2 = (bf16[96,512]{1,0:T(8,128)(2,1)S(1)}, bf16[96,512]{1,0:T(8,128)(2,1)S(1)}, u32[]{:S(2)}, u32[]{:S(2)}) collective-permute-start(bf16[96,512]{1,0:T(8,128)(2,1)S(1)} %get-tuple-element.26), channel_id=1, source_target_pairs={{0,4},{2,6},{4,0},{6,2},{8,12},{10,14},{12,8},{14,10},{16,20},{18,... | collective-permute-start | bytes 294920 | tf_op jit(solution)/shard_map/ppermute | solution.py:336
  31.2 1.6 %collective-permute-start.3 = (bf16[96,512]{1,0:T(8,128)(2,1)S(1)}, bf16[96,512]{1,0:T(8,128)(2,1)S(1)}, u32[]{:S(2)}, u32[]{:S(2)}) collective-permute-start(bf16[96,512]{1,0:T(8,128)(2,1)S(1)} %get-tuple-element.25), channel_id=1, source_target_pairs={{0,12},{2,14},{4,8},{6,10},{8,4},{10,6},{12,0},{14,2},{16,28},{18,... | collective-permute-start | bytes 294920 | tf_op jit(solution)/shard_map/ppermute | solution.py:336
  32.8 1.6 %collective-permute-done.7 = bf16[112,512]{1,0:T(8,128)(2,1)S(1)} collective-permute-done((bf16[112,512]{1,0:T(8,128)(2,1)S(1)}, bf16[112,512]{1,0:T(8,128)(2,1)S(1)}, u32[]{:S(2)}, u32[]{:S(2)}) %collective-permute-start.7) | collective-permute-done | bytes 114720 | tf_op jit(solution)/shard_map/ppermute | solution.py:336
  34.5 2.4 %collective-permute-start.9 = (bf16[64,512]{1,0:T(8,128)(2,1)S(1)}, bf16[64,512]{1,0:T(8,128)(2,1)S(1)}, u32[]{:S(2)}, u32[]{:S(2)}) collective-permute-start(bf16[64,512]{1,0:T(8,128)(2,1)S(1)} %pad_maximum_fusion.3), channel_id=1, source_target_pairs={{0,16},{2,18},{4,20},{6,22},{8,24},{10,26},{12,28},{14,30},{16,0},... | collective-permute-start | bytes 196616 | tf_op jit(solution)/shard_map/ppermute | solution.py:336
  36.9 0.5 %collective-permute-start.8 = (bf16[48,512]{1,0:T(8,128)(2,1)S(1)}, bf16[48,512]{1,0:T(8,128)(2,1)S(1)}, u32[]{:S(2)}, u32[]{:S(2)}) collective-permute-start(bf16[48,512]{1,0:T(8,128)(2,1)S(1)} %slice.89), channel_id=1, source_target_pairs={{0,16},{2,18},{4,20},{6,22},{8,24},{10,26},{12,28},{14,30},{16,0},... | collective-permute-start | bytes 147464 | tf_op jit(solution)/shard_map/ppermute | solution.py:336
  37.5 1.0 %collective-permute-done.3.refs_2_ = bf16[96,512]{1,0:T(8,128)(2,1)S(1)} collective-permute-done((bf16[96,512]{1,0:T(8,128)(2,1)S(1)}, bf16[96,512]{1,0:T(8,128)(2,1)S(1)}, u32[]{:S(2)}, u32[]{:S(2)}) %collective-permute-start.3) | collective-permute-done | bytes 98336 | tf_op jit(solution)/shard_map/ppermute | solution.py:336
  38.5 2.4 %collective-permute-done.9 = bf16[64,512]{1,0:T(8,128)(2,1)S(1)} collective-permute-done((bf16[64,512]{1,0:T(8,128)(2,1)S(1)}, bf16[64,512]{1,0:T(8,128)(2,1)S(1)}, u32[]{:S(2)}, u32[]{:S(2)}) %collective-permute-start.9) | collective-permute-done | bytes 65568 | tf_op jit(solution)/shard_map/ppermute | solution.py:336
  41.0 1.6 %collective-permute-start.11 = (bf16[64,512]{1,0:T(8,128)(2,1)S(1)}, bf16[64,512]{1,0:T(8,128)(2,1)S(1)}, u32[]{:S(2)}, u32[]{:S(2)}) collective-permute-start(bf16[64,512]{1,0:T(8,128)(2,1)S(1)} %pad_maximum_fusion.4.own_second), channel_id=1, source_target_pairs={{0,1},{1,0},{2,3},{3,2},{4,5},{5,4},{6,7},{7,6},{8,9},{9,8},{10,11... | collective-permute-start | bytes 196616 | tf_op jit(solution)/shard_map/ppermute | solution.py:336
  42.6 1.5 %collective-permute-start.10 = (bf16[48,512]{1,0:T(8,128)(2,1)S(1)}, bf16[48,512]{1,0:T(8,128)(2,1)S(1)}, u32[]{:S(2)}, u32[]{:S(2)}) collective-permute-start(bf16[48,512]{1,0:T(8,128)(2,1)S(1)} %reduce-precision_convert_fusion.1.own_first), channel_id=1, source_target_pairs={{0,1},{1,0},{2,3},{3,2},{4,5},{5,4},{6,7},{7,6},{8,9},{9,8},{10,11... | collective-permute-start | bytes 147464 | tf_op jit(solution)/shard_map/ppermute | solution.py:336
  44.1 2.7 %collective-permute-done.10.got_first = bf16[48,512]{1,0:T(8,128)(2,1)S(1)} collective-permute-done((bf16[48,512]{1,0:T(8,128)(2,1)S(1)}, bf16[48,512]{1,0:T(8,128)(2,1)S(1)}, u32[]{:S(2)}, u32[]{:S(2)}) %collective-permute-start.10) | collective-permute-done | bytes 49184 | tf_op jit(solution)/shard_map/ppermute | solution.py:336
  46.7 0.7 %shard_map.135 = (f32[96,512]{1,0:T(8,128)}, f32[16,512]{1,0:T(8,128)}) custom-call(bf16[48,512]{1,0:T(8,128)(2,1)S(1)} %reduce-precision_convert_fusion.1.own_first, bf16[64,512]{1,0:T(8,128)(2,1)S(1)} %pad_maximum_fusion.4.own_second, bf16[48,512]{1,0:T(8,128)(2,1)S(1)} %collective-permute-done.10.got_first, ...), custom_call_target="tpu_custom_call" | custom-call | tf_op jit(solution)/shard_map/pallas_call | solution.py:389
  (26 shorter events, 1.4 us)
Async XLA Ops:
  2.0 13.9 %all-to-all-start = ((f32[16,1,384]{2,1,0:T(1,128)}), f32[16,1,384]{2,1,0:T(1,128)S(1)}, u32[]{:S(2)}, u32[]{:S(2)}) async-start(f32[16,1,384]{2,1,0:T(1,128)} %shard_map.131), calls=%async_computation | async-start | bytes 49152 | tf_op jit(solution)/shard_map/all_to_all | solution.py:464
  10.9 1.4 %copy-start = (bf16[1536,512]{1,0:T(8,128)(2,1)S(1)}, bf16[1536,512]{1,0:T(8,128)(2,1)}, u32[]{:S(2)}) copy-start(bf16[1536,512]{1,0:T(8,128)(2,1)} %conv_two_ref.3) | copy-start | bytes 4718596
  12.3 1.0 %copy-start.2 = (bf16[16,32,512]{2,1,0:T(8,128)(2,1)S(1)}, bf16[16,32,512]{2,1,0:T(8,128)(2,1)}, u32[]{:S(2)}) copy-start(bf16[16,32,512]{2,1,0:T(8,128)(2,1)} %param.15) | copy-start | bytes 1572868
  13.3 2.6 %copy-start.1 = (bf16[1536,512]{1,0:T(8,128)(2,1)S(1)}, bf16[1536,512]{1,0:T(8,128)(2,1)}, u32[]{:S(2)}) copy-start(bf16[1536,512]{1,0:T(8,128)(2,1)} %conv_two_ref.3) | copy-start | bytes 4718596
  22.3 2.4 %collective-permute-start = (bf16[768,512]{1,0:T(8,128)(2,1)S(1)}, bf16[768,512]{1,0:T(8,128)(2,1)S(1)}, u32[]{:S(2)}, u32[]{:S(2)}) collective-permute-start(bf16[768,512]{1,0:T(8,128)(2,1)S(1)} %get-tuple-element.12), channel_id=1, source_target_pairs={{0,2},{2,0},{4,6},{6,4},{8,10},{10,8},{12,14},{14,12},{16,18},{18,... | collective-permute-start | bytes 2359304 | tf_op jit(solution)/shard_map/ppermute | solution.py:336
  22.4 2.3 %collective-permute-start.4 = (f32[16,512]{1,0:T(8,128)S(1)}, f32[16,512]{1,0:T(8,128)S(1)}, u32[]{:S(2)}, u32[]{:S(2)}) collective-permute-start(f32[16,512]{1,0:T(8,128)S(1)} %get-tuple-element.14), channel_id=1, source_target_pairs={{0,2},{2,0},{4,6},{6,4},{8,10},{10,8},{12,14},{14,12},{16,18},{18,... | collective-permute-start | bytes 98312 | tf_op jit(solution)/shard_map/ppermute | solution.py:336
  25.1 6.1 %collective-permute-start.5 = (bf16[112,512]{1,0:T(8,128)(2,1)S(1)}, bf16[112,512]{1,0:T(8,128)(2,1)S(1)}, u32[]{:S(2)}, u32[]{:S(2)}) collective-permute-start(bf16[112,512]{1,0:T(8,128)(2,1)S(1)} %get-tuple-element.28), channel_id=1, source_target_pairs={{0,8},{2,10},{4,12},{6,14},{8,0},{10,2},{12,4},{14,6},{16,24},{18,... | collective-permute-start | bytes 344072 | tf_op jit(solution)/shard_map/ppermute | solution.py:336
  25.9 6.9 %collective-permute-start.6 = (bf16[112,512]{1,0:T(8,128)(2,1)S(1)}, bf16[112,512]{1,0:T(8,128)(2,1)S(1)}, u32[]{:S(2)}, u32[]{:S(2)}) collective-permute-start(bf16[112,512]{1,0:T(8,128)(2,1)S(1)} %get-tuple-element.29), channel_id=1, source_target_pairs={{0,4},{2,6},{4,0},{6,2},{8,12},{10,14},{12,8},{14,10},{16,20},{18,... | collective-permute-start | bytes 344072 | tf_op jit(solution)/shard_map/ppermute | solution.py:336
  27.4 7.0 %collective-permute-start.7 = (bf16[112,512]{1,0:T(8,128)(2,1)S(1)}, bf16[112,512]{1,0:T(8,128)(2,1)S(1)}, u32[]{:S(2)}, u32[]{:S(2)}) collective-permute-start(bf16[112,512]{1,0:T(8,128)(2,1)S(1)} %get-tuple-element.30), channel_id=1, source_target_pairs={{0,12},{2,14},{4,8},{6,10},{8,4},{10,6},{12,0},{14,2},{16,28},{18,... | collective-permute-start | bytes 344072 | tf_op jit(solution)/shard_map/ppermute | solution.py:336
  28.7 8.8 %collective-permute-start.1 = (bf16[96,512]{1,0:T(8,128)(2,1)S(1)}, bf16[96,512]{1,0:T(8,128)(2,1)S(1)}, u32[]{:S(2)}, u32[]{:S(2)}) collective-permute-start(bf16[96,512]{1,0:T(8,128)(2,1)S(1)} %get-tuple-element.27), channel_id=1, source_target_pairs={{0,8},{2,10},{4,12},{6,14},{8,0},{10,2},{12,4},{14,6},{16,24},{18,... | collective-permute-start | bytes 294920 | tf_op jit(solution)/shard_map/ppermute | solution.py:336
  29.4 8.1 %collective-permute-start.2 = (bf16[96,512]{1,0:T(8,128)(2,1)S(1)}, bf16[96,512]{1,0:T(8,128)(2,1)S(1)}, u32[]{:S(2)}, u32[]{:S(2)}) collective-permute-start(bf16[96,512]{1,0:T(8,128)(2,1)S(1)} %get-tuple-element.26), channel_id=1, source_target_pairs={{0,4},{2,6},{4,0},{6,2},{8,12},{10,14},{12,8},{14,10},{16,20},{18,... | collective-permute-start | bytes 294920 | tf_op jit(solution)/shard_map/ppermute | solution.py:336
  31.2 7.3 %collective-permute-start.3 = (bf16[96,512]{1,0:T(8,128)(2,1)S(1)}, bf16[96,512]{1,0:T(8,128)(2,1)S(1)}, u32[]{:S(2)}, u32[]{:S(2)}) collective-permute-start(bf16[96,512]{1,0:T(8,128)(2,1)S(1)} %get-tuple-element.25), channel_id=1, source_target_pairs={{0,12},{2,14},{4,8},{6,10},{8,4},{10,6},{12,0},{14,2},{16,28},{18,... | collective-permute-start | bytes 294920 | tf_op jit(solution)/shard_map/ppermute | solution.py:336
  34.5 6.4 %collective-permute-start.9 = (bf16[64,512]{1,0:T(8,128)(2,1)S(1)}, bf16[64,512]{1,0:T(8,128)(2,1)S(1)}, u32[]{:S(2)}, u32[]{:S(2)}) collective-permute-start(bf16[64,512]{1,0:T(8,128)(2,1)S(1)} %pad_maximum_fusion.3), channel_id=1, source_target_pairs={{0,16},{2,18},{4,20},{6,22},{8,24},{10,26},{12,28},{14,30},{16,0},... | collective-permute-start | bytes 196616 | tf_op jit(solution)/shard_map/ppermute | solution.py:336
  36.9 5.6 %collective-permute-start.8 = (bf16[48,512]{1,0:T(8,128)(2,1)S(1)}, bf16[48,512]{1,0:T(8,128)(2,1)S(1)}, u32[]{:S(2)}, u32[]{:S(2)}) collective-permute-start(bf16[48,512]{1,0:T(8,128)(2,1)S(1)} %slice.89), channel_id=1, source_target_pairs={{0,16},{2,18},{4,20},{6,22},{8,24},{10,26},{12,28},{14,30},{16,0},... | collective-permute-start | bytes 147464 | tf_op jit(solution)/shard_map/ppermute | solution.py:336
  41.0 5.8 %collective-permute-start.11 = (bf16[64,512]{1,0:T(8,128)(2,1)S(1)}, bf16[64,512]{1,0:T(8,128)(2,1)S(1)}, u32[]{:S(2)}, u32[]{:S(2)}) collective-permute-start(bf16[64,512]{1,0:T(8,128)(2,1)S(1)} %pad_maximum_fusion.4.own_second), channel_id=1, source_target_pairs={{0,1},{1,0},{2,3},{3,2},{4,5},{5,4},{6,7},{7,6},{8,9},{9,8},{10,11... | collective-permute-start | bytes 196616 | tf_op jit(solution)/shard_map/ppermute | solution.py:336
  42.6 4.2 %collective-permute-start.10 = (bf16[48,512]{1,0:T(8,128)(2,1)S(1)}, bf16[48,512]{1,0:T(8,128)(2,1)S(1)}, u32[]{:S(2)}, u32[]{:S(2)}) collective-permute-start(bf16[48,512]{1,0:T(8,128)(2,1)S(1)} %reduce-precision_convert_fusion.1.own_first), channel_id=1, source_target_pairs={{0,1},{1,0},{2,3},{3,2},{4,5},{5,4},{6,7},{7,6},{8,9},{9,8},{10,11... | collective-permute-start | bytes 147464 | tf_op jit(solution)/shard_map/ppermute | solution.py:336

commit v14 on v11

--- a/solution.py
+++ b/solution.py
@@ -355,17 +355,23 @@
 
 
 def near_kernel(own_ref, *refs):
-    terms = [own_ref[...]] + [ref[...].astype(F32) for ref in refs[:-1]]
-    refs[-1][...] = tree(terms)
-
-
-def near_sum(own, *got):
+    terms = [own_ref[...]] + [ref[...].astype(F32) for ref in refs[:-2]]
+    total = tree(terms)
+    cut = refs[-2].shape[0]
+    refs[-2][...] = total[:cut]
+    refs[-1][...] = total[cut:]
+
+
+def near_sum(cut, own, *got):
     vmem = pl.BlockSpec(memory_space=pltpu.VMEM)
     return pl.pallas_call(
         near_kernel,
-        out_shape=jax.ShapeDtypeStruct(own.shape, F32),
+        out_shape=(
+            jax.ShapeDtypeStruct((cut, own.shape[1]), F32),
+            jax.ShapeDtypeStruct((own.shape[0] - cut, own.shape[1]), F32),
+        ),
         in_specs=[vmem] * (1 + len(got)),
-        out_specs=vmem,
+        out_specs=(vmem, vmem),
         cost_estimate=pl.CostEstimate(
             flops=4 * own.size, bytes_accessed=140 * own.size, transcendentals=0
         ),
@@ -417,10 +423,10 @@
         nears.append(exchange(sizes, chosen[code], near[code].astype(BF16)))
     cut = own.shape[0] // 2 // ROWS * ROWS
     first, second = (exchange(sizes, [onward], part) for part in (own[:cut], own[cut:]))
-    base = near_sum(near[0], *nears)
-    first = base[:cut] + first.astype(F32)
+    base = near_sum(cut, near[0], *nears)
+    first = base[0] + first.astype(F32)
     second, more = contents(second)
-    second, small = base[cut:] + second, small + more
+    second, small = base[1] + second, small + more
     for bit in left:
         total = jnp.concatenate([first, second], axis=0)
         half = total.shape[0] // 2

time: 50 us -> 48.4 us (0.968)
  waiting for transfers between devices: 14 us -> 11.4 us
  starting transfers between devices: 21.4 us -> 22.5 us
    ppermute x13, waiting for transfers between devices: 11.9 us -> 9.23 us  [exchange(): return lax.ppermute(message, axes if len(axes) > 1 else axes[0], pairs)]
    ppermute x13, starting transfers between devices: 14 us -> 15.1 us  [exchange(): return lax.ppermute(message, axes if len(axes) > 1 else axes[0], pairs)]
where the time goes in v14:
time: 48.4 us; the launch traced here: 48 us
  starting transfers between devices  22.5 us (46%)
  waiting for transfers between devices  11.4 us (24%)
  Pallas kernels  8.91 us (18%)
  local copies, waits for them, and re-layouts  4.02 us (8%)
  between operations  0.79 us (2%)
    ppermute x13, starting transfers between devices, exchange(): return lax.ppermute(message, axes if len(axes) > 1 else axes[0], pairs)  15.1 us
    ppermute x13, waiting for transfers between devices, exchange(): return lax.ppermute(message, axes if len(axes) > 1 else axes[0], pairs)  9.23 us
    all_to_all x1, starting transfers between devices, per_device(): got = lax.all_to_all(packed, 'dp', split_axis=0, concat_axis=0, tiled=True)  7.36 us
    pallas_call x1, Pallas kernels, local_pass(): pl.pallas_call(functools.partial(local_kernel, record, shares), out_shape...  6.36 us
    unnamed x6, local copies, waits for them, and re-layouts  2.45 us
    all_to_all x1, waiting for transfers between devices, per_device(): got = lax.all_to_all(packed, 'dp', split_axis=0, concat_axis=0, tiled=True)  2.15 us
    concatenate x1, local copies, waits for them, and re-layouts, per_device(): table = jnp.concatenate([conv_one.astype(F32), jnp.stack(vectors)], axis=0)  1.52 us
    pallas_call x1, Pallas kernels, pack(): pl.pallas_call(pack_kernel, out_shape=jax.ShapeDtypeStruct((count, 1, wid...  1.37 us
  transfers between devices with their start and end apart: 14, of which 8 were waited for; matrix products, arithmetic and copies ran while one was open for 4% of the time, Pallas kernels for 1%

profile of v14, /device:TPU:0, one launch (start us, length us, event | category | flops | bytes accessed | tf_op | source)
XLA Modules:
  0.0 48.0 jit_solution(13759425465993693661)
XLA Ops:
  0.6 1.4 %shard_map.131 = f32[16,1,384]{2,1,0:T(1,128)} custom-call(s32[1,16]{1,0:T(1,128)} %packing.1, s32[16]{0:T(128)} %bins.1, bf16[16,330]{1,0:T(8,128)(2,1)} %wave_ref.1), custom_call_target="tpu_custom_call" | custom-call | tf_op jit(solution)/shard_map/pallas_call | solution.py:39
  2.0 7.4 %all-to-all-start = ((f32[16,1,384]{2,1,0:T(1,128)}), f32[16,1,384]{2,1,0:T(1,128)S(1)}, u32[]{:S(2)}, u32[]{:S(2)}) async-start(f32[16,1,384]{2,1,0:T(1,128)} %shard_map.131), calls=%async_computation | async-start | bytes 49152 | tf_op jit(solution)/shard_map/all_to_all | solution.py:470
  9.4 1.5 %concatenate.18.table_ref = f32[16,512]{1,0:T(8,128)S(1)} concatenate(bf16[10,512]{1,0:T(8,128)(2,1)} %param.16, f32[1,512]{1,0:T(1,128)} %bitcast.9, f32[1,512]{1,0:T(1,128)} %bitcast.10, f32[1,512]{1,0:T(1,128)} %bitcast.11, f32[1,512]{1,0:T(1,128)} %bitcast.12, f32[1,512]{1,0:T(1,128)} %bitcast.13, f32[1,512]{1,0:T(1,128)} %bitcast.14), dimensions={0} | concatenate | bytes 55296 | tf_op jit(solution)/shard_map/concatenate | solution.py:472
  10.9 1.4 %copy-done = bf16[1536,512]{1,0:T(8,128)(2,1)S(1)} copy-done((bf16[1536,512]{1,0:T(8,128)(2,1)S(1)}, bf16[1536,512]{1,0:T(8,128)(2,1)}, u32[]{:S(2)}) %copy-start) | copy-done | bytes 1572888
  12.3 1.0 %copy-done.2 = bf16[16,32,512]{2,1,0:T(8,128)(2,1)S(1)} copy-done((bf16[16,32,512]{2,1,0:T(8,128)(2,1)S(1)}, bf16[16,32,512]{2,1,0:T(8,128)(2,1)}, u32[]{:S(2)}) %copy-start.2) | copy-done | bytes 524312
  13.8 2.2 %all-to-all-done.got_ref = f32[16,1,384]{2,1,0:T(1,128)S(1)} async-done(((f32[16,1,384]{2,1,0:T(1,128)}), f32[16,1,384]{2,1,0:T(1,128)S(1)}, u32[]{:S(2)}, u32[]{:S(2)}) %all-to-all-start) | async-done | bytes 24608 | tf_op jit(solution)/shard_map/all_to_all | solution.py:470
  15.9 6.4 %shard_map.133 = (bf16[384,512]{1,0:T(8,128)(2,1)S(1)}, bf16[384,512]{1,0:T(8,128)(2,1)S(1)}, f32[384,512]{1,0:T(8,128)S(1)}, f32[384,512]{1,0:T(8,128)S(1)}, f32[16,512]{1,0:T(8,128)S(1)}) custom-call(s32[1]{0:T(128)} %bitcast.place_ref, f32[16,1,384]{2,1,0:T(1,128)S(1)} %all-to-all-done.got_ref, bf16[512,512]{1,0:T(8,128)(2,1)S(1)} %get-tuple-element.11.cot_ref, ...), custom_call_target="tpu_custom_call" | custom-call | flops 2415919104 | bytes 4259840 | tf_op jit(solution)/shard_map/pallas_call | solution.py:293
  22.4 0.5 %collective-permute-start.5 = (f32[16,512]{1,0:T(8,128)S(1)}, f32[16,512]{1,0:T(8,128)S(1)}, u32[]{:S(2)}, u32[]{:S(2)}) collective-permute-start(f32[16,512]{1,0:T(8,128)S(1)} %get-tuple-element.18), channel_id=1, source_target_pairs={{0,2},{2,0},{4,6},{6,4},{8,10},{10,8},{12,14},{14,12},{16,18},{18,... | collective-permute-start | bytes 98312 | tf_op jit(solution)/shard_map/ppermute | solution.py:341
  23.0 1.2 %collective-permute-done.5 = f32[16,512]{1,0:T(8,128)S(1)} collective-permute-done((f32[16,512]{1,0:T(8,128)S(1)}, f32[16,512]{1,0:T(8,128)S(1)}, u32[]{:S(2)}, u32[]{:S(2)}) %collective-permute-start.5) | collective-permute-done | bytes 32800 | tf_op jit(solution)/shard_map/ppermute | solution.py:341
  24.4 1.7 %collective-permute-start.8 = (bf16[112,512]{1,0:T(8,128)(2,1)S(1)}, bf16[112,512]{1,0:T(8,128)(2,1)S(1)}, u32[]{:S(2)}, u32[]{:S(2)}) collective-permute-start(bf16[112,512]{1,0:T(8,128)(2,1)S(1)} %get-tuple-element.34), channel_id=1, source_target_pairs={{0,12},{2,14},{4,8},{6,10},{8,4},{10,6},{12,0},{14,2},{16,28},{18,... | collective-permute-start | bytes 344072 | tf_op jit(solution)/shard_map/ppermute | solution.py:341
  26.0 0.6 %collective-permute-start.7 = (bf16[112,512]{1,0:T(8,128)(2,1)S(1)}, bf16[112,512]{1,0:T(8,128)(2,1)S(1)}, u32[]{:S(2)}, u32[]{:S(2)}) collective-permute-start(bf16[112,512]{1,0:T(8,128)(2,1)S(1)} %get-tuple-element.33), channel_id=1, source_target_pairs={{0,4},{2,6},{4,0},{6,2},{8,12},{10,14},{12,8},{14,10},{16,20},{18,... | collective-permute-start | bytes 344072 | tf_op jit(solution)/shard_map/ppermute | solution.py:341
  26.6 1.3 %collective-permute-start.6 = (bf16[112,512]{1,0:T(8,128)(2,1)S(1)}, bf16[112,512]{1,0:T(8,128)(2,1)S(1)}, u32[]{:S(2)}, u32[]{:S(2)}) collective-permute-start(bf16[112,512]{1,0:T(8,128)(2,1)S(1)} %get-tuple-element.32), channel_id=1, source_target_pairs={{0,8},{2,10},{4,12},{6,14},{8,0},{10,2},{12,4},{14,6},{16,24},{18,... | collective-permute-start | bytes 344072 | tf_op jit(solution)/shard_map/ppermute | solution.py:341
  28.1 0.8 %collective-permute-start.1 = (bf16[96,512]{1,0:T(8,128)(2,1)S(1)}, bf16[96,512]{1,0:T(8,128)(2,1)S(1)}, u32[]{:S(2)}, u32[]{:S(2)}) collective-permute-start(bf16[96,512]{1,0:T(8,128)(2,1)S(1)} %get-tuple-element.31), channel_id=1, source_target_pairs={{0,8},{2,10},{4,12},{6,14},{8,0},{10,2},{12,4},{14,6},{16,24},{18,... | collective-permute-start | bytes 294920 | tf_op jit(solution)/shard_map/ppermute | solution.py:341
  28.9 1.5 %collective-permute-start.2 = (bf16[96,512]{1,0:T(8,128)(2,1)S(1)}, bf16[96,512]{1,0:T(8,128)(2,1)S(1)}, u32[]{:S(2)}, u32[]{:S(2)}) collective-permute-start(bf16[96,512]{1,0:T(8,128)(2,1)S(1)} %get-tuple-element.30), channel_id=1, source_target_pairs={{0,4},{2,6},{4,0},{6,2},{8,12},{10,14},{12,8},{14,10},{16,20},{18,... | collective-permute-start | bytes 294920 | tf_op jit(solution)/shard_map/ppermute | solution.py:341
  30.3 1.0 %collective-permute-done.8 = bf16[112,512]{1,0:T(8,128)(2,1)S(1)} collective-permute-done((bf16[112,512]{1,0:T(8,128)(2,1)S(1)}, bf16[112,512]{1,0:T(8,128)(2,1)S(1)}, u32[]{:S(2)}, u32[]{:S(2)}) %collective-permute-start.8) | collective-permute-done | bytes 114720 | tf_op jit(solution)/shard_map/ppermute | solution.py:341
  31.3 1.6 %collective-permute-start.3 = (bf16[96,512]{1,0:T(8,128)(2,1)S(1)}, bf16[96,512]{1,0:T(8,128)(2,1)S(1)}, u32[]{:S(2)}, u32[]{:S(2)}) collective-permute-start(bf16[96,512]{1,0:T(8,128)(2,1)S(1)} %get-tuple-element.29), channel_id=1, source_target_pairs={{0,12},{2,14},{4,8},{6,10},{8,4},{10,6},{12,0},{14,2},{16,28},{18,... | collective-permute-start | bytes 294920 | tf_op jit(solution)/shard_map/ppermute | solution.py:341
  33.2 2.4 %collective-permute-start.10 = (bf16[64,512]{1,0:T(8,128)(2,1)S(1)}, bf16[64,512]{1,0:T(8,128)(2,1)S(1)}, u32[]{:S(2)}, u32[]{:S(2)}) collective-permute-start(bf16[64,512]{1,0:T(8,128)(2,1)S(1)} %pad_maximum_fusion.3), channel_id=1, source_target_pairs={{0,16},{2,18},{4,20},{6,22},{8,24},{10,26},{12,28},{14,30},{16,0},... | collective-permute-start | bytes 196616 | tf_op jit(solution)/shard_map/ppermute | solution.py:341
  35.9 2.0 %collective-permute-done.3.refs_2_ = bf16[96,512]{1,0:T(8,128)(2,1)S(1)} collective-permute-done((bf16[96,512]{1,0:T(8,128)(2,1)S(1)}, bf16[96,512]{1,0:T(8,128)(2,1)S(1)}, u32[]{:S(2)}, u32[]{:S(2)}) %collective-permute-start.3) | collective-permute-done | bytes 98336 | tf_op jit(solution)/shard_map/ppermute | solution.py:341
  37.9 1.5 %collective-permute-start.9 = (bf16[48,512]{1,0:T(8,128)(2,1)S(1)}, bf16[48,512]{1,0:T(8,128)(2,1)S(1)}, u32[]{:S(2)}, u32[]{:S(2)}) collective-permute-start(bf16[48,512]{1,0:T(8,128)(2,1)S(1)} %slice.89), channel_id=1, source_target_pairs={{0,16},{2,18},{4,20},{6,22},{8,24},{10,26},{12,28},{14,30},{16,0},... | collective-permute-start | bytes 147464 | tf_op jit(solution)/shard_map/ppermute | solution.py:341
  39.5 1.6 %collective-permute-start.12 = (bf16[64,512]{1,0:T(8,128)(2,1)S(1)}, bf16[64,512]{1,0:T(8,128)(2,1)S(1)}, u32[]{:S(2)}, u32[]{:S(2)}) collective-permute-start(bf16[64,512]{1,0:T(8,128)(2,1)S(1)} %pad_maximum_fusion.4.own_second), channel_id=1, source_target_pairs={{0,1},{1,0},{2,3},{3,2},{4,5},{5,4},{6,7},{7,6},{8,9},{9,8},{10,11... | collective-permute-start | bytes 196616 | tf_op jit(solution)/shard_map/ppermute | solution.py:341
  41.1 2.1 %collective-permute-done.9 = bf16[48,512]{1,0:T(8,128)(2,1)S(1)} collective-permute-done((bf16[48,512]{1,0:T(8,128)(2,1)S(1)}, bf16[48,512]{1,0:T(8,128)(2,1)S(1)}, u32[]{:S(2)}, u32[]{:S(2)}) %collective-permute-start.9) | collective-permute-done | bytes 49184 | tf_op jit(solution)/shard_map/ppermute | solution.py:341
  43.2 1.6 %collective-permute-start.11 = (bf16[48,512]{1,0:T(8,128)(2,1)S(1)}, bf16[48,512]{1,0:T(8,128)(2,1)S(1)}, u32[]{:S(2)}, u32[]{:S(2)}) collective-permute-start(bf16[48,512]{1,0:T(8,128)(2,1)S(1)} %reduce-precision_convert_fusion.1.own_first), channel_id=1, source_target_pairs={{0,1},{1,0},{2,3},{3,2},{4,5},{5,4},{6,7},{7,6},{8,9},{9,8},{10,11... | collective-permute-start | bytes 147464 | tf_op jit(solution)/shard_map/ppermute | solution.py:341
  44.7 2.6 %collective-permute-done.11.got_first = bf16[48,512]{1,0:T(8,128)(2,1)S(1)} collective-permute-done((bf16[48,512]{1,0:T(8,128)(2,1)S(1)}, bf16[48,512]{1,0:T(8,128)(2,1)S(1)}, u32[]{:S(2)}, u32[]{:S(2)}) %collective-permute-start.11) | collective-permute-done | bytes 49184 | tf_op jit(solution)/shard_map/ppermute | solution.py:341
  47.3 0.7 %shard_map.135 = (f32[96,512]{1,0:T(8,128)}, f32[16,512]{1,0:T(8,128)}) custom-call(bf16[48,512]{1,0:T(8,128)(2,1)S(1)} %reduce-precision_convert_fusion.1.own_first, bf16[64,512]{1,0:T(8,128)(2,1)S(1)} %pad_maximum_fusion.4.own_second, bf16[48,512]{1,0:T(8,128)(2,1)S(1)} %collective-permute-done.11.got_first, ...), custom_call_target="tpu_custom_call" | custom-call | tf_op jit(solution)/shard_map/pallas_call | solution.py:394
  (31 shorter events, 1.5 us)
Async XLA Ops:
  2.0 13.9 %all-to-all-start = ((f32[16,1,384]{2,1,0:T(1,128)}), f32[16,1,384]{2,1,0:T(1,128)S(1)}, u32[]{:S(2)}, u32[]{:S(2)}) async-start(f32[16,1,384]{2,1,0:T(1,128)} %shard_map.131), calls=%async_computation | async-start | bytes 49152 | tf_op jit(solution)/shard_map/all_to_all | solution.py:470
  10.9 1.4 %copy-start = (bf16[1536,512]{1,0:T(8,128)(2,1)S(1)}, bf16[1536,512]{1,0:T(8,128)(2,1)}, u32[]{:S(2)}) copy-start(bf16[1536,512]{1,0:T(8,128)(2,1)} %conv_two_ref.3) | copy-start | bytes 4718596
  12.3 1.0 %copy-start.2 = (bf16[16,32,512]{2,1,0:T(8,128)(2,1)S(1)}, bf16[16,32,512]{2,1,0:T(8,128)(2,1)}, u32[]{:S(2)}) copy-start(bf16[16,32,512]{2,1,0:T(8,128)(2,1)} %param.15) | copy-start | bytes 1572868
  13.3 2.6 %copy-start.1 = (bf16[1536,512]{1,0:T(8,128)(2,1)S(1)}, bf16[1536,512]{1,0:T(8,128)(2,1)}, u32[]{:S(2)}) copy-start(bf16[1536,512]{1,0:T(8,128)(2,1)} %conv_two_ref.3) | copy-start | bytes 4718596
  22.3 1.8 %collective-permute-start.4 = (bf16[384,512]{1,0:T(8,128)(2,1)S(1)}, bf16[384,512]{1,0:T(8,128)(2,1)S(1)}, u32[]{:S(2)}, u32[]{:S(2)}) collective-permute-start(bf16[384,512]{1,0:T(8,128)(2,1)S(1)} %get-tuple-element.17), channel_id=1, source_target_pairs={{0,2},{2,0},{4,6},{6,4},{8,10},{10,8},{12,14},{14,12},{16,18},{18,... | collective-permute-start | bytes 1179656 | tf_op jit(solution)/shard_map/ppermute | solution.py:341
  22.4 1.8 %collective-permute-start.5 = (f32[16,512]{1,0:T(8,128)S(1)}, f32[16,512]{1,0:T(8,128)S(1)}, u32[]{:S(2)}, u32[]{:S(2)}) collective-permute-start(f32[16,512]{1,0:T(8,128)S(1)} %get-tuple-element.18), channel_id=1, source_target_pairs={{0,2},{2,0},{4,6},{6,4},{8,10},{10,8},{12,14},{14,12},{16,18},{18,... | collective-permute-start | bytes 98312 | tf_op jit(solution)/shard_map/ppermute | solution.py:341
  22.9 5.0 %collective-permute-start = (bf16[384,512]{1,0:T(8,128)(2,1)S(1)}, bf16[384,512]{1,0:T(8,128)(2,1)S(1)}, u32[]{:S(2)}, u32[]{:S(2)}) collective-permute-start(bf16[384,512]{1,0:T(8,128)(2,1)S(1)} %get-tuple-element.14), channel_id=1, source_target_pairs={{0,2},{2,0},{4,6},{6,4},{8,10},{10,8},{12,14},{14,12},{16,18},{18,... | collective-permute-start | bytes 1179656 | tf_op jit(solution)/shard_map/ppermute | solution.py:341
  24.4 7.0 %collective-permute-start.8 = (bf16[112,512]{1,0:T(8,128)(2,1)S(1)}, bf16[112,512]{1,0:T(8,128)(2,1)S(1)}, u32[]{:S(2)}, u32[]{:S(2)}) collective-permute-start(bf16[112,512]{1,0:T(8,128)(2,1)S(1)} %get-tuple-element.34), channel_id=1, source_target_pairs={{0,12},{2,14},{4,8},{6,10},{8,4},{10,6},{12,0},{14,2},{16,28},{18,... | collective-permute-start | bytes 344072 | tf_op jit(solution)/shard_map/ppermute | solution.py:341
  26.0 7.0 %collective-permute-start.7 = (bf16[112,512]{1,0:T(8,128)(2,1)S(1)}, bf16[112,512]{1,0:T(8,128)(2,1)S(1)}, u32[]{:S(2)}, u32[]{:S(2)}) collective-permute-start(bf16[112,512]{1,0:T(8,128)(2,1)S(1)} %get-tuple-element.33), channel_id=1, source_target_pairs={{0,4},{2,6},{4,0},{6,2},{8,12},{10,14},{12,8},{14,10},{16,20},{18,... | collective-permute-start | bytes 344072 | tf_op jit(solution)/shard_map/ppermute | solution.py:341
  26.6 6.5 %collective-permute-start.6 = (bf16[112,512]{1,0:T(8,128)(2,1)S(1)}, bf16[112,512]{1,0:T(8,128)(2,1)S(1)}, u32[]{:S(2)}, u32[]{:S(2)}) collective-permute-start(bf16[112,512]{1,0:T(8,128)(2,1)S(1)} %get-tuple-element.32), channel_id=1, source_target_pairs={{0,8},{2,10},{4,12},{6,14},{8,0},{10,2},{12,4},{14,6},{16,24},{18,... | collective-permute-start | bytes 344072 | tf_op jit(solution)/shard_map/ppermute | solution.py:341
  28.1 7.5 %collective-permute-start.1 = (bf16[96,512]{1,0:T(8,128)(2,1)S(1)}, bf16[96,512]{1,0:T(8,128)(2,1)S(1)}, u32[]{:S(2)}, u32[]{:S(2)}) collective-permute-start(bf16[96,512]{1,0:T(8,128)(2,1)S(1)} %get-tuple-element.31), channel_id=1, source_target_pairs={{0,8},{2,10},{4,12},{6,14},{8,0},{10,2},{12,4},{14,6},{16,24},{18,... | collective-permute-start | bytes 294920 | tf_op jit(solution)/shard_map/ppermute | solution.py:341
  28.9 7.0 %collective-permute-start.2 = (bf16[96,512]{1,0:T(8,128)(2,1)S(1)}, bf16[96,512]{1,0:T(8,128)(2,1)S(1)}, u32[]{:S(2)}, u32[]{:S(2)}) collective-permute-start(bf16[96,512]{1,0:T(8,128)(2,1)S(1)} %get-tuple-element.30), channel_id=1, source_target_pairs={{0,4},{2,6},{4,0},{6,2},{8,12},{10,14},{12,8},{14,10},{16,20},{18,... | collective-permute-start | bytes 294920 | tf_op jit(solution)/shard_map/ppermute | solution.py:341
  31.3 6.6 %collective-permute-start.3 = (bf16[96,512]{1,0:T(8,128)(2,1)S(1)}, bf16[96,512]{1,0:T(8,128)(2,1)S(1)}, u32[]{:S(2)}, u32[]{:S(2)}) collective-permute-start(bf16[96,512]{1,0:T(8,128)(2,1)S(1)} %get-tuple-element.29), channel_id=1, source_target_pairs={{0,12},{2,14},{4,8},{6,10},{8,4},{10,6},{12,0},{14,2},{16,28},{18,... | collective-permute-start | bytes 294920 | tf_op jit(solution)/shard_map/ppermute | solution.py:341
  33.2 6.3 %collective-permute-start.10 = (bf16[64,512]{1,0:T(8,128)(2,1)S(1)}, bf16[64,512]{1,0:T(8,128)(2,1)S(1)}, u32[]{:S(2)}, u32[]{:S(2)}) collective-permute-start(bf16[64,512]{1,0:T(8,128)(2,1)S(1)} %pad_maximum_fusion.3), channel_id=1, source_target_pairs={{0,16},{2,18},{4,20},{6,22},{8,24},{10,26},{12,28},{14,30},{16,0},... | collective-permute-start | bytes 196616 | tf_op jit(solution)/shard_map/ppermute | solution.py:341
  37.9 5.2 %collective-permute-start.9 = (bf16[48,512]{1,0:T(8,128)(2,1)S(1)}, bf16[48,512]{1,0:T(8,128)(2,1)S(1)}, u32[]{:S(2)}, u32[]{:S(2)}) collective-permute-start(bf16[48,512]{1,0:T(8,128)(2,1)S(1)} %slice.89), channel_id=1, source_target_pairs={{0,16},{2,18},{4,20},{6,22},{8,24},{10,26},{12,28},{14,30},{16,0},... | collective-permute-start | bytes 147464 | tf_op jit(solution)/shard_map/ppermute | solution.py:341
  39.5 7.8 %collective-permute-start.12 = (bf16[64,512]{1,0:T(8,128)(2,1)S(1)}, bf16[64,512]{1,0:T(8,128)(2,1)S(1)}, u32[]{:S(2)}, u32[]{:S(2)}) collective-permute-start(bf16[64,512]{1,0:T(8,128)(2,1)S(1)} %pad_maximum_fusion.4.own_second), channel_id=1, source_target_pairs={{0,1},{1,0},{2,3},{3,2},{4,5},{5,4},{6,7},{7,6},{8,9},{9,8},{10,11... | collective-permute-start | bytes 196616 | tf_op jit(solution)/shard_map/ppermute | solution.py:341
  43.2 4.2 %collective-permute-start.11 = (bf16[48,512]{1,0:T(8,128)(2,1)S(1)}, bf16[48,512]{1,0:T(8,128)(2,1)S(1)}, u32[]{:S(2)}, u32[]{:S(2)}) collective-permute-start(bf16[48,512]{1,0:T(8,128)(2,1)S(1)} %reduce-precision_convert_fusion.1.own_first), channel_id=1, source_target_pairs={{0,1},{1,0},{2,3},{3,2},{4,5},{5,4},{6,7},{7,6},{8,9},{9,8},{10,11... | collective-permute-start | bytes 147464 | tf_op jit(solution)/shard_map/ppermute | solution.py:341
